TPU v7x, 32 devices: a whole 2x2x4 slice. The times are simulated.
32 devices in a mesh: orb: 8 (over z, x), wall: 4 (over y, core).
Axes of the slice: x: 2, y: 2, z: 4, core: 2. Of those that a mesh axis runs over, the one named last changes fastest.
Arguments:
- fluid_state: float32 [8, 98304], P(None, ('orb', 'wall')), may hold values from -4 to 4, as said below
- ghost_list: int32 [7, 192], P(None, ('orb', 'wall')), may hold values from 0 to 23, as said below
- pair_list: int32 [768, 14], P(('orb', 'wall')), may hold values from 0 to 65, as said below
- wall_state: float32 [4, 24576], P(None, ('orb', 'wall')), may hold values from 0 to 0.6, as said below
- wall_count: int32 [192], P(('orb', 'wall')), may hold values from 1 to 128, as said below
- wall_pairs: int32 [768, 4], P(('orb', 'wall')), may hold values from 0 to 7, as said below
Outputs:
- density_rate: float32 [98304], P(('orb', 'wall'))
- acceleration: float32 [3, 98304], P(None, ('orb', 'wall'))
- time_step: float32 [], replicated
Inputs may be any that keep to these rules, and one draw needn't show every extreme that they name: `fluid_state`: rows: position from 0 to 0.6, velocity from -4 to 4, density from 0.97 to 1.03, mass from 0.001 to 0.003. `ghost_list`: the 6 entries of one mask and one domain are distinct. `pair_list`: the 14 entries of one block are distinct, and every candidate index is named by some block of each domain. `wall_state`: rows: x and y from 0 to 0.6, z from 0 to 0.15, mass from 0.001 to 0.003. `wall_count`: the live particles fill the first columns of their wall block. `wall_pairs`: the 4 entries of one block are distinct, and every wall candidate index is named by some block of each domain.
All inputs are finite; a program needn't handle non-finite values.
Results may differ from a plain program's by a relative error of at most 0.0003.
Values sent between devices are 32-bit elements; how exact they have to be, the bound alone decides.
No kernel may reach another device: no remote copies, remote signals or barrier semaphores. Data moves between devices by JAX's collectives and lax.ppermute only.
A program may use at most 64 MiB of HBM per device.

v0:
```python
import functools

import jax
import jax.numpy as jnp
import numpy as np
from jax import lax
from jax.experimental import pallas as pl
from jax.experimental.pallas import tpu as pltpu
from jax.sharding import PartitionSpec as P

EB = 1
LANES = 128
ROWS = 8
PIECES = 6 * ROWS
DEPTH = 80
MOMENTS = 4 * ROWS
UNROLL = 4

smoothing = 0.1
support = 0.3
kernel_norm = 21.0 / (2.0 * 3.141592653589793 * support**3)
grad_coeff = -20.0 / support**2 * kernel_norm
tait_coeff = 25.0 / 7.0
visc_coeff = 0.05
cohesion = 2000.0
adhesion = 2000.0
gravity = 9.81
courant = 0.25

center = 0.3
shift = 0.0001 / support**2
press_coeff = -grad_coeff / (4.0 * cohesion)
density_coeff = (support * 4.0 * cohesion) / (-grad_coeff * visc_coeff * 2.0)

SPLITS = ((0, 0), (0, 1), (1, 0), (0, 2), (2, 0), (1, 1), (1, 2), (2, 1))


def y_row(piece, row):
    return piece * ROWS + row


def z_row(piece, row):
    return (3 + piece) * ROWS + row


def selections():
    source = np.zeros((2 * DEPTH, PIECES), np.float32)
    target = np.zeros((PIECES, 4 * LANES), np.float32)
    one = z_row(0, 6)
    k = 0
    for p in range(3):
        for d in range(3):
            target[one, k] = 1.0
            source[k, z_row(p, d)] = 1.0
            source[DEPTH + k, z_row(p, 3 + d)] = -1.0
            target[z_row(p, d), k + 9] = 1.0
            source[k + 9, one] = 1.0
            target[z_row(p, 3 + d), k + 18] = 1.0
            source[DEPTH + k + 18, one] = -1.0
            k += 1
    k = 27
    for d in range(3):
        for p, t in SPLITS:
            target[y_row(p, d), k] = 1.0
            source[k, y_row(t, d)] = -2.0
            source[DEPTH + k, y_row(t, 3 + d)] = 1.0
            target[y_row(p, 3 + d), k + 24] = 1.0
            source[DEPTH + k + 24, y_row(t, d)] = 1.0
            k += 1
    for p in range(3):
        target[y_row(p, 6), LANES : 2 * LANES] = 1.0
        target[z_row(p, 7), 2 * LANES : 3 * LANES] = 1.0
        target[z_row(p, 7), 3 * LANES :] = 2.0 * cohesion / adhesion
    target[one, 2 * LANES :] = -0.75
    return jnp.asarray(source, jnp.bfloat16), jnp.asarray(target, jnp.bfloat16)


def split(value):
    first = value.astype(jnp.bfloat16).astype(jnp.float32)
    rest = value - first
    second = rest.astype(jnp.bfloat16).astype(jnp.float32)
    return [first, second, rest - second]


def pressure_ratio(density):
    square = density * density
    return tait_coeff * (square * square * square * density - 1.0) / square


def row_index():
    return lax.broadcasted_iota(jnp.int32, (ROWS, LANES), 0)


def state_of(block):
    row = row_index()
    y = jnp.where(row < 3, (block - center) * (1.0 / support), block)
    y = jnp.where(row == 6, block * density_coeff, y)
    density = jnp.where(row == 7, pltpu.roll(block, 1, axis=0), 1.0)
    press = press_coeff * pressure_ratio(density)
    z = y * jnp.where(row < 3, y, pltpu.roll(y, 3, axis=0))
    return y, jnp.where(row < 6, z, jnp.where(row == 6, 1.0, press))


def pieces_of(y, z):
    return jnp.concatenate(split(y) + split(z), axis=0)


def put_source(block, choice, s, src, mom, ys, zs, mass_factor=1.0):
    row = row_index()
    y, z = state_of(block)
    pieces = pieces_of(y, z).astype(jnp.bfloat16)
    chosen = jnp.dot(choice, pieces, preferred_element_type=jnp.float32).astype(jnp.bfloat16)
    src[s] = jnp.concatenate([chosen[:DEPTH], chosen[DEPTH:]], axis=1)
    moment = (mass_factor * block[7:8]) * jnp.where(row == 6, 1.0, y)
    rows = split(moment) + [jnp.zeros_like(moment)]
    moments = jnp.concatenate(rows, axis=0).astype(jnp.bfloat16)
    mom[s] = jnp.concatenate([moments, moments], axis=1)
    ys[s] = y
    zs[s] = z
    return y, z


def put_target(y, z, choice, b, tgt, wide):
    pieces = pieces_of(y, z).T.astype(jnp.bfloat16)
    chosen = jnp.dot(pieces, choice, preferred_element_type=jnp.float32)
    tgt[b] = chosen[:, :DEPTH].astype(jnp.bfloat16)
    for n in range(3):
        wide[b, n] = chosen[:, (n + 1) * LANES : (n + 2) * LANES]


def rows_at(index):
    return pl.ds(pl.multiple_of(index * ROWS, ROWS), ROWS)


def weights_of(product, wide, n_wide, y, z):
    guarded = jnp.maximum(product[:, :LANES], 1e-30)
    approach = product[:, LANES:]
    falloff = jnp.maximum(1.0 - guarded * lax.rsqrt(guarded), 0.0)
    cubed = falloff * falloff * falloff
    blend = falloff + wide[n_wide]
    if z is not None:
        spread = (guarded + shift) * (wide[0] + y[6:7])
        blend += z[7:8]
        blend += jnp.maximum(approach, 0.0) * pl.reciprocal(spread, approx=True)
    weight = cubed * blend
    high = weight.astype(jnp.bfloat16)
    low = (weight - high.astype(jnp.float32)).astype(jnp.bfloat16)
    return jnp.concatenate([high, low], axis=1), (cubed * approach) * y[7:8]


def across(left, right):
    return lax.dot_general(
        left, right, (((1,), (1,)), ((), ())), preferred_element_type=jnp.float32
    )


def run_tiles(target, wide, n_wide, tiles):
    def product_of(tile):
        return jnp.dot(target, tile[0][...], preferred_element_type=jnp.float32)

    total = jnp.zeros((MOMENTS, LANES), jnp.float32)
    rate = jnp.zeros((LANES, LANES), jnp.float32)
    ahead = product_of(tiles[0])
    waiting = None
    for n, (_, moments, y, z) in enumerate(tiles):
        product = ahead
        if n + 1 < len(tiles):
            ahead = product_of(tiles[n + 1])
        weights, part = weights_of(product, wide, n_wide, y, z)
        rate += part
        if waiting is not None:
            total += across(*waiting)
        waiting = (moments[...], weights)
    total += across(*waiting)
    ones = jnp.ones((ROWS, 3 * LANES), jnp.bfloat16)
    rates = across(ones, jnp.concatenate(split(rate), axis=1).astype(jnp.bfloat16))
    return total, rates


def moments_at(b):
    return pl.ds(pl.multiple_of(b * MOMENTS, MOMENTS), MOMENTS)


def own_kernel(
    blocks, walls, own_ref, wall_ref, wpair_ref, choice, target_choice,
    src, mom, ys, zs, tgt, wide, sums, rates, wsrc, wmom, wys, wzs,
):
    def build(b, carry):
        y, z = put_source(own_ref[rows_at(b), :], choice[...], b, src, mom, ys, zs)
        put_target(y, z, target_choice[...], b, tgt, wide)
        return carry

    lax.fori_loop(0, blocks, build, 0, unroll=UNROLL)
    row = row_index()
    for c in range(walls):
        held = wall_ref[4 * c : 4 * c + 4, :]
        both = jnp.concatenate([held, held], axis=0)
        block = jnp.where(
            (row < 3) | (row == 7), both, jnp.where(row == 6, 1.0, 0.0)
        )
        put_source(block, choice[...], c, wsrc, wmom, wys, wzs, adhesion / cohesion)

    def per_target(b, carry):
        tiles = []
        for k in range(wpair_ref.shape[1]):
            s = wpair_ref[b, k]
            tiles.append((wsrc.at[s], wmom.at[s], wys.at[s], None))
        total, rate = run_tiles(tgt[b], wide.at[b], 2, tiles)
        sums[moments_at(b), :] = total
        rates[rows_at(b), :] = rate
        return carry

    lax.fori_loop(0, blocks, per_target, 0, unroll=UNROLL)


def fluid_kernel(
    blocks, own_ref, ghost_ref, pair_ref, place_ref, choice, own_src, own_mom, own_ys, own_zs,
    tgt, wide, own_sums, own_rates, rate_ref, accel_ref, peak_ref,
    src, mom, ys, zs, sums, rates, stage, table,
):
    ghosts = ghost_ref.shape[0] // ROWS
    per_mask = ghosts // 8
    for c in range(blocks):
        table[c] = c
    for mask in range(1, 8):
        for g in range(per_mask):
            table[blocks + (mask - 1) * per_mask + g] = (
                blocks + jnp.bitwise_xor(place_ref[0], mask) * per_mask + g
            )
    src[:blocks] = own_src[...]
    mom[:blocks] = own_mom[...]
    ys[:blocks] = own_ys[...]
    zs[:blocks] = own_zs[...]

    def build(g, carry):
        put_source(ghost_ref[rows_at(g), :], choice[...], blocks + g, src, mom, ys, zs)
        return carry

    lax.fori_loop(0, ghosts, build, 0, unroll=UNROLL)

    def per_target(b, carry):
        tiles = []
        for k in range(pair_ref.shape[1]):
            s = table[pair_ref[b, k]]
            tiles.append((src.at[s], mom.at[s], ys.at[s], zs.at[s]))
        total, rate = run_tiles(tgt[b], wide.at[b], 1, tiles)
        sums[moments_at(b), :] = own_sums[moments_at(b), :] + total
        rates[rows_at(b), :] = own_rates[rows_at(b), :] + rate
        return carry

    lax.fori_loop(0, blocks, per_target, 0)

    rate_ref[...] = (-support * grad_coeff) * rates[pl.ds(0, blocks, stride=ROWS), :]

    def summed(row):
        parts = [sums[pl.ds(y_row(p, row), blocks, stride=MOMENTS), :] for p in range(3)]
        return parts[0] + parts[1] + parts[2]

    mass_sum = summed(6)
    square = jnp.zeros_like(mass_sum)
    for d in range(3):
        pos = (own_ref[pl.ds(d, blocks, stride=ROWS), :] - center) * (1.0 / support)
        force = (4.0 * cohesion * support) * (pos * mass_sum - summed(d))
        if d == 2:
            force -= gravity
        square += force * force
        stage[pl.ds(d, blocks, stride=ROWS), :] = force
    for b in range(blocks):
        accel_ref[:, b * LANES : (b + 1) * LANES] = stage[b * ROWS : b * ROWS + 3, :]
    peak_ref[...] = jnp.full(peak_ref.shape, jnp.sqrt(jnp.max(square)), jnp.float32)


SMEM = pl.BlockSpec(memory_space=pltpu.SMEM)
VMEM = pl.BlockSpec(memory_space=pltpu.VMEM)
PARAMS = pltpu.CompilerParams(vmem_limit_bytes=32 * 1024 * 1024)


def tile_cost(tiles):
    return pl.CostEstimate(
        flops=tiles * LANES * LANES * 1000, bytes_accessed=0, transcendentals=0
    )


def source_shapes(count):
    return [
        ((count, DEPTH, 2 * LANES), jnp.bfloat16),
        ((count, MOMENTS, 2 * LANES), jnp.bfloat16),
        ((count, ROWS, LANES), jnp.float32),
        ((count, ROWS, LANES), jnp.float32),
    ]


def own_pass(own, walls, wall_pairs, choices):
    blocks = own.shape[0] // ROWS
    wall_blocks = walls.shape[0] // 4
    outs = source_shapes(blocks) + [
        ((blocks, LANES, DEPTH), jnp.bfloat16),
        ((blocks, 3, LANES, LANES), jnp.float32),
        ((blocks * MOMENTS, LANES), jnp.float32),
        ((blocks * ROWS, LANES), jnp.float32),
    ]
    return pl.pallas_call(
        functools.partial(own_kernel, blocks, wall_blocks),
        out_shape=[jax.ShapeDtypeStruct(*out) for out in outs],
        in_specs=[VMEM, VMEM, SMEM, VMEM, VMEM],
        out_specs=[VMEM] * len(outs),
        scratch_shapes=[pltpu.VMEM(*shape) for shape in source_shapes(wall_blocks)],
        compiler_params=PARAMS,
        cost_estimate=tile_cost(wall_pairs.size),
        name="own_pass",
    )(own, walls, wall_pairs, *choices)


def fluid_pass(own, ghosts, pair_list, place, choice, own_results):
    blocks = own.shape[0] // ROWS
    total = blocks + ghosts.shape[0] // ROWS
    return pl.pallas_call(
        functools.partial(fluid_kernel, blocks),
        out_shape=(
            jax.ShapeDtypeStruct((blocks, LANES), jnp.float32),
            jax.ShapeDtypeStruct((3, blocks * LANES), jnp.float32),
            jax.ShapeDtypeStruct((ROWS, LANES), jnp.float32),
        ),
        in_specs=[VMEM, VMEM, SMEM, SMEM, VMEM] + [VMEM] * len(own_results),
        out_specs=(VMEM, VMEM, VMEM),
        scratch_shapes=[pltpu.VMEM(*shape) for shape in source_shapes(total)]
        + [
            pltpu.VMEM((blocks * MOMENTS, LANES), jnp.float32),
            pltpu.VMEM((blocks * ROWS, LANES), jnp.float32),
            pltpu.VMEM((blocks * ROWS, LANES), jnp.float32),
            pltpu.SMEM((total,), jnp.int32),
        ],
        compiler_params=PARAMS,
        cost_estimate=tile_cost(pair_list.size),
        name="fluid_pass",
    )(own, ghosts, pair_list, place, choice, *own_results)


def outgoing_kernel(own_ref, list_ref, place_ref, sent_ref):
    for slot in range(8):
        mask = jnp.bitwise_xor(place_ref[0], slot)
        for g in range(list_ref.shape[1]):
            block = list_ref[jnp.maximum(mask - 1, 0), g]
            first = (slot * list_ref.shape[1] + g) * ROWS
            sent_ref[first : first + ROWS, :] = own_ref[rows_at(block), :]


def outgoing_pass(own, ghost_list, place):
    count = 8 * ghost_list.shape[1]
    return pl.pallas_call(
        outgoing_kernel,
        out_shape=jax.ShapeDtypeStruct((count * ROWS, LANES), jnp.float32),
        in_specs=[VMEM, SMEM, SMEM],
        out_specs=VMEM,
        name="outgoing_pass",
    )(own, ghost_list, place)


def swapped(shard, axis, bit):
    return lax.ppermute(shard, axis, [(i, i ^ 1 << bit) for i in range(lax.axis_size(axis))])


def padded(block, sides, width):
    for axis, dim in sides:
        count = lax.axis_size(axis)
        forward = [(i, i + 1) for i in range(count - 1)]
        backward = [(target, source) for source, target in forward]
        low = lax.ppermute(
            lax.slice_in_dim(block, block.shape[dim] - width, None, axis=dim), axis, forward
        )
        high = lax.ppermute(lax.slice_in_dim(block, 0, width, axis=dim), axis, backward)
        block = jnp.concatenate([low, block, high], axis=dim)
    return block


def per_device(fluid_state, ghost_list, pair_list, wall_state, wall_count, wall_pairs):
    block_total = fluid_state.shape[1] // LANES
    own = jnp.transpose(fluid_state.reshape(8, block_total, LANES), (1, 0, 2)).reshape(-1, LANES)
    place = (lax.axis_index("orb") % 8).reshape(1)
    groups = [list(range(g, g + 8)) for g in range(0, lax.axis_size("orb"), 8)]
    landed = lax.all_to_all(
        outgoing_pass(own, ghost_list, place).reshape(8, -1, LANES),
        "orb",
        0,
        0,
        axis_index_groups=groups if len(groups) > 1 else None,
    )
    alive = (
        (jnp.arange(LANES, dtype=jnp.int32)[None, :] < wall_count[:, None])
        .astype(jnp.float32)
        .reshape(-1)
    )
    wall_live = jnp.concatenate([wall_state[0:3], wall_state[3:4] * alive[None, :]], axis=0)
    extended = padded(wall_live, (("wall", 1),), EB * LANES)
    wall_cands = jnp.transpose(extended.reshape(4, -1, LANES), (1, 0, 2))
    choices = selections()
    own_results = own_pass(own, wall_cands.reshape(-1, LANES), wall_pairs, choices)
    rate, acceleration, local_peak = fluid_pass(
        own, landed.reshape(-1, LANES), pair_list, place, choices[0], own_results
    )
    peak = local_peak
    for axis in ("wall", "orb"):
        for bit in range((lax.axis_size(axis) - 1).bit_length()):
            peak = jnp.maximum(peak, swapped(peak, axis, bit))
    peak = peak[0, 0]
    time_step = courant * jnp.sqrt(smoothing / (peak + 1e-06))
    return (rate.reshape(-1), acceleration, time_step)


def solution(mesh):
    return jax.shard_map(
        per_device,
        mesh=mesh,
        in_specs=(
            P(None, ("orb", "wall")),
            P(None, ("orb", "wall")),
            P(("orb", "wall"), None),
            P(None, ("orb", "wall")),
            P(("orb", "wall")),
            P(("orb", "wall"), None),
        ),
        out_specs=(P(("orb", "wall")), P(None, ("orb", "wall")), P()),
        check_vma=False,
    )
```

profile of v0, /device:TPU:0, one launch (start us, length us, event | category | flops | bytes accessed | tf_op | source)
XLA Modules:
  0.0 89.6 jit_solution(13216621512788209408)
XLA Ops:
  0.7 1.7 %outgoing_pass.1 = f32[384,128]{1,0:T(8,128)} custom-call(f32[192,128]{1,0:T(8,128)} %bitcast.22, s32[7,6]{1,0:T(8,128)} %list_ref.1, s32[1]{0:T(128)} %bitcast.5.place_ref), custom_call_target="tpu_custom_call" | custom-call | tf_op jit(solution)/shard_map/outgoing_pass/pallas_call | solution.py:350
  2.4 7.3 %all-to-all-start = ((f32[8,48,128]{2,1,0:T(8,128)}), f32[8,48,128]{2,1,0:T(8,128)S(1)}, u32[]{:S(2)}, u32[]{:S(2)}) async-start(f32[8,48,128]{2,1,0:T(8,128)} %bitcast.26), calls=%async_computation | async-start | bytes 393216 | tf_op jit(solution)/shard_map/all_to_all | solution.py:381
  9.6 0.7 fusion
  11.8 1.4 %collective-permute-start = (f32[4,128]{1,0:T(4,128)S(1)}, f32[4,128]{1,0:T(4,128)S(1)}, u32[]{:S(2)}, u32[]{:S(2)}) collective-permute-start(f32[4,128]{1,0:T(4,128)S(1)} %get-tuple-element.25), channel_id=1, source_target_pairs={{0,1},{1,2},{2,3},{4,5},{5,6},{6,7},{8,9},{9,10},{10,11},{12,13},{... | collective-permute-start | bytes 6152 | tf_op jit(solution)/shard_map/ppermute | solution.py:368
  13.2 1.3 %collective-permute-start.1 = (f32[4,128]{1,0:T(4,128)S(1)}, f32[4,128]{1,0:T(4,128)S(1)}, u32[]{:S(2)}, u32[]{:S(2)}) collective-permute-start(f32[4,128]{1,0:T(4,128)S(1)} %get-tuple-element.26), channel_id=1, source_target_pairs={{1,0},{2,1},{3,2},{5,4},{6,5},{7,6},{9,8},{10,9},{11,10},{13,12},{... | collective-permute-start | bytes 6152 | tf_op jit(solution)/shard_map/ppermute | solution.py:371
  14.5 0.8 copy.13.pair_ref
  15.3 0.8 copy.12.wpair_ref
  16.1 1.8 %collective-permute-done.1 = f32[4,128]{1,0:T(4,128)S(1)} collective-permute-done((f32[4,128]{1,0:T(4,128)S(1)}, f32[4,128]{1,0:T(4,128)S(1)}, u32[]{:S(2)}, u32[]{:S(2)}) %collective-permute-start.1) | collective-permute-done | bytes 2080 | tf_op jit(solution)/shard_map/ppermute | solution.py:371
  18.6 0.9 copy-done
  19.5 0.8 copy-done.2
  20.3 0.8 copy-done.3
  21.1 12.0 %own_pass.1 = (bf16[24,80,256]{2,1,0:T(8,128)(2,1)S(1)}, bf16[24,32,256]{2,1,0:T(8,128)(2,1)S(1)}, f32[24,8,128]{2,1,0:T(8,128)S(1)}, f32[24,8,128]{2,1,0:T(8,12...) custom-call(f32[192,128]{1,0:T(8,128)S(1)} %bitcast.23, ...), custom_call_target="tpu_custom_call" | custom-call | flops 1572864000 | tf_op jit(solution)/shard_map/own_pass/pallas_call | solution.py:302
  33.1 2.2 %copy-done.5 = f32[24,3,128,128]{3,2,1,0:T(8,128)} copy-done((f32[24,3,128,128]{3,2,1,0:T(8,128)}, f32[24,3,128,128]{3,2,1,0:T(8,128)S(1)}, u32[]{:S(2)}) %copy-start.5) | copy-done | bytes 4718616
  35.3 2.3 %copy-done.6 = f32[24,3,128,128]{3,2,1,0:T(8,128)S(1)} copy-done((f32[24,3,128,128]{3,2,1,0:T(8,128)S(1)}, f32[24,3,128,128]{3,2,1,0:T(8,128)}, u32[]{:S(2)}) %copy-start.6) | copy-done | bytes 4718616
  37.6 31.1 %fluid_pass.1 = (f32[24,128]{1,0:T(8,128)}, f32[3,3072]{1,0:T(4,128)}, f32[8,128]{1,0:T(8,128)S(1)}) custom-call(f32[192,128]{1,0:T(8,128)S(1)} %bitcast.24, f32[384,128]{1,0:T(8,128)S(1)} %bitcast.21, s32[24,14]{1,0:T(8,128)S(1)} %copy.13.pair_ref, s32[1]{0:T(128)} %bitcast.5.place_ref, bf16[160,48]{1,0:T(8,128)(2,1)S(1)} %copy-done.4, ...), custom_call_target="tpu_custom_call" | custom-call | flops 5505024000 | tf_op jit(solution)/shard_map/fluid_pass/pallas_call | solution.py:317
  68.7 2.4 %collective-permute-start.2 = (f32[8,128]{1,0:T(8,128)S(1)}, f32[8,128]{1,0:T(8,128)S(1)}, u32[]{:S(2)}, u32[]{:S(2)}) collective-permute-start(f32[8,128]{1,0:T(8,128)S(1)} %get-tuple-element.24), channel_id=1, source_target_pairs={{0,1},{1,0},{2,3},{3,2},{4,5},{5,4},{6,7},{7,6},{8,9},{9,8},{10,11... | collective-permute-start | bytes 12296 | tf_op jit(solution)/shard_map/ppermute | solution.py:360
  71.1 0.8 collective-permute-done.2
  72.4 3.1 %collective-permute-done.3 = f32[8,128]{1,0:T(8,128)S(1)} collective-permute-done((f32[8,128]{1,0:T(8,128)S(1)}, f32[8,128]{1,0:T(8,128)S(1)}, u32[]{:S(2)}, u32[]{:S(2)}) %collective-permute-start.3) | collective-permute-done | bytes 4128 | tf_op jit(solution)/shard_map/ppermute | solution.py:360
  75.5 2.0 %collective-permute-start.4 = (f32[8,128]{1,0:T(8,128)S(1)}, f32[8,128]{1,0:T(8,128)S(1)}, u32[]{:S(2)}, u32[]{:S(2)}) collective-permute-start(f32[8,128]{1,0:T(8,128)S(1)} %max.16), channel_id=1, source_target_pairs={{0,4},{4,0},{8,12},{12,8},{16,20},{20,16},{24,28},{28,24},{1,5},{5... | collective-permute-start | bytes 12296 | tf_op jit(solution)/shard_map/ppermute | solution.py:360
  77.5 1.6 %collective-permute-done.4 = f32[8,128]{1,0:T(8,128)S(1)} collective-permute-done((f32[8,128]{1,0:T(8,128)S(1)}, f32[8,128]{1,0:T(8,128)S(1)}, u32[]{:S(2)}, u32[]{:S(2)}) %collective-permute-start.4) | collective-permute-done | bytes 4128 | tf_op jit(solution)/shard_map/ppermute | solution.py:360
  79.1 1.9 %collective-permute-start.5 = (f32[8,128]{1,0:T(8,128)S(1)}, f32[8,128]{1,0:T(8,128)S(1)}, u32[]{:S(2)}, u32[]{:S(2)}) collective-permute-start(f32[8,128]{1,0:T(8,128)S(1)} %max.17), channel_id=1, source_target_pairs={{0,8},{4,12},{8,0},{12,4},{16,24},{20,28},{24,16},{28,20},{1,9},{5... | collective-permute-start | bytes 12296 | tf_op jit(solution)/shard_map/ppermute | solution.py:360
  81.1 1.7 %collective-permute-done.5 = f32[8,128]{1,0:T(8,128)S(1)} collective-permute-done((f32[8,128]{1,0:T(8,128)S(1)}, f32[8,128]{1,0:T(8,128)S(1)}, u32[]{:S(2)}, u32[]{:S(2)}) %collective-permute-start.5) | collective-permute-done | bytes 4128 | tf_op jit(solution)/shard_map/ppermute | solution.py:360
  82.7 2.9 %collective-permute-start.6 = (f32[8,128]{1,0:T(8,128)S(1)}, f32[8,128]{1,0:T(8,128)S(1)}, u32[]{:S(2)}, u32[]{:S(2)}) collective-permute-start(f32[8,128]{1,0:T(8,128)S(1)} %max.18), channel_id=1, source_target_pairs={{0,16},{4,20},{8,24},{12,28},{16,0},{20,4},{24,8},{28,12},{1,17},{... | collective-permute-start | bytes 12296 | tf_op jit(solution)/shard_map/ppermute | solution.py:360
  85.6 1.6 %collective-permute-done.6 = f32[8,128]{1,0:T(8,128)S(1)} collective-permute-done((f32[8,128]{1,0:T(8,128)S(1)}, f32[8,128]{1,0:T(8,128)S(1)}, u32[]{:S(2)}, u32[]{:S(2)}) %collective-permute-start.6) | collective-permute-done | bytes 4128 | tf_op jit(solution)/shard_map/ppermute | solution.py:360
  (21 shorter events, 3.2 us)
Async XLA Ops:
  0.6 34.6 %copy-start.4 = (bf16[160,48]{1,0:T(8,128)(2,1)S(1)}, bf16[160,48]{1,0:T(8,128)(2,1)}, u32[]{:S(2)}) copy-start(bf16[160,48]{1,0:T(8,128)(2,1)} %constant.34.clone.choice) | copy-start | bytes 46084
  0.6 34.6 %copy-start.1 = (f32[8,3072]{1,0:T(8,128)S(1)}, f32[8,3072]{1,0:T(8,128)}, u32[]{:S(2)}) copy-start(f32[8,3072]{1,0:T(8,128)} %param.8) | copy-start | bytes 294916
  2.4 32.9 %all-to-all-start = ((f32[8,48,128]{2,1,0:T(8,128)}), f32[8,48,128]{2,1,0:T(8,128)S(1)}, u32[]{:S(2)}, u32[]{:S(2)}) async-start(f32[8,48,128]{2,1,0:T(8,128)} %bitcast.26), calls=%async_computation | async-start | bytes 393216 | tf_op jit(solution)/shard_map/all_to_all | solution.py:381
  11.8 4.3 %collective-permute-start = (f32[4,128]{1,0:T(4,128)S(1)}, f32[4,128]{1,0:T(4,128)S(1)}, u32[]{:S(2)}, u32[]{:S(2)}) collective-permute-start(f32[4,128]{1,0:T(4,128)S(1)} %get-tuple-element.25), channel_id=1, source_target_pairs={{0,1},{1,2},{2,3},{4,5},{5,6},{6,7},{8,9},{9,10},{10,11},{12,13},{... | collective-permute-start | bytes 6152 | tf_op jit(solution)/shard_map/ppermute | solution.py:368
  13.2 4.6 %collective-permute-start.1 = (f32[4,128]{1,0:T(4,128)S(1)}, f32[4,128]{1,0:T(4,128)S(1)}, u32[]{:S(2)}, u32[]{:S(2)}) collective-permute-start(f32[4,128]{1,0:T(4,128)S(1)} %get-tuple-element.26), channel_id=1, source_target_pairs={{1,0},{2,1},{3,2},{5,4},{6,5},{7,6},{9,8},{10,9},{11,10},{13,12},{... | collective-permute-start | bytes 6152 | tf_op jit(solution)/shard_map/ppermute | solution.py:371
  18.6 0.9 copy-start
  19.5 0.8 copy-start.2
  20.3 0.8 copy-start.3
  33.1 2.2 %copy-start.5 = (f32[24,3,128,128]{3,2,1,0:T(8,128)}, f32[24,3,128,128]{3,2,1,0:T(8,128)S(1)}, u32[]{:S(2)}) copy-start(f32[24,3,128,128]{3,2,1,0:T(8,128)S(1)} %get-tuple-element.19.wide) | copy-start | bytes 14155780
  35.3 2.3 %copy-start.6 = (f32[24,3,128,128]{3,2,1,0:T(8,128)S(1)}, f32[24,3,128,128]{3,2,1,0:T(8,128)}, u32[]{:S(2)}) copy-start(f32[24,3,128,128]{3,2,1,0:T(8,128)} %copy-done.5) | copy-start | bytes 14155780
  68.7 3.2 %collective-permute-start.2 = (f32[8,128]{1,0:T(8,128)S(1)}, f32[8,128]{1,0:T(8,128)S(1)}, u32[]{:S(2)}, u32[]{:S(2)}) collective-permute-start(f32[8,128]{1,0:T(8,128)S(1)} %get-tuple-element.24), channel_id=1, source_target_pairs={{0,1},{1,0},{2,3},{3,2},{4,5},{5,4},{6,7},{7,6},{8,9},{9,8},{10,11... | collective-permute-start | bytes 12296 | tf_op jit(solution)/shard_map/ppermute | solution.py:360
  71.9 3.6 %collective-permute-start.3 = (f32[8,128]{1,0:T(8,128)S(1)}, f32[8,128]{1,0:T(8,128)S(1)}, u32[]{:S(2)}, u32[]{:S(2)}) collective-permute-start(f32[8,128]{1,0:T(8,128)S(1)} %max.15), channel_id=1, source_target_pairs={{0,2},{1,3},{2,0},{3,1},{4,6},{5,7},{6,4},{7,5},{8,10},{9,11},{10,... | collective-permute-start | bytes 12296 | tf_op jit(solution)/shard_map/ppermute | solution.py:360
  75.5 3.6 %collective-permute-start.4 = (f32[8,128]{1,0:T(8,128)S(1)}, f32[8,128]{1,0:T(8,128)S(1)}, u32[]{:S(2)}, u32[]{:S(2)}) collective-permute-start(f32[8,128]{1,0:T(8,128)S(1)} %max.16), channel_id=1, source_target_pairs={{0,4},{4,0},{8,12},{12,8},{16,20},{20,16},{24,28},{28,24},{1,5},{5... | collective-permute-start | bytes 12296 | tf_op jit(solution)/shard_map/ppermute | solution.py:360
  79.1 3.6 %collective-permute-start.5 = (f32[8,128]{1,0:T(8,128)S(1)}, f32[8,128]{1,0:T(8,128)S(1)}, u32[]{:S(2)}, u32[]{:S(2)}) collective-permute-start(f32[8,128]{1,0:T(8,128)S(1)} %max.17), channel_id=1, source_target_pairs={{0,8},{4,12},{8,0},{12,4},{16,24},{20,28},{24,16},{28,20},{1,9},{5... | collective-permute-start | bytes 12296 | tf_op jit(solution)/shard_map/ppermute | solution.py:360
  82.7 4.5 %collective-permute-start.6 = (f32[8,128]{1,0:T(8,128)S(1)}, f32[8,128]{1,0:T(8,128)S(1)}, u32[]{:S(2)}, u32[]{:S(2)}) collective-permute-start(f32[8,128]{1,0:T(8,128)S(1)} %max.18), channel_id=1, source_target_pairs={{0,16},{4,20},{8,24},{12,28},{16,0},{20,4},{24,8},{28,12},{1,17},{... | collective-permute-start | bytes 12296 | tf_op jit(solution)/shard_map/ppermute | solution.py:360
where the time goes:
time: 90.3 us; the launch traced here: 89.6 us
  Pallas kernels  44.8 us (50%)
  starting transfers between devices  19.7 us (22%)
  waiting for transfers between devices  10.6 us (12%)
  local copies, waits for them, and re-layouts  9.01 us (10%)
  other arithmetic  2.88 us (3%)
  between operations  2.57 us (3%)
    pallas_call x1, Pallas kernels, fluid_pass(): pl.pallas_call(functools.partial(fluid_kernel, blocks), out_shape=(jax.Sh...  31.1 us
    pallas_call x1, Pallas kernels, own_pass(): pl.pallas_call(functools.partial(own_kernel, blocks, wall_blocks), out_sh...  12 us
    ppermute x5, starting transfers between devices, swapped(): lax.ppermute(shard, axis, [(i, i ^ 1 << bit) for i in range(lax.axis_size...  9.67 us
    ppermute x5, waiting for transfers between devices, swapped(): lax.ppermute(shard, axis, [(i, i ^ 1 << bit) for i in range(lax.axis_size...  8.84 us
    unnamed x16, local copies, waits for them, and re-layouts  8.5 us
    all_to_all x1, starting transfers between devices, per_device(): lax.all_to_all(outgoing_pass(own, ghost_list, place).reshape(8, -1, LANES...  7.25 us
  transfers between devices with their start and end apart: 8, of which 6 were waited for; matrix products, arithmetic and copies ran while one was open for 5% of the time, Pallas kernels for 13%

commit v1 on v0

--- a/solution.py
+++ b/solution.py
@@ -135,13 +135,20 @@
 def weights_of(product, wide, n_wide, y, z):
     guarded = jnp.maximum(product[:, :LANES], 1e-30)
     approach = product[:, LANES:]
-    falloff = jnp.maximum(1.0 - guarded * lax.rsqrt(guarded), 0.0)
+    if z is not None:
+        spread = (guarded + shift) * (wide[0] + y[6:7])
+        scaled = guarded * spread
+        inverse = lax.rsqrt(scaled * spread)
+        root = scaled * inverse
+        viscous = jnp.maximum(approach, 0.0) * (inverse * root)
+    else:
+        root = guarded * lax.rsqrt(guarded)
+    falloff = jnp.maximum(1.0 - root, 0.0)
     cubed = falloff * falloff * falloff
     blend = falloff + wide[n_wide]
     if z is not None:
-        spread = (guarded + shift) * (wide[0] + y[6:7])
         blend += z[7:8]
-        blend += jnp.maximum(approach, 0.0) * pl.reciprocal(spread, approx=True)
+        blend += viscous
     weight = cubed * blend
     high = weight.astype(jnp.bfloat16)
     low = (weight - high.astype(jnp.float32)).astype(jnp.bfloat16)

time: 90.3 us -> 92.1 us (1.020)
  Pallas kernels: 44.8 us -> 46.7 us
    pallas_call x1, Pallas kernels: 31.1 us -> 33 us  [fluid_pass(): pl.pallas_call(functools.partial(fluid_kernel, blocks), out_shape=(jax.Sh...]
where the time goes in v1:
time: 92.1 us; the launch traced here: 91.5 us
  Pallas kernels  46.7 us (51%)
  starting transfers between devices  19.8 us (21%)
  waiting for transfers between devices  10.5 us (11%)
  local copies, waits for them, and re-layouts  9.01 us (10%)
  other arithmetic  2.88 us (3%)
  between operations  2.57 us (3%)
    pallas_call x1, Pallas kernels, fluid_pass(): pl.pallas_call(functools.partial(fluid_kernel, blocks), out_shape=(jax.Sh...  33 us
    pallas_call x1, Pallas kernels, own_pass(): pl.pallas_call(functools.partial(own_kernel, blocks, wall_blocks), out_sh...  12 us
    ppermute x5, starting transfers between devices, swapped(): lax.ppermute(shard, axis, [(i, i ^ 1 << bit) for i in range(lax.axis_size...  9.82 us
    ppermute x5, waiting for transfers between devices, swapped(): lax.ppermute(shard, axis, [(i, i ^ 1 << bit) for i in range(lax.axis_size...  8.69 us
    unnamed x16, local copies, waits for them, and re-layouts  8.5 us
    all_to_all x1, starting transfers between devices, per_device(): lax.all_to_all(outgoing_pass(own, ghost_list, place).reshape(8, -1, LANES...  7.25 us
  transfers between devices with their start and end apart: 8, of which 6 were waited for; matrix products, arithmetic and copies ran while one was open for 5% of the time, Pallas kernels for 13%

profile of v1, /device:TPU:0, one launch (start us, length us, event | category | flops | bytes accessed | tf_op | source)
XLA Modules:
  0.0 91.5 jit_solution(6224905829318872338)
XLA Ops:
  0.7 1.7 %outgoing_pass.1 = f32[384,128]{1,0:T(8,128)} custom-call(f32[192,128]{1,0:T(8,128)} %bitcast.22, s32[7,6]{1,0:T(8,128)} %list_ref.1, s32[1]{0:T(128)} %bitcast.5.place_ref), custom_call_target="tpu_custom_call" | custom-call | tf_op jit(solution)/shard_map/outgoing_pass/pallas_call | solution.py:357
  2.4 7.3 %all-to-all-start = ((f32[8,48,128]{2,1,0:T(8,128)}), f32[8,48,128]{2,1,0:T(8,128)S(1)}, u32[]{:S(2)}, u32[]{:S(2)}) async-start(f32[8,48,128]{2,1,0:T(8,128)} %bitcast.26), calls=%async_computation | async-start | bytes 393216 | tf_op jit(solution)/shard_map/all_to_all | solution.py:388
  9.6 0.7 fusion
  11.8 1.4 %collective-permute-start = (f32[4,128]{1,0:T(4,128)S(1)}, f32[4,128]{1,0:T(4,128)S(1)}, u32[]{:S(2)}, u32[]{:S(2)}) collective-permute-start(f32[4,128]{1,0:T(4,128)S(1)} %get-tuple-element.25), channel_id=1, source_target_pairs={{0,1},{1,2},{2,3},{4,5},{5,6},{6,7},{8,9},{9,10},{10,11},{12,13},{... | collective-permute-start | bytes 6152 | tf_op jit(solution)/shard_map/ppermute | solution.py:375
  13.2 1.3 %collective-permute-start.1 = (f32[4,128]{1,0:T(4,128)S(1)}, f32[4,128]{1,0:T(4,128)S(1)}, u32[]{:S(2)}, u32[]{:S(2)}) collective-permute-start(f32[4,128]{1,0:T(4,128)S(1)} %get-tuple-element.26), channel_id=1, source_target_pairs={{1,0},{2,1},{3,2},{5,4},{6,5},{7,6},{9,8},{10,9},{11,10},{13,12},{... | collective-permute-start | bytes 6152 | tf_op jit(solution)/shard_map/ppermute | solution.py:378
  14.5 0.8 copy.13.pair_ref
  15.3 0.8 copy.12.wpair_ref
  16.1 1.8 %collective-permute-done.1 = f32[4,128]{1,0:T(4,128)S(1)} collective-permute-done((f32[4,128]{1,0:T(4,128)S(1)}, f32[4,128]{1,0:T(4,128)S(1)}, u32[]{:S(2)}, u32[]{:S(2)}) %collective-permute-start.1) | collective-permute-done | bytes 2080 | tf_op jit(solution)/shard_map/ppermute | solution.py:378
  18.6 0.9 copy-done
  19.5 0.8 copy-done.2
  20.3 0.8 copy-done.3
  21.1 12.0 %own_pass.1 = (bf16[24,80,256]{2,1,0:T(8,128)(2,1)S(1)}, bf16[24,32,256]{2,1,0:T(8,128)(2,1)S(1)}, f32[24,8,128]{2,1,0:T(8,128)S(1)}, f32[24,8,128]{2,1,0:T(8,12...) custom-call(f32[192,128]{1,0:T(8,128)S(1)} %bitcast.23, ...), custom_call_target="tpu_custom_call" | custom-call | flops 1572864000 | tf_op jit(solution)/shard_map/own_pass/pallas_call | solution.py:309
  33.1 2.2 %copy-done.5 = f32[24,3,128,128]{3,2,1,0:T(8,128)} copy-done((f32[24,3,128,128]{3,2,1,0:T(8,128)}, f32[24,3,128,128]{3,2,1,0:T(8,128)S(1)}, u32[]{:S(2)}) %copy-start.5) | copy-done | bytes 4718616
  35.3 2.3 %copy-done.6 = f32[24,3,128,128]{3,2,1,0:T(8,128)S(1)} copy-done((f32[24,3,128,128]{3,2,1,0:T(8,128)S(1)}, f32[24,3,128,128]{3,2,1,0:T(8,128)}, u32[]{:S(2)}) %copy-start.6) | copy-done | bytes 4718616
  37.6 33.0 %fluid_pass.1 = (f32[24,128]{1,0:T(8,128)}, f32[3,3072]{1,0:T(4,128)}, f32[8,128]{1,0:T(8,128)S(1)}) custom-call(f32[192,128]{1,0:T(8,128)S(1)} %bitcast.24, f32[384,128]{1,0:T(8,128)S(1)} %bitcast.21, s32[24,14]{1,0:T(8,128)S(1)} %copy.13.pair_ref, s32[1]{0:T(128)} %bitcast.5.place_ref, bf16[160,48]{1,0:T(8,128)(2,1)S(1)} %copy-done.4, ...), custom_call_target="tpu_custom_call" | custom-call | flops 5505024000 | tf_op jit(solution)/shard_map/fluid_pass/pallas_call | solution.py:324
  70.6 2.3 %collective-permute-start.2 = (f32[8,128]{1,0:T(8,128)S(1)}, f32[8,128]{1,0:T(8,128)S(1)}, u32[]{:S(2)}, u32[]{:S(2)}) collective-permute-start(f32[8,128]{1,0:T(8,128)S(1)} %get-tuple-element.24), channel_id=1, source_target_pairs={{0,1},{1,0},{2,3},{3,2},{4,5},{5,4},{6,7},{7,6},{8,9},{9,8},{10,11... | collective-permute-start | bytes 12296 | tf_op jit(solution)/shard_map/ppermute | solution.py:367
  72.9 0.8 collective-permute-done.2
  74.2 3.1 %collective-permute-done.3 = f32[8,128]{1,0:T(8,128)S(1)} collective-permute-done((f32[8,128]{1,0:T(8,128)S(1)}, f32[8,128]{1,0:T(8,128)S(1)}, u32[]{:S(2)}, u32[]{:S(2)}) %collective-permute-start.3) | collective-permute-done | bytes 4128 | tf_op jit(solution)/shard_map/ppermute | solution.py:367
  77.3 2.1 %collective-permute-start.4 = (f32[8,128]{1,0:T(8,128)S(1)}, f32[8,128]{1,0:T(8,128)S(1)}, u32[]{:S(2)}, u32[]{:S(2)}) collective-permute-start(f32[8,128]{1,0:T(8,128)S(1)} %max.16), channel_id=1, source_target_pairs={{0,4},{4,0},{8,12},{12,8},{16,20},{20,16},{24,28},{28,24},{1,5},{5... | collective-permute-start | bytes 12296 | tf_op jit(solution)/shard_map/ppermute | solution.py:367
  79.4 1.6 %collective-permute-done.4 = f32[8,128]{1,0:T(8,128)S(1)} collective-permute-done((f32[8,128]{1,0:T(8,128)S(1)}, f32[8,128]{1,0:T(8,128)S(1)}, u32[]{:S(2)}, u32[]{:S(2)}) %collective-permute-start.4) | collective-permute-done | bytes 4128 | tf_op jit(solution)/shard_map/ppermute | solution.py:367
  81.0 2.0 %collective-permute-start.5 = (f32[8,128]{1,0:T(8,128)S(1)}, f32[8,128]{1,0:T(8,128)S(1)}, u32[]{:S(2)}, u32[]{:S(2)}) collective-permute-start(f32[8,128]{1,0:T(8,128)S(1)} %max.17), channel_id=1, source_target_pairs={{0,8},{4,12},{8,0},{12,4},{16,24},{20,28},{24,16},{28,20},{1,9},{5... | collective-permute-start | bytes 12296 | tf_op jit(solution)/shard_map/ppermute | solution.py:367
  83.0 1.6 %collective-permute-done.5 = f32[8,128]{1,0:T(8,128)S(1)} collective-permute-done((f32[8,128]{1,0:T(8,128)S(1)}, f32[8,128]{1,0:T(8,128)S(1)}, u32[]{:S(2)}, u32[]{:S(2)}) %collective-permute-start.5) | collective-permute-done | bytes 4128 | tf_op jit(solution)/shard_map/ppermute | solution.py:367
  84.6 2.9 %collective-permute-start.6 = (f32[8,128]{1,0:T(8,128)S(1)}, f32[8,128]{1,0:T(8,128)S(1)}, u32[]{:S(2)}, u32[]{:S(2)}) collective-permute-start(f32[8,128]{1,0:T(8,128)S(1)} %max.18), channel_id=1, source_target_pairs={{0,16},{4,20},{8,24},{12,28},{16,0},{20,4},{24,8},{28,12},{1,17},{... | collective-permute-start | bytes 12296 | tf_op jit(solution)/shard_map/ppermute | solution.py:367
  87.5 1.6 %collective-permute-done.6 = f32[8,128]{1,0:T(8,128)S(1)} collective-permute-done((f32[8,128]{1,0:T(8,128)S(1)}, f32[8,128]{1,0:T(8,128)S(1)}, u32[]{:S(2)}, u32[]{:S(2)}) %collective-permute-start.6) | collective-permute-done | bytes 4128 | tf_op jit(solution)/shard_map/ppermute | solution.py:367
  (21 shorter events, 3.3 us)
Async XLA Ops:
  0.6 34.6 %copy-start.4 = (bf16[160,48]{1,0:T(8,128)(2,1)S(1)}, bf16[160,48]{1,0:T(8,128)(2,1)}, u32[]{:S(2)}) copy-start(bf16[160,48]{1,0:T(8,128)(2,1)} %constant.34.clone.choice) | copy-start | bytes 46084
  0.6 34.6 %copy-start.1 = (f32[8,3072]{1,0:T(8,128)S(1)}, f32[8,3072]{1,0:T(8,128)}, u32[]{:S(2)}) copy-start(f32[8,3072]{1,0:T(8,128)} %param.8) | copy-start | bytes 294916
  2.4 32.9 %all-to-all-start = ((f32[8,48,128]{2,1,0:T(8,128)}), f32[8,48,128]{2,1,0:T(8,128)S(1)}, u32[]{:S(2)}, u32[]{:S(2)}) async-start(f32[8,48,128]{2,1,0:T(8,128)} %bitcast.26), calls=%async_computation | async-start | bytes 393216 | tf_op jit(solution)/shard_map/all_to_all | solution.py:388
  11.8 4.3 %collective-permute-start = (f32[4,128]{1,0:T(4,128)S(1)}, f32[4,128]{1,0:T(4,128)S(1)}, u32[]{:S(2)}, u32[]{:S(2)}) collective-permute-start(f32[4,128]{1,0:T(4,128)S(1)} %get-tuple-element.25), channel_id=1, source_target_pairs={{0,1},{1,2},{2,3},{4,5},{5,6},{6,7},{8,9},{9,10},{10,11},{12,13},{... | collective-permute-start | bytes 6152 | tf_op jit(solution)/shard_map/ppermute | solution.py:375
  13.2 4.6 %collective-permute-start.1 = (f32[4,128]{1,0:T(4,128)S(1)}, f32[4,128]{1,0:T(4,128)S(1)}, u32[]{:S(2)}, u32[]{:S(2)}) collective-permute-start(f32[4,128]{1,0:T(4,128)S(1)} %get-tuple-element.26), channel_id=1, source_target_pairs={{1,0},{2,1},{3,2},{5,4},{6,5},{7,6},{9,8},{10,9},{11,10},{13,12},{... | collective-permute-start | bytes 6152 | tf_op jit(solution)/shard_map/ppermute | solution.py:378
  18.6 0.9 copy-start
  19.5 0.8 copy-start.2
  20.3 0.8 copy-start.3
  33.1 2.2 %copy-start.5 = (f32[24,3,128,128]{3,2,1,0:T(8,128)}, f32[24,3,128,128]{3,2,1,0:T(8,128)S(1)}, u32[]{:S(2)}) copy-start(f32[24,3,128,128]{3,2,1,0:T(8,128)S(1)} %get-tuple-element.19.wide) | copy-start | bytes 14155780
  35.3 2.3 %copy-start.6 = (f32[24,3,128,128]{3,2,1,0:T(8,128)S(1)}, f32[24,3,128,128]{3,2,1,0:T(8,128)}, u32[]{:S(2)}) copy-start(f32[24,3,128,128]{3,2,1,0:T(8,128)} %copy-done.5) | copy-start | bytes 14155780
  70.6 3.1 %collective-permute-start.2 = (f32[8,128]{1,0:T(8,128)S(1)}, f32[8,128]{1,0:T(8,128)S(1)}, u32[]{:S(2)}, u32[]{:S(2)}) collective-permute-start(f32[8,128]{1,0:T(8,128)S(1)} %get-tuple-element.24), channel_id=1, source_target_pairs={{0,1},{1,0},{2,3},{3,2},{4,5},{5,4},{6,7},{7,6},{8,9},{9,8},{10,11... | collective-permute-start | bytes 12296 | tf_op jit(solution)/shard_map/ppermute | solution.py:367
  73.7 3.6 %collective-permute-start.3 = (f32[8,128]{1,0:T(8,128)S(1)}, f32[8,128]{1,0:T(8,128)S(1)}, u32[]{:S(2)}, u32[]{:S(2)}) collective-permute-start(f32[8,128]{1,0:T(8,128)S(1)} %max.15), channel_id=1, source_target_pairs={{0,2},{1,3},{2,0},{3,1},{4,6},{5,7},{6,4},{7,5},{8,10},{9,11},{10,... | collective-permute-start | bytes 12296 | tf_op jit(solution)/shard_map/ppermute | solution.py:367
  77.3 3.7 %collective-permute-start.4 = (f32[8,128]{1,0:T(8,128)S(1)}, f32[8,128]{1,0:T(8,128)S(1)}, u32[]{:S(2)}, u32[]{:S(2)}) collective-permute-start(f32[8,128]{1,0:T(8,128)S(1)} %max.16), channel_id=1, source_target_pairs={{0,4},{4,0},{8,12},{12,8},{16,20},{20,16},{24,28},{28,24},{1,5},{5... | collective-permute-start | bytes 12296 | tf_op jit(solution)/shard_map/ppermute | solution.py:367
  81.0 3.6 %collective-permute-start.5 = (f32[8,128]{1,0:T(8,128)S(1)}, f32[8,128]{1,0:T(8,128)S(1)}, u32[]{:S(2)}, u32[]{:S(2)}) collective-permute-start(f32[8,128]{1,0:T(8,128)S(1)} %max.17), channel_id=1, source_target_pairs={{0,8},{4,12},{8,0},{12,4},{16,24},{20,28},{24,16},{28,20},{1,9},{5... | collective-permute-start | bytes 12296 | tf_op jit(solution)/shard_map/ppermute | solution.py:367
  84.6 4.5 %collective-permute-start.6 = (f32[8,128]{1,0:T(8,128)S(1)}, f32[8,128]{1,0:T(8,128)S(1)}, u32[]{:S(2)}, u32[]{:S(2)}) collective-permute-start(f32[8,128]{1,0:T(8,128)S(1)} %max.18), channel_id=1, source_target_pairs={{0,16},{4,20},{8,24},{12,28},{16,0},{20,4},{24,8},{28,12},{1,17},{... | collective-permute-start | bytes 12296 | tf_op jit(solution)/shard_map/ppermute | solution.py:367

commit v2 on v0

v2 whole, which is shorter than its diff:
```python
import functools

import jax
import jax.numpy as jnp
import numpy as np
from jax import lax
from jax.experimental import pallas as pl
from jax.experimental.pallas import tpu as pltpu
from jax.sharding import PartitionSpec as P

EB = 1
LANES = 128
ROWS = 8
PIECES = 6 * ROWS
DEPTH = 64
MOMENTS = 4 * ROWS
UNROLL = 4
GROUP = 2

smoothing = 0.1
support = 0.3
kernel_norm = 21.0 / (2.0 * 3.141592653589793 * support**3)
grad_coeff = -20.0 / support**2 * kernel_norm
tait_coeff = 25.0 / 7.0
visc_coeff = 0.05
cohesion = 2000.0
adhesion = 2000.0
gravity = 9.81
courant = 0.25

center = 0.3
shift = 0.0001 / support**2
press_coeff = -grad_coeff / (4.0 * cohesion)
density_coeff = (support * 4.0 * cohesion) / (-grad_coeff * visc_coeff * 2.0)

SPLITS = ((0, 0), (0, 1), (1, 0), (0, 2), (2, 0), (1, 1))


def y_row(piece, row):
    return piece * ROWS + row


def z_row(piece, row):
    return (3 + piece) * ROWS + row


def selections():
    source = np.zeros((2 * DEPTH, LANES), np.float32)
    target = np.zeros((PIECES, LANES), np.float32)
    one = z_row(0, 6)
    k = 0
    for p in range(3):
        for d in range(3):
            target[one, k] = 1.0
            source[k, z_row(p, d)] = 1.0
            source[DEPTH + k, z_row(p, 3 + d)] = -1.0
            target[z_row(p, d), k + 9] = 1.0
            source[k + 9, one] = 1.0
            target[z_row(p, 3 + d), k + 18] = 1.0
            source[DEPTH + k + 18, one] = -1.0
            k += 1
    k = 27
    for d in range(3):
        for p, t in SPLITS:
            target[y_row(p, d), k] = 1.0
            source[k, y_row(t, d)] = -2.0
            source[DEPTH + k, y_row(t, 3 + d)] = 1.0
            target[y_row(p, 3 + d), k + 18] = 1.0
            source[DEPTH + k + 18, y_row(t, d)] = 1.0
            k += 1
    spread = np.zeros((3, LANES, LANES), np.float32)
    for p in range(3):
        target[y_row(p, 6), DEPTH + p] = 1.0
        target[z_row(p, 7), DEPTH + 3 + p] = 1.0
        spread[0, DEPTH + p] = 1.0
        spread[1, DEPTH + 3 + p] = 1.0
        spread[2, DEPTH + 3 + p] = 2.0 * cohesion / adhesion
    target[one, DEPTH + 6] = 1.0
    spread[1:, DEPTH + 6] = -0.75
    parts = [source, target, spread.reshape(-1, LANES)]
    return jnp.asarray(np.concatenate(parts), jnp.bfloat16)


def source_choice(choices):
    return choices[: 2 * DEPTH, :PIECES]


def target_choice(choices):
    return choices[2 * DEPTH : 2 * DEPTH + PIECES, :]


def spread_choice(choices, which):
    first = 2 * DEPTH + PIECES + which * LANES
    return choices[first : first + LANES, :]


def split(value):
    first = value.astype(jnp.bfloat16).astype(jnp.float32)
    rest = value - first
    second = rest.astype(jnp.bfloat16).astype(jnp.float32)
    return [first, second, rest - second]


def pressure_ratio(density):
    square = density * density
    return tait_coeff * (square * square * square * density - 1.0) / square


def row_index():
    return lax.broadcasted_iota(jnp.int32, (ROWS, LANES), 0)


def state_of(block):
    row = row_index()
    y = jnp.where(row < 3, (block - center) * (1.0 / support), block)
    y = jnp.where(row == 6, block * density_coeff, y)
    density = jnp.where(row == 7, pltpu.roll(block, 1, axis=0), 1.0)
    press = press_coeff * pressure_ratio(density)
    z = y * jnp.where(row < 3, y, pltpu.roll(y, 3, axis=0))
    return y, jnp.where(row < 6, z, jnp.where(row == 6, 1.0, press))


def pieces_of(y, z):
    return jnp.concatenate(split(y) + split(z), axis=0)


def put_source(block, choices, s, src, mom, rows, mass_factor=1.0):
    row = row_index()
    y, z = state_of(block)
    pieces = pieces_of(y, z).astype(jnp.bfloat16)
    chosen = jnp.dot(source_choice(choices), pieces, preferred_element_type=jnp.float32)
    chosen = chosen.astype(jnp.bfloat16)
    src[s] = jnp.concatenate([chosen[:DEPTH], chosen[DEPTH:]], axis=1)
    moment = (mass_factor * block[7:8]) * jnp.where(row == 6, 1.0, y)
    moments = jnp.concatenate(split(moment) + [jnp.zeros_like(moment)], axis=0)
    moments = moments.astype(jnp.bfloat16)
    mom[s] = jnp.concatenate([moments, moments], axis=1)
    rows[s, :ROWS] = y
    rows[s, ROWS:] = z
    return y, z


def put_target(y, z, choices, b, tgt):
    pieces = pieces_of(y, z).T.astype(jnp.bfloat16)
    chosen = jnp.dot(pieces, target_choice(choices), preferred_element_type=jnp.float32)
    tgt[b] = chosen.astype(jnp.bfloat16)


def rows_at(index):
    return pl.ds(pl.multiple_of(index * ROWS, ROWS), ROWS)


def weights_of(product, press_i, rho_i, rows):
    guarded = jnp.maximum(product[:, :LANES], 1e-30)
    approach = product[:, LANES:]
    falloff = jnp.maximum(1.0 - guarded * lax.rsqrt(guarded), 0.0)
    cubed = falloff * falloff * falloff
    blend = falloff + press_i
    if rho_i is not None:
        spread = (guarded + shift) * (rho_i + rows[6:7])
        blend += rows[ROWS + 7 : ROWS + 8]
        blend += jnp.maximum(approach, 0.0) * pl.reciprocal(spread, approx=True)
    weight = cubed * blend
    high = weight.astype(jnp.bfloat16)
    low = (weight - high.astype(jnp.float32)).astype(jnp.bfloat16)
    return [high, low], (cubed * approach) * rows[7:8]


def across(left, right):
    return lax.dot_general(
        left, right, (((1,), (1,)), ((), ())), preferred_element_type=jnp.float32
    )


def run_tiles(target, press_i, rho_i, tiles):
    features = target[:, :DEPTH]

    def product_of(group):
        columns = jnp.concatenate([tile[0][...] for tile in group], axis=1)
        return jnp.dot(features, columns, preferred_element_type=jnp.float32)

    groups = [tiles[n : n + GROUP] for n in range(0, len(tiles), GROUP)]
    total = jnp.zeros((MOMENTS, LANES), jnp.float32)
    rate = jnp.zeros((LANES, LANES), jnp.float32)
    ahead = product_of(groups[0])
    waiting = None
    for n, group in enumerate(groups):
        product = ahead
        if n + 1 < len(groups):
            ahead = product_of(groups[n + 1])
        weights = []
        for m, (_, _, rows) in enumerate(group):
            columns = slice(2 * m * LANES, 2 * (m + 1) * LANES)
            pair, part = weights_of(product[:, columns], press_i, rho_i, rows)
            weights += pair
            rate += part
        if waiting is not None:
            total += across(*waiting)
        moments = jnp.concatenate([tile[1][...] for tile in group], axis=1)
        waiting = (moments, jnp.concatenate(weights, axis=1))
    total += across(*waiting)
    ones = jnp.ones((ROWS, 3 * LANES), jnp.bfloat16)
    rates = across(ones, jnp.concatenate(split(rate), axis=1).astype(jnp.bfloat16))
    return total, rates


def moments_at(b):
    return pl.ds(pl.multiple_of(b * MOMENTS, MOMENTS), MOMENTS)


def spread_of(target, choices, which):
    return jnp.dot(target, spread_choice(choices, which), preferred_element_type=jnp.float32)


def own_kernel(
    own_ref, low_ref, wall_ref, high_ref, wpair_ref, choices,
    src, mom, rows, tgt, sums, rates, wsrc, wmom, wrows,
):
    blocks = tgt.shape[0]

    def build(b, carry):
        y, z = put_source(own_ref[rows_at(b), :], choices, b, src, mom, rows)
        put_target(y, z, choices, b, tgt)
        return carry

    lax.fori_loop(0, blocks, build, 0, unroll=UNROLL)
    row = row_index()
    count = 0
    for ref in (low_ref, wall_ref, high_ref):
        for c in range(ref.shape[0] // 4):
            held = ref[4 * c : 4 * c + 4, :]
            both = jnp.concatenate([held, held], axis=0)
            density = jnp.where(row == 6, 1.0, 0.0)
            block = jnp.where((row < 3) | (row == 7), both, density)
            put_source(block, choices, count, wsrc, wmom, wrows, adhesion / cohesion)
            count += 1

    def per_target(b, carry):
        tiles = []
        for k in range(wpair_ref.shape[1]):
            s = wpair_ref[b, k]
            tiles.append((wsrc.at[s], wmom.at[s], wrows.at[s]))
        target = tgt[b]
        total, rate = run_tiles(target, spread_of(target, choices, 2), None, tiles)
        sums[moments_at(b), :] = total
        rates[rows_at(b), :] = rate
        return carry

    lax.fori_loop(0, blocks, per_target, 0, unroll=UNROLL)


def fluid_kernel(
    own_ref, ghost_ref, pair_ref, place_ref, choices, own_src, own_mom, own_rows,
    tgt, own_sums, own_rates, rate_ref, accel_ref, peak_ref,
    src, mom, rows, sums, rates, stage, table,
):
    blocks = tgt.shape[0]
    ghosts = ghost_ref.shape[0] // ROWS
    per_mask = ghosts // 8
    for c in range(blocks):
        table[c] = c
    for mask in range(1, 8):
        for g in range(per_mask):
            table[blocks + (mask - 1) * per_mask + g] = (
                blocks + jnp.bitwise_xor(place_ref[0], mask) * per_mask + g
            )
    src[:blocks] = own_src[...]
    mom[:blocks] = own_mom[...]
    rows[:blocks] = own_rows[...]

    def build(g, carry):
        put_source(ghost_ref[rows_at(g), :], choices, blocks + g, src, mom, rows)
        return carry

    lax.fori_loop(0, ghosts, build, 0, unroll=UNROLL)

    def per_target(b, carry):
        tiles = []
        for k in range(pair_ref.shape[1]):
            s = table[pair_ref[b, k]]
            tiles.append((src.at[s], mom.at[s], rows.at[s]))
        target = tgt[b]
        spreads = [spread_of(target, choices, which) for which in (1, 0)]
        total, rate = run_tiles(target, *spreads, tiles)
        sums[moments_at(b), :] = own_sums[moments_at(b), :] + total
        rates[rows_at(b), :] = own_rates[rows_at(b), :] + rate
        return carry

    lax.fori_loop(0, blocks, per_target, 0)

    rate_ref[...] = (-support * grad_coeff) * rates[pl.ds(0, blocks, stride=ROWS), :]

    def summed(row):
        parts = [sums[pl.ds(y_row(p, row), blocks, stride=MOMENTS), :] for p in range(3)]
        return parts[0] + parts[1] + parts[2]

    mass_sum = summed(6)
    square = jnp.zeros_like(mass_sum)
    for d in range(3):
        pos = (own_ref[pl.ds(d, blocks, stride=ROWS), :] - center) * (1.0 / support)
        force = (4.0 * cohesion * support) * (pos * mass_sum - summed(d))
        if d == 2:
            force -= gravity
        square += force * force
        stage[pl.ds(d, blocks, stride=ROWS), :] = force
    for b in range(blocks):
        accel_ref[:, b * LANES : (b + 1) * LANES] = stage[b * ROWS : b * ROWS + 3, :]
    peak_ref[...] = jnp.full(peak_ref.shape, jnp.sqrt(jnp.max(square)), jnp.float32)


SMEM = pl.BlockSpec(memory_space=pltpu.SMEM)
VMEM = pl.BlockSpec(memory_space=pltpu.VMEM)
PARAMS = pltpu.CompilerParams(vmem_limit_bytes=32 * 1024 * 1024)


def tile_cost(tiles):
    return pl.CostEstimate(
        flops=tiles * LANES * LANES * 1000, bytes_accessed=0, transcendentals=0
    )


def source_shapes(count):
    return [
        ((count, DEPTH, 2 * LANES), jnp.bfloat16),
        ((count, MOMENTS, 2 * LANES), jnp.bfloat16),
        ((count, 2 * ROWS, LANES), jnp.float32),
    ]


def own_pass(own, walls, wall_pairs, choices):
    blocks = own.shape[0] // ROWS
    wall_blocks = sum(part.shape[0] for part in walls) // 4
    outs = source_shapes(blocks) + [
        ((blocks, LANES, LANES), jnp.bfloat16),
        ((blocks * MOMENTS, LANES), jnp.float32),
        ((blocks * ROWS, LANES), jnp.float32),
    ]
    return pl.pallas_call(
        own_kernel,
        out_shape=[jax.ShapeDtypeStruct(*out) for out in outs],
        in_specs=[VMEM, VMEM, VMEM, VMEM, SMEM, VMEM],
        out_specs=[VMEM] * len(outs),
        scratch_shapes=[pltpu.VMEM(*shape) for shape in source_shapes(wall_blocks)],
        compiler_params=PARAMS,
        cost_estimate=tile_cost(wall_pairs.size),
        name="own_pass",
    )(own, *walls, wall_pairs, choices)


def fluid_pass(own, ghosts, pair_list, place, choices, own_results):
    blocks = own.shape[0] // ROWS
    total = blocks + ghosts.shape[0] // ROWS
    return pl.pallas_call(
        fluid_kernel,
        out_shape=(
            jax.ShapeDtypeStruct((blocks, LANES), jnp.float32),
            jax.ShapeDtypeStruct((3, blocks * LANES), jnp.float32),
            jax.ShapeDtypeStruct((ROWS, LANES), jnp.float32),
        ),
        in_specs=[VMEM, VMEM, SMEM, SMEM, VMEM] + [VMEM] * len(own_results),
        out_specs=(VMEM, VMEM, VMEM),
        scratch_shapes=[pltpu.VMEM(*shape) for shape in source_shapes(total)]
        + [
            pltpu.VMEM((blocks * MOMENTS, LANES), jnp.float32),
            pltpu.VMEM((blocks * ROWS, LANES), jnp.float32),
            pltpu.VMEM((blocks * ROWS, LANES), jnp.float32),
            pltpu.SMEM((total,), jnp.int32),
        ],
        compiler_params=PARAMS,
        cost_estimate=tile_cost(pair_list.size),
        name="fluid_pass",
    )(own, ghosts, pair_list, place, choices, *own_results)


def outgoing_kernel(own_ref, list_ref, place_ref, wall_ref, count_ref, sent_ref, live_ref):
    for slot in range(8):
        mask = jnp.bitwise_xor(place_ref[0], slot)
        for g in range(list_ref.shape[1]):
            block = list_ref[jnp.maximum(mask - 1, 0), g]
            first = (slot * list_ref.shape[1] + g) * ROWS
            sent_ref[first : first + ROWS, :] = own_ref[rows_at(block), :]
    lane = lax.broadcasted_iota(jnp.int32, (4, LANES), 1)
    row = lax.broadcasted_iota(jnp.int32, (4, LANES), 0)
    for c in range(wall_ref.shape[1] // LANES):
        block = wall_ref[:, c * LANES : (c + 1) * LANES]
        kept = (row < 3) | (lane < count_ref[c])
        live_ref[4 * c : 4 * c + 4, :] = jnp.where(kept, block, 0.0)


def outgoing_pass(own, ghost_list, place, wall_state, wall_count):
    count = 8 * ghost_list.shape[1]
    walls = wall_state.shape[1] // LANES
    return pl.pallas_call(
        outgoing_kernel,
        out_shape=(
            jax.ShapeDtypeStruct((count * ROWS, LANES), jnp.float32),
            jax.ShapeDtypeStruct((walls * 4, LANES), jnp.float32),
        ),
        in_specs=[VMEM, SMEM, SMEM, VMEM, SMEM],
        out_specs=(VMEM, VMEM),
        name="outgoing_pass",
    )(own, ghost_list, place, wall_state, wall_count)


def swapped(shard, axis, bit):
    return lax.ppermute(shard, axis, [(i, i ^ 1 << bit) for i in range(lax.axis_size(axis))])


def edges(walls, axis, width):
    count = lax.axis_size(axis)
    forward = [(i, i + 1) for i in range(count - 1)]
    backward = [(target, source) for source, target in forward]
    return (
        lax.ppermute(walls[walls.shape[0] - width :], axis, forward),
        lax.ppermute(walls[:width], axis, backward),
    )


def per_device(fluid_state, ghost_list, pair_list, wall_state, wall_count, wall_pairs):
    block_total = fluid_state.shape[1] // LANES
    own = jnp.transpose(fluid_state.reshape(8, block_total, LANES), (1, 0, 2)).reshape(-1, LANES)
    place = (lax.axis_index("orb") % 8).reshape(1)
    sent, walls = outgoing_pass(own, ghost_list, place, wall_state, wall_count)
    low, high = edges(walls, "wall", 4 * EB)
    groups = [list(range(g, g + 8)) for g in range(0, lax.axis_size("orb"), 8)]
    landed = lax.all_to_all(
        sent.reshape(8, -1, LANES),
        "orb",
        0,
        0,
        axis_index_groups=groups if len(groups) > 1 else None,
    )
    choices = selections()
    own_results = own_pass(own, (low, walls, high), wall_pairs, choices)
    rate, acceleration, local_peak = fluid_pass(
        own, landed.reshape(-1, LANES), pair_list, place, choices, own_results
    )
    peak = local_peak
    for axis in ("wall", "orb"):
        for bit in range((lax.axis_size(axis) - 1).bit_length()):
            peak = jnp.maximum(peak, swapped(peak, axis, bit))
    peak = peak[0, 0]
    time_step = courant * jnp.sqrt(smoothing / (peak + 1e-06))
    return (rate.reshape(-1), acceleration, time_step)


def solution(mesh):
    return jax.shard_map(
        per_device,
        mesh=mesh,
        in_specs=(
            P(None, ("orb", "wall")),
            P(None, ("orb", "wall")),
            P(("orb", "wall"), None),
            P(None, ("orb", "wall")),
            P(("orb", "wall")),
            P(("orb", "wall"), None),
        ),
        out_specs=(P(("orb", "wall")), P(None, ("orb", "wall")), P()),
        check_vma=False,
    )
```

time: 90.3 us -> 77.8 us (0.86)
  local copies, waits for them, and re-layouts: 9.01 us -> 0.71 us
  other arithmetic: 2.88 us -> 0.02 us
  waiting for transfers between devices: 10.6 us -> 7.82 us
  starting transfers between devices: 19.7 us -> 22.2 us
    unnamed x16 -> x12, local copies, waits for them, and re-layouts: 8.5 us -> 0.19 us
    ppermute x5, waiting for transfers between devices: 8.84 us -> 7.2 us  [swapped(): lax.ppermute(shard, axis, [(i, i ^ 1 << bit) for i in range(lax.axis_size...]
    ppermute x2, starting transfers between devices: 2.74 us -> 4.32 us  [the longest x1 3.03 us: edges(): lax.ppermute(walls[walls.shape[0] - width:], axis, forward)]
    ppermute x2, waiting for transfers between devices: 1.8 us -> 0.62 us  [the longest x1 0.62 us: edges(): lax.ppermute(walls[walls.shape[0] - width:], axis, forward)]
  transfers between devices with their start and end apart: 8 -> 8, of which waited for: 6 -> 6; matrix products, arithmetic and copies ran while one was open for 5% -> 0% of each run, Pallas kernels for 13% -> 15%
where the time goes in v2:
time: 77.8 us; the launch traced here: 77.5 us
  Pallas kernels  44.2 us (57%)
  starting transfers between devices  22.2 us (29%)
  waiting for transfers between devices  7.82 us (10%)
  between operations  2.58 us (3%)
    pallas_call x1, Pallas kernels, fluid_pass(): pl.pallas_call(fluid_kernel, out_shape=(jax.ShapeDtypeStruct((blocks, LAN...  30.7 us
    pallas_call x1, Pallas kernels, own_pass(): pl.pallas_call(own_kernel, out_shape=[jax.ShapeDtypeStruct(*out) for out...  11.8 us
    ppermute x5, starting transfers between devices, swapped(): lax.ppermute(shard, axis, [(i, i ^ 1 << bit) for i in range(lax.axis_size...  10.5 us
    all_to_all x1, starting transfers between devices, per_device(): lax.all_to_all(sent.reshape(8, -1, LANES), 'orb', 0, 0, axis_index_groups...  7.4 us
    ppermute x5, waiting for transfers between devices, swapped(): lax.ppermute(shard, axis, [(i, i ^ 1 << bit) for i in range(lax.axis_size...  7.2 us
    ppermute x1, starting transfers between devices, edges(): lax.ppermute(walls[walls.shape[0] - width:], axis, forward)  3.03 us
    pallas_call x1, Pallas kernels, outgoing_pass(): pl.pallas_call(outgoing_kernel, out_shape=(jax.ShapeDtypeStruct((count *...  1.64 us
  transfers between devices with their start and end apart: 8, of which 6 were waited for; matrix products, arithmetic and copies ran while one was open for 0% of the time, Pallas kernels for 15%

profile of v2, /device:TPU:0, one launch (start us, length us, event | category | flops | bytes accessed | tf_op | source)
XLA Modules:
  0.0 77.5 jit_solution(6064944808589087762)
XLA Ops:
  0.6 1.6 %outgoing_pass.1 = (f32[384,128]{1,0:T(8,128)}, f32[24,128]{1,0:T(8,128)}) custom-call(f32[192,128]{1,0:T(8,128)} %bitcast.11, s32[7,6]{1,0:T(8,128)} %list_ref.1, s32[1]{0:T(128)} %bitcast.5.place_ref, f32[4,768]{1,0:T(4,128)} %wall_ref.1, s32[6]{0:T(128)} %count_ref.1), custom_call_target="tpu_custom_call" | custom-call | tf_op jit(solution)/shard_map/outgoing_pass/pallas_call | solution.py:393
  2.3 7.4 %all-to-all-start = ((f32[8,48,128]{2,1,0:T(8,128)}), f32[8,48,128]{2,1,0:T(8,128)S(1)}, u32[]{:S(2)}, u32[]{:S(2)}) async-start(f32[8,48,128]{2,1,0:T(8,128)} %bitcast.14), calls=%async_computation | async-start | bytes 393216 | tf_op jit(solution)/shard_map/all_to_all | solution.py:426
  9.7 1.3 %collective-permute-start.1 = (f32[4,128]{1,0:T(4,128)S(1)}, f32[4,128]{1,0:T(4,128)S(1)}, u32[]{:S(2)}, u32[]{:S(2)}) collective-permute-start(f32[4,128]{1,0:T(4,128)S(1)} %get-tuple-element.25), channel_id=1, source_target_pairs={{1,0},{2,1},{3,2},{5,4},{6,5},{7,6},{9,8},{10,9},{11,10},{13,12},{... | collective-permute-start | bytes 6152 | tf_op jit(solution)/shard_map/ppermute | solution.py:415
  11.0 0.0 copy-start.4
  11.0 3.0 %collective-permute-start = (f32[4,128]{1,0:T(4,128)S(1)}, f32[4,128]{1,0:T(4,128)S(1)}, u32[]{:S(2)}, u32[]{:S(2)}) collective-permute-start(f32[4,128]{1,0:T(4,128)S(1)} %get-tuple-element.26), channel_id=1, source_target_pairs={{0,1},{1,2},{2,3},{4,5},{5,6},{6,7},{8,9},{9,10},{10,11},{12,13},{... | collective-permute-start | bytes 6152 | tf_op jit(solution)/shard_map/ppermute | solution.py:414
  14.1 0.1 copy.11.pair_ref
  14.2 0.0 copy-done.4
  14.2 0.1 copy.10.wpair_ref
  14.3 0.0 collective-permute-done.1.high_ref
  14.3 0.6 collective-permute-done.low_ref
  14.9 11.8 %own_pass.1 = (bf16[24,64,256]{2,1,0:T(8,128)(2,1)S(1)}, bf16[24,32,256]{2,1,0:T(8,128)(2,1)S(1)}, f32[24,16,128]{2,1,0:T(8,128)S(1)}, bf16[24,128,128]{2,1,0:T(...) custom-call(f32[192,128]{1,0:T(8,128)S(1)} %bitcast.12, f32[4,128]{1,0:T(4,128)S(1)} %collective-permute-done.low_ref, ...), custom_call_target="tpu_custom_call" | custom-call | flops 1572864000 | tf_op jit(solution)/shard_map/own_pass/pallas_call | solution.py:338
  26.7 0.0 all-to-all-done
  26.7 30.7 %fluid_pass.1 = (f32[24,128]{1,0:T(8,128)}, f32[3,3072]{1,0:T(4,128)}, f32[8,128]{1,0:T(8,128)S(1)}) custom-call(f32[192,128]{1,0:T(8,128)S(1)} %bitcast.13, f32[384,128]{1,0:T(8,128)S(1)} %bitcast.10, s32[24,14]{1,0:T(8,128)S(1)} %copy.11.pair_ref, s32[1]{0:T(128)} %bitcast.5.place_ref, bf16[560,128]{1,0:T(8,128)(2,1)S(1)} %copy-done.2, ...), custom_call_target="tpu_custom_call" | custom-call | flops 5505024000 | tf_op jit(solution)/shard_map/fluid_pass/pallas_call | solution.py:353
  57.4 1.0 %collective-permute-start.2 = (f32[8,128]{1,0:T(8,128)S(1)}, f32[8,128]{1,0:T(8,128)S(1)}, u32[]{:S(2)}, u32[]{:S(2)}) collective-permute-start(f32[8,128]{1,0:T(8,128)S(1)} %get-tuple-element.24), channel_id=1, source_target_pairs={{0,1},{1,0},{2,3},{3,2},{4,5},{5,4},{6,7},{7,6},{8,9},{9,8},{10,11... | collective-permute-start | bytes 12296 | tf_op jit(solution)/shard_map/ppermute | solution.py:406
  58.5 0.8 %collective-permute-done.2 = f32[8,128]{1,0:T(8,128)S(1)} collective-permute-done((f32[8,128]{1,0:T(8,128)S(1)}, f32[8,128]{1,0:T(8,128)S(1)}, u32[]{:S(2)}, u32[]{:S(2)}) %collective-permute-start.2) | collective-permute-done | bytes 4128 | tf_op jit(solution)/shard_map/ppermute | solution.py:406
  59.3 2.5 %collective-permute-start.3 = (f32[8,128]{1,0:T(8,128)S(1)}, f32[8,128]{1,0:T(8,128)S(1)}, u32[]{:S(2)}, u32[]{:S(2)}) collective-permute-start(f32[8,128]{1,0:T(8,128)S(1)} %max.15), channel_id=1, source_target_pairs={{0,2},{1,3},{2,0},{3,1},{4,6},{5,7},{6,4},{7,5},{8,10},{9,11},{10,... | collective-permute-start | bytes 12296 | tf_op jit(solution)/shard_map/ppermute | solution.py:406
  61.8 1.6 %collective-permute-done.3 = f32[8,128]{1,0:T(8,128)S(1)} collective-permute-done((f32[8,128]{1,0:T(8,128)S(1)}, f32[8,128]{1,0:T(8,128)S(1)}, u32[]{:S(2)}, u32[]{:S(2)}) %collective-permute-start.3) | collective-permute-done | bytes 4128 | tf_op jit(solution)/shard_map/ppermute | solution.py:406
  63.4 2.0 %collective-permute-start.4 = (f32[8,128]{1,0:T(8,128)S(1)}, f32[8,128]{1,0:T(8,128)S(1)}, u32[]{:S(2)}, u32[]{:S(2)}) collective-permute-start(f32[8,128]{1,0:T(8,128)S(1)} %max.16), channel_id=1, source_target_pairs={{0,4},{4,0},{8,12},{12,8},{16,20},{20,16},{24,28},{28,24},{1,5},{5... | collective-permute-start | bytes 12296 | tf_op jit(solution)/shard_map/ppermute | solution.py:406
  65.4 1.6 %collective-permute-done.4 = f32[8,128]{1,0:T(8,128)S(1)} collective-permute-done((f32[8,128]{1,0:T(8,128)S(1)}, f32[8,128]{1,0:T(8,128)S(1)}, u32[]{:S(2)}, u32[]{:S(2)}) %collective-permute-start.4) | collective-permute-done | bytes 4128 | tf_op jit(solution)/shard_map/ppermute | solution.py:406
  67.0 2.0 %collective-permute-start.5 = (f32[8,128]{1,0:T(8,128)S(1)}, f32[8,128]{1,0:T(8,128)S(1)}, u32[]{:S(2)}, u32[]{:S(2)}) collective-permute-start(f32[8,128]{1,0:T(8,128)S(1)} %max.17), channel_id=1, source_target_pairs={{0,8},{4,12},{8,0},{12,4},{16,24},{20,28},{24,16},{28,20},{1,9},{5... | collective-permute-start | bytes 12296 | tf_op jit(solution)/shard_map/ppermute | solution.py:406
  69.0 1.6 %collective-permute-done.5 = f32[8,128]{1,0:T(8,128)S(1)} collective-permute-done((f32[8,128]{1,0:T(8,128)S(1)}, f32[8,128]{1,0:T(8,128)S(1)}, u32[]{:S(2)}, u32[]{:S(2)}) %collective-permute-start.5) | collective-permute-done | bytes 4128 | tf_op jit(solution)/shard_map/ppermute | solution.py:406
  70.6 2.9 %collective-permute-start.6 = (f32[8,128]{1,0:T(8,128)S(1)}, f32[8,128]{1,0:T(8,128)S(1)}, u32[]{:S(2)}, u32[]{:S(2)}) collective-permute-start(f32[8,128]{1,0:T(8,128)S(1)} %max.18), channel_id=1, source_target_pairs={{0,16},{4,20},{8,24},{12,28},{16,0},{20,4},{24,8},{28,12},{1,17},{... | collective-permute-start | bytes 12296 | tf_op jit(solution)/shard_map/ppermute | solution.py:406
  73.5 1.6 %collective-permute-done.6 = f32[8,128]{1,0:T(8,128)S(1)} collective-permute-done((f32[8,128]{1,0:T(8,128)S(1)}, f32[8,128]{1,0:T(8,128)S(1)}, u32[]{:S(2)}, u32[]{:S(2)}) %collective-permute-start.6) | collective-permute-done | bytes 4128 | tf_op jit(solution)/shard_map/ppermute | solution.py:406
  75.1 0.5 slice.11
  (14 shorter events, 0.0 us)
Async XLA Ops:
  2.3 7.4 %copy-start.1 = (f32[24,128]{1,0:T(8,128)S(1)}, f32[24,128]{1,0:T(8,128)}, u32[]{:S(2)}) copy-start(f32[24,128]{1,0:T(8,128)} %get-tuple-element.15.wall_ref) | copy-start | bytes 36868
  2.3 12.6 %copy-start = (f32[8,3072]{1,0:T(8,128)S(1)}, f32[8,3072]{1,0:T(8,128)}, u32[]{:S(2)}) copy-start(f32[8,3072]{1,0:T(8,128)} %param.7) | copy-start | bytes 294916
  2.3 12.6 %copy-start.2 = (bf16[560,128]{1,0:T(8,128)(2,1)S(1)}, bf16[560,128]{1,0:T(8,128)(2,1)}, u32[]{:S(2)}) copy-start(bf16[560,128]{1,0:T(8,128)(2,1)} %constant.30.clone.choices) | copy-start | bytes 430084
  2.3 24.4 %all-to-all-start = ((f32[8,48,128]{2,1,0:T(8,128)}), f32[8,48,128]{2,1,0:T(8,128)S(1)}, u32[]{:S(2)}, u32[]{:S(2)}) async-start(f32[8,48,128]{2,1,0:T(8,128)} %bitcast.14), calls=%async_computation | async-start | bytes 393216 | tf_op jit(solution)/shard_map/all_to_all | solution.py:426
  9.7 4.4 %copy-start.3 = (s32[24,14]{0,1:T(8,128)S(1)}, s32[24,14]{0,1:T(8,128)}, u32[]{:S(2)}) copy-start(s32[24,14]{0,1:T(8,128)} %param.9) | copy-start | bytes 4036
  9.7 4.5 %collective-permute-start.1 = (f32[4,128]{1,0:T(4,128)S(1)}, f32[4,128]{1,0:T(4,128)S(1)}, u32[]{:S(2)}, u32[]{:S(2)}) collective-permute-start(f32[4,128]{1,0:T(4,128)S(1)} %get-tuple-element.25), channel_id=1, source_target_pairs={{1,0},{2,1},{3,2},{5,4},{6,5},{7,6},{9,8},{10,9},{11,10},{13,12},{... | collective-permute-start | bytes 6152 | tf_op jit(solution)/shard_map/ppermute | solution.py:415
  11.0 3.1 %copy-start.4 = (s32[24,4]{0,1:T(4,128)S(1)}, s32[24,4]{0,1:T(4,128)}, u32[]{:S(2)}) copy-start(s32[24,4]{0,1:T(4,128)} %param.12) | copy-start | bytes 1156
  11.0 3.8 %collective-permute-start = (f32[4,128]{1,0:T(4,128)S(1)}, f32[4,128]{1,0:T(4,128)S(1)}, u32[]{:S(2)}, u32[]{:S(2)}) collective-permute-start(f32[4,128]{1,0:T(4,128)S(1)} %get-tuple-element.26), channel_id=1, source_target_pairs={{0,1},{1,2},{2,3},{4,5},{5,6},{6,7},{8,9},{9,10},{10,11},{12,13},{... | collective-permute-start | bytes 6152 | tf_op jit(solution)/shard_map/ppermute | solution.py:414
  57.4 1.8 %collective-permute-start.2 = (f32[8,128]{1,0:T(8,128)S(1)}, f32[8,128]{1,0:T(8,128)S(1)}, u32[]{:S(2)}, u32[]{:S(2)}) collective-permute-start(f32[8,128]{1,0:T(8,128)S(1)} %get-tuple-element.24), channel_id=1, source_target_pairs={{0,1},{1,0},{2,3},{3,2},{4,5},{5,4},{6,7},{7,6},{8,9},{9,8},{10,11... | collective-permute-start | bytes 12296 | tf_op jit(solution)/shard_map/ppermute | solution.py:406
  59.3 4.1 %collective-permute-start.3 = (f32[8,128]{1,0:T(8,128)S(1)}, f32[8,128]{1,0:T(8,128)S(1)}, u32[]{:S(2)}, u32[]{:S(2)}) collective-permute-start(f32[8,128]{1,0:T(8,128)S(1)} %max.15), channel_id=1, source_target_pairs={{0,2},{1,3},{2,0},{3,1},{4,6},{5,7},{6,4},{7,5},{8,10},{9,11},{10,... | collective-permute-start | bytes 12296 | tf_op jit(solution)/shard_map/ppermute | solution.py:406
  63.4 3.6 %collective-permute-start.4 = (f32[8,128]{1,0:T(8,128)S(1)}, f32[8,128]{1,0:T(8,128)S(1)}, u32[]{:S(2)}, u32[]{:S(2)}) collective-permute-start(f32[8,128]{1,0:T(8,128)S(1)} %max.16), channel_id=1, source_target_pairs={{0,4},{4,0},{8,12},{12,8},{16,20},{20,16},{24,28},{28,24},{1,5},{5... | collective-permute-start | bytes 12296 | tf_op jit(solution)/shard_map/ppermute | solution.py:406
  67.0 3.6 %collective-permute-start.5 = (f32[8,128]{1,0:T(8,128)S(1)}, f32[8,128]{1,0:T(8,128)S(1)}, u32[]{:S(2)}, u32[]{:S(2)}) collective-permute-start(f32[8,128]{1,0:T(8,128)S(1)} %max.17), channel_id=1, source_target_pairs={{0,8},{4,12},{8,0},{12,4},{16,24},{20,28},{24,16},{28,20},{1,9},{5... | collective-permute-start | bytes 12296 | tf_op jit(solution)/shard_map/ppermute | solution.py:406
  70.6 4.5 %collective-permute-start.6 = (f32[8,128]{1,0:T(8,128)S(1)}, f32[8,128]{1,0:T(8,128)S(1)}, u32[]{:S(2)}, u32[]{:S(2)}) collective-permute-start(f32[8,128]{1,0:T(8,128)S(1)} %max.18), channel_id=1, source_target_pairs={{0,16},{4,20},{8,24},{12,28},{16,0},{20,4},{24,8},{28,12},{1,17},{... | collective-permute-start | bytes 12296 | tf_op jit(solution)/shard_map/ppermute | solution.py:406

commit v3 on v2

v3 whole, which is shorter than its diff:
```python
import functools

import jax
import jax.numpy as jnp
from jax import lax
from jax.experimental import pallas as pl
from jax.experimental.pallas import tpu as pltpu
from jax.sharding import PartitionSpec as P

EB = 1
LANES = 128
ROWS = 8
DEPTH = 12 * ROWS
MOMENTS = 4 * ROWS
UNROLL = 4

smoothing = 0.1
support = 0.3
kernel_norm = 21.0 / (2.0 * 3.141592653589793 * support**3)
grad_coeff = -20.0 / support**2 * kernel_norm
tait_coeff = 25.0 / 7.0
visc_coeff = 0.05
cohesion = 2000.0
adhesion = 2000.0
gravity = 9.81
courant = 0.25

center = 0.3
shift = 0.0001 / support**2
press_coeff = -grad_coeff / (4.0 * cohesion)
density_coeff = (support * 4.0 * cohesion) / (-grad_coeff * visc_coeff * 2.0)

SPLITS = ((0, 0), (0, 1), (1, 0), (0, 2), (2, 0), (1, 1))


def split(value):
    first = value.astype(jnp.bfloat16).astype(jnp.float32)
    rest = value - first
    second = rest.astype(jnp.bfloat16).astype(jnp.float32)
    return [first, second, rest - second]


def pressure_ratio(density):
    square = density * density
    return tait_coeff * (square * square * square * density - 1.0) / square


def row_index():
    return lax.broadcasted_iota(jnp.int32, (ROWS, LANES), 0)


def state_of(block):
    row = row_index()
    y = jnp.where(row < 3, (block - center) * (1.0 / support), block)
    y = jnp.where(row == 6, block * density_coeff, y)
    products = y * jnp.where(row < 3, y, pltpu.roll(y, 3, axis=0))
    sums = products + pltpu.roll(products, ROWS - 1, axis=0) + pltpu.roll(products, ROWS - 2, axis=0)

    def everywhere(value, index):
        return jnp.broadcast_to(value[index : index + 1], (ROWS, LANES))

    press = press_coeff * pressure_ratio(everywhere(block, 6))
    return (
        y, everywhere(sums, 0), everywhere(sums, 3), everywhere(y, 6), everywhere(y, 7), press,
    )


def chosen(default, *cases):
    row = row_index()
    value = jnp.full((ROWS, LANES), default, jnp.float32)
    for index, case in cases:
        value = jnp.where(row == index, case, value)
    return value


def target_groups(state):
    y, n, e, r, _, press = state
    row = row_index()
    first = jnp.where(row < 6, y, jnp.where(row == 6, n + shift, e))
    scaled = r * jnp.where(row < 3, y, jnp.where(row == 3, 1.0, n + shift))
    second = jnp.where(row < 5, scaled, chosen(0.0, (5, press), (6, 1.0)))
    return first, second


def source_groups(state, wall):
    y, n, e, r, m, press = state
    row = row_index()
    minus = jnp.where(row < 3, -2.0 * y, 0.0)
    near = chosen(minus, (6, 1.0)), chosen(0.0, (6, n - shift))
    turned = jnp.where(row < 3, pltpu.roll(y, 5, axis=0), pltpu.roll(y, 3, axis=0))
    along = m * jnp.where(row < 6, turned, chosen(0.0, (7, -1.0))), chosen(0.0, (6, -m * e))
    if wall:
        press_part = chosen(0.0, (5, 2.0 * cohesion / adhesion), (6, -0.75))
        return near, along, (None, press_part)
    spread = m * r * near[0], m * chosen(minus, (3, n), (4, 1.0), (6, r * n))
    return near, along, spread, (None, chosen(0.0, (5, 1.0), (6, press - 0.75)))


def put_source(block, s, src, mom, mass_factor=1.0, wall=False):
    state = state_of(block)
    for n, (first, second) in enumerate(source_groups(state, wall)):
        firsts = split(first) if first is not None else [jnp.zeros((ROWS, LANES))] * 3
        pieces = [
            jnp.concatenate(pair, axis=0).astype(jnp.bfloat16)
            for pair in zip(firsts, split(second))
        ]
        lanes = slice(n * LANES, (n + 1) * LANES)
        for k, (_, piece) in enumerate(SPLITS):
            src[s, 2 * ROWS * k : 2 * ROWS * (k + 1), lanes] = pieces[piece]
    moment = (mass_factor * state[4]) * jnp.where(row_index() == 6, 1.0, state[0])
    moments = jnp.concatenate(split(moment) + [jnp.zeros_like(moment)], axis=0)
    moments = moments.astype(jnp.bfloat16)
    mom[s] = jnp.concatenate([moments, moments], axis=1)
    return state


def put_target(state, b, tgt):
    pieces = [jnp.concatenate(pair, axis=0) for pair in zip(*map(split, target_groups(state)))]
    rows = jnp.concatenate([pieces[piece] for piece, _ in SPLITS], axis=0)
    tgt[b] = rows.T.astype(jnp.bfloat16)


def rows_at(index):
    return pl.ds(pl.multiple_of(index * ROWS, ROWS), ROWS)


def weights_of(product, wall):
    values = [product[:, n * LANES : (n + 1) * LANES] for n in range(3 if wall else 4)]
    guarded = jnp.maximum(values[0], 1e-30)
    approach, press = values[1], values[-1]
    falloff = jnp.maximum(1.0 - guarded * lax.rsqrt(guarded), 0.0)
    cubed = falloff * falloff * falloff
    blend = falloff + press
    if not wall:
        blend += jnp.maximum(approach, 0.0) * pl.reciprocal(values[2], approx=True)
    weight = cubed * blend
    high = weight.astype(jnp.bfloat16)
    low = (weight - high.astype(jnp.float32)).astype(jnp.bfloat16)
    return jnp.concatenate([high, low], axis=1), cubed * approach


def across(left, right):
    return lax.dot_general(
        left, right, (((1,), (1,)), ((), ())), preferred_element_type=jnp.float32
    )


def run_tiles(target, tiles, wall):
    def product_of(tile):
        return jnp.dot(target, tile[0][...], preferred_element_type=jnp.float32)

    total = jnp.zeros((MOMENTS, LANES), jnp.float32)
    rate = jnp.zeros((LANES, LANES), jnp.float32)
    ahead = product_of(tiles[0])
    waiting = None
    for n, (_, moments) in enumerate(tiles):
        product = ahead
        if n + 1 < len(tiles):
            ahead = product_of(tiles[n + 1])
        weights, part = weights_of(product, wall)
        rate += part
        if waiting is not None:
            total += across(*waiting)
        waiting = (moments[...], weights)
    total += across(*waiting)
    ones = jnp.ones((ROWS, 3 * LANES), jnp.bfloat16)
    rates = across(ones, jnp.concatenate(split(rate), axis=1).astype(jnp.bfloat16))
    return total, rates


def moments_at(b):
    return pl.ds(pl.multiple_of(b * MOMENTS, MOMENTS), MOMENTS)


def own_kernel(
    own_ref, wall_ref, edge0_ref, edge1_ref, wpair_ref, odd_ref,
    src, mom, tgt, sums, rates, wsrc, wmom, table,
):
    blocks = tgt.shape[0]

    def build(b, carry):
        state = put_source(own_ref[rows_at(b), :], b, src, mom)
        put_target(state, b, tgt)
        return carry

    lax.fori_loop(0, blocks, build, 0, unroll=UNROLL)
    row = row_index()
    count = 0
    for ref in (wall_ref, edge0_ref, edge1_ref):
        for c in range(ref.shape[0] // 4):
            held = ref[4 * c : 4 * c + 4, :]
            both = jnp.concatenate([held, held], axis=0)
            density = jnp.where(row == 6, 1.0, 0.0)
            block = jnp.where((row < 3) | (row == 7), both, density)
            put_source(block, count, wsrc, wmom, adhesion / cohesion, True)
            count += 1
    inner, edge = wall_ref.shape[0] // 4, edge0_ref.shape[0] // 4
    odd = odd_ref[0]
    for c in range(inner):
        table[edge + c] = c
    for c in range(edge):
        table[c] = inner + (1 - odd) * edge + c
        table[edge + inner + c] = inner + odd * edge + c

    def per_target(b, carry):
        tiles = []
        for k in range(wpair_ref.shape[1]):
            s = table[wpair_ref[b, k]]
            tiles.append((wsrc.at[s], wmom.at[s]))
        total, rate = run_tiles(tgt[b], tiles, True)
        sums[moments_at(b), :] = total
        rates[rows_at(b), :] = rate
        return carry

    lax.fori_loop(0, blocks, per_target, 0, unroll=UNROLL)


def fluid_kernel(
    own_ref, ghost_ref, pair_ref, place_ref, own_src, own_mom,
    tgt, own_sums, own_rates, rate_ref, accel_ref, peak_ref,
    src, mom, sums, rates, stage, table, copied,
):
    blocks = tgt.shape[0]
    ghosts = ghost_ref.shape[0] // ROWS
    per_mask = ghosts // 8
    copies = [
        pltpu.make_async_copy(own_src, src.at[pl.ds(0, blocks)], copied.at[0]),
        pltpu.make_async_copy(own_mom, mom.at[pl.ds(0, blocks)], copied.at[1]),
    ]
    for copy in copies:
        copy.start()
    for c in range(blocks):
        table[c] = c
    for mask in range(1, 8):
        for g in range(per_mask):
            table[blocks + (mask - 1) * per_mask + g] = (
                blocks + jnp.bitwise_xor(place_ref[0], mask) * per_mask + g
            )

    def build(g, carry):
        put_source(ghost_ref[rows_at(g), :], blocks + g, src, mom)
        return carry

    lax.fori_loop(0, ghosts, build, 0, unroll=UNROLL)
    for copy in copies:
        copy.wait()

    def per_target(b, carry):
        tiles = []
        for k in range(pair_ref.shape[1]):
            s = table[pair_ref[b, k]]
            tiles.append((src.at[s], mom.at[s]))
        total, rate = run_tiles(tgt[b], tiles, False)
        sums[moments_at(b), :] = own_sums[moments_at(b), :] + total
        rates[rows_at(b), :] = own_rates[rows_at(b), :] + rate
        return carry

    lax.fori_loop(0, blocks, per_target, 0)

    rate_ref[...] = (-support * grad_coeff) * rates[pl.ds(0, blocks, stride=ROWS), :]

    def summed(row):
        parts = [sums[pl.ds(p * ROWS + row, blocks, stride=MOMENTS), :] for p in range(3)]
        return parts[0] + parts[1] + parts[2]

    mass_sum = summed(6)
    square = jnp.zeros_like(mass_sum)
    for d in range(3):
        pos = (own_ref[pl.ds(d, blocks, stride=ROWS), :] - center) * (1.0 / support)
        force = (4.0 * cohesion * support) * (pos * mass_sum - summed(d))
        if d == 2:
            force -= gravity
        square += force * force
        stage[pl.ds(d, blocks, stride=ROWS), :] = force
    for b in range(blocks):
        accel_ref[:, b * LANES : (b + 1) * LANES] = stage[b * ROWS : b * ROWS + 3, :]
    peak_ref[...] = jnp.full(peak_ref.shape, jnp.sqrt(jnp.max(square)), jnp.float32)


SMEM = pl.BlockSpec(memory_space=pltpu.SMEM)
VMEM = pl.BlockSpec(memory_space=pltpu.VMEM)
PARAMS = pltpu.CompilerParams(vmem_limit_bytes=32 * 1024 * 1024)


def tile_cost(tiles):
    return pl.CostEstimate(
        flops=tiles * LANES * LANES * 1000, bytes_accessed=0, transcendentals=0
    )


def source_shapes(count, values):
    return [
        ((count, DEPTH, values * LANES), jnp.bfloat16),
        ((count, MOMENTS, 2 * LANES), jnp.bfloat16),
    ]


def own_pass(own, walls, edges, wall_pairs, odd):
    blocks = own.shape[0] // ROWS
    wall_blocks = (walls.shape[0] + 2 * edges[0].shape[0]) // 4
    outs = source_shapes(blocks, 4) + [
        ((blocks, LANES, DEPTH), jnp.bfloat16),
        ((blocks * MOMENTS, LANES), jnp.float32),
        ((blocks * ROWS, LANES), jnp.float32),
    ]
    return pl.pallas_call(
        own_kernel,
        out_shape=[jax.ShapeDtypeStruct(*out) for out in outs],
        in_specs=[VMEM, VMEM, VMEM, VMEM, SMEM, SMEM],
        out_specs=[VMEM] * len(outs),
        scratch_shapes=[pltpu.VMEM(*shape) for shape in source_shapes(wall_blocks, 3)]
        + [pltpu.SMEM((wall_blocks,), jnp.int32)],
        compiler_params=PARAMS,
        cost_estimate=tile_cost(wall_pairs.size),
        name="own_pass",
    )(own, walls, *edges, wall_pairs, odd)


def fluid_pass(own, ghosts, pair_list, place, own_results):
    blocks = own.shape[0] // ROWS
    total = blocks + ghosts.shape[0] // ROWS
    return pl.pallas_call(
        fluid_kernel,
        out_shape=(
            jax.ShapeDtypeStruct((blocks, LANES), jnp.float32),
            jax.ShapeDtypeStruct((3, blocks * LANES), jnp.float32),
            jax.ShapeDtypeStruct((ROWS, LANES), jnp.float32),
        ),
        in_specs=[VMEM, VMEM, SMEM, SMEM] + [VMEM] * len(own_results),
        out_specs=(VMEM, VMEM, VMEM),
        scratch_shapes=[pltpu.VMEM(*shape) for shape in source_shapes(total, 4)]
        + [
            pltpu.VMEM((blocks * MOMENTS, LANES), jnp.float32),
            pltpu.VMEM((blocks * ROWS, LANES), jnp.float32),
            pltpu.VMEM((blocks * ROWS, LANES), jnp.float32),
            pltpu.SMEM((total,), jnp.int32),
            pltpu.SemaphoreType.DMA((2,)),
        ],
        compiler_params=PARAMS,
        cost_estimate=tile_cost(pair_list.size),
        name="fluid_pass",
    )(own, ghosts, pair_list, place, *own_results)


def outgoing_kernel(own_ref, list_ref, place_ref, wall_ref, count_ref, sent_ref, live_ref):
    for slot in range(8):
        mask = jnp.bitwise_xor(place_ref[0], slot)
        for g in range(list_ref.shape[1]):
            block = list_ref[jnp.maximum(mask - 1, 0), g]
            first = (slot * list_ref.shape[1] + g) * ROWS
            sent_ref[first : first + ROWS, :] = own_ref[rows_at(block), :]
    lane = lax.broadcasted_iota(jnp.int32, (4, LANES), 1)
    row = lax.broadcasted_iota(jnp.int32, (4, LANES), 0)
    for c in range(wall_ref.shape[1] // LANES):
        block = wall_ref[:, c * LANES : (c + 1) * LANES]
        kept = (row < 3) | (lane < count_ref[c])
        live_ref[4 * c : 4 * c + 4, :] = jnp.where(kept, block, 0.0)


def outgoing_pass(own, ghost_list, place, wall_state, wall_count):
    count = 8 * ghost_list.shape[1]
    walls = wall_state.shape[1] // LANES
    return pl.pallas_call(
        outgoing_kernel,
        out_shape=(
            jax.ShapeDtypeStruct((count * ROWS, LANES), jnp.float32),
            jax.ShapeDtypeStruct((walls * 4, LANES), jnp.float32),
        ),
        in_specs=[VMEM, SMEM, SMEM, VMEM, SMEM],
        out_specs=(VMEM, VMEM),
        name="outgoing_pass",
    )(own, ghost_list, place, wall_state, wall_count)


def swapped(shard, axis, bit):
    return lax.ppermute(shard, axis, [(i, i ^ 1 << bit) for i in range(lax.axis_size(axis))])


def edges(walls, axis, width):
    count = lax.axis_size(axis)
    odd = lax.axis_index(axis) % 2
    first, last = walls[:width], walls[walls.shape[0] - width :]
    landed = []
    for start in range(2):
        pairs = [(i, i + 1) for i in range(start, count - 1, 2)]
        pairs += [(j, i) for i, j in pairs]
        sent = jnp.where(odd == start, last, first)
        landed.append(lax.ppermute(sent, axis, pairs))
    return landed, odd.reshape(1)


def per_device(fluid_state, ghost_list, pair_list, wall_state, wall_count, wall_pairs):
    block_total = fluid_state.shape[1] // LANES
    own = jnp.transpose(fluid_state.reshape(8, block_total, LANES), (1, 0, 2)).reshape(-1, LANES)
    place = (lax.axis_index("orb") % 8).reshape(1)
    sent, walls = outgoing_pass(own, ghost_list, place, wall_state, wall_count)
    facing, odd = edges(walls, "wall", 4 * EB)
    groups = [list(range(g, g + 8)) for g in range(0, lax.axis_size("orb"), 8)]
    landed = lax.all_to_all(
        sent.reshape(8, -1, LANES),
        "orb",
        0,
        0,
        axis_index_groups=groups if len(groups) > 1 else None,
    )
    own_results = own_pass(own, walls, facing, wall_pairs, odd)
    rate, acceleration, local_peak = fluid_pass(
        own, landed.reshape(-1, LANES), pair_list, place, own_results
    )
    peak = local_peak
    for axis in ("wall", "orb"):
        for bit in range((lax.axis_size(axis) - 1).bit_length()):
            peak = jnp.maximum(peak, swapped(peak, axis, bit))
    peak = peak[0, 0]
    time_step = courant * jnp.sqrt(smoothing / (peak + 1e-06))
    return (rate.reshape(-1), acceleration, time_step)


def solution(mesh):
    return jax.shard_map(
        per_device,
        mesh=mesh,
        in_specs=(
            P(None, ("orb", "wall")),
            P(None, ("orb", "wall")),
            P(("orb", "wall"), None),
            P(None, ("orb", "wall")),
            P(("orb", "wall")),
            P(("orb", "wall"), None),
        ),
        out_specs=(P(("orb", "wall")), P(None, ("orb", "wall")), P()),
        check_vma=False,
    )
```

time: 77.8 us -> 82.6 us (1.062)
  local copies, waits for them, and re-layouts: 0.71 us -> 8.69 us
  starting transfers between devices: 22.2 us -> 19.2 us
  Pallas kernels: 44.2 us -> 42.6 us
    unnamed x12 -> x20, local copies, waits for them, and re-layouts: 0.19 us -> 8.17 us
    ppermute x5, starting transfers between devices: 10.5 us -> 8.3 us  [swapped(): lax.ppermute(shard, axis, [(i, i ^ 1 << bit) for i in range(lax.axis_size...]
    ppermute x5, waiting for transfers between devices: 7.2 us -> 8.26 us  [swapped(): lax.ppermute(shard, axis, [(i, i ^ 1 << bit) for i in range(lax.axis_size...]
    pallas_call x1, Pallas kernels: 11.8 us -> 10.9 us  [own_pass(): pl.pallas_call(own_kernel, out_shape=[jax.ShapeDtypeStruct(*out) for out...]
  transfers between devices with their start and end apart: 8 -> 8, of which waited for: 6 -> 5; matrix products, arithmetic and copies ran while one was open for 0% -> 3% of each run, Pallas kernels for 15% -> 13%
where the time goes in v3:
time: 82.6 us; the launch traced here: 82 us
  Pallas kernels  42.6 us (52%)
  starting transfers between devices  19.2 us (23%)
  local copies, waits for them, and re-layouts  8.69 us (11%)
  waiting for transfers between devices  8.27 us (10%)
  between operations  2.55 us (3%)
    pallas_call x1, Pallas kernels, fluid_pass(): pl.pallas_call(fluid_kernel, out_shape=(jax.ShapeDtypeStruct((blocks, LAN...  30 us
    pallas_call x1, Pallas kernels, own_pass(): pl.pallas_call(own_kernel, out_shape=[jax.ShapeDtypeStruct(*out) for out...  10.9 us
    ppermute x5, starting transfers between devices, swapped(): lax.ppermute(shard, axis, [(i, i ^ 1 << bit) for i in range(lax.axis_size...  8.3 us
    ppermute x5, waiting for transfers between devices, swapped(): lax.ppermute(shard, axis, [(i, i ^ 1 << bit) for i in range(lax.axis_size...  8.26 us
    unnamed x20, local copies, waits for them, and re-layouts  8.17 us
    all_to_all x1, starting transfers between devices, per_device(): lax.all_to_all(sent.reshape(8, -1, LANES), 'orb', 0, 0, axis_index_groups...  7.25 us
    ppermute x2, starting transfers between devices, edges(): landed.append(lax.ppermute(sent, axis, pairs))  3.6 us
  transfers between devices with their start and end apart: 8, of which 5 were waited for; matrix products, arithmetic and copies ran while one was open for 3% of the time, Pallas kernels for 13%

profile of v3, /device:TPU:0, one launch (start us, length us, event | category | flops | bytes accessed | tf_op | source)
XLA Modules:
  0.0 82.0 jit_solution(15447099674872805845)
XLA Ops:
  0.6 1.7 %outgoing_pass.1 = (f32[384,128]{1,0:T(8,128)}, f32[24,128]{1,0:T(8,128)}) custom-call(f32[192,128]{1,0:T(8,128)} %bitcast.12, s32[7,6]{1,0:T(8,128)} %list_ref.1, s32[1]{0:T(128)} %bitcast.5.place_ref, f32[4,768]{1,0:T(4,128)} %wall_ref.1, s32[6]{0:T(128)} %count_ref.1), custom_call_target="tpu_custom_call" | custom-call | tf_op jit(solution)/shard_map/outgoing_pass/pallas_call | solution.py:363
  2.3 7.3 %all-to-all-start = ((f32[8,48,128]{2,1,0:T(8,128)}), f32[8,48,128]{2,1,0:T(8,128)S(1)}, u32[]{:S(2)}, u32[]{:S(2)}) async-start(f32[8,48,128]{2,1,0:T(8,128)} %bitcast.15), calls=%async_computation | async-start | bytes 393216 | tf_op jit(solution)/shard_map/all_to_all | solution.py:399
  9.5 0.7 slice_select_fusion
  10.9 2.9 %collective-permute-start = (f32[4,128]{1,0:T(4,128)S(1)}, f32[4,128]{1,0:T(4,128)S(1)}, u32[]{:S(2)}, u32[]{:S(2)}) collective-permute-start(f32[4,128]{1,0:T(4,128)S(1)} %get-tuple-element.24), channel_id=1, source_target_pairs={{0,1},{2,3},{1,0},{3,2},{4,5},{6,7},{5,4},{7,6},{8,9},{10,11},{9,8... | collective-permute-start | bytes 6152 | tf_op jit(solution)/shard_map/ppermute | solution.py:388
  13.9 0.8 copy.10.pair_ref
  14.6 0.8 copy.9.wpair_ref
  15.4 0.9 %copy-done = f32[8,3072]{1,0:T(8,128)S(1)} copy-done((f32[8,3072]{1,0:T(8,128)S(1)}, f32[8,3072]{1,0:T(8,128)}, u32[]{:S(2)}) %copy-start) | copy-done | bytes 98328
  16.3 0.7 copy-done.2
  17.0 10.9 %own_pass.1 = (bf16[24,96,512]{2,1,0:T(8,128)(2,1)S(1)}, bf16[24,32,256]{2,1,0:T(8,128)(2,1)S(1)}, bf16[24,128,96]{2,1,0:T(8,128)(2,1)S(1)}, f32[768,128]{1,0:T(8,128)S(1)}, f32[192,128]{1,0:T(8,128)S(1)}) custom-call(f32[192,128]{1,0:T(8,128)S(1)} %bitcast.13, f32[24,128]{1,0:T(8,128)S(1)} %copy-done.2, f32[4,128]{1,0:T(4,128)S(1)} %collective-permute-done.edge0_ref, ...), custom_call_target="tpu_custom_call" | custom-call | flops 1572864000 | tf_op jit(solution)/shard_map/own_pass/pallas_call | solution.py:306
  28.0 0.8 copy-done.3
  28.7 0.7 copy-done.5
  30.1 1.0 %copy-done.4 = bf16[24,32,256]{2,1,0:T(8,128)(2,1)S(1)} copy-done((bf16[24,32,256]{2,1,0:T(8,128)(2,1)S(1)}, bf16[24,32,256]{2,1,0:T(8,128)(2,1)}, u32[]{:S(2)}) %copy-start.4) | copy-done | bytes 393240
  31.1 1.0 %copy-done.6 = f32[768,128]{1,0:T(8,128)S(1)} copy-done((f32[768,128]{1,0:T(8,128)S(1)}, f32[768,128]{1,0:T(8,128)}, u32[]{:S(2)}) %copy-start.6) | copy-done | bytes 393240
  32.1 0.9 %copy-done.8 = f32[192,128]{1,0:T(8,128)S(1)} copy-done((f32[192,128]{1,0:T(8,128)S(1)}, f32[192,128]{1,0:T(8,128)}, u32[]{:S(2)}) %copy-start.8) | copy-done | bytes 98328
  33.0 30.0 %fluid_pass.1 = (f32[24,128]{1,0:T(8,128)}, f32[3,3072]{1,0:T(4,128)}, f32[8,128]{1,0:T(8,128)S(1)}) custom-call(f32[192,128]{1,0:T(8,128)S(1)} %bitcast.14, f32[384,128]{1,0:T(8,128)S(1)} %bitcast.11, s32[24,14]{1,0:T(8,128)S(1)} %copy.10.pair_ref, s32[1]{0:T(128)} %bitcast.5.place_ref, bf16[24,96,512]{2,1,0:T(8,128)(2,1)S(1)} %get-tuple-element.15.own_src, ...), custom_call_target="tpu_custom_call" | custom-call | flops 5505024000 | tf_op jit(solution)/shard_map/fluid_pass/pallas_call | solution.py:322
  63.1 1.2 %collective-permute-done.2 = f32[8,128]{1,0:T(8,128)S(1)} collective-permute-done((f32[8,128]{1,0:T(8,128)S(1)}, f32[8,128]{1,0:T(8,128)S(1)}, u32[]{:S(2)}, u32[]{:S(2)}) %collective-permute-start.2) | collective-permute-done | bytes 4128 | tf_op jit(solution)/shard_map/ppermute | solution.py:376
  64.3 1.3 %collective-permute-start.3 = (f32[8,128]{1,0:T(8,128)S(1)}, f32[8,128]{1,0:T(8,128)S(1)}, u32[]{:S(2)}, u32[]{:S(2)}) collective-permute-start(f32[8,128]{1,0:T(8,128)S(1)} %max.15), channel_id=1, source_target_pairs={{0,2},{1,3},{2,0},{3,1},{4,6},{5,7},{6,4},{7,5},{8,10},{9,11},{10,... | collective-permute-start | bytes 12296 | tf_op jit(solution)/shard_map/ppermute | solution.py:376
  65.6 2.3 %collective-permute-done.3 = f32[8,128]{1,0:T(8,128)S(1)} collective-permute-done((f32[8,128]{1,0:T(8,128)S(1)}, f32[8,128]{1,0:T(8,128)S(1)}, u32[]{:S(2)}, u32[]{:S(2)}) %collective-permute-start.3) | collective-permute-done | bytes 4128 | tf_op jit(solution)/shard_map/ppermute | solution.py:376
  67.9 2.0 %collective-permute-start.4 = (f32[8,128]{1,0:T(8,128)S(1)}, f32[8,128]{1,0:T(8,128)S(1)}, u32[]{:S(2)}, u32[]{:S(2)}) collective-permute-start(f32[8,128]{1,0:T(8,128)S(1)} %max.16), channel_id=1, source_target_pairs={{0,4},{4,0},{8,12},{12,8},{16,20},{20,16},{24,28},{28,24},{1,5},{5... | collective-permute-start | bytes 12296 | tf_op jit(solution)/shard_map/ppermute | solution.py:376
  69.9 1.6 %collective-permute-done.4 = f32[8,128]{1,0:T(8,128)S(1)} collective-permute-done((f32[8,128]{1,0:T(8,128)S(1)}, f32[8,128]{1,0:T(8,128)S(1)}, u32[]{:S(2)}, u32[]{:S(2)}) %collective-permute-start.4) | collective-permute-done | bytes 4128 | tf_op jit(solution)/shard_map/ppermute | solution.py:376
  71.5 2.0 %collective-permute-start.5 = (f32[8,128]{1,0:T(8,128)S(1)}, f32[8,128]{1,0:T(8,128)S(1)}, u32[]{:S(2)}, u32[]{:S(2)}) collective-permute-start(f32[8,128]{1,0:T(8,128)S(1)} %max.17), channel_id=1, source_target_pairs={{0,8},{4,12},{8,0},{12,4},{16,24},{20,28},{24,16},{28,20},{1,9},{5... | collective-permute-start | bytes 12296 | tf_op jit(solution)/shard_map/ppermute | solution.py:376
  73.5 1.6 %collective-permute-done.5 = f32[8,128]{1,0:T(8,128)S(1)} collective-permute-done((f32[8,128]{1,0:T(8,128)S(1)}, f32[8,128]{1,0:T(8,128)S(1)}, u32[]{:S(2)}, u32[]{:S(2)}) %collective-permute-start.5) | collective-permute-done | bytes 4128 | tf_op jit(solution)/shard_map/ppermute | solution.py:376
  75.1 2.9 %collective-permute-start.6 = (f32[8,128]{1,0:T(8,128)S(1)}, f32[8,128]{1,0:T(8,128)S(1)}, u32[]{:S(2)}, u32[]{:S(2)}) collective-permute-start(f32[8,128]{1,0:T(8,128)S(1)} %max.18), channel_id=1, source_target_pairs={{0,16},{4,20},{8,24},{12,28},{16,0},{20,4},{24,8},{28,12},{1,17},{... | collective-permute-start | bytes 12296 | tf_op jit(solution)/shard_map/ppermute | solution.py:376
  78.0 1.6 %collective-permute-done.6 = f32[8,128]{1,0:T(8,128)S(1)} collective-permute-done((f32[8,128]{1,0:T(8,128)S(1)}, f32[8,128]{1,0:T(8,128)S(1)}, u32[]{:S(2)}, u32[]{:S(2)}) %collective-permute-start.6) | collective-permute-done | bytes 4128 | tf_op jit(solution)/shard_map/ppermute | solution.py:376
  (22 shorter events, 1.9 us)
Async XLA Ops:
  2.3 27.8 %all-to-all-start = ((f32[8,48,128]{2,1,0:T(8,128)}), f32[8,48,128]{2,1,0:T(8,128)S(1)}, u32[]{:S(2)}, u32[]{:S(2)}) async-start(f32[8,48,128]{2,1,0:T(8,128)} %bitcast.15), calls=%async_computation | async-start | bytes 393216 | tf_op jit(solution)/shard_map/all_to_all | solution.py:399
  10.3 5.1 %collective-permute-start.1 = (f32[4,128]{1,0:T(4,128)S(1)}, f32[4,128]{1,0:T(4,128)S(1)}, u32[]{:S(2)}, u32[]{:S(2)}) collective-permute-start(f32[4,128]{1,0:T(4,128)S(1)} %get-tuple-element.23), channel_id=1, source_target_pairs={{1,2},{2,1},{5,6},{6,5},{9,10},{10,9},{13,14},{14,13},{17,18},{18,... | collective-permute-start | bytes 6152 | tf_op jit(solution)/shard_map/ppermute | solution.py:388
  10.9 4.5 %collective-permute-start = (f32[4,128]{1,0:T(4,128)S(1)}, f32[4,128]{1,0:T(4,128)S(1)}, u32[]{:S(2)}, u32[]{:S(2)}) collective-permute-start(f32[4,128]{1,0:T(4,128)S(1)} %get-tuple-element.24), channel_id=1, source_target_pairs={{0,1},{2,3},{1,0},{3,2},{4,5},{6,7},{5,4},{7,6},{8,9},{10,11},{9,8... | collective-permute-start | bytes 6152 | tf_op jit(solution)/shard_map/ppermute | solution.py:388
  15.4 0.9 %copy-start = (f32[8,3072]{1,0:T(8,128)S(1)}, f32[8,3072]{1,0:T(8,128)}, u32[]{:S(2)}) copy-start(f32[8,3072]{1,0:T(8,128)} %param.6) | copy-start | bytes 294916
  16.3 0.7 copy-start.2
  17.0 13.1 %copy-start.1 = (f32[8,3072]{1,0:T(8,128)S(1)}, f32[8,3072]{1,0:T(8,128)}, u32[]{:S(2)}) copy-start(f32[8,3072]{1,0:T(8,128)} %param.6) | copy-start | bytes 294916
  28.0 0.8 copy-start.3
  28.7 0.7 copy-start.5
  29.5 0.6 copy-start.7
  30.1 1.0 %copy-start.4 = (bf16[24,32,256]{2,1,0:T(8,128)(2,1)S(1)}, bf16[24,32,256]{2,1,0:T(8,128)(2,1)}, u32[]{:S(2)}) copy-start(bf16[24,32,256]{2,1,0:T(8,128)(2,1)} %copy-done.3) | copy-start | bytes 1179652
  31.1 1.0 %copy-start.6 = (f32[768,128]{1,0:T(8,128)S(1)}, f32[768,128]{1,0:T(8,128)}, u32[]{:S(2)}) copy-start(f32[768,128]{1,0:T(8,128)} %copy-done.5) | copy-start | bytes 1179652
  32.1 0.9 %copy-start.8 = (f32[192,128]{1,0:T(8,128)S(1)}, f32[192,128]{1,0:T(8,128)}, u32[]{:S(2)}) copy-start(f32[192,128]{1,0:T(8,128)} %copy-done.7) | copy-start | bytes 294916
  63.0 1.2 %collective-permute-start.2 = (f32[8,128]{1,0:T(8,128)S(1)}, f32[8,128]{1,0:T(8,128)S(1)}, u32[]{:S(2)}, u32[]{:S(2)}) collective-permute-start(f32[8,128]{1,0:T(8,128)S(1)} %get-tuple-element.22), channel_id=1, source_target_pairs={{0,1},{1,0},{2,3},{3,2},{4,5},{5,4},{6,7},{7,6},{8,9},{9,8},{10,11... | collective-permute-start | bytes 12296 | tf_op jit(solution)/shard_map/ppermute | solution.py:376
  64.3 3.6 %collective-permute-start.3 = (f32[8,128]{1,0:T(8,128)S(1)}, f32[8,128]{1,0:T(8,128)S(1)}, u32[]{:S(2)}, u32[]{:S(2)}) collective-permute-start(f32[8,128]{1,0:T(8,128)S(1)} %max.15), channel_id=1, source_target_pairs={{0,2},{1,3},{2,0},{3,1},{4,6},{5,7},{6,4},{7,5},{8,10},{9,11},{10,... | collective-permute-start | bytes 12296 | tf_op jit(solution)/shard_map/ppermute | solution.py:376
  67.9 3.6 %collective-permute-start.4 = (f32[8,128]{1,0:T(8,128)S(1)}, f32[8,128]{1,0:T(8,128)S(1)}, u32[]{:S(2)}, u32[]{:S(2)}) collective-permute-start(f32[8,128]{1,0:T(8,128)S(1)} %max.16), channel_id=1, source_target_pairs={{0,4},{4,0},{8,12},{12,8},{16,20},{20,16},{24,28},{28,24},{1,5},{5... | collective-permute-start | bytes 12296 | tf_op jit(solution)/shard_map/ppermute | solution.py:376
  71.5 3.6 %collective-permute-start.5 = (f32[8,128]{1,0:T(8,128)S(1)}, f32[8,128]{1,0:T(8,128)S(1)}, u32[]{:S(2)}, u32[]{:S(2)}) collective-permute-start(f32[8,128]{1,0:T(8,128)S(1)} %max.17), channel_id=1, source_target_pairs={{0,8},{4,12},{8,0},{12,4},{16,24},{20,28},{24,16},{28,20},{1,9},{5... | collective-permute-start | bytes 12296 | tf_op jit(solution)/shard_map/ppermute | solution.py:376
  75.1 4.5 %collective-permute-start.6 = (f32[8,128]{1,0:T(8,128)S(1)}, f32[8,128]{1,0:T(8,128)S(1)}, u32[]{:S(2)}, u32[]{:S(2)}) collective-permute-start(f32[8,128]{1,0:T(8,128)S(1)} %max.18), channel_id=1, source_target_pairs={{0,16},{4,20},{8,24},{12,28},{16,0},{20,4},{24,8},{28,12},{1,17},{... | collective-permute-start | bytes 12296 | tf_op jit(solution)/shard_map/ppermute | solution.py:376

commit v4 on v3

--- a/solution.py
+++ b/solution.py
@@ -13,6 +13,8 @@
 DEPTH = 12 * ROWS
 MOMENTS = 4 * ROWS
 UNROLL = 4
+WALL_TARGETS = 6
+FLUID_TARGETS = 3
 
 smoothing = 0.1
 support = 0.3
@@ -145,27 +147,34 @@
     )
 
 
-def run_tiles(target, tiles, wall):
-    def product_of(tile):
-        return jnp.dot(target, tile[0][...], preferred_element_type=jnp.float32)
-
-    total = jnp.zeros((MOMENTS, LANES), jnp.float32)
-    rate = jnp.zeros((LANES, LANES), jnp.float32)
-    ahead = product_of(tiles[0])
+def run_targets(targets, wall, finish):
+    steps = [(n, tile) for n, (_, tiles) in enumerate(targets) for tile in tiles]
+    totals = [jnp.zeros((MOMENTS, LANES), jnp.float32)] * len(targets)
+    rates = [jnp.zeros((LANES, LANES), jnp.float32)] * len(targets)
+
+    def product_of(step):
+        n, tile = step
+        return jnp.dot(targets[n][0], tile[0][...], preferred_element_type=jnp.float32)
+
+    def add_up(n, moments, weights, last):
+        totals[n] += across(moments, weights)
+        if last:
+            ones = jnp.ones((ROWS, 3 * LANES), jnp.bfloat16)
+            pieces = jnp.concatenate(split(rates[n]), axis=1).astype(jnp.bfloat16)
+            finish(n, totals[n], across(ones, pieces))
+
+    ahead = product_of(steps[0])
     waiting = None
-    for n, (_, moments) in enumerate(tiles):
+    for k, (n, (_, moments)) in enumerate(steps):
         product = ahead
-        if n + 1 < len(tiles):
-            ahead = product_of(tiles[n + 1])
+        if k + 1 < len(steps):
+            ahead = product_of(steps[k + 1])
         weights, part = weights_of(product, wall)
-        rate += part
+        rates[n] += part
         if waiting is not None:
-            total += across(*waiting)
-        waiting = (moments[...], weights)
-    total += across(*waiting)
-    ones = jnp.ones((ROWS, 3 * LANES), jnp.bfloat16)
-    rates = across(ones, jnp.concatenate(split(rate), axis=1).astype(jnp.bfloat16))
-    return total, rates
+            add_up(*waiting, waiting[0] != n)
+        waiting = (n, moments[...], weights)
+    add_up(*waiting, True)
 
 
 def moments_at(b):
@@ -202,17 +211,21 @@
         table[c] = inner + (1 - odd) * edge + c
         table[edge + inner + c] = inner + odd * edge + c
 
-    def per_target(b, carry):
-        tiles = []
-        for k in range(wpair_ref.shape[1]):
-            s = table[wpair_ref[b, k]]
-            tiles.append((wsrc.at[s], wmom.at[s]))
-        total, rate = run_tiles(tgt[b], tiles, True)
-        sums[moments_at(b), :] = total
-        rates[rows_at(b), :] = rate
+    def targets_from(i, carry):
+        first = i * WALL_TARGETS
+        targets = []
+        for n in range(WALL_TARGETS):
+            slots = [table[wpair_ref[first + n, k]] for k in range(wpair_ref.shape[1])]
+            targets.append((tgt[first + n], [(wsrc.at[s], wmom.at[s]) for s in slots]))
+
+        def finish(n, total, rate):
+            sums[moments_at(first + n), :] = total
+            rates[rows_at(first + n), :] = rate
+
+        run_targets(targets, True, finish)
         return carry
 
-    lax.fori_loop(0, blocks, per_target, 0, unroll=UNROLL)
+    lax.fori_loop(0, blocks // WALL_TARGETS, targets_from, 0)
 
 
 def fluid_kernel(
@@ -245,17 +258,22 @@
     for copy in copies:
         copy.wait()
 
-    def per_target(b, carry):
-        tiles = []
-        for k in range(pair_ref.shape[1]):
-            s = table[pair_ref[b, k]]
-            tiles.append((src.at[s], mom.at[s]))
-        total, rate = run_tiles(tgt[b], tiles, False)
-        sums[moments_at(b), :] = own_sums[moments_at(b), :] + total
-        rates[rows_at(b), :] = own_rates[rows_at(b), :] + rate
+    def targets_from(i, carry):
+        first = i * FLUID_TARGETS
+        targets = []
+        for n in range(FLUID_TARGETS):
+            slots = [table[pair_ref[first + n, k]] for k in range(pair_ref.shape[1])]
+            targets.append((tgt[first + n], [(src.at[s], mom.at[s]) for s in slots]))
+
+        def finish(n, total, rate):
+            b = first + n
+            sums[moments_at(b), :] = own_sums[moments_at(b), :] + total
+            rates[rows_at(b), :] = own_rates[rows_at(b), :] + rate
+
+        run_targets(targets, False, finish)
         return carry
 
-    lax.fori_loop(0, blocks, per_target, 0)
+    lax.fori_loop(0, blocks // FLUID_TARGETS, targets_from, 0)
 
     rate_ref[...] = (-support * grad_coeff) * rates[pl.ds(0, blocks, stride=ROWS), :]
 
@@ -279,7 +297,7 @@
 
 SMEM = pl.BlockSpec(memory_space=pltpu.SMEM)
 VMEM = pl.BlockSpec(memory_space=pltpu.VMEM)
-PARAMS = pltpu.CompilerParams(vmem_limit_bytes=32 * 1024 * 1024)
+PARAMS = pltpu.CompilerParams(vmem_limit_bytes=18 * 1024 * 1024)
 
 
 def tile_cost(tiles):
@@ -368,6 +386,7 @@
         ),
         in_specs=[VMEM, SMEM, SMEM, VMEM, SMEM],
         out_specs=(VMEM, VMEM),
+        compiler_params=PARAMS,
         name="outgoing_pass",
     )(own, ghost_list, place, wall_state, wall_count)
 

time: 82.6 us -> 77.8 us (0.942)
  Pallas kernels: 42.6 us -> 36.3 us
  local copies, waits for them, and re-layouts: 8.69 us -> 10.9 us
    pallas_call x1, Pallas kernels: 30 us -> 25.8 us  [fluid_pass(): pl.pallas_call(fluid_kernel, out_shape=(jax.ShapeDtypeStruct((blocks, LAN...]
    unnamed x20 -> x26, local copies, waits for them, and re-layouts: 8.17 us -> 10.4 us
    pallas_call x1, Pallas kernels: 10.9 us -> 9.18 us  [own_pass(): pl.pallas_call(own_kernel, out_shape=[jax.ShapeDtypeStruct(*out) for out...]
  transfers between devices with their start and end apart: 8 -> 8, of which waited for: 5 -> 5; matrix products, arithmetic and copies ran while one was open for 3% -> 2% of each run, Pallas kernels for 13% -> 12%
where the time goes in v4:
time: 77.8 us; the launch traced here: 77.2 us
  Pallas kernels  36.3 us (47%)
  starting transfers between devices  19.2 us (25%)
  local copies, waits for them, and re-layouts  10.9 us (14%)
  waiting for transfers between devices  8.25 us (11%)
  between operations  2.56 us (3%)
    pallas_call x1, Pallas kernels, fluid_pass(): pl.pallas_call(fluid_kernel, out_shape=(jax.ShapeDtypeStruct((blocks, LAN...  25.8 us
    unnamed x26, local copies, waits for them, and re-layouts  10.4 us
    pallas_call x1, Pallas kernels, own_pass(): pl.pallas_call(own_kernel, out_shape=[jax.ShapeDtypeStruct(*out) for out...  9.18 us
    ppermute x5, starting transfers between devices, swapped(): lax.ppermute(shard, axis, [(i, i ^ 1 << bit) for i in range(lax.axis_size...  8.33 us
    ppermute x5, waiting for transfers between devices, swapped(): lax.ppermute(shard, axis, [(i, i ^ 1 << bit) for i in range(lax.axis_size...  8.24 us
    all_to_all x1, starting transfers between devices, per_device(): lax.all_to_all(sent.reshape(8, -1, LANES), 'orb', 0, 0, axis_index_groups...  7.25 us
    ppermute x2, starting transfers between devices, edges(): landed.append(lax.ppermute(sent, axis, pairs))  3.61 us
  transfers between devices with their start and end apart: 8, of which 5 were waited for; matrix products, arithmetic and copies ran while one was open for 2% of the time, Pallas kernels for 12%

profile of v4, /device:TPU:0, one launch (start us, length us, event | category | flops | bytes accessed | tf_op | source)
XLA Modules:
  0.0 77.2 jit_solution(1352713435303461418)
XLA Ops:
  0.7 0.9 %copy-done = f32[8,3072]{1,0:T(8,128)S(1)} copy-done((f32[8,3072]{1,0:T(8,128)S(1)}, f32[8,3072]{1,0:T(8,128)}, u32[]{:S(2)}) %copy-start) | copy-done | bytes 98328
  1.5 0.7 copy-done.3
  3.6 1.3 %outgoing_pass.1 = (f32[384,128]{1,0:T(8,128)}, f32[24,128]{1,0:T(8,128)S(1)}) custom-call(f32[192,128]{1,0:T(8,128)S(1)} %bitcast.12, s32[7,6]{1,0:T(8,128)S(1)} %copy-done.4, s32[1]{0:T(128)} %bitcast.5.place_ref, f32[4,768]{1,0:T(4,128)S(1)} %copy-done.3, s32[6]{0:T(128)S(1)} %copy-done.5), custom_call_target="tpu_custom_call" | custom-call | tf_op jit(solution)/shard_map/outgoing_pass/pallas_call | solution.py:381
  4.9 7.3 %all-to-all-start = ((f32[8,48,128]{2,1,0:T(8,128)}), f32[8,48,128]{2,1,0:T(8,128)S(1)}, u32[]{:S(2)}, u32[]{:S(2)}) async-start(f32[8,48,128]{2,1,0:T(8,128)} %bitcast.6), calls=%async_computation | async-start | bytes 393216 | tf_op jit(solution)/shard_map/all_to_all | solution.py:418
  12.9 2.9 %collective-permute-start = (f32[4,128]{1,0:T(4,128)S(1)}, f32[4,128]{1,0:T(4,128)S(1)}, u32[]{:S(2)}, u32[]{:S(2)}) collective-permute-start(f32[4,128]{1,0:T(4,128)S(1)} %get-tuple-element.24), channel_id=1, source_target_pairs={{0,1},{2,3},{1,0},{3,2},{4,5},{6,7},{5,4},{7,6},{8,9},{10,11},{9,8... | collective-permute-start | bytes 6152 | tf_op jit(solution)/shard_map/ppermute | solution.py:407
  15.8 0.8 %copy.10.pair_ref = s32[24,14]{1,0:T(8,128)S(1)} copy(s32[24,14]{0,1:T(8,128)} %param.8) | data formatting | bytes 2688 | tf_op args[2]
  16.6 0.8 copy.9.wpair_ref
  17.4 0.9 %copy-done.1 = f32[8,3072]{1,0:T(8,128)S(1)} copy-done((f32[8,3072]{1,0:T(8,128)S(1)}, f32[8,3072]{1,0:T(8,128)}, u32[]{:S(2)}) %copy-start.1) | copy-done | bytes 98328
  18.2 9.2 %own_pass.1 = (bf16[24,96,512]{2,1,0:T(8,128)(2,1)S(1)}, bf16[24,32,256]{2,1,0:T(8,128)(2,1)S(1)}, bf16[24,128,96]{2,1,0:T(8,128)(2,1)S(1)}, f32[768,128]{1,0:T(8,128)S(1)}, f32[192,128]{1,0:T(8,128)S(1)}) custom-call(f32[192,128]{1,0:T(8,128)S(1)} %bitcast.13, f32[24,128]{1,0:T(8,128)S(1)} %get-tuple-element.14.wall_ref, ...), custom_call_target="tpu_custom_call" | custom-call | flops 1572864000 | tf_op jit(solution)/shard_map/own_pass/pallas_call | solution.py:324
  27.4 0.8 copy-done.6
  28.2 0.7 copy-done.8
  29.6 1.0 %copy-done.7 = bf16[24,32,256]{2,1,0:T(8,128)(2,1)S(1)} copy-done((bf16[24,32,256]{2,1,0:T(8,128)(2,1)S(1)}, bf16[24,32,256]{2,1,0:T(8,128)(2,1)}, u32[]{:S(2)}) %copy-start.7) | copy-done | bytes 393240
  30.6 1.0 %copy-done.9 = f32[768,128]{1,0:T(8,128)S(1)} copy-done((f32[768,128]{1,0:T(8,128)S(1)}, f32[768,128]{1,0:T(8,128)}, u32[]{:S(2)}) %copy-start.9) | copy-done | bytes 393240
  31.6 0.9 %copy-done.11 = f32[192,128]{1,0:T(8,128)S(1)} copy-done((f32[192,128]{1,0:T(8,128)S(1)}, f32[192,128]{1,0:T(8,128)}, u32[]{:S(2)}) %copy-start.11) | copy-done | bytes 98328
  32.5 25.8 %fluid_pass.1 = (f32[24,128]{1,0:T(8,128)}, f32[3,3072]{1,0:T(4,128)}, f32[8,128]{1,0:T(8,128)S(1)}) custom-call(f32[192,128]{1,0:T(8,128)S(1)} %bitcast.14, f32[384,128]{1,0:T(8,128)S(1)} %bitcast.11, s32[24,14]{1,0:T(8,128)S(1)} %copy.10.pair_ref, s32[1]{0:T(128)} %bitcast.5.place_ref, bf16[24,96,512]{2,1,0:T(8,128)(2,1)S(1)} %get-tuple-element.15.own_src, ...), custom_call_target="tpu_custom_call" | custom-call | flops 5505024000 | tf_op jit(solution)/shard_map/fluid_pass/pallas_call | solution.py:340
  58.4 1.1 %collective-permute-done.2 = f32[8,128]{1,0:T(8,128)S(1)} collective-permute-done((f32[8,128]{1,0:T(8,128)S(1)}, f32[8,128]{1,0:T(8,128)S(1)}, u32[]{:S(2)}, u32[]{:S(2)}) %collective-permute-start.2) | collective-permute-done | bytes 4128 | tf_op jit(solution)/shard_map/ppermute | solution.py:395
  59.5 1.3 %collective-permute-start.3 = (f32[8,128]{1,0:T(8,128)S(1)}, f32[8,128]{1,0:T(8,128)S(1)}, u32[]{:S(2)}, u32[]{:S(2)}) collective-permute-start(f32[8,128]{1,0:T(8,128)S(1)} %max.15), channel_id=1, source_target_pairs={{0,2},{1,3},{2,0},{3,1},{4,6},{5,7},{6,4},{7,5},{8,10},{9,11},{10,... | collective-permute-start | bytes 12296 | tf_op jit(solution)/shard_map/ppermute | solution.py:395
  60.8 2.3 %collective-permute-done.3 = f32[8,128]{1,0:T(8,128)S(1)} collective-permute-done((f32[8,128]{1,0:T(8,128)S(1)}, f32[8,128]{1,0:T(8,128)S(1)}, u32[]{:S(2)}, u32[]{:S(2)}) %collective-permute-start.3) | collective-permute-done | bytes 4128 | tf_op jit(solution)/shard_map/ppermute | solution.py:395
  63.1 2.0 %collective-permute-start.4 = (f32[8,128]{1,0:T(8,128)S(1)}, f32[8,128]{1,0:T(8,128)S(1)}, u32[]{:S(2)}, u32[]{:S(2)}) collective-permute-start(f32[8,128]{1,0:T(8,128)S(1)} %max.16), channel_id=1, source_target_pairs={{0,4},{4,0},{8,12},{12,8},{16,20},{20,16},{24,28},{28,24},{1,5},{5... | collective-permute-start | bytes 12296 | tf_op jit(solution)/shard_map/ppermute | solution.py:395
  65.2 1.6 %collective-permute-done.4 = f32[8,128]{1,0:T(8,128)S(1)} collective-permute-done((f32[8,128]{1,0:T(8,128)S(1)}, f32[8,128]{1,0:T(8,128)S(1)}, u32[]{:S(2)}, u32[]{:S(2)}) %collective-permute-start.4) | collective-permute-done | bytes 4128 | tf_op jit(solution)/shard_map/ppermute | solution.py:395
  66.7 2.0 %collective-permute-start.5 = (f32[8,128]{1,0:T(8,128)S(1)}, f32[8,128]{1,0:T(8,128)S(1)}, u32[]{:S(2)}, u32[]{:S(2)}) collective-permute-start(f32[8,128]{1,0:T(8,128)S(1)} %max.17), channel_id=1, source_target_pairs={{0,8},{4,12},{8,0},{12,4},{16,24},{20,28},{24,16},{28,20},{1,9},{5... | collective-permute-start | bytes 12296 | tf_op jit(solution)/shard_map/ppermute | solution.py:395
  68.7 1.6 %collective-permute-done.5 = f32[8,128]{1,0:T(8,128)S(1)} collective-permute-done((f32[8,128]{1,0:T(8,128)S(1)}, f32[8,128]{1,0:T(8,128)S(1)}, u32[]{:S(2)}, u32[]{:S(2)}) %collective-permute-start.5) | collective-permute-done | bytes 4128 | tf_op jit(solution)/shard_map/ppermute | solution.py:395
  70.4 2.9 %collective-permute-start.6 = (f32[8,128]{1,0:T(8,128)S(1)}, f32[8,128]{1,0:T(8,128)S(1)}, u32[]{:S(2)}, u32[]{:S(2)}) collective-permute-start(f32[8,128]{1,0:T(8,128)S(1)} %max.18), channel_id=1, source_target_pairs={{0,16},{4,20},{8,24},{12,28},{16,0},{20,4},{24,8},{28,12},{1,17},{... | collective-permute-start | bytes 12296 | tf_op jit(solution)/shard_map/ppermute | solution.py:395
  73.2 1.6 %collective-permute-done.6 = f32[8,128]{1,0:T(8,128)S(1)} collective-permute-done((f32[8,128]{1,0:T(8,128)S(1)}, f32[8,128]{1,0:T(8,128)S(1)}, u32[]{:S(2)}, u32[]{:S(2)}) %collective-permute-start.6) | collective-permute-done | bytes 4128 | tf_op jit(solution)/shard_map/ppermute | solution.py:395
  (28 shorter events, 3.3 us)
Async XLA Ops:
  0.6 0.9 %copy-start = (f32[8,3072]{1,0:T(8,128)S(1)}, f32[8,3072]{1,0:T(8,128)}, u32[]{:S(2)}) copy-start(f32[8,3072]{1,0:T(8,128)} %param.6) | copy-start | bytes 294916
  1.5 0.7 copy-start.3
  2.2 0.7 copy-start.4
  2.9 0.7 copy-start.5
  4.9 24.7 %all-to-all-start = ((f32[8,48,128]{2,1,0:T(8,128)}), f32[8,48,128]{2,1,0:T(8,128)S(1)}, u32[]{:S(2)}, u32[]{:S(2)}) async-start(f32[8,48,128]{2,1,0:T(8,128)} %bitcast.6), calls=%async_computation | async-start | bytes 393216 | tf_op jit(solution)/shard_map/all_to_all | solution.py:418
  12.2 5.2 %collective-permute-start.1 = (f32[4,128]{1,0:T(4,128)S(1)}, f32[4,128]{1,0:T(4,128)S(1)}, u32[]{:S(2)}, u32[]{:S(2)}) collective-permute-start(f32[4,128]{1,0:T(4,128)S(1)} %get-tuple-element.23), channel_id=1, source_target_pairs={{1,2},{2,1},{5,6},{6,5},{9,10},{10,9},{13,14},{14,13},{17,18},{18,... | collective-permute-start | bytes 6152 | tf_op jit(solution)/shard_map/ppermute | solution.py:407
  12.9 4.5 %collective-permute-start = (f32[4,128]{1,0:T(4,128)S(1)}, f32[4,128]{1,0:T(4,128)S(1)}, u32[]{:S(2)}, u32[]{:S(2)}) collective-permute-start(f32[4,128]{1,0:T(4,128)S(1)} %get-tuple-element.24), channel_id=1, source_target_pairs={{0,1},{2,3},{1,0},{3,2},{4,5},{6,7},{5,4},{7,6},{8,9},{10,11},{9,8... | collective-permute-start | bytes 6152 | tf_op jit(solution)/shard_map/ppermute | solution.py:407
  17.3 0.9 %copy-start.1 = (f32[8,3072]{1,0:T(8,128)S(1)}, f32[8,3072]{1,0:T(8,128)}, u32[]{:S(2)}) copy-start(f32[8,3072]{1,0:T(8,128)} %param.6) | copy-start | bytes 294916
  18.2 11.3 %copy-start.2 = (f32[8,3072]{1,0:T(8,128)S(1)}, f32[8,3072]{1,0:T(8,128)}, u32[]{:S(2)}) copy-start(f32[8,3072]{1,0:T(8,128)} %param.6) | copy-start | bytes 294916
  27.4 0.8 copy-start.6
  28.2 0.7 copy-start.8
  28.9 0.6 copy-start.10
  29.6 1.0 %copy-start.7 = (bf16[24,32,256]{2,1,0:T(8,128)(2,1)S(1)}, bf16[24,32,256]{2,1,0:T(8,128)(2,1)}, u32[]{:S(2)}) copy-start(bf16[24,32,256]{2,1,0:T(8,128)(2,1)} %copy-done.6) | copy-start | bytes 1179652
  30.6 1.0 %copy-start.9 = (f32[768,128]{1,0:T(8,128)S(1)}, f32[768,128]{1,0:T(8,128)}, u32[]{:S(2)}) copy-start(f32[768,128]{1,0:T(8,128)} %copy-done.8) | copy-start | bytes 1179652
  31.6 0.9 %copy-start.11 = (f32[192,128]{1,0:T(8,128)S(1)}, f32[192,128]{1,0:T(8,128)}, u32[]{:S(2)}) copy-start(f32[192,128]{1,0:T(8,128)} %copy-done.10) | copy-start | bytes 294916
  58.3 1.2 %collective-permute-start.2 = (f32[8,128]{1,0:T(8,128)S(1)}, f32[8,128]{1,0:T(8,128)S(1)}, u32[]{:S(2)}, u32[]{:S(2)}) collective-permute-start(f32[8,128]{1,0:T(8,128)S(1)} %get-tuple-element.22), channel_id=1, source_target_pairs={{0,1},{1,0},{2,3},{3,2},{4,5},{5,4},{6,7},{7,6},{8,9},{9,8},{10,11... | collective-permute-start | bytes 12296 | tf_op jit(solution)/shard_map/ppermute | solution.py:395
  59.5 3.6 %collective-permute-start.3 = (f32[8,128]{1,0:T(8,128)S(1)}, f32[8,128]{1,0:T(8,128)S(1)}, u32[]{:S(2)}, u32[]{:S(2)}) collective-permute-start(f32[8,128]{1,0:T(8,128)S(1)} %max.15), channel_id=1, source_target_pairs={{0,2},{1,3},{2,0},{3,1},{4,6},{5,7},{6,4},{7,5},{8,10},{9,11},{10,... | collective-permute-start | bytes 12296 | tf_op jit(solution)/shard_map/ppermute | solution.py:395
  63.1 3.6 %collective-permute-start.4 = (f32[8,128]{1,0:T(8,128)S(1)}, f32[8,128]{1,0:T(8,128)S(1)}, u32[]{:S(2)}, u32[]{:S(2)}) collective-permute-start(f32[8,128]{1,0:T(8,128)S(1)} %max.16), channel_id=1, source_target_pairs={{0,4},{4,0},{8,12},{12,8},{16,20},{20,16},{24,28},{28,24},{1,5},{5... | collective-permute-start | bytes 12296 | tf_op jit(solution)/shard_map/ppermute | solution.py:395
  66.7 3.6 %collective-permute-start.5 = (f32[8,128]{1,0:T(8,128)S(1)}, f32[8,128]{1,0:T(8,128)S(1)}, u32[]{:S(2)}, u32[]{:S(2)}) collective-permute-start(f32[8,128]{1,0:T(8,128)S(1)} %max.17), channel_id=1, source_target_pairs={{0,8},{4,12},{8,0},{12,4},{16,24},{20,28},{24,16},{28,20},{1,9},{5... | collective-permute-start | bytes 12296 | tf_op jit(solution)/shard_map/ppermute | solution.py:395
  70.4 4.5 %collective-permute-start.6 = (f32[8,128]{1,0:T(8,128)S(1)}, f32[8,128]{1,0:T(8,128)S(1)}, u32[]{:S(2)}, u32[]{:S(2)}) collective-permute-start(f32[8,128]{1,0:T(8,128)S(1)} %max.18), channel_id=1, source_target_pairs={{0,16},{4,20},{8,24},{12,28},{16,0},{20,4},{24,8},{28,12},{1,17},{... | collective-permute-start | bytes 12296 | tf_op jit(solution)/shard_map/ppermute | solution.py:395

commit v5 on v4

--- a/solution.py
+++ b/solution.py
@@ -12,9 +12,10 @@
 ROWS = 8
 DEPTH = 12 * ROWS
 MOMENTS = 4 * ROWS
+SUMS = MOMENTS + ROWS
 UNROLL = 4
-WALL_TARGETS = 6
-FLUID_TARGETS = 3
+WALL_TARGETS = 12
+FLUID_TARGETS = 6
 
 smoothing = 0.1
 support = 0.3
@@ -98,7 +99,7 @@
     return near, along, spread, (None, chosen(0.0, (5, 1.0), (6, press - 0.75)))
 
 
-def put_source(block, s, src, mom, mass_factor=1.0, wall=False):
+def put_source(block, s, src, mass_factor=1.0, wall=False):
     state = state_of(block)
     for n, (first, second) in enumerate(source_groups(state, wall)):
         firsts = split(first) if first is not None else [jnp.zeros((ROWS, LANES))] * 3
@@ -112,7 +113,10 @@
     moment = (mass_factor * state[4]) * jnp.where(row_index() == 6, 1.0, state[0])
     moments = jnp.concatenate(split(moment) + [jnp.zeros_like(moment)], axis=0)
     moments = moments.astype(jnp.bfloat16)
-    mom[s] = jnp.concatenate([moments, moments], axis=1)
+    for n in range(MOMENTS // (2 * ROWS)):
+        part = moments[2 * ROWS * n : 2 * ROWS * (n + 1)]
+        lanes = slice(2 * n * LANES, 2 * (n + 1) * LANES)
+        src[s, DEPTH:, lanes] = jnp.concatenate([part, part], axis=1)
     return state
 
 
@@ -154,18 +158,19 @@
 
     def product_of(step):
         n, tile = step
-        return jnp.dot(targets[n][0], tile[0][...], preferred_element_type=jnp.float32)
+        columns = tile[:DEPTH, : (3 if wall else 4) * LANES]
+        return jnp.dot(targets[n][0], columns, preferred_element_type=jnp.float32)
 
     def add_up(n, moments, weights, last):
         totals[n] += across(moments, weights)
         if last:
             ones = jnp.ones((ROWS, 3 * LANES), jnp.bfloat16)
             pieces = jnp.concatenate(split(rates[n]), axis=1).astype(jnp.bfloat16)
-            finish(n, totals[n], across(ones, pieces))
+            finish(n, jnp.concatenate([totals[n], across(ones, pieces)], axis=0))
 
     ahead = product_of(steps[0])
     waiting = None
-    for k, (n, (_, moments)) in enumerate(steps):
+    for k, (n, tile) in enumerate(steps):
         product = ahead
         if k + 1 < len(steps):
             ahead = product_of(steps[k + 1])
@@ -173,23 +178,23 @@
         rates[n] += part
         if waiting is not None:
             add_up(*waiting, waiting[0] != n)
-        waiting = (n, moments[...], weights)
+        halves = [tile[DEPTH:, lanes] for lanes in (slice(0, 2 * LANES), slice(2 * LANES, None))]
+        waiting = (n, jnp.concatenate(halves, axis=0), weights)
     add_up(*waiting, True)
 
 
-def moments_at(b):
-    return pl.ds(pl.multiple_of(b * MOMENTS, MOMENTS), MOMENTS)
+def sums_at(b):
+    return pl.ds(pl.multiple_of(b * SUMS, ROWS), SUMS)
 
 
 def own_kernel(
     own_ref, wall_ref, edge0_ref, edge1_ref, wpair_ref, odd_ref,
-    src, mom, tgt, sums, rates, wsrc, wmom, table,
+    tgt, sums, wsrc, table,
 ):
     blocks = tgt.shape[0]
 
     def build(b, carry):
-        state = put_source(own_ref[rows_at(b), :], b, src, mom)
-        put_target(state, b, tgt)
+        put_target(state_of(own_ref[rows_at(b), :]), b, tgt)
         return carry
 
     lax.fori_loop(0, blocks, build, 0, unroll=UNROLL)
@@ -201,7 +206,7 @@
             both = jnp.concatenate([held, held], axis=0)
             density = jnp.where(row == 6, 1.0, 0.0)
             block = jnp.where((row < 3) | (row == 7), both, density)
-            put_source(block, count, wsrc, wmom, adhesion / cohesion, True)
+            put_source(block, count, wsrc, adhesion / cohesion, True)
             count += 1
     inner, edge = wall_ref.shape[0] // 4, edge0_ref.shape[0] // 4
     odd = odd_ref[0]
@@ -216,11 +221,10 @@
         targets = []
         for n in range(WALL_TARGETS):
             slots = [table[wpair_ref[first + n, k]] for k in range(wpair_ref.shape[1])]
-            targets.append((tgt[first + n], [(wsrc.at[s], wmom.at[s]) for s in slots]))
-
-        def finish(n, total, rate):
-            sums[moments_at(first + n), :] = total
-            rates[rows_at(first + n), :] = rate
+            targets.append((tgt[first + n], [wsrc.at[s] for s in slots]))
+
+        def finish(n, total):
+            sums[sums_at(first + n), :] = total
 
         run_targets(targets, True, finish)
         return carry
@@ -229,19 +233,12 @@
 
 
 def fluid_kernel(
-    own_ref, ghost_ref, pair_ref, place_ref, own_src, own_mom,
-    tgt, own_sums, own_rates, rate_ref, accel_ref, peak_ref,
-    src, mom, sums, rates, stage, table, copied,
+    own_ref, ghost_ref, pair_ref, place_ref, tgt, own_sums,
+    rate_ref, accel_ref, peak_ref, src, sums, stage, table,
 ):
     blocks = tgt.shape[0]
     ghosts = ghost_ref.shape[0] // ROWS
     per_mask = ghosts // 8
-    copies = [
-        pltpu.make_async_copy(own_src, src.at[pl.ds(0, blocks)], copied.at[0]),
-        pltpu.make_async_copy(own_mom, mom.at[pl.ds(0, blocks)], copied.at[1]),
-    ]
-    for copy in copies:
-        copy.start()
     for c in range(blocks):
         table[c] = c
     for mask in range(1, 8):
@@ -250,35 +247,38 @@
                 blocks + jnp.bitwise_xor(place_ref[0], mask) * per_mask + g
             )
 
+    def build_own(b, carry):
+        put_source(own_ref[rows_at(b), :], b, src)
+        return carry
+
     def build(g, carry):
-        put_source(ghost_ref[rows_at(g), :], blocks + g, src, mom)
+        put_source(ghost_ref[rows_at(g), :], blocks + g, src)
         return carry
 
+    lax.fori_loop(0, blocks, build_own, 0, unroll=UNROLL)
+
     lax.fori_loop(0, ghosts, build, 0, unroll=UNROLL)
-    for copy in copies:
-        copy.wait()
 
     def targets_from(i, carry):
         first = i * FLUID_TARGETS
         targets = []
         for n in range(FLUID_TARGETS):
             slots = [table[pair_ref[first + n, k]] for k in range(pair_ref.shape[1])]
-            targets.append((tgt[first + n], [(src.at[s], mom.at[s]) for s in slots]))
-
-        def finish(n, total, rate):
-            b = first + n
-            sums[moments_at(b), :] = own_sums[moments_at(b), :] + total
-            rates[rows_at(b), :] = own_rates[rows_at(b), :] + rate
+            targets.append((tgt[first + n], [src.at[s] for s in slots]))
+
+        def finish(n, total):
+            rows = sums_at(first + n)
+            sums[rows, :] = own_sums[rows, :] + total
 
         run_targets(targets, False, finish)
         return carry
 
     lax.fori_loop(0, blocks // FLUID_TARGETS, targets_from, 0)
 
-    rate_ref[...] = (-support * grad_coeff) * rates[pl.ds(0, blocks, stride=ROWS), :]
+    rate_ref[...] = (-support * grad_coeff) * sums[pl.ds(MOMENTS, blocks, stride=SUMS), :]
 
     def summed(row):
-        parts = [sums[pl.ds(p * ROWS + row, blocks, stride=MOMENTS), :] for p in range(3)]
+        parts = [sums[pl.ds(p * ROWS + row, blocks, stride=SUMS), :] for p in range(3)]
         return parts[0] + parts[1] + parts[2]
 
     mass_sum = summed(6)
@@ -306,28 +306,26 @@
     )
 
 
-def source_shapes(count, values):
-    return [
-        ((count, DEPTH, values * LANES), jnp.bfloat16),
-        ((count, MOMENTS, 2 * LANES), jnp.bfloat16),
-    ]
+def source_shape(count):
+    return (count, DEPTH + 2 * ROWS, 4 * LANES), jnp.bfloat16
 
 
 def own_pass(own, walls, edges, wall_pairs, odd):
     blocks = own.shape[0] // ROWS
     wall_blocks = (walls.shape[0] + 2 * edges[0].shape[0]) // 4
-    outs = source_shapes(blocks, 4) + [
+    outs = [
         ((blocks, LANES, DEPTH), jnp.bfloat16),
-        ((blocks * MOMENTS, LANES), jnp.float32),
-        ((blocks * ROWS, LANES), jnp.float32),
+        ((blocks * SUMS, LANES), jnp.float32),
     ]
     return pl.pallas_call(
         own_kernel,
         out_shape=[jax.ShapeDtypeStruct(*out) for out in outs],
         in_specs=[VMEM, VMEM, VMEM, VMEM, SMEM, SMEM],
         out_specs=[VMEM] * len(outs),
-        scratch_shapes=[pltpu.VMEM(*shape) for shape in source_shapes(wall_blocks, 3)]
-        + [pltpu.SMEM((wall_blocks,), jnp.int32)],
+        scratch_shapes=[
+            pltpu.VMEM(*source_shape(wall_blocks)),
+            pltpu.SMEM((wall_blocks,), jnp.int32),
+        ],
         compiler_params=PARAMS,
         cost_estimate=tile_cost(wall_pairs.size),
         name="own_pass",
@@ -346,13 +344,11 @@
         ),
         in_specs=[VMEM, VMEM, SMEM, SMEM] + [VMEM] * len(own_results),
         out_specs=(VMEM, VMEM, VMEM),
-        scratch_shapes=[pltpu.VMEM(*shape) for shape in source_shapes(total, 4)]
-        + [
-            pltpu.VMEM((blocks * MOMENTS, LANES), jnp.float32),
-            pltpu.VMEM((blocks * ROWS, LANES), jnp.float32),
+        scratch_shapes=[
+            pltpu.VMEM(*source_shape(total)),
+            pltpu.VMEM((blocks * SUMS, LANES), jnp.float32),
             pltpu.VMEM((blocks * ROWS, LANES), jnp.float32),
             pltpu.SMEM((total,), jnp.int32),
-            pltpu.SemaphoreType.DMA((2,)),
         ],
         compiler_params=PARAMS,
         cost_estimate=tile_cost(pair_list.size),
@@ -386,7 +382,6 @@
         ),
         in_specs=[VMEM, SMEM, SMEM, VMEM, SMEM],
         out_specs=(VMEM, VMEM),
-        compiler_params=PARAMS,
         name="outgoing_pass",
     )(own, ghost_list, place, wall_state, wall_count)
 

time: 77.8 us -> 67.6 us (0.87)
  local copies, waits for them, and re-layouts: 10.9 us -> 1.38 us
  Pallas kernels: 36.3 us -> 34.8 us
  starting transfers between devices: 19.2 us -> 20.3 us
    unnamed x26 -> x10, local copies, waits for them, and re-layouts: 10.4 us -> 0.86 us
    pallas_call x1, Pallas kernels: 25.8 us -> 24.7 us  [fluid_pass(): pl.pallas_call(fluid_kernel, out_shape=(jax.ShapeDtypeStruct((blocks, LAN...]
    ppermute x5, starting transfers between devices: 8.33 us -> 9.28 us  [swapped(): lax.ppermute(shard, axis, [(i, i ^ 1 << bit) for i in range(lax.axis_size...]
  transfers between devices with their start and end apart: 8 -> 8, of which waited for: 5 -> 6; matrix products, arithmetic and copies ran while one was open for 2% -> 0% of each run, Pallas kernels for 12% -> 13%
where the time goes in v5:
time: 67.6 us; the launch traced here: 67.2 us
  Pallas kernels  34.8 us (51%)
  starting transfers between devices  20.3 us (30%)
  waiting for transfers between devices  8.19 us (12%)
  between operations  2.56 us (4%)
  local copies, waits for them, and re-layouts  1.38 us (2%)
    pallas_call x1, Pallas kernels, fluid_pass(): pl.pallas_call(fluid_kernel, out_shape=(jax.ShapeDtypeStruct((blocks, LAN...  24.7 us
    ppermute x5, starting transfers between devices, swapped(): lax.ppermute(shard, axis, [(i, i ^ 1 << bit) for i in range(lax.axis_size...  9.28 us
    pallas_call x1, Pallas kernels, own_pass(): pl.pallas_call(own_kernel, out_shape=[jax.ShapeDtypeStruct(*out) for out...  8.49 us
    ppermute x5, waiting for transfers between devices, swapped(): lax.ppermute(shard, axis, [(i, i ^ 1 << bit) for i in range(lax.axis_size...  7.52 us
    all_to_all x1, starting transfers between devices, per_device(): lax.all_to_all(sent.reshape(8, -1, LANES), 'orb', 0, 0, axis_index_groups...  7.38 us
    ppermute x2, starting transfers between devices, edges(): landed.append(lax.ppermute(sent, axis, pairs))  3.6 us
    pallas_call x1, Pallas kernels, outgoing_pass(): pl.pallas_call(outgoing_kernel, out_shape=(jax.ShapeDtypeStruct((count *...  1.65 us
  transfers between devices with their start and end apart: 8, of which 6 were waited for; matrix products, arithmetic and copies ran while one was open for 0% of the time, Pallas kernels for 13%

profile of v5, /device:TPU:0, one launch (start us, length us, event | category | flops | bytes accessed | tf_op | source)
XLA Modules:
  0.0 67.2 jit_solution(17819568292060985875)
XLA Ops:
  0.6 1.6 %outgoing_pass.1 = (f32[384,128]{1,0:T(8,128)}, f32[24,128]{1,0:T(8,128)}) custom-call(f32[192,128]{1,0:T(8,128)} %bitcast.12, s32[7,6]{1,0:T(8,128)} %list_ref.1, s32[1]{0:T(128)} %bitcast.5.place_ref, f32[4,768]{1,0:T(4,128)} %wall_ref.1, s32[6]{0:T(128)} %count_ref.1), custom_call_target="tpu_custom_call" | custom-call | tf_op jit(solution)/shard_map/outgoing_pass/pallas_call | solution.py:377
  2.3 7.4 %all-to-all-start = ((f32[8,48,128]{2,1,0:T(8,128)}), f32[8,48,128]{2,1,0:T(8,128)S(1)}, u32[]{:S(2)}, u32[]{:S(2)}) async-start(f32[8,48,128]{2,1,0:T(8,128)} %bitcast.15), calls=%async_computation | async-start | bytes 393216 | tf_op jit(solution)/shard_map/all_to_all | solution.py:413
  9.7 0.0 copy-start.2
  9.7 0.7 %copy-done.1 = f32[24,128]{1,0:T(8,128)S(1)} copy-done((f32[24,128]{1,0:T(8,128)S(1)}, f32[24,128]{1,0:T(8,128)}, u32[]{:S(2)}) %copy-start.1) | copy-done | bytes 12312
  10.4 0.6 collective-permute-start.1
  11.1 0.0 copy-start.3
  11.1 2.9 %collective-permute-start = (f32[4,128]{1,0:T(4,128)S(1)}, f32[4,128]{1,0:T(4,128)S(1)}, u32[]{:S(2)}, u32[]{:S(2)}) collective-permute-start(f32[4,128]{1,0:T(4,128)S(1)} %get-tuple-element.18), channel_id=1, source_target_pairs={{0,1},{2,3},{1,0},{3,2},{4,5},{6,7},{5,4},{7,6},{8,9},{10,11},{9,8... | collective-permute-start | bytes 6152 | tf_op jit(solution)/shard_map/ppermute | solution.py:402
  14.0 0.1 copy.10.pair_ref
  14.1 0.1 copy.9.wpair_ref
  14.2 0.6 collective-permute-done.edge0_ref
  14.8 8.5 %own_pass.1 = (bf16[24,128,96]{2,1,0:T(8,128)(2,1)S(1)}, f32[960,128]{1,0:T(8,128)S(1)}) custom-call(f32[192,128]{1,0:T(8,128)S(1)} %bitcast.13, f32[24,128]{1,0:T(8,128)S(1)} %copy-done.1, f32[4,128]{1,0:T(4,128)S(1)} %collective-permute-done.edge0_ref, f32[4,128]{1,0:T(4,128)S(1)} %collective-permute-done.1.edge1_ref, s32[24,4]{1,0:T(8,128)S(1)} %copy.9.wpair_ref, ...), custom_call_target="tpu_custom_call" | custom-call | flops 1572864000 | tf_op jit(solution)/shard_map/own_pass/pallas_call | solution.py:320
  23.3 0.0 all-to-all-done
  23.3 24.7 %fluid_pass.1 = (f32[24,128]{1,0:T(8,128)}, f32[3,3072]{1,0:T(4,128)}, f32[8,128]{1,0:T(8,128)S(1)}) custom-call(f32[192,128]{1,0:T(8,128)S(1)} %bitcast.14, f32[384,128]{1,0:T(8,128)S(1)} %bitcast.11, s32[24,14]{1,0:T(8,128)S(1)} %copy.10.pair_ref, s32[1]{0:T(128)} %bitcast.5.place_ref, bf16[24,128,96]{2,1,0:T(8,128)(2,1)S(1)} %get-tuple-element.12.tgt, ...), custom_call_target="tpu_custom_call" | custom-call | flops 5505024000 | tf_op jit(solution)/shard_map/fluid_pass/pallas_call | solution.py:338
  48.0 0.7 collective-permute-start.2
  48.7 0.8 %collective-permute-done.2 = f32[8,128]{1,0:T(8,128)S(1)} collective-permute-done((f32[8,128]{1,0:T(8,128)S(1)}, f32[8,128]{1,0:T(8,128)S(1)}, u32[]{:S(2)}, u32[]{:S(2)}) %collective-permute-start.2) | collective-permute-done | bytes 4128 | tf_op jit(solution)/shard_map/ppermute | solution.py:390
  49.5 1.7 %collective-permute-start.3 = (f32[8,128]{1,0:T(8,128)S(1)}, f32[8,128]{1,0:T(8,128)S(1)}, u32[]{:S(2)}, u32[]{:S(2)}) collective-permute-start(f32[8,128]{1,0:T(8,128)S(1)} %max.15), channel_id=1, source_target_pairs={{0,2},{1,3},{2,0},{3,1},{4,6},{5,7},{6,4},{7,5},{8,10},{9,11},{10,... | collective-permute-start | bytes 12296 | tf_op jit(solution)/shard_map/ppermute | solution.py:390
  51.2 1.9 %collective-permute-done.3 = f32[8,128]{1,0:T(8,128)S(1)} collective-permute-done((f32[8,128]{1,0:T(8,128)S(1)}, f32[8,128]{1,0:T(8,128)S(1)}, u32[]{:S(2)}, u32[]{:S(2)}) %collective-permute-start.3) | collective-permute-done | bytes 4128 | tf_op jit(solution)/shard_map/ppermute | solution.py:390
  53.1 2.0 %collective-permute-start.4 = (f32[8,128]{1,0:T(8,128)S(1)}, f32[8,128]{1,0:T(8,128)S(1)}, u32[]{:S(2)}, u32[]{:S(2)}) collective-permute-start(f32[8,128]{1,0:T(8,128)S(1)} %max.16), channel_id=1, source_target_pairs={{0,4},{4,0},{8,12},{12,8},{16,20},{20,16},{24,28},{28,24},{1,5},{5... | collective-permute-start | bytes 12296 | tf_op jit(solution)/shard_map/ppermute | solution.py:390
  55.1 1.6 %collective-permute-done.4 = f32[8,128]{1,0:T(8,128)S(1)} collective-permute-done((f32[8,128]{1,0:T(8,128)S(1)}, f32[8,128]{1,0:T(8,128)S(1)}, u32[]{:S(2)}, u32[]{:S(2)}) %collective-permute-start.4) | collective-permute-done | bytes 4128 | tf_op jit(solution)/shard_map/ppermute | solution.py:390
  56.7 2.0 %collective-permute-start.5 = (f32[8,128]{1,0:T(8,128)S(1)}, f32[8,128]{1,0:T(8,128)S(1)}, u32[]{:S(2)}, u32[]{:S(2)}) collective-permute-start(f32[8,128]{1,0:T(8,128)S(1)} %max.17), channel_id=1, source_target_pairs={{0,8},{4,12},{8,0},{12,4},{16,24},{20,28},{24,16},{28,20},{1,9},{5... | collective-permute-start | bytes 12296 | tf_op jit(solution)/shard_map/ppermute | solution.py:390
  58.7 1.6 %collective-permute-done.5 = f32[8,128]{1,0:T(8,128)S(1)} collective-permute-done((f32[8,128]{1,0:T(8,128)S(1)}, f32[8,128]{1,0:T(8,128)S(1)}, u32[]{:S(2)}, u32[]{:S(2)}) %collective-permute-start.5) | collective-permute-done | bytes 4128 | tf_op jit(solution)/shard_map/ppermute | solution.py:390
  60.3 2.9 %collective-permute-start.6 = (f32[8,128]{1,0:T(8,128)S(1)}, f32[8,128]{1,0:T(8,128)S(1)}, u32[]{:S(2)}, u32[]{:S(2)}) collective-permute-start(f32[8,128]{1,0:T(8,128)S(1)} %max.18), channel_id=1, source_target_pairs={{0,16},{4,20},{8,24},{12,28},{16,0},{20,4},{24,8},{28,12},{1,17},{... | collective-permute-start | bytes 12296 | tf_op jit(solution)/shard_map/ppermute | solution.py:390
  63.3 1.6 %collective-permute-done.6 = f32[8,128]{1,0:T(8,128)S(1)} collective-permute-done((f32[8,128]{1,0:T(8,128)S(1)}, f32[8,128]{1,0:T(8,128)S(1)}, u32[]{:S(2)}, u32[]{:S(2)}) %collective-permute-start.6) | collective-permute-done | bytes 4128 | tf_op jit(solution)/shard_map/ppermute | solution.py:390
  64.8 0.5 slice.11
  (12 shorter events, 0.0 us)
Async XLA Ops:
  2.3 12.5 %copy-start = (f32[8,3072]{1,0:T(8,128)S(1)}, f32[8,3072]{1,0:T(8,128)}, u32[]{:S(2)}) copy-start(f32[8,3072]{1,0:T(8,128)} %param.6) | copy-start | bytes 294916
  2.3 21.0 %all-to-all-start = ((f32[8,48,128]{2,1,0:T(8,128)}), f32[8,48,128]{2,1,0:T(8,128)S(1)}, u32[]{:S(2)}, u32[]{:S(2)}) async-start(f32[8,48,128]{2,1,0:T(8,128)} %bitcast.15), calls=%async_computation | async-start | bytes 393216 | tf_op jit(solution)/shard_map/all_to_all | solution.py:413
  9.7 0.7 %copy-start.1 = (f32[24,128]{1,0:T(8,128)S(1)}, f32[24,128]{1,0:T(8,128)}, u32[]{:S(2)}) copy-start(f32[24,128]{1,0:T(8,128)} %get-tuple-element.11.wall_ref) | copy-start | bytes 36868
  9.7 4.3 %copy-start.2 = (s32[24,14]{0,1:T(8,128)S(1)}, s32[24,14]{0,1:T(8,128)}, u32[]{:S(2)}) copy-start(s32[24,14]{0,1:T(8,128)} %param.8) | copy-start | bytes 4036
  10.4 3.8 %collective-permute-start.1 = (f32[4,128]{1,0:T(4,128)S(1)}, f32[4,128]{1,0:T(4,128)S(1)}, u32[]{:S(2)}, u32[]{:S(2)}) collective-permute-start(f32[4,128]{1,0:T(4,128)S(1)} %get-tuple-element.17), channel_id=1, source_target_pairs={{1,2},{2,1},{5,6},{6,5},{9,10},{10,9},{13,14},{14,13},{17,18},{18,... | collective-permute-start | bytes 6152 | tf_op jit(solution)/shard_map/ppermute | solution.py:402
  11.1 3.0 %copy-start.3 = (s32[24,4]{0,1:T(4,128)S(1)}, s32[24,4]{0,1:T(4,128)}, u32[]{:S(2)}) copy-start(s32[24,4]{0,1:T(4,128)} %param.11) | copy-start | bytes 1156
  11.1 3.8 %collective-permute-start = (f32[4,128]{1,0:T(4,128)S(1)}, f32[4,128]{1,0:T(4,128)S(1)}, u32[]{:S(2)}, u32[]{:S(2)}) collective-permute-start(f32[4,128]{1,0:T(4,128)S(1)} %get-tuple-element.18), channel_id=1, source_target_pairs={{0,1},{2,3},{1,0},{3,2},{4,5},{6,7},{5,4},{7,6},{8,9},{10,11},{9,8... | collective-permute-start | bytes 6152 | tf_op jit(solution)/shard_map/ppermute | solution.py:402
  48.0 1.5 %collective-permute-start.2 = (f32[8,128]{1,0:T(8,128)S(1)}, f32[8,128]{1,0:T(8,128)S(1)}, u32[]{:S(2)}, u32[]{:S(2)}) collective-permute-start(f32[8,128]{1,0:T(8,128)S(1)} %get-tuple-element.16), channel_id=1, source_target_pairs={{0,1},{1,0},{2,3},{3,2},{4,5},{5,4},{6,7},{7,6},{8,9},{9,8},{10,11... | collective-permute-start | bytes 12296 | tf_op jit(solution)/shard_map/ppermute | solution.py:390
  49.5 3.6 %collective-permute-start.3 = (f32[8,128]{1,0:T(8,128)S(1)}, f32[8,128]{1,0:T(8,128)S(1)}, u32[]{:S(2)}, u32[]{:S(2)}) collective-permute-start(f32[8,128]{1,0:T(8,128)S(1)} %max.15), channel_id=1, source_target_pairs={{0,2},{1,3},{2,0},{3,1},{4,6},{5,7},{6,4},{7,5},{8,10},{9,11},{10,... | collective-permute-start | bytes 12296 | tf_op jit(solution)/shard_map/ppermute | solution.py:390
  53.1 3.6 %collective-permute-start.4 = (f32[8,128]{1,0:T(8,128)S(1)}, f32[8,128]{1,0:T(8,128)S(1)}, u32[]{:S(2)}, u32[]{:S(2)}) collective-permute-start(f32[8,128]{1,0:T(8,128)S(1)} %max.16), channel_id=1, source_target_pairs={{0,4},{4,0},{8,12},{12,8},{16,20},{20,16},{24,28},{28,24},{1,5},{5... | collective-permute-start | bytes 12296 | tf_op jit(solution)/shard_map/ppermute | solution.py:390
  56.7 3.6 %collective-permute-start.5 = (f32[8,128]{1,0:T(8,128)S(1)}, f32[8,128]{1,0:T(8,128)S(1)}, u32[]{:S(2)}, u32[]{:S(2)}) collective-permute-start(f32[8,128]{1,0:T(8,128)S(1)} %max.17), channel_id=1, source_target_pairs={{0,8},{4,12},{8,0},{12,4},{16,24},{20,28},{24,16},{28,20},{1,9},{5... | collective-permute-start | bytes 12296 | tf_op jit(solution)/shard_map/ppermute | solution.py:390
  60.3 4.5 %collective-permute-start.6 = (f32[8,128]{1,0:T(8,128)S(1)}, f32[8,128]{1,0:T(8,128)S(1)}, u32[]{:S(2)}, u32[]{:S(2)}) collective-permute-start(f32[8,128]{1,0:T(8,128)S(1)} %max.18), channel_id=1, source_target_pairs={{0,16},{4,20},{8,24},{12,28},{16,0},{20,4},{24,8},{28,12},{1,17},{... | collective-permute-start | bytes 12296 | tf_op jit(solution)/shard_map/ppermute | solution.py:390

commit v6 on v5

--- a/solution.py
+++ b/solution.py
@@ -232,38 +232,25 @@
     lax.fori_loop(0, blocks // WALL_TARGETS, targets_from, 0)
 
 
-def fluid_kernel(
-    own_ref, ghost_ref, pair_ref, place_ref, tgt, own_sums,
-    rate_ref, accel_ref, peak_ref, src, sums, stage, table,
-):
+def fluid_kernel(own_ref, pair_ref, tgt, own_sums, *refs):
+    *ghost_refs, rate_ref, accel_ref, peak_ref, src, sums, stage = refs
     blocks = tgt.shape[0]
-    ghosts = ghost_ref.shape[0] // ROWS
-    per_mask = ghosts // 8
-    for c in range(blocks):
-        table[c] = c
-    for mask in range(1, 8):
-        for g in range(per_mask):
-            table[blocks + (mask - 1) * per_mask + g] = (
-                blocks + jnp.bitwise_xor(place_ref[0], mask) * per_mask + g
-            )
 
     def build_own(b, carry):
         put_source(own_ref[rows_at(b), :], b, src)
         return carry
 
-    def build(g, carry):
-        put_source(ghost_ref[rows_at(g), :], blocks + g, src)
-        return carry
-
     lax.fori_loop(0, blocks, build_own, 0, unroll=UNROLL)
-
-    lax.fori_loop(0, ghosts, build, 0, unroll=UNROLL)
+    per_mask = ghost_refs[0].shape[0] // ROWS
+    for n, ghost_ref in enumerate(ghost_refs):
+        for g in range(per_mask):
+            put_source(ghost_ref[g * ROWS : (g + 1) * ROWS, :], blocks + n * per_mask + g, src)
 
     def targets_from(i, carry):
         first = i * FLUID_TARGETS
         targets = []
         for n in range(FLUID_TARGETS):
-            slots = [table[pair_ref[first + n, k]] for k in range(pair_ref.shape[1])]
+            slots = [pair_ref[first + n, k] for k in range(pair_ref.shape[1])]
             targets.append((tgt[first + n], [src.at[s] for s in slots]))
 
         def finish(n, total):
@@ -332,9 +319,9 @@
     )(own, walls, *edges, wall_pairs, odd)
 
 
-def fluid_pass(own, ghosts, pair_list, place, own_results):
+def fluid_pass(own, ghosts, pair_list, own_results):
     blocks = own.shape[0] // ROWS
-    total = blocks + ghosts.shape[0] // ROWS
+    total = blocks + sum(part.shape[0] for part in ghosts) // ROWS
     return pl.pallas_call(
         fluid_kernel,
         out_shape=(
@@ -342,90 +329,81 @@
             jax.ShapeDtypeStruct((3, blocks * LANES), jnp.float32),
             jax.ShapeDtypeStruct((ROWS, LANES), jnp.float32),
         ),
-        in_specs=[VMEM, VMEM, SMEM, SMEM] + [VMEM] * len(own_results),
+        in_specs=[VMEM, SMEM, VMEM, VMEM] + [VMEM] * len(ghosts),
         out_specs=(VMEM, VMEM, VMEM),
         scratch_shapes=[
             pltpu.VMEM(*source_shape(total)),
             pltpu.VMEM((blocks * SUMS, LANES), jnp.float32),
             pltpu.VMEM((blocks * ROWS, LANES), jnp.float32),
-            pltpu.SMEM((total,), jnp.int32),
         ],
         compiler_params=PARAMS,
         cost_estimate=tile_cost(pair_list.size),
         name="fluid_pass",
-    )(own, ghosts, pair_list, place, *own_results)
-
-
-def outgoing_kernel(own_ref, list_ref, place_ref, wall_ref, count_ref, sent_ref, live_ref):
-    for slot in range(8):
-        mask = jnp.bitwise_xor(place_ref[0], slot)
+    )(own, pair_list, *own_results, *ghosts)
+
+
+def outgoing_kernel(own_ref, list_ref, wall_ref, count_ref, odd_ref, *outs):
+    sent_refs, (live_ref, edge0_ref, edge1_ref) = outs[:-3], outs[-3:]
+    for n, sent_ref in enumerate(sent_refs):
         for g in range(list_ref.shape[1]):
-            block = list_ref[jnp.maximum(mask - 1, 0), g]
-            first = (slot * list_ref.shape[1] + g) * ROWS
-            sent_ref[first : first + ROWS, :] = own_ref[rows_at(block), :]
+            sent_ref[rows_at(g), :] = own_ref[rows_at(list_ref[n, g]), :]
     lane = lax.broadcasted_iota(jnp.int32, (4, LANES), 1)
     row = lax.broadcasted_iota(jnp.int32, (4, LANES), 0)
     for c in range(wall_ref.shape[1] // LANES):
         block = wall_ref[:, c * LANES : (c + 1) * LANES]
         kept = (row < 3) | (lane < count_ref[c])
         live_ref[4 * c : 4 * c + 4, :] = jnp.where(kept, block, 0.0)
-
-
-def outgoing_pass(own, ghost_list, place, wall_state, wall_count):
-    count = 8 * ghost_list.shape[1]
+    first = live_ref[: edge0_ref.shape[0], :]
+    last = live_ref[live_ref.shape[0] - edge0_ref.shape[0] :, :]
+    edge0_ref[...] = jnp.where(odd_ref[0] == 0, last, first)
+    edge1_ref[...] = jnp.where(odd_ref[0] == 0, first, last)
+
+
+def outgoing_pass(own, ghost_list, wall_state, wall_count, odd):
+    masks, count = ghost_list.shape
     walls = wall_state.shape[1] // LANES
+    rows = [count * ROWS] * masks + [walls * 4, EB * 4, EB * 4]
     return pl.pallas_call(
         outgoing_kernel,
-        out_shape=(
-            jax.ShapeDtypeStruct((count * ROWS, LANES), jnp.float32),
-            jax.ShapeDtypeStruct((walls * 4, LANES), jnp.float32),
-        ),
-        in_specs=[VMEM, SMEM, SMEM, VMEM, SMEM],
-        out_specs=(VMEM, VMEM),
+        out_shape=[jax.ShapeDtypeStruct((row, LANES), jnp.float32) for row in rows],
+        in_specs=[VMEM, SMEM, VMEM, SMEM, SMEM],
+        out_specs=[VMEM] * len(rows),
         name="outgoing_pass",
-    )(own, ghost_list, place, wall_state, wall_count)
-
-
-def swapped(shard, axis, bit):
-    return lax.ppermute(shard, axis, [(i, i ^ 1 << bit) for i in range(lax.axis_size(axis))])
-
-
-def edges(walls, axis, width):
+    )(own, ghost_list, wall_state, wall_count, odd)
+
+
+def swapped(shard, axis, mask):
+    return lax.ppermute(shard, axis, [(i, i ^ mask) for i in range(lax.axis_size(axis))])
+
+
+def largest(peak, axis):
+    bits = (lax.axis_size(axis) - 1).bit_length()
+    for low in range(0, bits, 3):
+        masks = range(1, 1 << min(3, bits - low))
+        for other in [swapped(peak, axis, mask << low) for mask in masks]:
+            peak = jnp.maximum(peak, other)
+    return peak
+
+
+def facing(edges, axis):
     count = lax.axis_size(axis)
-    odd = lax.axis_index(axis) % 2
-    first, last = walls[:width], walls[walls.shape[0] - width :]
     landed = []
-    for start in range(2):
+    for start, sent in enumerate(edges):
         pairs = [(i, i + 1) for i in range(start, count - 1, 2)]
-        pairs += [(j, i) for i, j in pairs]
-        sent = jnp.where(odd == start, last, first)
-        landed.append(lax.ppermute(sent, axis, pairs))
-    return landed, odd.reshape(1)
+        landed.append(lax.ppermute(sent, axis, pairs + [(j, i) for i, j in pairs]))
+    return landed
 
 
 def per_device(fluid_state, ghost_list, pair_list, wall_state, wall_count, wall_pairs):
     block_total = fluid_state.shape[1] // LANES
     own = jnp.transpose(fluid_state.reshape(8, block_total, LANES), (1, 0, 2)).reshape(-1, LANES)
-    place = (lax.axis_index("orb") % 8).reshape(1)
-    sent, walls = outgoing_pass(own, ghost_list, place, wall_state, wall_count)
-    facing, odd = edges(walls, "wall", 4 * EB)
-    groups = [list(range(g, g + 8)) for g in range(0, lax.axis_size("orb"), 8)]
-    landed = lax.all_to_all(
-        sent.reshape(8, -1, LANES),
-        "orb",
-        0,
-        0,
-        axis_index_groups=groups if len(groups) > 1 else None,
-    )
-    own_results = own_pass(own, walls, facing, wall_pairs, odd)
-    rate, acceleration, local_peak = fluid_pass(
-        own, landed.reshape(-1, LANES), pair_list, place, own_results
-    )
-    peak = local_peak
-    for axis in ("wall", "orb"):
-        for bit in range((lax.axis_size(axis) - 1).bit_length()):
-            peak = jnp.maximum(peak, swapped(peak, axis, bit))
-    peak = peak[0, 0]
+    odd = (lax.axis_index("wall") % 2).reshape(1)
+    *sent, walls, edge0, edge1 = outgoing_pass(own, ghost_list, wall_state, wall_count, odd)
+    edges = facing((edge0, edge1), "wall")
+    ghosts = [swapped(blocks, "orb", n + 1) for n, blocks in enumerate(sent)]
+    own_results = own_pass(own, walls, edges, wall_pairs, odd)
+    rate, acceleration, local_peak = fluid_pass(own, ghosts, pair_list, own_results)
+    peak = largest(largest(local_peak, "wall"), "orb")[0, 0]
     time_step = courant * jnp.sqrt(smoothing / (peak + 1e-06))
     return (rate.reshape(-1), acceleration, time_step)
 

time: 67.6 us -> 71.6 us (1.059)
  starting transfers between devices: 20.3 us -> 29.1 us
  waiting for transfers between devices: 8.19 us -> 3.66 us
    ppermute x7 -> x19, starting transfers between devices: 12.9 us -> 29.1 us  [the longest x17 28.5 us: swapped(): lax.ppermute(shard, axis, [(i, i ^ mask) for i in range(lax.axis_size(axi...]
    all_to_all x1 -> x0, starting transfers between devices: 7.38 us -> none  [per_device(): lax.all_to_all(sent.reshape(8, -1, LANES), 'orb', 0, 0, axis_index_groups...]
    ppermute x7 -> x19, waiting for transfers between devices: 8.17 us -> 3.66 us  [the longest x17 3.66 us: swapped(): lax.ppermute(shard, axis, [(i, i ^ mask) for i in range(lax.axis_size(axi...]
  transfers between devices with their start and end apart: 8 -> 19, of which waited for: 6 -> 3; matrix products, arithmetic and copies ran while one was open for 0% -> 0% of each run, Pallas kernels for 13% -> 12%
where the time goes in v6:
time: 71.6 us; the launch traced here: 71.4 us
  Pallas kernels  34.7 us (48%)
  starting transfers between devices  29.1 us (41%)
  waiting for transfers between devices  3.66 us (5%)
  between operations  2.62 us (4%)
  local copies, waits for them, and re-layouts  1.19 us (2%)
    ppermute x17, starting transfers between devices, swapped(): lax.ppermute(shard, axis, [(i, i ^ mask) for i in range(lax.axis_size(axi...  28.5 us
    pallas_call x1, Pallas kernels, fluid_pass(): pl.pallas_call(fluid_kernel, out_shape=(jax.ShapeDtypeStruct((blocks, LAN...  24.6 us
    pallas_call x1, Pallas kernels, own_pass(): pl.pallas_call(own_kernel, out_shape=[jax.ShapeDtypeStruct(*out) for out...  8.52 us
    ppermute x17, waiting for transfers between devices, swapped(): lax.ppermute(shard, axis, [(i, i ^ mask) for i in range(lax.axis_size(axi...  3.66 us
    pallas_call x1, Pallas kernels, outgoing_pass(): pl.pallas_call(outgoing_kernel, out_shape=[jax.ShapeDtypeStruct((row, LAN...  1.63 us
  transfers between devices with their start and end apart: 19, of which 3 were waited for; matrix products, arithmetic and copies ran while one was open for 0% of the time, Pallas kernels for 12%

profile of v6, /device:TPU:0, one launch (start us, length us, event | category | flops | bytes accessed | tf_op | source)
XLA Modules:
  0.0 71.4 jit_solution(14382886570377949324)
XLA Ops:
  0.7 1.6 %outgoing_pass.1 = (f32[48,128]{1,0:T(8,128)}, f32[48,128]{1,0:T(8,128)}, f32[48,128]{1,0:T(8,128)}, f32[48,128]{1,0:T(8,128)}, f32[48,128]{1,0:T(8,128)}, /*ind...) custom-call(f32[192,128]{1,0:T(8,128)} %bitcast.8, ...), custom_call_target="tpu_custom_call" | custom-call | tf_op jit(solution)/shard_map/outgoing_pass/pallas_call | solution.py:366
  2.3 3.0 %collective-permute-start.2 = (f32[48,128]{1,0:T(8,128)}, f32[48,128]{1,0:T(8,128)S(1)}, u32[]{:S(2)}, u32[]{:S(2)}) collective-permute-start(f32[48,128]{1,0:T(8,128)} %get-tuple-element.23), channel_id=1, source_target_pairs={{0,4},{4,0},{8,12},{12,8},{16,20},{20,16},{24,28},{28,24},{1,5},{5... | collective-permute-start | bytes 73736 | tf_op jit(solution)/shard_map/ppermute | solution.py:376
  5.3 1.6 %collective-permute-start.3 = (f32[48,128]{1,0:T(8,128)}, f32[48,128]{1,0:T(8,128)S(1)}, u32[]{:S(2)}, u32[]{:S(2)}) collective-permute-start(f32[48,128]{1,0:T(8,128)} %get-tuple-element.24), channel_id=1, source_target_pairs={{0,8},{4,12},{8,0},{12,4},{16,24},{20,28},{24,16},{28,20},{1,9},{5... | collective-permute-start | bytes 73736 | tf_op jit(solution)/shard_map/ppermute | solution.py:376
  6.9 0.7 collective-permute-start.1
  7.7 0.5 copy-done.3
  8.2 0.1 copy.9.wpair_ref
  8.3 2.6 %collective-permute-start.5 = (f32[48,128]{1,0:T(8,128)}, f32[48,128]{1,0:T(8,128)S(1)}, u32[]{:S(2)}, u32[]{:S(2)}) collective-permute-start(f32[48,128]{1,0:T(8,128)} %get-tuple-element.26), channel_id=1, source_target_pairs={{0,16},{4,20},{8,24},{12,28},{16,0},{20,4},{24,8},{28,12},{1,17},{... | collective-permute-start | bytes 73736 | tf_op jit(solution)/shard_map/ppermute | solution.py:376
  10.9 1.2 %collective-permute-start.6 = (f32[48,128]{1,0:T(8,128)}, f32[48,128]{1,0:T(8,128)S(1)}, u32[]{:S(2)}, u32[]{:S(2)}) collective-permute-start(f32[48,128]{1,0:T(8,128)} %get-tuple-element.27), channel_id=1, source_target_pairs={{0,20},{4,16},{8,28},{12,24},{16,4},{20,0},{24,12},{28,8},{1,21},{... | collective-permute-start | bytes 73736 | tf_op jit(solution)/shard_map/ppermute | solution.py:376
  12.1 3.6 %collective-permute-start.7 = (f32[48,128]{1,0:T(8,128)}, f32[48,128]{1,0:T(8,128)S(1)}, u32[]{:S(2)}, u32[]{:S(2)}) collective-permute-start(f32[48,128]{1,0:T(8,128)} %get-tuple-element.28), channel_id=1, source_target_pairs={{0,24},{4,28},{8,16},{12,20},{16,8},{20,12},{24,0},{28,4},{1,25},{... | collective-permute-start | bytes 73736 | tf_op jit(solution)/shard_map/ppermute | solution.py:376
  15.7 0.3 collective-permute-start.8
  16.0 8.5 %own_pass.1 = (bf16[24,128,96]{2,1,0:T(8,128)(2,1)S(1)}, f32[960,128]{1,0:T(8,128)S(1)}) custom-call(f32[192,128]{1,0:T(8,128)S(1)} %bitcast.9, f32[24,128]{1,0:T(8,128)S(1)} %copy-done.1, f32[4,128]{1,0:T(4,128)S(1)} %collective-permute-done.edge0_ref, f32[4,128]{1,0:T(4,128)S(1)} %collective-permute-done.1.edge1_ref, s32[24,4]{1,0:T(8,128)S(1)} %copy.9.wpair_ref, ...), custom_call_target="tpu_custom_call" | custom-call | flops 1572864000 | tf_op jit(solution)/shard_map/own_pass/pallas_call | solution.py:307
  24.6 24.6 %fluid_pass.1 = (f32[24,128]{1,0:T(8,128)}, f32[3,3072]{1,0:T(4,128)}, f32[8,128]{1,0:T(8,128)S(1)}) custom-call(f32[192,128]{1,0:T(8,128)S(1)} %bitcast.10, s32[24,14]{1,0:T(8,128)S(1)} %copy.10.pair_ref, bf16[24,128,96]{2,1,0:T(8,128)(2,1)S(1)} %get-tuple-element.21.tgt, f32[960,128]{1,0:T(8,128)S(1)} %get-tuple-element.22.own_sums, ...), custom_call_target="tpu_custom_call" | custom-call | flops 5505024000 | tf_op jit(solution)/shard_map/fluid_pass/pallas_call | solution.py:325
  49.1 0.5 collective-permute-start.11
  49.7 4.3 %collective-permute-start.10 = (f32[8,128]{1,0:T(8,128)S(1)}, f32[8,128]{1,0:T(8,128)S(1)}, u32[]{:S(2)}, u32[]{:S(2)}) collective-permute-start(f32[8,128]{1,0:T(8,128)S(1)} %get-tuple-element.32), channel_id=1, source_target_pairs={{0,2},{1,3},{2,0},{3,1},{4,6},{5,7},{6,4},{7,5},{8,10},{9,11},{10,... | collective-permute-start | bytes 12296 | tf_op jit(solution)/shard_map/ppermute | solution.py:376
  54.1 1.5 %collective-permute-done.10 = f32[8,128]{1,0:T(8,128)S(1)} collective-permute-done((f32[8,128]{1,0:T(8,128)S(1)}, f32[8,128]{1,0:T(8,128)S(1)}, u32[]{:S(2)}, u32[]{:S(2)}) %collective-permute-start.10) | collective-permute-done | bytes 4128 | tf_op jit(solution)/shard_map/ppermute | solution.py:376
  55.6 3.0 %collective-permute-start.18 = (f32[8,128]{1,0:T(8,128)S(1)}, f32[8,128]{1,0:T(8,128)S(1)}, u32[]{:S(2)}, u32[]{:S(2)}) collective-permute-start(f32[8,128]{1,0:T(8,128)S(1)} %maximum_maximum_fusion.1), channel_id=1, source_target_pairs={{0,28},{4,24},{8,20},{12,16},{16,12},{20,8},{24,4},{28,0},{1,29},{... | collective-permute-start | bytes 12296 | tf_op jit(solution)/shard_map/ppermute | solution.py:376
  58.7 0.8 %collective-permute-start.17 = (f32[8,128]{1,0:T(8,128)S(1)}, f32[8,128]{1,0:T(8,128)S(1)}, u32[]{:S(2)}, u32[]{:S(2)}) collective-permute-start(f32[8,128]{1,0:T(8,128)S(1)} %maximum_maximum_fusion.1), channel_id=1, source_target_pairs={{0,24},{4,28},{8,16},{12,20},{16,8},{20,12},{24,0},{28,4},{1,25},{... | collective-permute-start | bytes 12296 | tf_op jit(solution)/shard_map/ppermute | solution.py:376
  59.5 3.9 %collective-permute-start.15 = (f32[8,128]{1,0:T(8,128)S(1)}, f32[8,128]{1,0:T(8,128)S(1)}, u32[]{:S(2)}, u32[]{:S(2)}) collective-permute-start(f32[8,128]{1,0:T(8,128)S(1)} %maximum_maximum_fusion.1), channel_id=1, source_target_pairs={{0,16},{4,20},{8,24},{12,28},{16,0},{20,4},{24,8},{28,12},{1,17},{... | collective-permute-start | bytes 12296 | tf_op jit(solution)/shard_map/ppermute | solution.py:376
  63.4 0.6 collective-permute-start.14
  64.0 1.4 %collective-permute-start.13 = (f32[8,128]{1,0:T(8,128)S(1)}, f32[8,128]{1,0:T(8,128)S(1)}, u32[]{:S(2)}, u32[]{:S(2)}) collective-permute-start(f32[8,128]{1,0:T(8,128)S(1)} %maximum_maximum_fusion.1), channel_id=1, source_target_pairs={{0,8},{4,12},{8,0},{12,4},{16,24},{20,28},{24,16},{28,20},{1,9},{5... | collective-permute-start | bytes 12296 | tf_op jit(solution)/shard_map/ppermute | solution.py:376
  65.4 1.5 %collective-permute-start.12 = (f32[8,128]{1,0:T(8,128)S(1)}, f32[8,128]{1,0:T(8,128)S(1)}, u32[]{:S(2)}, u32[]{:S(2)}) collective-permute-start(f32[8,128]{1,0:T(8,128)S(1)} %maximum_maximum_fusion.1), channel_id=1, source_target_pairs={{0,4},{4,0},{8,12},{12,8},{16,20},{20,16},{24,28},{28,24},{1,5},{5... | collective-permute-start | bytes 12296 | tf_op jit(solution)/shard_map/ppermute | solution.py:376
  66.9 1.0 %collective-permute-done.14 = f32[8,128]{1,0:T(8,128)S(1)} collective-permute-done((f32[8,128]{1,0:T(8,128)S(1)}, f32[8,128]{1,0:T(8,128)S(1)}, u32[]{:S(2)}, u32[]{:S(2)}) %collective-permute-start.14) | collective-permute-done | bytes 4128 | tf_op jit(solution)/shard_map/ppermute | solution.py:376
  67.9 1.1 %collective-permute-done.12 = f32[8,128]{1,0:T(8,128)S(1)} collective-permute-done((f32[8,128]{1,0:T(8,128)S(1)}, f32[8,128]{1,0:T(8,128)S(1)}, u32[]{:S(2)}, u32[]{:S(2)}) %collective-permute-start.12) | collective-permute-done | bytes 4128 | tf_op jit(solution)/shard_map/ppermute | solution.py:376
  69.0 0.5 slice.3
  (32 shorter events, 0.3 us)
Async XLA Ops:
  0.6 15.3 %copy-start = (f32[8,3072]{1,0:T(8,128)S(1)}, f32[8,3072]{1,0:T(8,128)}, u32[]{:S(2)}) copy-start(f32[8,3072]{1,0:T(8,128)} %param.6) | copy-start | bytes 294916
  2.3 5.4 %copy-start.2 = (s32[24,14]{0,1:T(8,128)S(1)}, s32[24,14]{0,1:T(8,128)}, u32[]{:S(2)}) copy-start(s32[24,14]{0,1:T(8,128)} %param.8) | copy-start | bytes 4036
  2.3 9.8 %collective-permute-start.2 = (f32[48,128]{1,0:T(8,128)}, f32[48,128]{1,0:T(8,128)S(1)}, u32[]{:S(2)}, u32[]{:S(2)}) collective-permute-start(f32[48,128]{1,0:T(8,128)} %get-tuple-element.23), channel_id=1, source_target_pairs={{0,4},{4,0},{8,12},{12,8},{16,20},{20,16},{24,28},{28,24},{1,5},{5... | collective-permute-start | bytes 73736 | tf_op jit(solution)/shard_map/ppermute | solution.py:376
  5.3 10.4 %collective-permute-start.3 = (f32[48,128]{1,0:T(8,128)}, f32[48,128]{1,0:T(8,128)S(1)}, u32[]{:S(2)}, u32[]{:S(2)}) collective-permute-start(f32[48,128]{1,0:T(8,128)} %get-tuple-element.24), channel_id=1, source_target_pairs={{0,8},{4,12},{8,0},{12,4},{16,24},{20,28},{24,16},{28,20},{1,9},{5... | collective-permute-start | bytes 73736 | tf_op jit(solution)/shard_map/ppermute | solution.py:376
  6.9 1.4 %collective-permute-start = (f32[4,128]{1,0:T(4,128)}, f32[4,128]{1,0:T(4,128)S(1)}, u32[]{:S(2)}, u32[]{:S(2)}) collective-permute-start(f32[4,128]{1,0:T(4,128)} %get-tuple-element.19), channel_id=1, source_target_pairs={{0,1},{2,3},{1,0},{3,2},{4,5},{6,7},{5,4},{7,6},{8,9},{10,11},{9,8... | collective-permute-start | bytes 6152 | tf_op jit(solution)/shard_map/ppermute | solution.py:393
  6.9 4.0 %collective-permute-start.1 = (f32[4,128]{1,0:T(4,128)}, f32[4,128]{1,0:T(4,128)S(1)}, u32[]{:S(2)}, u32[]{:S(2)}) collective-permute-start(f32[4,128]{1,0:T(4,128)} %get-tuple-element.20), channel_id=1, source_target_pairs={{1,2},{2,1},{5,6},{6,5},{9,10},{10,9},{13,14},{14,13},{17,18},{18,... | collective-permute-start | bytes 6152 | tf_op jit(solution)/shard_map/ppermute | solution.py:393
  7.5 0.7 copy-start.3
  7.5 8.1 %copy-start.4 = (f32[48,128]{1,0:T(8,128)S(1)}, f32[48,128]{1,0:T(8,128)}, u32[]{:S(2)}) copy-start(f32[48,128]{1,0:T(8,128)} %get-tuple-element.29) | copy-start | bytes 73732
  7.6 17.0 %collective-permute-start.4 = (f32[48,128]{1,0:T(8,128)}, f32[48,128]{1,0:T(8,128)S(1)}, u32[]{:S(2)}, u32[]{:S(2)}) collective-permute-start(f32[48,128]{1,0:T(8,128)} %get-tuple-element.25), channel_id=1, source_target_pairs={{0,12},{4,8},{8,4},{12,0},{16,28},{20,24},{24,20},{28,16},{1,13},{... | collective-permute-start | bytes 73736 | tf_op jit(solution)/shard_map/ppermute | solution.py:376
  8.2 7.8 %copy-start.1 = (f32[24,128]{1,0:T(8,128)S(1)}, f32[24,128]{1,0:T(8,128)}, u32[]{:S(2)}) copy-start(f32[24,128]{1,0:T(8,128)} %get-tuple-element.18.wall_ref) | copy-start | bytes 36868
  8.3 16.2 %collective-permute-start.5 = (f32[48,128]{1,0:T(8,128)}, f32[48,128]{1,0:T(8,128)S(1)}, u32[]{:S(2)}, u32[]{:S(2)}) collective-permute-start(f32[48,128]{1,0:T(8,128)} %get-tuple-element.26), channel_id=1, source_target_pairs={{0,16},{4,20},{8,24},{12,28},{16,0},{20,4},{24,8},{28,12},{1,17},{... | collective-permute-start | bytes 73736 | tf_op jit(solution)/shard_map/ppermute | solution.py:376
  10.9 13.6 %collective-permute-start.6 = (f32[48,128]{1,0:T(8,128)}, f32[48,128]{1,0:T(8,128)S(1)}, u32[]{:S(2)}, u32[]{:S(2)}) collective-permute-start(f32[48,128]{1,0:T(8,128)} %get-tuple-element.27), channel_id=1, source_target_pairs={{0,20},{4,16},{8,28},{12,24},{16,4},{20,0},{24,12},{28,8},{1,21},{... | collective-permute-start | bytes 73736 | tf_op jit(solution)/shard_map/ppermute | solution.py:376
  12.1 12.5 %collective-permute-start.7 = (f32[48,128]{1,0:T(8,128)}, f32[48,128]{1,0:T(8,128)S(1)}, u32[]{:S(2)}, u32[]{:S(2)}) collective-permute-start(f32[48,128]{1,0:T(8,128)} %get-tuple-element.28), channel_id=1, source_target_pairs={{0,24},{4,28},{8,16},{12,20},{16,8},{20,12},{24,0},{28,4},{1,25},{... | collective-permute-start | bytes 73736 | tf_op jit(solution)/shard_map/ppermute | solution.py:376
  15.7 8.9 %collective-permute-start.8 = (f32[48,128]{1,0:T(8,128)S(1)}, f32[48,128]{1,0:T(8,128)S(1)}, u32[]{:S(2)}, u32[]{:S(2)}) collective-permute-start(f32[48,128]{1,0:T(8,128)S(1)} %copy-done.4), channel_id=1, source_target_pairs={{0,28},{4,24},{8,20},{12,16},{16,12},{20,8},{24,4},{28,0},{1,29},{... | collective-permute-start | bytes 73736 | tf_op jit(solution)/shard_map/ppermute | solution.py:376
  49.1 5.0 %collective-permute-start.11 = (f32[8,128]{1,0:T(8,128)S(1)}, f32[8,128]{1,0:T(8,128)S(1)}, u32[]{:S(2)}, u32[]{:S(2)}) collective-permute-start(f32[8,128]{1,0:T(8,128)S(1)} %get-tuple-element.32), channel_id=1, source_target_pairs={{0,3},{1,2},{2,1},{3,0},{4,7},{5,6},{6,5},{7,4},{8,11},{9,10},{10,... | collective-permute-start | bytes 12296 | tf_op jit(solution)/shard_map/ppermute | solution.py:376
  49.7 5.9 %collective-permute-start.10 = (f32[8,128]{1,0:T(8,128)S(1)}, f32[8,128]{1,0:T(8,128)S(1)}, u32[]{:S(2)}, u32[]{:S(2)}) collective-permute-start(f32[8,128]{1,0:T(8,128)S(1)} %get-tuple-element.32), channel_id=1, source_target_pairs={{0,2},{1,3},{2,0},{3,1},{4,6},{5,7},{6,4},{7,5},{8,10},{9,11},{10,... | collective-permute-start | bytes 12296 | tf_op jit(solution)/shard_map/ppermute | solution.py:376
  54.0 1.6 %collective-permute-start.9 = (f32[8,128]{1,0:T(8,128)S(1)}, f32[8,128]{1,0:T(8,128)S(1)}, u32[]{:S(2)}, u32[]{:S(2)}) collective-permute-start(f32[8,128]{1,0:T(8,128)S(1)} %get-tuple-element.32), channel_id=1, source_target_pairs={{0,1},{1,0},{2,3},{3,2},{4,5},{5,4},{6,7},{7,6},{8,9},{9,8},{10,11... | collective-permute-start | bytes 12296 | tf_op jit(solution)/shard_map/ppermute | solution.py:376
  55.6 8.4 %collective-permute-start.18 = (f32[8,128]{1,0:T(8,128)S(1)}, f32[8,128]{1,0:T(8,128)S(1)}, u32[]{:S(2)}, u32[]{:S(2)}) collective-permute-start(f32[8,128]{1,0:T(8,128)S(1)} %maximum_maximum_fusion.1), channel_id=1, source_target_pairs={{0,28},{4,24},{8,20},{12,16},{16,12},{20,8},{24,4},{28,0},{1,29},{... | collective-permute-start | bytes 12296 | tf_op jit(solution)/shard_map/ppermute | solution.py:376
  58.7 6.7 %collective-permute-start.17 = (f32[8,128]{1,0:T(8,128)S(1)}, f32[8,128]{1,0:T(8,128)S(1)}, u32[]{:S(2)}, u32[]{:S(2)}) collective-permute-start(f32[8,128]{1,0:T(8,128)S(1)} %maximum_maximum_fusion.1), channel_id=1, source_target_pairs={{0,24},{4,28},{8,16},{12,20},{16,8},{20,12},{24,0},{28,4},{1,25},{... | collective-permute-start | bytes 12296 | tf_op jit(solution)/shard_map/ppermute | solution.py:376
  59.5 7.4 %collective-permute-start.16 = (f32[8,128]{1,0:T(8,128)S(1)}, f32[8,128]{1,0:T(8,128)S(1)}, u32[]{:S(2)}, u32[]{:S(2)}) collective-permute-start(f32[8,128]{1,0:T(8,128)S(1)} %maximum_maximum_fusion.1), channel_id=1, source_target_pairs={{0,20},{4,16},{8,28},{12,24},{16,4},{20,0},{24,12},{28,8},{1,21},{... | collective-permute-start | bytes 12296 | tf_op jit(solution)/shard_map/ppermute | solution.py:376
  59.5 7.4 %collective-permute-start.15 = (f32[8,128]{1,0:T(8,128)S(1)}, f32[8,128]{1,0:T(8,128)S(1)}, u32[]{:S(2)}, u32[]{:S(2)}) collective-permute-start(f32[8,128]{1,0:T(8,128)S(1)} %maximum_maximum_fusion.1), channel_id=1, source_target_pairs={{0,16},{4,20},{8,24},{12,28},{16,0},{20,4},{24,8},{28,12},{1,17},{... | collective-permute-start | bytes 12296 | tf_op jit(solution)/shard_map/ppermute | solution.py:376
  63.4 4.5 %collective-permute-start.14 = (f32[8,128]{1,0:T(8,128)S(1)}, f32[8,128]{1,0:T(8,128)S(1)}, u32[]{:S(2)}, u32[]{:S(2)}) collective-permute-start(f32[8,128]{1,0:T(8,128)S(1)} %maximum_maximum_fusion.1), channel_id=1, source_target_pairs={{0,12},{4,8},{8,4},{12,0},{16,28},{20,24},{24,20},{28,16},{1,13},{... | collective-permute-start | bytes 12296 | tf_op jit(solution)/shard_map/ppermute | solution.py:376
  64.0 3.9 %collective-permute-start.13 = (f32[8,128]{1,0:T(8,128)S(1)}, f32[8,128]{1,0:T(8,128)S(1)}, u32[]{:S(2)}, u32[]{:S(2)}) collective-permute-start(f32[8,128]{1,0:T(8,128)S(1)} %maximum_maximum_fusion.1), channel_id=1, source_target_pairs={{0,8},{4,12},{8,0},{12,4},{16,24},{20,28},{24,16},{28,20},{1,9},{5... | collective-permute-start | bytes 12296 | tf_op jit(solution)/shard_map/ppermute | solution.py:376
  65.4 3.6 %collective-permute-start.12 = (f32[8,128]{1,0:T(8,128)S(1)}, f32[8,128]{1,0:T(8,128)S(1)}, u32[]{:S(2)}, u32[]{:S(2)}) collective-permute-start(f32[8,128]{1,0:T(8,128)S(1)} %maximum_maximum_fusion.1), channel_id=1, source_target_pairs={{0,4},{4,0},{8,12},{12,8},{16,20},{20,16},{24,28},{28,24},{1,5},{5... | collective-permute-start | bytes 12296 | tf_op jit(solution)/shard_map/ppermute | solution.py:376

commit v7 on v5

--- a/solution.py
+++ b/solution.py
@@ -1,4 +1,4 @@
-import functools
+import math
 
 import jax
 import jax.numpy as jnp
@@ -14,8 +14,10 @@
 MOMENTS = 4 * ROWS
 SUMS = MOMENTS + ROWS
 UNROLL = 4
-WALL_TARGETS = 12
-FLUID_TARGETS = 6
+VALUES = 3
+GROUP = 2
+WALL_TARGETS = 24
+FLUID_TARGETS = 8
 
 smoothing = 0.1
 support = 0.3
@@ -95,13 +97,12 @@
     if wall:
         press_part = chosen(0.0, (5, 2.0 * cohesion / adhesion), (6, -0.75))
         return near, along, (None, press_part)
-    spread = m * r * near[0], m * chosen(minus, (3, n), (4, 1.0), (6, r * n))
-    return near, along, spread, (None, chosen(0.0, (5, 1.0), (6, press - 0.75)))
-
-
-def put_source(block, s, src, mass_factor=1.0, wall=False):
+    return near, along, (m * r * near[0], m * chosen(minus, (3, n), (4, 1.0), (6, r * n)))
+
+
+def put_source(block, s, src, press=None, mass_factor=1.0):
     state = state_of(block)
-    for n, (first, second) in enumerate(source_groups(state, wall)):
+    for n, (first, second) in enumerate(source_groups(state, press is None)):
         firsts = split(first) if first is not None else [jnp.zeros((ROWS, LANES))] * 3
         pieces = [
             jnp.concatenate(pair, axis=0).astype(jnp.bfloat16)
@@ -111,38 +112,51 @@
         for k, (_, piece) in enumerate(SPLITS):
             src[s, 2 * ROWS * k : 2 * ROWS * (k + 1), lanes] = pieces[piece]
     moment = (mass_factor * state[4]) * jnp.where(row_index() == 6, 1.0, state[0])
-    moments = jnp.concatenate(split(moment) + [jnp.zeros_like(moment)], axis=0)
-    moments = moments.astype(jnp.bfloat16)
-    for n in range(MOMENTS // (2 * ROWS)):
-        part = moments[2 * ROWS * n : 2 * ROWS * (n + 1)]
-        lanes = slice(2 * n * LANES, 2 * (n + 1) * LANES)
-        src[s, DEPTH:, lanes] = jnp.concatenate([part, part], axis=1)
-    return state
+    moments = split(moment) + [jnp.zeros_like(moment)]
+    for n in range(2):
+        half = jnp.concatenate(moments[2 * n : 2 * n + 2], axis=0)
+        src[s, DEPTH:, n * LANES : (n + 1) * LANES] = half.astype(jnp.bfloat16)
+    if press is not None:
+        press[s] = state[5]
 
 
 def put_target(state, b, tgt):
     pieces = [jnp.concatenate(pair, axis=0) for pair in zip(*map(split, target_groups(state)))]
-    rows = jnp.concatenate([pieces[piece] for piece, _ in SPLITS], axis=0)
-    tgt[b] = rows.T.astype(jnp.bfloat16)
+    rows = jnp.concatenate([pieces[piece] for piece, _ in SPLITS], axis=0).astype(jnp.bfloat16)
+    row = lax.broadcasted_iota(jnp.int32, (LANES, LANES), 0)
+    lane = lax.broadcasted_iota(jnp.int32, (LANES, LANES), 1)
+    unit = jnp.where(row == lane, 1.0, 0.0).astype(jnp.bfloat16)
+    tgt[b] = across(unit, rows).astype(jnp.bfloat16)
+
+
+def press_choice():
+    row = lax.broadcasted_iota(jnp.int32, (DEPTH, LANES), 0)
+    value = jnp.where(row == ROWS + 6, -0.75, 0.0)
+    for k, (_, piece) in enumerate(SPLITS):
+        if piece == 0:
+            value = jnp.where(row == 2 * ROWS * k + ROWS + 5, 1.0, value)
+    return value.astype(jnp.bfloat16)
 
 
 def rows_at(index):
     return pl.ds(pl.multiple_of(index * ROWS, ROWS), ROWS)
 
 
-def weights_of(product, wall):
-    values = [product[:, n * LANES : (n + 1) * LANES] for n in range(3 if wall else 4)]
-    guarded = jnp.maximum(values[0], 1e-30)
-    approach, press = values[1], values[-1]
+def weights_of(product, press_i, press_j):
+    near, approach, last = [product[:, n * LANES : (n + 1) * LANES] for n in range(VALUES)]
+    guarded = jnp.maximum(near, 1e-30)
     falloff = jnp.maximum(1.0 - guarded * lax.rsqrt(guarded), 0.0)
     cubed = falloff * falloff * falloff
-    blend = falloff + press
-    if not wall:
-        blend += jnp.maximum(approach, 0.0) * pl.reciprocal(values[2], approx=True)
+    if press_j is None:
+        blend = falloff + last
+    else:
+        blend = falloff + press_i
+        blend += jnp.concatenate([press_j[...]] * (LANES // ROWS), axis=0)
+        blend += jnp.maximum(approach, 0.0) * pl.reciprocal(last, approx=True)
     weight = cubed * blend
     high = weight.astype(jnp.bfloat16)
     low = (weight - high.astype(jnp.float32)).astype(jnp.bfloat16)
-    return jnp.concatenate([high, low], axis=1), cubed * approach
+    return [high, low], cubed * approach
 
 
 def across(left, right):
@@ -151,14 +165,18 @@
     )
 
 
-def run_targets(targets, wall, finish):
-    steps = [(n, tile) for n, (_, tiles) in enumerate(targets) for tile in tiles]
+def run_targets(targets, finish):
+    steps = [
+        (n, tiles[k : k + GROUP])
+        for n, (_, _, tiles) in enumerate(targets)
+        for k in range(0, len(tiles), GROUP)
+    ]
     totals = [jnp.zeros((MOMENTS, LANES), jnp.float32)] * len(targets)
     rates = [jnp.zeros((LANES, LANES), jnp.float32)] * len(targets)
 
     def product_of(step):
-        n, tile = step
-        columns = tile[:DEPTH, : (3 if wall else 4) * LANES]
+        n, group = step
+        columns = jnp.concatenate([source[:DEPTH, :] for source, _ in group], axis=1)
         return jnp.dot(targets[n][0], columns, preferred_element_type=jnp.float32)
 
     def add_up(n, moments, weights, last):
@@ -170,16 +188,21 @@
 
     ahead = product_of(steps[0])
     waiting = None
-    for k, (n, tile) in enumerate(steps):
+    for k, (n, group) in enumerate(steps):
         product = ahead
         if k + 1 < len(steps):
             ahead = product_of(steps[k + 1])
-        weights, part = weights_of(product, wall)
-        rates[n] += part
+        moments, weights = [], []
+        for m, (source, press_j) in enumerate(group):
+            columns = slice(m * VALUES * LANES, (m + 1) * VALUES * LANES)
+            pair, part = weights_of(product[:, columns], targets[n][1], press_j)
+            rates[n] += part
+            weights += pair
+            halves = [source[DEPTH:, :LANES], source[DEPTH:, LANES : 2 * LANES]]
+            moments += [jnp.concatenate(halves, axis=0)] * 2
         if waiting is not None:
             add_up(*waiting, waiting[0] != n)
-        halves = [tile[DEPTH:, lanes] for lanes in (slice(0, 2 * LANES), slice(2 * LANES, None))]
-        waiting = (n, jnp.concatenate(halves, axis=0), weights)
+        waiting = (n, jnp.concatenate(moments, axis=1), jnp.concatenate(weights, axis=1))
     add_up(*waiting, True)
 
 
@@ -206,7 +229,7 @@
             both = jnp.concatenate([held, held], axis=0)
             density = jnp.where(row == 6, 1.0, 0.0)
             block = jnp.where((row < 3) | (row == 7), both, density)
-            put_source(block, count, wsrc, adhesion / cohesion, True)
+            put_source(block, count, wsrc, None, adhesion / cohesion)
             count += 1
     inner, edge = wall_ref.shape[0] // 4, edge0_ref.shape[0] // 4
     odd = odd_ref[0]
@@ -216,25 +239,27 @@
         table[c] = inner + (1 - odd) * edge + c
         table[edge + inner + c] = inner + odd * edge + c
 
+    together = math.gcd(blocks, WALL_TARGETS)
+
     def targets_from(i, carry):
-        first = i * WALL_TARGETS
+        first = i * together
         targets = []
-        for n in range(WALL_TARGETS):
+        for n in range(together):
             slots = [table[wpair_ref[first + n, k]] for k in range(wpair_ref.shape[1])]
-            targets.append((tgt[first + n], [wsrc.at[s] for s in slots]))
+            targets.append((tgt[first + n], None, [(wsrc.at[s], None) for s in slots]))
 
         def finish(n, total):
             sums[sums_at(first + n), :] = total
 
-        run_targets(targets, True, finish)
+        run_targets(targets, finish)
         return carry
 
-    lax.fori_loop(0, blocks // WALL_TARGETS, targets_from, 0)
+    lax.fori_loop(0, blocks // together, targets_from, 0)
 
 
 def fluid_kernel(
     own_ref, ghost_ref, pair_ref, place_ref, tgt, own_sums,
-    rate_ref, accel_ref, peak_ref, src, sums, stage, table,
+    rate_ref, accel_ref, peak_ref, src, press, sums, stage, table,
 ):
     blocks = tgt.shape[0]
     ghosts = ghost_ref.shape[0] // ROWS
@@ -248,32 +273,37 @@
             )
 
     def build_own(b, carry):
-        put_source(own_ref[rows_at(b), :], b, src)
+        put_source(own_ref[rows_at(b), :], b, src, press)
         return carry
 
     def build(g, carry):
-        put_source(ghost_ref[rows_at(g), :], blocks + g, src)
+        put_source(ghost_ref[rows_at(g), :], blocks + g, src, press)
         return carry
 
     lax.fori_loop(0, blocks, build_own, 0, unroll=UNROLL)
 
     lax.fori_loop(0, ghosts, build, 0, unroll=UNROLL)
 
+    choice = press_choice()
+    together = math.gcd(blocks, FLUID_TARGETS)
+
     def targets_from(i, carry):
-        first = i * FLUID_TARGETS
+        first = i * together
         targets = []
-        for n in range(FLUID_TARGETS):
+        for n in range(together):
             slots = [table[pair_ref[first + n, k]] for k in range(pair_ref.shape[1])]
-            targets.append((tgt[first + n], [src.at[s] for s in slots]))
+            target = tgt[first + n]
+            press_i = jnp.dot(target, choice, preferred_element_type=jnp.float32)
+            targets.append((target, press_i, [(src.at[s], press.at[s]) for s in slots]))
 
         def finish(n, total):
             rows = sums_at(first + n)
             sums[rows, :] = own_sums[rows, :] + total
 
-        run_targets(targets, False, finish)
+        run_targets(targets, finish)
         return carry
 
-    lax.fori_loop(0, blocks // FLUID_TARGETS, targets_from, 0)
+    lax.fori_loop(0, blocks // together, targets_from, 0)
 
     rate_ref[...] = (-support * grad_coeff) * sums[pl.ds(MOMENTS, blocks, stride=SUMS), :]
 
@@ -307,7 +337,7 @@
 
 
 def source_shape(count):
-    return (count, DEPTH + 2 * ROWS, 4 * LANES), jnp.bfloat16
+    return (count, DEPTH + 2 * ROWS, VALUES * LANES), jnp.bfloat16
 
 
 def own_pass(own, walls, edges, wall_pairs, odd):
@@ -346,6 +376,7 @@
         out_specs=(VMEM, VMEM, VMEM),
         scratch_shapes=[
             pltpu.VMEM(*source_shape(total)),
+            pltpu.VMEM((total, ROWS, LANES), jnp.float32),
             pltpu.VMEM((blocks * SUMS, LANES), jnp.float32),
             pltpu.VMEM((blocks * ROWS, LANES), jnp.float32),
             pltpu.SMEM((total,), jnp.int32),

time: 67.6 us -> 62.3 us (0.922)
  Pallas kernels: 34.8 us -> 29.5 us
    pallas_call x1, Pallas kernels: 24.7 us -> 20.8 us  [fluid_pass(): pl.pallas_call(fluid_kernel, out_shape=(jax.ShapeDtypeStruct((blocks, LAN...]
    pallas_call x1, Pallas kernels: 8.49 us -> 7.07 us  [own_pass(): pl.pallas_call(own_kernel, out_shape=[jax.ShapeDtypeStruct(*out) for out...]
  transfers between devices with their start and end apart: 8 -> 8, of which waited for: 6 -> 6; matrix products, arithmetic and copies ran while one was open for 0% -> 0% of each run, Pallas kernels for 13% -> 11%
where the time goes in v7:
time: 62.3 us; the launch traced here: 61.9 us
  Pallas kernels  29.5 us (47%)
  starting transfers between devices  20.3 us (33%)
  waiting for transfers between devices  8.18 us (13%)
  between operations  2.56 us (4%)
  local copies, waits for them, and re-layouts  1.38 us (2%)
    pallas_call x1, Pallas kernels, fluid_pass(): pl.pallas_call(fluid_kernel, out_shape=(jax.ShapeDtypeStruct((blocks, LAN...  20.8 us
    ppermute x5, starting transfers between devices, swapped(): lax.ppermute(shard, axis, [(i, i ^ 1 << bit) for i in range(lax.axis_size...  9.29 us
    ppermute x5, waiting for transfers between devices, swapped(): lax.ppermute(shard, axis, [(i, i ^ 1 << bit) for i in range(lax.axis_size...  7.53 us
    all_to_all x1, starting transfers between devices, per_device(): lax.all_to_all(sent.reshape(8, -1, LANES), 'orb', 0, 0, axis_index_groups...  7.38 us
    pallas_call x1, Pallas kernels, own_pass(): pl.pallas_call(own_kernel, out_shape=[jax.ShapeDtypeStruct(*out) for out...  7.07 us
    ppermute x2, starting transfers between devices, edges(): landed.append(lax.ppermute(sent, axis, pairs))  3.6 us
    pallas_call x1, Pallas kernels, outgoing_pass(): pl.pallas_call(outgoing_kernel, out_shape=(jax.ShapeDtypeStruct((count *...  1.65 us
  transfers between devices with their start and end apart: 8, of which 6 were waited for; matrix products, arithmetic and copies ran while one was open for 0% of the time, Pallas kernels for 11%

profile of v7, /device:TPU:0, one launch (start us, length us, event | category | flops | bytes accessed | tf_op | source)
XLA Modules:
  0.0 61.9 jit_solution(5320382415788991266)
XLA Ops:
  0.6 1.6 %outgoing_pass.1 = (f32[384,128]{1,0:T(8,128)}, f32[24,128]{1,0:T(8,128)}) custom-call(f32[192,128]{1,0:T(8,128)} %bitcast.12, s32[7,6]{1,0:T(8,128)} %list_ref.1, s32[1]{0:T(128)} %bitcast.5.place_ref, f32[4,768]{1,0:T(4,128)} %wall_ref.1, s32[6]{0:T(128)} %count_ref.1), custom_call_target="tpu_custom_call" | custom-call | tf_op jit(solution)/shard_map/outgoing_pass/pallas_call | solution.py:408
  2.3 7.4 %all-to-all-start = ((f32[8,48,128]{2,1,0:T(8,128)}), f32[8,48,128]{2,1,0:T(8,128)S(1)}, u32[]{:S(2)}, u32[]{:S(2)}) async-start(f32[8,48,128]{2,1,0:T(8,128)} %bitcast.15), calls=%async_computation | async-start | bytes 393216 | tf_op jit(solution)/shard_map/all_to_all | solution.py:444
  9.7 0.0 copy-start.2
  9.7 0.7 %copy-done.1 = f32[24,128]{1,0:T(8,128)S(1)} copy-done((f32[24,128]{1,0:T(8,128)S(1)}, f32[24,128]{1,0:T(8,128)}, u32[]{:S(2)}) %copy-start.1) | copy-done | bytes 12312
  10.4 0.6 %collective-permute-start.1 = (f32[4,128]{1,0:T(4,128)S(1)}, f32[4,128]{1,0:T(4,128)S(1)}, u32[]{:S(2)}, u32[]{:S(2)}) collective-permute-start(f32[4,128]{1,0:T(4,128)S(1)} %get-tuple-element.17), channel_id=1, source_target_pairs={{1,2},{2,1},{5,6},{6,5},{9,10},{10,9},{13,14},{14,13},{17,18},{18,... | collective-permute-start | bytes 6152 | tf_op jit(solution)/shard_map/ppermute | solution.py:433
  11.1 0.0 copy-start.3
  11.1 2.9 %collective-permute-start = (f32[4,128]{1,0:T(4,128)S(1)}, f32[4,128]{1,0:T(4,128)S(1)}, u32[]{:S(2)}, u32[]{:S(2)}) collective-permute-start(f32[4,128]{1,0:T(4,128)S(1)} %get-tuple-element.18), channel_id=1, source_target_pairs={{0,1},{2,3},{1,0},{3,2},{4,5},{6,7},{5,4},{7,6},{8,9},{10,11},{9,8... | collective-permute-start | bytes 6152 | tf_op jit(solution)/shard_map/ppermute | solution.py:433
  14.0 0.1 copy.10.pair_ref
  14.1 0.1 copy.9.wpair_ref
  14.2 0.0 collective-permute-done.1.edge1_ref
  14.2 0.6 %collective-permute-done.edge0_ref = f32[4,128]{1,0:T(4,128)S(1)} collective-permute-done((f32[4,128]{1,0:T(4,128)S(1)}, f32[4,128]{1,0:T(4,128)S(1)}, u32[]{:S(2)}, u32[]{:S(2)}) %collective-permute-start) | collective-permute-done | bytes 2080 | tf_op jit(solution)/shard_map/ppermute | solution.py:433
  14.8 7.1 %own_pass.1 = (bf16[24,128,96]{2,1,0:T(8,128)(2,1)S(1)}, f32[960,128]{1,0:T(8,128)S(1)}) custom-call(f32[192,128]{1,0:T(8,128)S(1)} %bitcast.13, f32[24,128]{1,0:T(8,128)S(1)} %copy-done.1, f32[4,128]{1,0:T(4,128)S(1)} %collective-permute-done.edge0_ref, f32[4,128]{1,0:T(4,128)S(1)} %collective-permute-done.1.edge1_ref, s32[24,4]{1,0:T(8,128)S(1)} %copy.9.wpair_ref, ...), custom_call_target="tpu_custom_call" | custom-call | flops 1572864000 | tf_op jit(solution)/shard_map/own_pass/pallas_call | solution.py:350
  21.9 20.8 %fluid_pass.1 = (f32[24,128]{1,0:T(8,128)}, f32[3,3072]{1,0:T(4,128)}, f32[8,128]{1,0:T(8,128)S(1)}) custom-call(f32[192,128]{1,0:T(8,128)S(1)} %bitcast.14, f32[384,128]{1,0:T(8,128)S(1)} %bitcast.11, s32[24,14]{1,0:T(8,128)S(1)} %copy.10.pair_ref, s32[1]{0:T(128)} %bitcast.5.place_ref, bf16[24,128,96]{2,1,0:T(8,128)(2,1)S(1)} %get-tuple-element.12.tgt, ...), custom_call_target="tpu_custom_call" | custom-call | flops 5505024000 | tf_op jit(solution)/shard_map/fluid_pass/pallas_call | solution.py:368
  42.7 0.6 %collective-permute-start.2 = (f32[8,128]{1,0:T(8,128)S(1)}, f32[8,128]{1,0:T(8,128)S(1)}, u32[]{:S(2)}, u32[]{:S(2)}) collective-permute-start(f32[8,128]{1,0:T(8,128)S(1)} %get-tuple-element.16), channel_id=1, source_target_pairs={{0,1},{1,0},{2,3},{3,2},{4,5},{5,4},{6,7},{7,6},{8,9},{9,8},{10,11... | collective-permute-start | bytes 12296 | tf_op jit(solution)/shard_map/ppermute | solution.py:421
  43.3 0.8 %collective-permute-done.2 = f32[8,128]{1,0:T(8,128)S(1)} collective-permute-done((f32[8,128]{1,0:T(8,128)S(1)}, f32[8,128]{1,0:T(8,128)S(1)}, u32[]{:S(2)}, u32[]{:S(2)}) %collective-permute-start.2) | collective-permute-done | bytes 4128 | tf_op jit(solution)/shard_map/ppermute | solution.py:421
  44.2 1.7 %collective-permute-start.3 = (f32[8,128]{1,0:T(8,128)S(1)}, f32[8,128]{1,0:T(8,128)S(1)}, u32[]{:S(2)}, u32[]{:S(2)}) collective-permute-start(f32[8,128]{1,0:T(8,128)S(1)} %max.15), channel_id=1, source_target_pairs={{0,2},{1,3},{2,0},{3,1},{4,6},{5,7},{6,4},{7,5},{8,10},{9,11},{10,... | collective-permute-start | bytes 12296 | tf_op jit(solution)/shard_map/ppermute | solution.py:421
  45.8 1.9 %collective-permute-done.3 = f32[8,128]{1,0:T(8,128)S(1)} collective-permute-done((f32[8,128]{1,0:T(8,128)S(1)}, f32[8,128]{1,0:T(8,128)S(1)}, u32[]{:S(2)}, u32[]{:S(2)}) %collective-permute-start.3) | collective-permute-done | bytes 4128 | tf_op jit(solution)/shard_map/ppermute | solution.py:421
  47.8 2.0 %collective-permute-start.4 = (f32[8,128]{1,0:T(8,128)S(1)}, f32[8,128]{1,0:T(8,128)S(1)}, u32[]{:S(2)}, u32[]{:S(2)}) collective-permute-start(f32[8,128]{1,0:T(8,128)S(1)} %max.16), channel_id=1, source_target_pairs={{0,4},{4,0},{8,12},{12,8},{16,20},{20,16},{24,28},{28,24},{1,5},{5... | collective-permute-start | bytes 12296 | tf_op jit(solution)/shard_map/ppermute | solution.py:421
  49.8 1.6 %collective-permute-done.4 = f32[8,128]{1,0:T(8,128)S(1)} collective-permute-done((f32[8,128]{1,0:T(8,128)S(1)}, f32[8,128]{1,0:T(8,128)S(1)}, u32[]{:S(2)}, u32[]{:S(2)}) %collective-permute-start.4) | collective-permute-done | bytes 4128 | tf_op jit(solution)/shard_map/ppermute | solution.py:421
  51.4 2.0 %collective-permute-start.5 = (f32[8,128]{1,0:T(8,128)S(1)}, f32[8,128]{1,0:T(8,128)S(1)}, u32[]{:S(2)}, u32[]{:S(2)}) collective-permute-start(f32[8,128]{1,0:T(8,128)S(1)} %max.17), channel_id=1, source_target_pairs={{0,8},{4,12},{8,0},{12,4},{16,24},{20,28},{24,16},{28,20},{1,9},{5... | collective-permute-start | bytes 12296 | tf_op jit(solution)/shard_map/ppermute | solution.py:421
  53.4 1.6 %collective-permute-done.5 = f32[8,128]{1,0:T(8,128)S(1)} collective-permute-done((f32[8,128]{1,0:T(8,128)S(1)}, f32[8,128]{1,0:T(8,128)S(1)}, u32[]{:S(2)}, u32[]{:S(2)}) %collective-permute-start.5) | collective-permute-done | bytes 4128 | tf_op jit(solution)/shard_map/ppermute | solution.py:421
  55.0 3.0 %collective-permute-start.6 = (f32[8,128]{1,0:T(8,128)S(1)}, f32[8,128]{1,0:T(8,128)S(1)}, u32[]{:S(2)}, u32[]{:S(2)}) collective-permute-start(f32[8,128]{1,0:T(8,128)S(1)} %max.18), channel_id=1, source_target_pairs={{0,16},{4,20},{8,24},{12,28},{16,0},{20,4},{24,8},{28,12},{1,17},{... | collective-permute-start | bytes 12296 | tf_op jit(solution)/shard_map/ppermute | solution.py:421
  58.0 1.6 %collective-permute-done.6 = f32[8,128]{1,0:T(8,128)S(1)} collective-permute-done((f32[8,128]{1,0:T(8,128)S(1)}, f32[8,128]{1,0:T(8,128)S(1)}, u32[]{:S(2)}, u32[]{:S(2)}) %collective-permute-start.6) | collective-permute-done | bytes 4128 | tf_op jit(solution)/shard_map/ppermute | solution.py:421
  59.6 0.5 slice.11
  (12 shorter events, 0.0 us)
Async XLA Ops:
  2.3 12.5 %copy-start = (f32[8,3072]{1,0:T(8,128)S(1)}, f32[8,3072]{1,0:T(8,128)}, u32[]{:S(2)}) copy-start(f32[8,3072]{1,0:T(8,128)} %param.6) | copy-start | bytes 294916
  2.3 19.6 %all-to-all-start = ((f32[8,48,128]{2,1,0:T(8,128)}), f32[8,48,128]{2,1,0:T(8,128)S(1)}, u32[]{:S(2)}, u32[]{:S(2)}) async-start(f32[8,48,128]{2,1,0:T(8,128)} %bitcast.15), calls=%async_computation | async-start | bytes 393216 | tf_op jit(solution)/shard_map/all_to_all | solution.py:444
  9.7 0.7 %copy-start.1 = (f32[24,128]{1,0:T(8,128)S(1)}, f32[24,128]{1,0:T(8,128)}, u32[]{:S(2)}) copy-start(f32[24,128]{1,0:T(8,128)} %get-tuple-element.11.wall_ref) | copy-start | bytes 36868
  9.7 4.3 %copy-start.2 = (s32[24,14]{0,1:T(8,128)S(1)}, s32[24,14]{0,1:T(8,128)}, u32[]{:S(2)}) copy-start(s32[24,14]{0,1:T(8,128)} %param.8) | copy-start | bytes 4036
  10.4 3.8 %collective-permute-start.1 = (f32[4,128]{1,0:T(4,128)S(1)}, f32[4,128]{1,0:T(4,128)S(1)}, u32[]{:S(2)}, u32[]{:S(2)}) collective-permute-start(f32[4,128]{1,0:T(4,128)S(1)} %get-tuple-element.17), channel_id=1, source_target_pairs={{1,2},{2,1},{5,6},{6,5},{9,10},{10,9},{13,14},{14,13},{17,18},{18,... | collective-permute-start | bytes 6152 | tf_op jit(solution)/shard_map/ppermute | solution.py:433
  11.1 3.0 %copy-start.3 = (s32[24,4]{0,1:T(4,128)S(1)}, s32[24,4]{0,1:T(4,128)}, u32[]{:S(2)}) copy-start(s32[24,4]{0,1:T(4,128)} %param.11) | copy-start | bytes 1156
  11.1 3.8 %collective-permute-start = (f32[4,128]{1,0:T(4,128)S(1)}, f32[4,128]{1,0:T(4,128)S(1)}, u32[]{:S(2)}, u32[]{:S(2)}) collective-permute-start(f32[4,128]{1,0:T(4,128)S(1)} %get-tuple-element.18), channel_id=1, source_target_pairs={{0,1},{2,3},{1,0},{3,2},{4,5},{6,7},{5,4},{7,6},{8,9},{10,11},{9,8... | collective-permute-start | bytes 6152 | tf_op jit(solution)/shard_map/ppermute | solution.py:433
  42.7 1.5 %collective-permute-start.2 = (f32[8,128]{1,0:T(8,128)S(1)}, f32[8,128]{1,0:T(8,128)S(1)}, u32[]{:S(2)}, u32[]{:S(2)}) collective-permute-start(f32[8,128]{1,0:T(8,128)S(1)} %get-tuple-element.16), channel_id=1, source_target_pairs={{0,1},{1,0},{2,3},{3,2},{4,5},{5,4},{6,7},{7,6},{8,9},{9,8},{10,11... | collective-permute-start | bytes 12296 | tf_op jit(solution)/shard_map/ppermute | solution.py:421
  44.2 3.6 %collective-permute-start.3 = (f32[8,128]{1,0:T(8,128)S(1)}, f32[8,128]{1,0:T(8,128)S(1)}, u32[]{:S(2)}, u32[]{:S(2)}) collective-permute-start(f32[8,128]{1,0:T(8,128)S(1)} %max.15), channel_id=1, source_target_pairs={{0,2},{1,3},{2,0},{3,1},{4,6},{5,7},{6,4},{7,5},{8,10},{9,11},{10,... | collective-permute-start | bytes 12296 | tf_op jit(solution)/shard_map/ppermute | solution.py:421
  47.8 3.6 %collective-permute-start.4 = (f32[8,128]{1,0:T(8,128)S(1)}, f32[8,128]{1,0:T(8,128)S(1)}, u32[]{:S(2)}, u32[]{:S(2)}) collective-permute-start(f32[8,128]{1,0:T(8,128)S(1)} %max.16), channel_id=1, source_target_pairs={{0,4},{4,0},{8,12},{12,8},{16,20},{20,16},{24,28},{28,24},{1,5},{5... | collective-permute-start | bytes 12296 | tf_op jit(solution)/shard_map/ppermute | solution.py:421
  51.4 3.6 %collective-permute-start.5 = (f32[8,128]{1,0:T(8,128)S(1)}, f32[8,128]{1,0:T(8,128)S(1)}, u32[]{:S(2)}, u32[]{:S(2)}) collective-permute-start(f32[8,128]{1,0:T(8,128)S(1)} %max.17), channel_id=1, source_target_pairs={{0,8},{4,12},{8,0},{12,4},{16,24},{20,28},{24,16},{28,20},{1,9},{5... | collective-permute-start | bytes 12296 | tf_op jit(solution)/shard_map/ppermute | solution.py:421
  55.0 4.5 %collective-permute-start.6 = (f32[8,128]{1,0:T(8,128)S(1)}, f32[8,128]{1,0:T(8,128)S(1)}, u32[]{:S(2)}, u32[]{:S(2)}) collective-permute-start(f32[8,128]{1,0:T(8,128)S(1)} %max.18), channel_id=1, source_target_pairs={{0,16},{4,20},{8,24},{12,28},{16,0},{20,4},{24,8},{28,12},{1,17},{... | collective-permute-start | bytes 12296 | tf_op jit(solution)/shard_map/ppermute | solution.py:421

commit v8 on v7

--- a/solution.py
+++ b/solution.py
@@ -13,11 +13,11 @@
 DEPTH = 12 * ROWS
 MOMENTS = 4 * ROWS
 SUMS = MOMENTS + ROWS
-UNROLL = 4
+UNROLL = 12
 VALUES = 3
 GROUP = 2
 WALL_TARGETS = 24
-FLUID_TARGETS = 8
+FLUID_TARGETS = 12
 
 smoothing = 0.1
 support = 0.3
@@ -387,7 +387,9 @@
     )(own, ghosts, pair_list, place, *own_results)
 
 
-def outgoing_kernel(own_ref, list_ref, place_ref, wall_ref, count_ref, sent_ref, live_ref):
+def outgoing_kernel(
+    own_ref, list_ref, place_ref, wall_ref, count_ref, odd_ref, sent_ref, live_ref, edge0_ref, edge1_ref,
+):
     for slot in range(8):
         mask = jnp.bitwise_xor(place_ref[0], slot)
         for g in range(list_ref.shape[1]):
@@ -400,46 +402,44 @@
         block = wall_ref[:, c * LANES : (c + 1) * LANES]
         kept = (row < 3) | (lane < count_ref[c])
         live_ref[4 * c : 4 * c + 4, :] = jnp.where(kept, block, 0.0)
-
-
-def outgoing_pass(own, ghost_list, place, wall_state, wall_count):
-    count = 8 * ghost_list.shape[1]
+    first = live_ref[: edge0_ref.shape[0], :]
+    last = live_ref[live_ref.shape[0] - edge0_ref.shape[0] :, :]
+    edge0_ref[...] = jnp.where(odd_ref[0] == 0, last, first)
+    edge1_ref[...] = jnp.where(odd_ref[0] == 0, first, last)
+
+
+def outgoing_pass(own, ghost_list, place, wall_state, wall_count, odd):
     walls = wall_state.shape[1] // LANES
+    rows = [8 * ghost_list.shape[1] * ROWS, walls * 4, EB * 4, EB * 4]
     return pl.pallas_call(
         outgoing_kernel,
-        out_shape=(
-            jax.ShapeDtypeStruct((count * ROWS, LANES), jnp.float32),
-            jax.ShapeDtypeStruct((walls * 4, LANES), jnp.float32),
-        ),
-        in_specs=[VMEM, SMEM, SMEM, VMEM, SMEM],
-        out_specs=(VMEM, VMEM),
+        out_shape=[jax.ShapeDtypeStruct((row, LANES), jnp.float32) for row in rows],
+        in_specs=[VMEM, SMEM, SMEM, VMEM, SMEM, SMEM],
+        out_specs=[VMEM] * len(rows),
         name="outgoing_pass",
-    )(own, ghost_list, place, wall_state, wall_count)
+    )(own, ghost_list, place, wall_state, wall_count, odd)
 
 
 def swapped(shard, axis, bit):
     return lax.ppermute(shard, axis, [(i, i ^ 1 << bit) for i in range(lax.axis_size(axis))])
 
 
-def edges(walls, axis, width):
+def facing(edges, axis):
     count = lax.axis_size(axis)
-    odd = lax.axis_index(axis) % 2
-    first, last = walls[:width], walls[walls.shape[0] - width :]
     landed = []
-    for start in range(2):
+    for start, sent in enumerate(edges):
         pairs = [(i, i + 1) for i in range(start, count - 1, 2)]
-        pairs += [(j, i) for i, j in pairs]
-        sent = jnp.where(odd == start, last, first)
-        landed.append(lax.ppermute(sent, axis, pairs))
-    return landed, odd.reshape(1)
+        landed.append(lax.ppermute(sent, axis, pairs + [(j, i) for i, j in pairs]))
+    return landed
 
 
 def per_device(fluid_state, ghost_list, pair_list, wall_state, wall_count, wall_pairs):
     block_total = fluid_state.shape[1] // LANES
     own = jnp.transpose(fluid_state.reshape(8, block_total, LANES), (1, 0, 2)).reshape(-1, LANES)
     place = (lax.axis_index("orb") % 8).reshape(1)
-    sent, walls = outgoing_pass(own, ghost_list, place, wall_state, wall_count)
-    facing, odd = edges(walls, "wall", 4 * EB)
+    odd = (lax.axis_index("wall") % 2).reshape(1)
+    sent, walls, *edges = outgoing_pass(own, ghost_list, place, wall_state, wall_count, odd)
+    edges = facing(edges, "wall")
     groups = [list(range(g, g + 8)) for g in range(0, lax.axis_size("orb"), 8)]
     landed = lax.all_to_all(
         sent.reshape(8, -1, LANES),
@@ -448,7 +448,7 @@
         0,
         axis_index_groups=groups if len(groups) > 1 else None,
     )
-    own_results = own_pass(own, walls, facing, wall_pairs, odd)
+    own_results = own_pass(own, walls, edges, wall_pairs, odd)
     rate, acceleration, local_peak = fluid_pass(
         own, landed.reshape(-1, LANES), pair_list, place, own_results
     )

time: 62.3 us -> 61.9 us (level)
    ppermute x5, starting transfers between devices: 9.29 us -> 12.1 us  [swapped(): lax.ppermute(shard, axis, [(i, i ^ 1 << bit) for i in range(lax.axis_size...]
    ppermute x2, starting transfers between devices: 3.6 us -> 0.85 us  [facing(): landed.append(lax.ppermute(sent, axis, pairs + [(j, i) for i, j in pairs]))]
    ppermute x2, waiting for transfers between devices: 0.65 us -> 0.01 us  [facing(): landed.append(lax.ppermute(sent, axis, pairs + [(j, i) for i, j in pairs]))]
    unnamed x10 -> x14, local copies, waits for them, and re-layouts: 0.86 us -> 1.37 us
  transfers between devices with their start and end apart: 8 -> 8, of which waited for: 6 -> 5; matrix products, arithmetic and copies ran while one was open for 0% -> 0% of each run, Pallas kernels for 11% -> 11%
where the time goes in v8:
time: 61.9 us; the launch traced here: 61.5 us
  Pallas kernels  28.9 us (47%)
  starting transfers between devices  20.3 us (33%)
  waiting for transfers between devices  7.77 us (13%)
  between operations  2.58 us (4%)
  local copies, waits for them, and re-layouts  1.89 us (3%)
    pallas_call x1, Pallas kernels, fluid_pass(): pl.pallas_call(fluid_kernel, out_shape=(jax.ShapeDtypeStruct((blocks, LAN...  20.7 us
    ppermute x5, starting transfers between devices, swapped(): lax.ppermute(shard, axis, [(i, i ^ 1 << bit) for i in range(lax.axis_size...  12.1 us
    ppermute x5, waiting for transfers between devices, swapped(): lax.ppermute(shard, axis, [(i, i ^ 1 << bit) for i in range(lax.axis_size...  7.76 us
    all_to_all x1, starting transfers between devices, per_device(): lax.all_to_all(sent.reshape(8, -1, LANES), 'orb', 0, 0, axis_index_groups...  7.4 us
    pallas_call x1, Pallas kernels, own_pass(): pl.pallas_call(own_kernel, out_shape=[jax.ShapeDtypeStruct(*out) for out...  6.54 us
    pallas_call x1, Pallas kernels, outgoing_pass(): pl.pallas_call(outgoing_kernel, out_shape=[jax.ShapeDtypeStruct((row, LAN...  1.65 us
    unnamed x14, local copies, waits for them, and re-layouts  1.37 us
  transfers between devices with their start and end apart: 8, of which 5 were waited for; matrix products, arithmetic and copies ran while one was open for 0% of the time, Pallas kernels for 11%

profile of v8, /device:TPU:0, one launch (start us, length us, event | category | flops | bytes accessed | tf_op | source)
XLA Modules:
  0.0 61.5 jit_solution(17300333794791583970)
XLA Ops:
  0.7 1.6 %outgoing_pass.1 = (f32[384,128]{1,0:T(8,128)}, f32[24,128]{1,0:T(8,128)}, f32[4,128]{1,0:T(4,128)}, f32[4,128]{1,0:T(4,128)}) custom-call(f32[192,128]{1,0:T(8,128)} %bitcast.12, s32[7,6]{1,0:T(8,128)} %list_ref.1, s32[1]{0:T(128)} %bitcast.5.place_ref, f32[4,768]{1,0:T(4,128)} %wall_ref.1, s32[6]{0:T(128)} %count_ref.1, s32[1]{0:T(128)} %bitcast.6.odd_ref), custom_call_target="tpu_custom_call" | custom-call | tf_op jit(solution)/shard_map/outgoing_pass/pallas_call | solution.py:414
  2.3 0.0 copy-start
  2.3 7.4 %all-to-all-start = ((f32[8,48,128]{2,1,0:T(8,128)}), f32[8,48,128]{2,1,0:T(8,128)S(1)}, u32[]{:S(2)}, u32[]{:S(2)}) async-start(f32[8,48,128]{2,1,0:T(8,128)} %bitcast.15), calls=%async_computation | async-start | bytes 393216 | tf_op jit(solution)/shard_map/all_to_all | solution.py:444
  9.7 0.1 collective-permute-start
  9.8 0.6 copy-done.4
  10.4 0.8 %collective-permute-start.1 = (f32[4,128]{1,0:T(4,128)S(1)}, f32[4,128]{1,0:T(4,128)S(1)}, u32[]{:S(2)}, u32[]{:S(2)}) collective-permute-start(f32[4,128]{1,0:T(4,128)S(1)} %copy-done.4), channel_id=1, source_target_pairs={{1,2},{2,1},{5,6},{6,5},{9,10},{10,9},{13,14},{14,13},{17,18},{18,... | collective-permute-start | bytes 6152 | tf_op jit(solution)/shard_map/ppermute | solution.py:432
  11.2 0.1 copy.10.pair_ref
  11.3 0.1 copy.9.wpair_ref
  11.4 0.0 collective-permute-done.edge0_ref
  11.4 0.0 collective-permute-done.1.edge1_ref
  11.4 0.6 copy-done.1
  12.0 6.5 %own_pass.1 = (bf16[24,128,96]{2,1,0:T(8,128)(2,1)S(1)}, f32[960,128]{1,0:T(8,128)S(1)}) custom-call(f32[192,128]{1,0:T(8,128)S(1)} %bitcast.13, f32[24,128]{1,0:T(8,128)S(1)} %copy-done.1, f32[4,128]{1,0:T(4,128)S(1)} %collective-permute-done.edge0_ref, f32[4,128]{1,0:T(4,128)S(1)} %collective-permute-done.1.edge1_ref, s32[24,4]{1,0:T(8,128)S(1)} %copy.9.wpair_ref, ...), custom_call_target="tpu_custom_call" | custom-call | flops 1572864000 | tf_op jit(solution)/shard_map/own_pass/pallas_call | solution.py:350
  18.5 20.7 %fluid_pass.1 = (f32[24,128]{1,0:T(8,128)}, f32[3,3072]{1,0:T(4,128)}, f32[8,128]{1,0:T(8,128)S(1)}) custom-call(f32[192,128]{1,0:T(8,128)S(1)} %bitcast.14, f32[384,128]{1,0:T(8,128)S(1)} %bitcast.11, s32[24,14]{1,0:T(8,128)S(1)} %copy.10.pair_ref, s32[1]{0:T(128)} %bitcast.5.place_ref, bf16[24,128,96]{2,1,0:T(8,128)(2,1)S(1)} %get-tuple-element.16.tgt, ...), custom_call_target="tpu_custom_call" | custom-call | flops 5505024000 | tf_op jit(solution)/shard_map/fluid_pass/pallas_call | solution.py:368
  39.3 3.7 %collective-permute-start.2 = (f32[8,128]{1,0:T(8,128)S(1)}, f32[8,128]{1,0:T(8,128)S(1)}, u32[]{:S(2)}, u32[]{:S(2)}) collective-permute-start(f32[8,128]{1,0:T(8,128)S(1)} %get-tuple-element.20), channel_id=1, source_target_pairs={{0,1},{1,0},{2,3},{3,2},{4,5},{5,4},{6,7},{7,6},{8,9},{9,8},{10,11... | collective-permute-start | bytes 12296 | tf_op jit(solution)/shard_map/ppermute | solution.py:424
  43.0 0.8 %collective-permute-done.2 = f32[8,128]{1,0:T(8,128)S(1)} collective-permute-done((f32[8,128]{1,0:T(8,128)S(1)}, f32[8,128]{1,0:T(8,128)S(1)}, u32[]{:S(2)}, u32[]{:S(2)}) %collective-permute-start.2) | collective-permute-done | bytes 4128 | tf_op jit(solution)/shard_map/ppermute | solution.py:424
  43.8 1.6 %collective-permute-start.3 = (f32[8,128]{1,0:T(8,128)S(1)}, f32[8,128]{1,0:T(8,128)S(1)}, u32[]{:S(2)}, u32[]{:S(2)}) collective-permute-start(f32[8,128]{1,0:T(8,128)S(1)} %max.15), channel_id=1, source_target_pairs={{0,2},{1,3},{2,0},{3,1},{4,6},{5,7},{6,4},{7,5},{8,10},{9,11},{10,... | collective-permute-start | bytes 12296 | tf_op jit(solution)/shard_map/ppermute | solution.py:424
  45.4 2.0 %collective-permute-done.3 = f32[8,128]{1,0:T(8,128)S(1)} collective-permute-done((f32[8,128]{1,0:T(8,128)S(1)}, f32[8,128]{1,0:T(8,128)S(1)}, u32[]{:S(2)}, u32[]{:S(2)}) %collective-permute-start.3) | collective-permute-done | bytes 4128 | tf_op jit(solution)/shard_map/ppermute | solution.py:424
  47.4 2.0 %collective-permute-start.4 = (f32[8,128]{1,0:T(8,128)S(1)}, f32[8,128]{1,0:T(8,128)S(1)}, u32[]{:S(2)}, u32[]{:S(2)}) collective-permute-start(f32[8,128]{1,0:T(8,128)S(1)} %max.16), channel_id=1, source_target_pairs={{0,4},{4,0},{8,12},{12,8},{16,20},{20,16},{24,28},{28,24},{1,5},{5... | collective-permute-start | bytes 12296 | tf_op jit(solution)/shard_map/ppermute | solution.py:424
  49.3 1.7 %collective-permute-done.4 = f32[8,128]{1,0:T(8,128)S(1)} collective-permute-done((f32[8,128]{1,0:T(8,128)S(1)}, f32[8,128]{1,0:T(8,128)S(1)}, u32[]{:S(2)}, u32[]{:S(2)}) %collective-permute-start.4) | collective-permute-done | bytes 4128 | tf_op jit(solution)/shard_map/ppermute | solution.py:424
  51.0 2.0 %collective-permute-start.5 = (f32[8,128]{1,0:T(8,128)S(1)}, f32[8,128]{1,0:T(8,128)S(1)}, u32[]{:S(2)}, u32[]{:S(2)}) collective-permute-start(f32[8,128]{1,0:T(8,128)S(1)} %max.17), channel_id=1, source_target_pairs={{0,8},{4,12},{8,0},{12,4},{16,24},{20,28},{24,16},{28,20},{1,9},{5... | collective-permute-start | bytes 12296 | tf_op jit(solution)/shard_map/ppermute | solution.py:424
  53.0 1.6 %collective-permute-done.5 = f32[8,128]{1,0:T(8,128)S(1)} collective-permute-done((f32[8,128]{1,0:T(8,128)S(1)}, f32[8,128]{1,0:T(8,128)S(1)}, u32[]{:S(2)}, u32[]{:S(2)}) %collective-permute-start.5) | collective-permute-done | bytes 4128 | tf_op jit(solution)/shard_map/ppermute | solution.py:424
  54.6 2.9 %collective-permute-start.6 = (f32[8,128]{1,0:T(8,128)S(1)}, f32[8,128]{1,0:T(8,128)S(1)}, u32[]{:S(2)}, u32[]{:S(2)}) collective-permute-start(f32[8,128]{1,0:T(8,128)S(1)} %max.18), channel_id=1, source_target_pairs={{0,16},{4,20},{8,24},{12,28},{16,0},{20,4},{24,8},{28,12},{1,17},{... | collective-permute-start | bytes 12296 | tf_op jit(solution)/shard_map/ppermute | solution.py:424
  57.5 1.6 %collective-permute-done.6 = f32[8,128]{1,0:T(8,128)S(1)} collective-permute-done((f32[8,128]{1,0:T(8,128)S(1)}, f32[8,128]{1,0:T(8,128)S(1)}, u32[]{:S(2)}, u32[]{:S(2)}) %collective-permute-start.6) | collective-permute-done | bytes 4128 | tf_op jit(solution)/shard_map/ppermute | solution.py:424
  59.1 0.5 slice.3
  (15 shorter events, 0.0 us)
Async XLA Ops:
  2.3 7.4 %copy-start.5 = (f32[4,128]{1,0:T(4,128)S(1)}, f32[4,128]{1,0:T(4,128)}, u32[]{:S(2)}) copy-start(f32[4,128]{1,0:T(4,128)} %get-tuple-element.14) | copy-start | bytes 6148
  2.3 8.9 %copy-start.2 = (s32[24,14]{0,1:T(8,128)S(1)}, s32[24,14]{0,1:T(8,128)}, u32[]{:S(2)}) copy-start(s32[24,14]{0,1:T(8,128)} %param.8) | copy-start | bytes 4036
  2.3 9.1 %copy-start = (f32[8,3072]{1,0:T(8,128)S(1)}, f32[8,3072]{1,0:T(8,128)}, u32[]{:S(2)}) copy-start(f32[8,3072]{1,0:T(8,128)} %param.6) | copy-start | bytes 294916
  2.3 16.2 %all-to-all-start = ((f32[8,48,128]{2,1,0:T(8,128)}), f32[8,48,128]{2,1,0:T(8,128)S(1)}, u32[]{:S(2)}, u32[]{:S(2)}) async-start(f32[8,48,128]{2,1,0:T(8,128)} %bitcast.15), calls=%async_computation | async-start | bytes 393216 | tf_op jit(solution)/shard_map/all_to_all | solution.py:444
  9.7 0.7 %copy-start.4 = (f32[4,128]{1,0:T(4,128)S(1)}, f32[4,128]{1,0:T(4,128)}, u32[]{:S(2)}) copy-start(f32[4,128]{1,0:T(4,128)} %get-tuple-element.15) | copy-start | bytes 6148
  9.7 1.6 %collective-permute-start = (f32[4,128]{1,0:T(4,128)S(1)}, f32[4,128]{1,0:T(4,128)S(1)}, u32[]{:S(2)}, u32[]{:S(2)}) collective-permute-start(f32[4,128]{1,0:T(4,128)S(1)} %copy-done.5), channel_id=1, source_target_pairs={{0,1},{2,3},{1,0},{3,2},{4,5},{6,7},{5,4},{7,6},{8,9},{10,11},{9,8... | collective-permute-start | bytes 6152 | tf_op jit(solution)/shard_map/ppermute | solution.py:432
  10.4 0.9 %copy-start.3 = (s32[24,4]{0,1:T(4,128)S(1)}, s32[24,4]{0,1:T(4,128)}, u32[]{:S(2)}) copy-start(s32[24,4]{0,1:T(4,128)} %param.11) | copy-start | bytes 1156
  10.4 1.0 %collective-permute-start.1 = (f32[4,128]{1,0:T(4,128)S(1)}, f32[4,128]{1,0:T(4,128)S(1)}, u32[]{:S(2)}, u32[]{:S(2)}) collective-permute-start(f32[4,128]{1,0:T(4,128)S(1)} %copy-done.4), channel_id=1, source_target_pairs={{1,2},{2,1},{5,6},{6,5},{9,10},{10,9},{13,14},{14,13},{17,18},{18,... | collective-permute-start | bytes 6152 | tf_op jit(solution)/shard_map/ppermute | solution.py:432
  11.3 0.7 %copy-start.1 = (f32[24,128]{1,0:T(8,128)S(1)}, f32[24,128]{1,0:T(8,128)}, u32[]{:S(2)}) copy-start(f32[24,128]{1,0:T(8,128)} %get-tuple-element.13.wall_ref) | copy-start | bytes 36868
  39.3 4.5 %collective-permute-start.2 = (f32[8,128]{1,0:T(8,128)S(1)}, f32[8,128]{1,0:T(8,128)S(1)}, u32[]{:S(2)}, u32[]{:S(2)}) collective-permute-start(f32[8,128]{1,0:T(8,128)S(1)} %get-tuple-element.20), channel_id=1, source_target_pairs={{0,1},{1,0},{2,3},{3,2},{4,5},{5,4},{6,7},{7,6},{8,9},{9,8},{10,11... | collective-permute-start | bytes 12296 | tf_op jit(solution)/shard_map/ppermute | solution.py:424
  43.8 3.6 %collective-permute-start.3 = (f32[8,128]{1,0:T(8,128)S(1)}, f32[8,128]{1,0:T(8,128)S(1)}, u32[]{:S(2)}, u32[]{:S(2)}) collective-permute-start(f32[8,128]{1,0:T(8,128)S(1)} %max.15), channel_id=1, source_target_pairs={{0,2},{1,3},{2,0},{3,1},{4,6},{5,7},{6,4},{7,5},{8,10},{9,11},{10,... | collective-permute-start | bytes 12296 | tf_op jit(solution)/shard_map/ppermute | solution.py:424
  47.4 3.6 %collective-permute-start.4 = (f32[8,128]{1,0:T(8,128)S(1)}, f32[8,128]{1,0:T(8,128)S(1)}, u32[]{:S(2)}, u32[]{:S(2)}) collective-permute-start(f32[8,128]{1,0:T(8,128)S(1)} %max.16), channel_id=1, source_target_pairs={{0,4},{4,0},{8,12},{12,8},{16,20},{20,16},{24,28},{28,24},{1,5},{5... | collective-permute-start | bytes 12296 | tf_op jit(solution)/shard_map/ppermute | solution.py:424
  51.0 3.6 %collective-permute-start.5 = (f32[8,128]{1,0:T(8,128)S(1)}, f32[8,128]{1,0:T(8,128)S(1)}, u32[]{:S(2)}, u32[]{:S(2)}) collective-permute-start(f32[8,128]{1,0:T(8,128)S(1)} %max.17), channel_id=1, source_target_pairs={{0,8},{4,12},{8,0},{12,4},{16,24},{20,28},{24,16},{28,20},{1,9},{5... | collective-permute-start | bytes 12296 | tf_op jit(solution)/shard_map/ppermute | solution.py:424
  54.6 4.5 %collective-permute-start.6 = (f32[8,128]{1,0:T(8,128)S(1)}, f32[8,128]{1,0:T(8,128)S(1)}, u32[]{:S(2)}, u32[]{:S(2)}) collective-permute-start(f32[8,128]{1,0:T(8,128)S(1)} %max.18), channel_id=1, source_target_pairs={{0,16},{4,20},{8,24},{12,28},{16,0},{20,4},{24,8},{28,12},{1,17},{... | collective-permute-start | bytes 12296 | tf_op jit(solution)/shard_map/ppermute | solution.py:424

commit v9 on v8

--- a/solution.py
+++ b/solution.py
@@ -420,8 +420,23 @@
     )(own, ghost_list, place, wall_state, wall_count, odd)
 
 
-def swapped(shard, axis, bit):
-    return lax.ppermute(shard, axis, [(i, i ^ 1 << bit) for i in range(lax.axis_size(axis))])
+def largest(peak, outer, inner):
+    count, width = lax.axis_size(outer), lax.axis_size(inner)
+    leaders = [(o, i) for o in range(count) for i in range(width) if i % 2 == 1]
+
+    def exchanged(value, outer_mask, inner_mask, places):
+        steps = [(o * width + i, (o ^ outer_mask) * width + (i ^ inner_mask)) for o, i in places]
+        return jnp.maximum(value, lax.ppermute(value, (outer, inner), steps))
+
+    if width > 1:
+        peak = exchanged(peak, 0, 1, [(o, i) for o in range(count) for i in range(width)])
+    for bit in range(1, (width - 1).bit_length()):
+        peak = exchanged(peak, 0, 1 << bit, leaders)
+    for bit in range((count - 1).bit_length()):
+        peak = exchanged(peak, 1 << bit, 0, leaders if width > 1 else [(o, 0) for o in range(count)])
+    if width > 1:
+        peak = exchanged(peak, 0, 1, leaders)
+    return peak
 
 
 def facing(edges, axis):
@@ -452,11 +467,7 @@
     rate, acceleration, local_peak = fluid_pass(
         own, landed.reshape(-1, LANES), pair_list, place, own_results
     )
-    peak = local_peak
-    for axis in ("wall", "orb"):
-        for bit in range((lax.axis_size(axis) - 1).bit_length()):
-            peak = jnp.maximum(peak, swapped(peak, axis, bit))
-    peak = peak[0, 0]
+    peak = largest(local_peak, "orb", "wall")[0, 0]
     time_step = courant * jnp.sqrt(smoothing / (peak + 1e-06))
     return (rate.reshape(-1), acceleration, time_step)
 

time: 61.9 us -> 67.4 us (1.089)
  waiting for transfers between devices: 7.77 us -> 17.6 us
  starting transfers between devices: 20.3 us -> 15.8 us
    ppermute x5 -> x6, waiting for transfers between devices: 7.76 us -> 17.6 us  [exchanged(): return jnp.maximum(value, lax.ppermute(value, (outer, inner), steps))]
    ppermute x5 -> x6, starting transfers between devices: 12.1 us -> 7.58 us  [exchanged(): return jnp.maximum(value, lax.ppermute(value, (outer, inner), steps))]
  transfers between devices with their start and end apart: 8 -> 9, of which waited for: 5 -> 2; matrix products, arithmetic and copies ran while one was open for 0% -> 0% of each run, Pallas kernels for 11% -> 10%
where the time goes in v9:
time: 67.4 us; the launch traced here: 67 us
  Pallas kernels  28.9 us (43%)
  waiting for transfers between devices  17.6 us (26%)
  starting transfers between devices  15.8 us (23%)
  between operations  2.67 us (4%)
  local copies, waits for them, and re-layouts  1.88 us (3%)
    pallas_call x1, Pallas kernels, fluid_pass(): pl.pallas_call(fluid_kernel, out_shape=(jax.ShapeDtypeStruct((blocks, LAN...  20.7 us
    ppermute x6, waiting for transfers between devices, exchanged(): return jnp.maximum(value, lax.ppermute(value, (outer, inner), steps))  17.6 us
    ppermute x6, starting transfers between devices, exchanged(): return jnp.maximum(value, lax.ppermute(value, (outer, inner), steps))  7.58 us
    all_to_all x1, starting transfers between devices, per_device(): lax.all_to_all(sent.reshape(8, -1, LANES), 'orb', 0, 0, axis_index_groups...  7.4 us
    pallas_call x1, Pallas kernels, own_pass(): pl.pallas_call(own_kernel, out_shape=[jax.ShapeDtypeStruct(*out) for out...  6.53 us
    pallas_call x1, Pallas kernels, outgoing_pass(): pl.pallas_call(outgoing_kernel, out_shape=[jax.ShapeDtypeStruct((row, LAN...  1.67 us
    unnamed x14, local copies, waits for them, and re-layouts  1.37 us
  transfers between devices with their start and end apart: 9, of which 2 were waited for; matrix products, arithmetic and copies ran while one was open for 0% of the time, Pallas kernels for 10%

profile of v9, /device:TPU:0, one launch (start us, length us, event | category | flops | bytes accessed | tf_op | source)
XLA Modules:
  0.0 67.0 jit_solution(5322570325004481848)
XLA Ops:
  0.7 1.7 %outgoing_pass.1 = (f32[384,128]{1,0:T(8,128)}, f32[24,128]{1,0:T(8,128)}, f32[4,128]{1,0:T(4,128)}, f32[4,128]{1,0:T(4,128)}) custom-call(f32[192,128]{1,0:T(8,128)} %bitcast.12, s32[7,6]{1,0:T(8,128)} %list_ref.1, s32[1]{0:T(128)} %bitcast.5.place_ref, f32[4,768]{1,0:T(4,128)} %wall_ref.1, s32[6]{0:T(128)} %count_ref.1, s32[1]{0:T(128)} %bitcast.6.odd_ref), custom_call_target="tpu_custom_call" | custom-call | tf_op jit(solution)/shard_map/outgoing_pass/pallas_call | solution.py:414
  2.3 0.0 copy-start
  2.3 7.4 %all-to-all-start = ((f32[8,48,128]{2,1,0:T(8,128)}), f32[8,48,128]{2,1,0:T(8,128)S(1)}, u32[]{:S(2)}, u32[]{:S(2)}) async-start(f32[8,48,128]{2,1,0:T(8,128)} %bitcast.15), calls=%async_computation | async-start | bytes 393216 | tf_op jit(solution)/shard_map/all_to_all | solution.py:459
  9.8 0.1 collective-permute-start
  9.8 0.6 copy-done.4
  10.4 0.8 %collective-permute-start.1 = (f32[4,128]{1,0:T(4,128)S(1)}, f32[4,128]{1,0:T(4,128)S(1)}, u32[]{:S(2)}, u32[]{:S(2)}) collective-permute-start(f32[4,128]{1,0:T(4,128)S(1)} %copy-done.4), channel_id=1, source_target_pairs={{1,2},{2,1},{5,6},{6,5},{9,10},{10,9},{13,14},{14,13},{17,18},{18,... | collective-permute-start | bytes 6152 | tf_op jit(solution)/shard_map/ppermute | solution.py:447
  11.2 0.1 copy.10.pair_ref
  11.3 0.1 copy.9.wpair_ref
  11.4 0.0 collective-permute-done.edge0_ref
  11.4 0.6 copy-done.1
  12.0 6.5 %own_pass.1 = (bf16[24,128,96]{2,1,0:T(8,128)(2,1)S(1)}, f32[960,128]{1,0:T(8,128)S(1)}) custom-call(f32[192,128]{1,0:T(8,128)S(1)} %bitcast.13, f32[24,128]{1,0:T(8,128)S(1)} %copy-done.1, f32[4,128]{1,0:T(4,128)S(1)} %collective-permute-done.edge0_ref, f32[4,128]{1,0:T(4,128)S(1)} %collective-permute-done.1.edge1_ref, s32[24,4]{1,0:T(8,128)S(1)} %copy.9.wpair_ref, ...), custom_call_target="tpu_custom_call" | custom-call | flops 1572864000 | tf_op jit(solution)/shard_map/own_pass/pallas_call | solution.py:350
  18.5 20.7 %fluid_pass.1 = (f32[24,128]{1,0:T(8,128)}, f32[3,3072]{1,0:T(4,128)}, f32[8,128]{1,0:T(8,128)S(1)}) custom-call(f32[192,128]{1,0:T(8,128)S(1)} %bitcast.14, f32[384,128]{1,0:T(8,128)S(1)} %bitcast.11, s32[24,14]{1,0:T(8,128)S(1)} %copy.10.pair_ref, s32[1]{0:T(128)} %bitcast.5.place_ref, bf16[24,128,96]{2,1,0:T(8,128)(2,1)S(1)} %get-tuple-element.16.tgt, ...), custom_call_target="tpu_custom_call" | custom-call | flops 5505024000 | tf_op jit(solution)/shard_map/fluid_pass/pallas_call | solution.py:368
  39.3 3.7 %collective-permute-start.2 = (f32[8,128]{1,0:T(8,128)S(1)}, f32[8,128]{1,0:T(8,128)S(1)}, u32[]{:S(2)}, u32[]{:S(2)}) collective-permute-start(f32[8,128]{1,0:T(8,128)S(1)} %get-tuple-element.20), channel_id=1, source_target_pairs={{0,1},{1,0},{2,3},{3,2},{4,5},{5,4},{6,7},{7,6},{8,9},{9,8},{10,11... | collective-permute-start | bytes 12296 | tf_op jit(solution)/shard_map/ppermute | solution.py:429
  42.9 0.8 %collective-permute-done.2 = f32[8,128]{1,0:T(8,128)S(1)} collective-permute-done((f32[8,128]{1,0:T(8,128)S(1)}, f32[8,128]{1,0:T(8,128)S(1)}, u32[]{:S(2)}, u32[]{:S(2)}) %collective-permute-start.2) | collective-permute-done | bytes 4128 | tf_op jit(solution)/shard_map/ppermute | solution.py:429
  43.7 0.6 collective-permute-start.3
  44.4 0.0 collective-permute-done.3
  44.4 0.7 collective-permute-start.4
  45.1 0.7 collective-permute-start.5
  45.8 0.0 collective-permute-done.5
  45.8 0.7 collective-permute-start.6
  46.5 0.0 collective-permute-done.6
  46.5 1.3 %collective-permute-start.7 = (f32[8,128]{1,0:T(8,128)S(1)}, f32[8,128]{1,0:T(8,128)S(1)}, u32[]{:S(2)}, u32[]{:S(2)}) collective-permute-start(f32[8,128]{1,0:T(8,128)S(1)} %max.22), channel_id=1, source_target_pairs={{1,0},{3,2},{5,4},{7,6},{9,8},{11,10},{13,12},{15,14},{17,16},{19,... | collective-permute-start | bytes 12296 | tf_op jit(solution)/shard_map/ppermute | solution.py:429
  47.8 16.8 %collective-permute-done.7 = f32[8,128]{1,0:T(8,128)S(1)} collective-permute-done((f32[8,128]{1,0:T(8,128)S(1)}, f32[8,128]{1,0:T(8,128)S(1)}, u32[]{:S(2)}, u32[]{:S(2)}) %collective-permute-start.7) | collective-permute-done | bytes 4128 | tf_op jit(solution)/shard_map/ppermute | solution.py:429
  64.6 0.5 slice.3
  (18 shorter events, 0.0 us)
Async XLA Ops:
  2.3 7.4 %copy-start.5 = (f32[4,128]{1,0:T(4,128)S(1)}, f32[4,128]{1,0:T(4,128)}, u32[]{:S(2)}) copy-start(f32[4,128]{1,0:T(4,128)} %get-tuple-element.14) | copy-start | bytes 6148
  2.3 8.9 %copy-start.2 = (s32[24,14]{0,1:T(8,128)S(1)}, s32[24,14]{0,1:T(8,128)}, u32[]{:S(2)}) copy-start(s32[24,14]{0,1:T(8,128)} %param.8) | copy-start | bytes 4036
  2.3 9.1 %copy-start = (f32[8,3072]{1,0:T(8,128)S(1)}, f32[8,3072]{1,0:T(8,128)}, u32[]{:S(2)}) copy-start(f32[8,3072]{1,0:T(8,128)} %param.6) | copy-start | bytes 294916
  2.3 16.2 %all-to-all-start = ((f32[8,48,128]{2,1,0:T(8,128)}), f32[8,48,128]{2,1,0:T(8,128)S(1)}, u32[]{:S(2)}, u32[]{:S(2)}) async-start(f32[8,48,128]{2,1,0:T(8,128)} %bitcast.15), calls=%async_computation | async-start | bytes 393216 | tf_op jit(solution)/shard_map/all_to_all | solution.py:459
  9.7 0.7 copy-start.4
  9.8 1.6 %collective-permute-start = (f32[4,128]{1,0:T(4,128)S(1)}, f32[4,128]{1,0:T(4,128)S(1)}, u32[]{:S(2)}, u32[]{:S(2)}) collective-permute-start(f32[4,128]{1,0:T(4,128)S(1)} %copy-done.5), channel_id=1, source_target_pairs={{0,1},{2,3},{1,0},{3,2},{4,5},{6,7},{5,4},{7,6},{8,9},{10,11},{9,8... | collective-permute-start | bytes 6152 | tf_op jit(solution)/shard_map/ppermute | solution.py:447
  10.4 0.9 %copy-start.3 = (s32[24,4]{0,1:T(4,128)S(1)}, s32[24,4]{0,1:T(4,128)}, u32[]{:S(2)}) copy-start(s32[24,4]{0,1:T(4,128)} %param.11) | copy-start | bytes 1156
  10.4 1.0 %collective-permute-start.1 = (f32[4,128]{1,0:T(4,128)S(1)}, f32[4,128]{1,0:T(4,128)S(1)}, u32[]{:S(2)}, u32[]{:S(2)}) collective-permute-start(f32[4,128]{1,0:T(4,128)S(1)} %copy-done.4), channel_id=1, source_target_pairs={{1,2},{2,1},{5,6},{6,5},{9,10},{10,9},{13,14},{14,13},{17,18},{18,... | collective-permute-start | bytes 6152 | tf_op jit(solution)/shard_map/ppermute | solution.py:447
  11.3 0.7 %copy-start.1 = (f32[24,128]{1,0:T(8,128)S(1)}, f32[24,128]{1,0:T(8,128)}, u32[]{:S(2)}) copy-start(f32[24,128]{1,0:T(8,128)} %get-tuple-element.13.wall_ref) | copy-start | bytes 36868
  39.3 4.5 %collective-permute-start.2 = (f32[8,128]{1,0:T(8,128)S(1)}, f32[8,128]{1,0:T(8,128)S(1)}, u32[]{:S(2)}, u32[]{:S(2)}) collective-permute-start(f32[8,128]{1,0:T(8,128)S(1)} %get-tuple-element.20), channel_id=1, source_target_pairs={{0,1},{1,0},{2,3},{3,2},{4,5},{5,4},{6,7},{7,6},{8,9},{9,8},{10,11... | collective-permute-start | bytes 12296 | tf_op jit(solution)/shard_map/ppermute | solution.py:429
  43.7 0.7 collective-permute-start.3
  44.4 0.7 %collective-permute-start.4 = (f32[8,128]{1,0:T(8,128)S(1)}, f32[8,128]{1,0:T(8,128)S(1)}, u32[]{:S(2)}, u32[]{:S(2)}) collective-permute-start(f32[8,128]{1,0:T(8,128)S(1)} %max.19), channel_id=1, source_target_pairs={{1,5},{3,7},{5,1},{7,3},{9,13},{11,15},{13,9},{15,11},{17,21},{19,... | collective-permute-start | bytes 12296 | tf_op jit(solution)/shard_map/ppermute | solution.py:429
  45.1 0.7 %collective-permute-start.5 = (f32[8,128]{1,0:T(8,128)S(1)}, f32[8,128]{1,0:T(8,128)S(1)}, u32[]{:S(2)}, u32[]{:S(2)}) collective-permute-start(f32[8,128]{1,0:T(8,128)S(1)} %max.20), channel_id=1, source_target_pairs={{1,9},{3,11},{5,13},{7,15},{9,1},{11,3},{13,5},{15,7},{17,25},{19,... | collective-permute-start | bytes 12296 | tf_op jit(solution)/shard_map/ppermute | solution.py:429
  45.8 0.7 %collective-permute-start.6 = (f32[8,128]{1,0:T(8,128)S(1)}, f32[8,128]{1,0:T(8,128)S(1)}, u32[]{:S(2)}, u32[]{:S(2)}) collective-permute-start(f32[8,128]{1,0:T(8,128)S(1)} %max.21), channel_id=1, source_target_pairs={{1,17},{3,19},{5,21},{7,23},{9,25},{11,27},{13,29},{15,31},{17,1},... | collective-permute-start | bytes 12296 | tf_op jit(solution)/shard_map/ppermute | solution.py:429
  46.5 18.1 %collective-permute-start.7 = (f32[8,128]{1,0:T(8,128)S(1)}, f32[8,128]{1,0:T(8,128)S(1)}, u32[]{:S(2)}, u32[]{:S(2)}) collective-permute-start(f32[8,128]{1,0:T(8,128)S(1)} %max.22), channel_id=1, source_target_pairs={{1,0},{3,2},{5,4},{7,6},{9,8},{11,10},{13,12},{15,14},{17,16},{19,... | collective-permute-start | bytes 12296 | tf_op jit(solution)/shard_map/ppermute | solution.py:429

commit v10 on v9

--- a/solution.py
+++ b/solution.py
@@ -405,7 +405,8 @@
     first = live_ref[: edge0_ref.shape[0], :]
     last = live_ref[live_ref.shape[0] - edge0_ref.shape[0] :, :]
     edge0_ref[...] = jnp.where(odd_ref[0] == 0, last, first)
-    edge1_ref[...] = jnp.where(odd_ref[0] == 0, first, last)
+    inside = jnp.where(odd_ref[1] == 0, 1.0, 0.0)
+    edge1_ref[...] = jnp.where(odd_ref[0] == 0, first, last) * inside
 
 
 def outgoing_pass(own, ghost_list, place, wall_state, wall_count, odd):
@@ -425,7 +426,9 @@
     leaders = [(o, i) for o in range(count) for i in range(width) if i % 2 == 1]
 
     def exchanged(value, outer_mask, inner_mask, places):
-        steps = [(o * width + i, (o ^ outer_mask) * width + (i ^ inner_mask)) for o, i in places]
+        steps = [(n, n) for n in range(count * width)]
+        for o, i in places:
+            steps[o * width + i] = (o * width + i, (o ^ outer_mask) * width + (i ^ inner_mask))
         return jnp.maximum(value, lax.ppermute(value, (outer, inner), steps))
 
     if width > 1:
@@ -435,7 +438,7 @@
     for bit in range((count - 1).bit_length()):
         peak = exchanged(peak, 1 << bit, 0, leaders if width > 1 else [(o, 0) for o in range(count)])
     if width > 1:
-        peak = exchanged(peak, 0, 1, leaders)
+        peak = exchanged(peak, 0, 1, [(o, i) for o in range(count) for i in range(width)])
     return peak
 
 
@@ -443,7 +446,7 @@
     count = lax.axis_size(axis)
     landed = []
     for start, sent in enumerate(edges):
-        pairs = [(i, i + 1) for i in range(start, count - 1, 2)]
+        pairs = [(i, (i + 1) % count) for i in range(start, count - count % 2, 2)]
         landed.append(lax.ppermute(sent, axis, pairs + [(j, i) for i, j in pairs]))
     return landed
 
@@ -452,7 +455,9 @@
     block_total = fluid_state.shape[1] // LANES
     own = jnp.transpose(fluid_state.reshape(8, block_total, LANES), (1, 0, 2)).reshape(-1, LANES)
     place = (lax.axis_index("orb") % 8).reshape(1)
-    odd = (lax.axis_index("wall") % 2).reshape(1)
+    along, row_length = lax.axis_index("wall"), lax.axis_size("wall")
+    at_end = (along == 0) | (along == row_length - row_length % 2 - 1)
+    odd = jnp.stack([along % 2, at_end.astype(along.dtype)])
     sent, walls, *edges = outgoing_pass(own, ghost_list, place, wall_state, wall_count, odd)
     edges = facing(edges, "wall")
     groups = [list(range(g, g + 8)) for g in range(0, lax.axis_size("orb"), 8)]

time: 67.4 us -> 64.8 us (0.961)
  waiting for transfers between devices: 17.6 us -> 3.58 us
  starting transfers between devices: 15.8 us -> 27.4 us
    ppermute x6, waiting for transfers between devices: 17.6 us -> 1.78 us  [exchanged(): return jnp.maximum(value, lax.ppermute(value, (outer, inner), steps))]
    ppermute x6, starting transfers between devices: 7.58 us -> 18.9 us  [exchanged(): return jnp.maximum(value, lax.ppermute(value, (outer, inner), steps))]
    ppermute x2, waiting for transfers between devices: 0.01 us -> 1.8 us  [facing(): landed.append(lax.ppermute(sent, axis, pairs + [(j, i) for i, j in pairs]))]
    unnamed x14 -> x16, local copies, waits for them, and re-layouts: 1.37 us -> 0.78 us
  transfers between devices with their start and end apart: 9 -> 9, of which waited for: 2 -> 3; matrix products, arithmetic and copies ran while one was open for 0% -> 0% of each run, Pallas kernels for 10% -> 10%
where the time goes in v10:
time: 64.8 us; the launch traced here: 64.4 us
  Pallas kernels  28.9 us (45%)
  starting transfers between devices  27.4 us (42%)
  waiting for transfers between devices  3.58 us (6%)
  between operations  2.66 us (4%)
  local copies, waits for them, and re-layouts  1.3 us (2%)
    pallas_call x1, Pallas kernels, fluid_pass(): pl.pallas_call(fluid_kernel, out_shape=(jax.ShapeDtypeStruct((blocks, LAN...  20.7 us
    ppermute x6, starting transfers between devices, exchanged(): return jnp.maximum(value, lax.ppermute(value, (outer, inner), steps))  18.9 us
    all_to_all x1, starting transfers between devices, per_device(): lax.all_to_all(sent.reshape(8, -1, LANES), 'orb', 0, 0, axis_index_groups...  7.4 us
    pallas_call x1, Pallas kernels, own_pass(): pl.pallas_call(own_kernel, out_shape=[jax.ShapeDtypeStruct(*out) for out...  6.56 us
    ppermute x2, waiting for transfers between devices, facing(): landed.append(lax.ppermute(sent, axis, pairs + [(j, i) for i, j in pairs]))  1.8 us
    ppermute x6, waiting for transfers between devices, exchanged(): return jnp.maximum(value, lax.ppermute(value, (outer, inner), steps))  1.78 us
    pallas_call x1, Pallas kernels, outgoing_pass(): pl.pallas_call(outgoing_kernel, out_shape=[jax.ShapeDtypeStruct((row, LAN...  1.65 us
  transfers between devices with their start and end apart: 9, of which 3 were waited for; matrix products, arithmetic and copies ran while one was open for 0% of the time, Pallas kernels for 10%

profile of v10, /device:TPU:0, one launch (start us, length us, event | category | flops | bytes accessed | tf_op | source)
XLA Modules:
  0.0 64.4 jit_solution(7082863982510222091)
XLA Ops:
  0.7 0.6 pad_add_fusion.odd_ref
  1.2 1.6 %outgoing_pass.1 = (f32[384,128]{1,0:T(8,128)}, f32[24,128]{1,0:T(8,128)}, f32[4,128]{1,0:T(4,128)}, f32[4,128]{1,0:T(4,128)}) custom-call(f32[192,128]{1,0:T(8,128)} %bitcast.13, s32[7,6]{1,0:T(8,128)} %list_ref.1, s32[1]{0:T(128)} %bitcast.5.place_ref, f32[4,768]{1,0:T(4,128)} %wall_ref.1, s32[6]{0:T(128)} %count_ref.1, s32[2]{0:T(128)} %pad_add_fusion.odd_ref), custom_call_target="tpu_custom_call" | custom-call | tf_op jit(solution)/shard_map/outgoing_pass/pallas_call | solution.py:415
  2.9 0.0 copy-start
  2.9 7.4 %all-to-all-start = ((f32[8,48,128]{2,1,0:T(8,128)}), f32[8,48,128]{2,1,0:T(8,128)S(1)}, u32[]{:S(2)}, u32[]{:S(2)}) async-start(f32[8,48,128]{2,1,0:T(8,128)} %bitcast.16), calls=%async_computation | async-start | bytes 393216 | tf_op jit(solution)/shard_map/all_to_all | solution.py:464
  10.3 0.1 collective-permute-start
  10.4 0.6 copy-done.5
  11.0 1.0 %collective-permute-start.1 = (f32[4,128]{1,0:T(4,128)S(1)}, f32[4,128]{1,0:T(4,128)S(1)}, u32[]{:S(2)}, u32[]{:S(2)}) collective-permute-start(f32[4,128]{1,0:T(4,128)S(1)} %copy-done.5), channel_id=1, source_target_pairs={{1,2},{3,0},{2,1},{0,3},{5,6},{7,4},{6,5},{4,7},{9,10},{11,8},{10,... | collective-permute-start | bytes 6152 | tf_op jit(solution)/shard_map/ppermute | solution.py:450
  12.0 0.1 copy.10.pair_ref
  12.1 0.1 copy.9.wpair_ref
  12.2 1.8 %collective-permute-done.1.edge1_ref = f32[4,128]{1,0:T(4,128)S(1)} collective-permute-done((f32[4,128]{1,0:T(4,128)S(1)}, f32[4,128]{1,0:T(4,128)S(1)}, u32[]{:S(2)}, u32[]{:S(2)}) %collective-permute-start.1) | collective-permute-done | bytes 2080 | tf_op jit(solution)/shard_map/ppermute | solution.py:450
  14.0 6.6 %own_pass.1 = (bf16[24,128,96]{2,1,0:T(8,128)(2,1)S(1)}, f32[960,128]{1,0:T(8,128)S(1)}) custom-call(f32[192,128]{1,0:T(8,128)S(1)} %bitcast.14, f32[24,128]{1,0:T(8,128)S(1)} %copy-done.2, f32[4,128]{1,0:T(4,128)S(1)} %collective-permute-done.edge0_ref, f32[4,128]{1,0:T(4,128)S(1)} %collective-permute-done.1.edge1_ref, s32[24,4]{1,0:T(8,128)S(1)} %copy.9.wpair_ref, ...), custom_call_target="tpu_custom_call" | custom-call | flops 1572864000 | tf_op jit(solution)/shard_map/own_pass/pallas_call | solution.py:350
  20.6 0.0 all-to-all-done
  20.6 20.7 %fluid_pass.1 = (f32[24,128]{1,0:T(8,128)}, f32[3,3072]{1,0:T(4,128)}, f32[8,128]{1,0:T(8,128)S(1)}) custom-call(f32[192,128]{1,0:T(8,128)S(1)} %bitcast.15, f32[384,128]{1,0:T(8,128)S(1)} %bitcast.12, s32[24,14]{1,0:T(8,128)S(1)} %copy.10.pair_ref, s32[1]{0:T(128)} %bitcast.5.place_ref, bf16[24,128,96]{2,1,0:T(8,128)(2,1)S(1)} %get-tuple-element.16.tgt, ...), custom_call_target="tpu_custom_call" | custom-call | flops 5505024000 | tf_op jit(solution)/shard_map/fluid_pass/pallas_call | solution.py:368
  41.3 0.2 collective-permute-start.2
  41.5 0.9 %collective-permute-done.2 = f32[8,128]{1,0:T(8,128)S(1)} collective-permute-done((f32[8,128]{1,0:T(8,128)S(1)}, f32[8,128]{1,0:T(8,128)S(1)}, u32[]{:S(2)}, u32[]{:S(2)}) %collective-permute-start.2) | collective-permute-done | bytes 4128 | tf_op jit(solution)/shard_map/ppermute | solution.py:432
  42.5 0.7 %collective-permute-start.3 = (f32[8,128]{1,0:T(8,128)S(1)}, f32[8,128]{1,0:T(8,128)S(1)}, u32[]{:S(2)}, u32[]{:S(2)}) collective-permute-start(f32[8,128]{1,0:T(8,128)S(1)} %max.18), channel_id=1, source_target_pairs={{0,0},{1,3},{2,2},{3,1},{4,4},{5,7},{6,6},{7,5},{8,8},{9,11},{10,1... | collective-permute-start | bytes 12296 | tf_op jit(solution)/shard_map/ppermute | solution.py:432
  43.1 0.7 %collective-permute-start.4 = (f32[8,128]{1,0:T(8,128)S(1)}, f32[8,128]{1,0:T(8,128)S(1)}, u32[]{:S(2)}, u32[]{:S(2)}) collective-permute-start(f32[8,128]{1,0:T(8,128)S(1)} %max.19), channel_id=1, source_target_pairs={{0,0},{1,5},{2,2},{3,7},{4,4},{5,1},{6,6},{7,3},{8,8},{9,13},{10,1... | collective-permute-start | bytes 12296 | tf_op jit(solution)/shard_map/ppermute | solution.py:432
  43.8 0.0 collective-permute-done.4
  43.8 0.7 %collective-permute-start.5 = (f32[8,128]{1,0:T(8,128)S(1)}, f32[8,128]{1,0:T(8,128)S(1)}, u32[]{:S(2)}, u32[]{:S(2)}) collective-permute-start(f32[8,128]{1,0:T(8,128)S(1)} %max.20), channel_id=1, source_target_pairs={{0,0},{1,9},{2,2},{3,11},{4,4},{5,13},{6,6},{7,15},{8,8},{9,1},{10... | collective-permute-start | bytes 12296 | tf_op jit(solution)/shard_map/ppermute | solution.py:432
  44.5 0.0 collective-permute-done.5
  44.5 0.7 %collective-permute-start.6 = (f32[8,128]{1,0:T(8,128)S(1)}, f32[8,128]{1,0:T(8,128)S(1)}, u32[]{:S(2)}, u32[]{:S(2)}) collective-permute-start(f32[8,128]{1,0:T(8,128)S(1)} %max.21), channel_id=1, source_target_pairs={{0,0},{1,17},{2,2},{3,19},{4,4},{5,21},{6,6},{7,23},{8,8},{9,25},{... | collective-permute-start | bytes 12296 | tf_op jit(solution)/shard_map/ppermute | solution.py:432
  45.2 16.0 %collective-permute-start.7 = (f32[8,128]{1,0:T(8,128)S(1)}, f32[8,128]{1,0:T(8,128)S(1)}, u32[]{:S(2)}, u32[]{:S(2)}) collective-permute-start(f32[8,128]{1,0:T(8,128)S(1)} %max.22), channel_id=1, source_target_pairs={{0,1},{1,0},{2,3},{3,2},{4,5},{5,4},{6,7},{7,6},{8,9},{9,8},{10,11... | collective-permute-start | bytes 12296 | tf_op jit(solution)/shard_map/ppermute | solution.py:432
  61.2 0.8 %collective-permute-done.7 = f32[8,128]{1,0:T(8,128)S(1)} collective-permute-done((f32[8,128]{1,0:T(8,128)S(1)}, f32[8,128]{1,0:T(8,128)S(1)}, u32[]{:S(2)}, u32[]{:S(2)}) %collective-permute-start.7) | collective-permute-done | bytes 4128 | tf_op jit(solution)/shard_map/ppermute | solution.py:432
  62.0 0.5 slice.3
  (21 shorter events, 0.1 us)
Async XLA Ops:
  2.9 7.4 %copy-start.6 = (f32[4,128]{1,0:T(4,128)S(1)}, f32[4,128]{1,0:T(4,128)}, u32[]{:S(2)}) copy-start(f32[4,128]{1,0:T(4,128)} %get-tuple-element.14) | copy-start | bytes 6148
  2.9 9.1 %copy-start.3 = (s32[24,14]{0,1:T(8,128)S(1)}, s32[24,14]{0,1:T(8,128)}, u32[]{:S(2)}) copy-start(s32[24,14]{0,1:T(8,128)} %param.8) | copy-start | bytes 4036
  2.9 11.1 %copy-start = (f32[8,3072]{1,0:T(8,128)S(1)}, f32[8,3072]{1,0:T(8,128)}, u32[]{:S(2)}) copy-start(f32[8,3072]{1,0:T(8,128)} %param.6) | copy-start | bytes 294916
  2.9 17.7 %all-to-all-start = ((f32[8,48,128]{2,1,0:T(8,128)}), f32[8,48,128]{2,1,0:T(8,128)S(1)}, u32[]{:S(2)}, u32[]{:S(2)}) async-start(f32[8,48,128]{2,1,0:T(8,128)} %bitcast.16), calls=%async_computation | async-start | bytes 393216 | tf_op jit(solution)/shard_map/all_to_all | solution.py:464
  10.3 0.7 %copy-start.5 = (f32[4,128]{1,0:T(4,128)S(1)}, f32[4,128]{1,0:T(4,128)}, u32[]{:S(2)}) copy-start(f32[4,128]{1,0:T(4,128)} %get-tuple-element.15) | copy-start | bytes 6148
  10.3 1.9 %collective-permute-start = (f32[4,128]{1,0:T(4,128)S(1)}, f32[4,128]{1,0:T(4,128)S(1)}, u32[]{:S(2)}, u32[]{:S(2)}) collective-permute-start(f32[4,128]{1,0:T(4,128)S(1)} %copy-done.6), channel_id=1, source_target_pairs={{0,1},{2,3},{1,0},{3,2},{4,5},{6,7},{5,4},{7,6},{8,9},{10,11},{9,8... | collective-permute-start | bytes 6152 | tf_op jit(solution)/shard_map/ppermute | solution.py:450
  11.0 1.1 %copy-start.4 = (s32[24,4]{0,1:T(4,128)S(1)}, s32[24,4]{0,1:T(4,128)}, u32[]{:S(2)}) copy-start(s32[24,4]{0,1:T(4,128)} %param.11) | copy-start | bytes 1156
  11.0 3.0 %collective-permute-start.1 = (f32[4,128]{1,0:T(4,128)S(1)}, f32[4,128]{1,0:T(4,128)S(1)}, u32[]{:S(2)}, u32[]{:S(2)}) collective-permute-start(f32[4,128]{1,0:T(4,128)S(1)} %copy-done.5), channel_id=1, source_target_pairs={{1,2},{3,0},{2,1},{0,3},{5,6},{7,4},{6,5},{4,7},{9,10},{11,8},{10,... | collective-permute-start | bytes 6152 | tf_op jit(solution)/shard_map/ppermute | solution.py:450
  12.1 1.9 %copy-start.2 = (f32[24,128]{1,0:T(8,128)S(1)}, f32[24,128]{1,0:T(8,128)}, u32[]{:S(2)}) copy-start(f32[24,128]{1,0:T(8,128)} %get-tuple-element.13.wall_ref) | copy-start | bytes 36868
  12.2 1.8 %copy-start.1 = (s32[2]{0:T(128)S(1)}, s32[2]{0:T(128)}, u32[]{:S(2)}) copy-start(s32[2]{0:T(128)} %pad_add_fusion.odd_ref) | copy-start | bytes 28
  41.3 1.2 %collective-permute-start.2 = (f32[8,128]{1,0:T(8,128)S(1)}, f32[8,128]{1,0:T(8,128)S(1)}, u32[]{:S(2)}, u32[]{:S(2)}) collective-permute-start(f32[8,128]{1,0:T(8,128)S(1)} %get-tuple-element.20), channel_id=1, source_target_pairs={{0,1},{1,0},{2,3},{3,2},{4,5},{5,4},{6,7},{7,6},{8,9},{9,8},{10,11... | collective-permute-start | bytes 12296 | tf_op jit(solution)/shard_map/ppermute | solution.py:432
  42.5 0.7 %collective-permute-start.3 = (f32[8,128]{1,0:T(8,128)S(1)}, f32[8,128]{1,0:T(8,128)S(1)}, u32[]{:S(2)}, u32[]{:S(2)}) collective-permute-start(f32[8,128]{1,0:T(8,128)S(1)} %max.18), channel_id=1, source_target_pairs={{0,0},{1,3},{2,2},{3,1},{4,4},{5,7},{6,6},{7,5},{8,8},{9,11},{10,1... | collective-permute-start | bytes 12296 | tf_op jit(solution)/shard_map/ppermute | solution.py:432
  43.1 0.7 %collective-permute-start.4 = (f32[8,128]{1,0:T(8,128)S(1)}, f32[8,128]{1,0:T(8,128)S(1)}, u32[]{:S(2)}, u32[]{:S(2)}) collective-permute-start(f32[8,128]{1,0:T(8,128)S(1)} %max.19), channel_id=1, source_target_pairs={{0,0},{1,5},{2,2},{3,7},{4,4},{5,1},{6,6},{7,3},{8,8},{9,13},{10,1... | collective-permute-start | bytes 12296 | tf_op jit(solution)/shard_map/ppermute | solution.py:432
  43.8 0.7 %collective-permute-start.5 = (f32[8,128]{1,0:T(8,128)S(1)}, f32[8,128]{1,0:T(8,128)S(1)}, u32[]{:S(2)}, u32[]{:S(2)}) collective-permute-start(f32[8,128]{1,0:T(8,128)S(1)} %max.20), channel_id=1, source_target_pairs={{0,0},{1,9},{2,2},{3,11},{4,4},{5,13},{6,6},{7,15},{8,8},{9,1},{10... | collective-permute-start | bytes 12296 | tf_op jit(solution)/shard_map/ppermute | solution.py:432
  44.5 0.7 %collective-permute-start.6 = (f32[8,128]{1,0:T(8,128)S(1)}, f32[8,128]{1,0:T(8,128)S(1)}, u32[]{:S(2)}, u32[]{:S(2)}) collective-permute-start(f32[8,128]{1,0:T(8,128)S(1)} %max.21), channel_id=1, source_target_pairs={{0,0},{1,17},{2,2},{3,19},{4,4},{5,21},{6,6},{7,23},{8,8},{9,25},{... | collective-permute-start | bytes 12296 | tf_op jit(solution)/shard_map/ppermute | solution.py:432
  45.2 16.8 %collective-permute-start.7 = (f32[8,128]{1,0:T(8,128)S(1)}, f32[8,128]{1,0:T(8,128)S(1)}, u32[]{:S(2)}, u32[]{:S(2)}) collective-permute-start(f32[8,128]{1,0:T(8,128)S(1)} %max.22), channel_id=1, source_target_pairs={{0,1},{1,0},{2,3},{3,2},{4,5},{5,4},{6,7},{7,6},{8,9},{9,8},{10,11... | collective-permute-start | bytes 12296 | tf_op jit(solution)/shard_map/ppermute | solution.py:432

commit v11 on v8

--- a/solution.py
+++ b/solution.py
@@ -1,3 +1,4 @@
+import functools
 import math
 
 import jax
@@ -211,7 +212,7 @@
 
 
 def own_kernel(
-    own_ref, wall_ref, edge0_ref, edge1_ref, wpair_ref, odd_ref,
+    own_ref, wall_ref, edge0_ref, edge1_ref, wpair_ref, along_ref,
     tgt, sums, wsrc, table,
 ):
     blocks = tgt.shape[0]
@@ -232,7 +233,7 @@
             put_source(block, count, wsrc, None, adhesion / cohesion)
             count += 1
     inner, edge = wall_ref.shape[0] // 4, edge0_ref.shape[0] // 4
-    odd = odd_ref[0]
+    odd = along_ref[0] % 2
     for c in range(inner):
         table[edge + c] = c
     for c in range(edge):
@@ -340,7 +341,7 @@
     return (count, DEPTH + 2 * ROWS, VALUES * LANES), jnp.bfloat16
 
 
-def own_pass(own, walls, edges, wall_pairs, odd):
+def own_pass(own, walls, edges, wall_pairs, along):
     blocks = own.shape[0] // ROWS
     wall_blocks = (walls.shape[0] + 2 * edges[0].shape[0]) // 4
     outs = [
@@ -359,7 +360,7 @@
         compiler_params=PARAMS,
         cost_estimate=tile_cost(wall_pairs.size),
         name="own_pass",
-    )(own, walls, *edges, wall_pairs, odd)
+    )(own, walls, *edges, wall_pairs, along)
 
 
 def fluid_pass(own, ghosts, pair_list, place, own_results):
@@ -388,7 +389,8 @@
 
 
 def outgoing_kernel(
-    own_ref, list_ref, place_ref, wall_ref, count_ref, odd_ref, sent_ref, live_ref, edge0_ref, edge1_ref,
+    row_length, own_ref, list_ref, place_ref, wall_ref, count_ref, along_ref,
+    sent_ref, live_ref, edge0_ref, edge1_ref,
 ):
     for slot in range(8):
         mask = jnp.bitwise_xor(place_ref[0], slot)
@@ -404,20 +406,23 @@
         live_ref[4 * c : 4 * c + 4, :] = jnp.where(kept, block, 0.0)
     first = live_ref[: edge0_ref.shape[0], :]
     last = live_ref[live_ref.shape[0] - edge0_ref.shape[0] :, :]
-    edge0_ref[...] = jnp.where(odd_ref[0] == 0, last, first)
-    edge1_ref[...] = jnp.where(odd_ref[0] == 0, first, last)
-
-
-def outgoing_pass(own, ghost_list, place, wall_state, wall_count, odd):
+    along = along_ref[0]
+    edge0_ref[...] = jnp.where(along % 2 == 0, last, first)
+    end = row_length - row_length % 2 - 1
+    inside = jnp.where((along == 0) | (along == end), 0.0, 1.0)
+    edge1_ref[...] = jnp.where(along % 2 == 0, first, last) * inside
+
+
+def outgoing_pass(own, ghost_list, place, wall_state, wall_count, along):
     walls = wall_state.shape[1] // LANES
     rows = [8 * ghost_list.shape[1] * ROWS, walls * 4, EB * 4, EB * 4]
     return pl.pallas_call(
-        outgoing_kernel,
+        functools.partial(outgoing_kernel, lax.axis_size("wall")),
         out_shape=[jax.ShapeDtypeStruct((row, LANES), jnp.float32) for row in rows],
         in_specs=[VMEM, SMEM, SMEM, VMEM, SMEM, SMEM],
         out_specs=[VMEM] * len(rows),
         name="outgoing_pass",
-    )(own, ghost_list, place, wall_state, wall_count, odd)
+    )(own, ghost_list, place, wall_state, wall_count, along)
 
 
 def swapped(shard, axis, bit):
@@ -428,7 +433,7 @@
     count = lax.axis_size(axis)
     landed = []
     for start, sent in enumerate(edges):
-        pairs = [(i, i + 1) for i in range(start, count - 1, 2)]
+        pairs = [(i, (i + 1) % count) for i in range(start, count - count % 2, 2)]
         landed.append(lax.ppermute(sent, axis, pairs + [(j, i) for i, j in pairs]))
     return landed
 
@@ -437,8 +442,8 @@
     block_total = fluid_state.shape[1] // LANES
     own = jnp.transpose(fluid_state.reshape(8, block_total, LANES), (1, 0, 2)).reshape(-1, LANES)
     place = (lax.axis_index("orb") % 8).reshape(1)
-    odd = (lax.axis_index("wall") % 2).reshape(1)
-    sent, walls, *edges = outgoing_pass(own, ghost_list, place, wall_state, wall_count, odd)
+    along = lax.axis_index("wall").reshape(1)
+    sent, walls, *edges = outgoing_pass(own, ghost_list, place, wall_state, wall_count, along)
     edges = facing(edges, "wall")
     groups = [list(range(g, g + 8)) for g in range(0, lax.axis_size("orb"), 8)]
     landed = lax.all_to_all(
@@ -448,7 +453,7 @@
         0,
         axis_index_groups=groups if len(groups) > 1 else None,
     )
-    own_results = own_pass(own, walls, edges, wall_pairs, odd)
+    own_results = own_pass(own, walls, edges, wall_pairs, along)
     rate, acceleration, local_peak = fluid_pass(
         own, landed.reshape(-1, LANES), pair_list, place, own_results
     )

time: 61.9 us -> 59.9 us (0.968)
  starting transfers between devices: 20.3 us -> 17.4 us
  waiting for transfers between devices: 7.77 us -> 9.44 us
    ppermute x5, starting transfers between devices: 12.1 us -> 8.92 us  [swapped(): lax.ppermute(shard, axis, [(i, i ^ 1 << bit) for i in range(lax.axis_size...]
    ppermute x2, waiting for transfers between devices: 0.01 us -> 1.78 us  [facing(): landed.append(lax.ppermute(sent, axis, pairs + [(j, i) for i, j in pairs]))]
  transfers between devices with their start and end apart: 8 -> 8, of which waited for: 5 -> 6; matrix products, arithmetic and copies ran while one was open for 0% -> 0% of each run, Pallas kernels for 11% -> 11%
where the time goes in v11:
time: 59.9 us; the launch traced here: 59.6 us
  Pallas kernels  28.9 us (48%)
  starting transfers between devices  17.4 us (29%)
  waiting for transfers between devices  9.44 us (16%)
  between operations  2.55 us (4%)
  local copies, waits for them, and re-layouts  1.28 us (2%)
    pallas_call x1, Pallas kernels, fluid_pass(): pl.pallas_call(fluid_kernel, out_shape=(jax.ShapeDtypeStruct((blocks, LAN...  20.7 us
    ppermute x5, starting transfers between devices, swapped(): lax.ppermute(shard, axis, [(i, i ^ 1 << bit) for i in range(lax.axis_size...  8.92 us
    ppermute x5, waiting for transfers between devices, swapped(): lax.ppermute(shard, axis, [(i, i ^ 1 << bit) for i in range(lax.axis_size...  7.65 us
    all_to_all x1, starting transfers between devices, per_device(): lax.all_to_all(sent.reshape(8, -1, LANES), 'orb', 0, 0, axis_index_groups...  7.4 us
    pallas_call x1, Pallas kernels, own_pass(): pl.pallas_call(own_kernel, out_shape=[jax.ShapeDtypeStruct(*out) for out...  6.55 us
    ppermute x2, waiting for transfers between devices, facing(): landed.append(lax.ppermute(sent, axis, pairs + [(j, i) for i, j in pairs]))  1.78 us
    pallas_call x1, Pallas kernels, outgoing_pass(): pl.pallas_call(functools.partial(outgoing_kernel, lax.axis_size('wall')),...  1.65 us
  transfers between devices with their start and end apart: 8, of which 6 were waited for; matrix products, arithmetic and copies ran while one was open for 0% of the time, Pallas kernels for 11%

profile of v11, /device:TPU:0, one launch (start us, length us, event | category | flops | bytes accessed | tf_op | source)
XLA Modules:
  0.0 59.6 jit_solution(12447384288274154154)
XLA Ops:
  0.6 1.7 %outgoing_pass.1 = (f32[384,128]{1,0:T(8,128)}, f32[24,128]{1,0:T(8,128)}, f32[4,128]{1,0:T(4,128)}, f32[4,128]{1,0:T(4,128)}) custom-call(f32[192,128]{1,0:T(8,128)} %bitcast.12, s32[7,6]{1,0:T(8,128)} %list_ref.1, s32[1]{0:T(128)} %bitcast.5.place_ref, f32[4,768]{1,0:T(4,128)} %wall_ref.1, s32[6]{0:T(128)} %count_ref.1, s32[1]{0:T(128)} %bitcast.6.along_ref), custom_call_target="tpu_custom_call" | custom-call | tf_op jit(solution)/shard_map/outgoing_pass/pallas_call | solution.py:419
  2.3 0.0 copy-start
  2.3 7.4 %all-to-all-start = ((f32[8,48,128]{2,1,0:T(8,128)}), f32[8,48,128]{2,1,0:T(8,128)S(1)}, u32[]{:S(2)}, u32[]{:S(2)}) async-start(f32[8,48,128]{2,1,0:T(8,128)} %bitcast.15), calls=%async_computation | async-start | bytes 393216 | tf_op jit(solution)/shard_map/all_to_all | solution.py:449
  9.7 0.1 collective-permute-start
  9.8 0.6 copy-done.4
  10.4 1.0 %collective-permute-start.1 = (f32[4,128]{1,0:T(4,128)S(1)}, f32[4,128]{1,0:T(4,128)S(1)}, u32[]{:S(2)}, u32[]{:S(2)}) collective-permute-start(f32[4,128]{1,0:T(4,128)S(1)} %copy-done.4), channel_id=1, source_target_pairs={{1,2},{3,0},{2,1},{0,3},{5,6},{7,4},{6,5},{4,7},{9,10},{11,8},{10,... | collective-permute-start | bytes 6152 | tf_op jit(solution)/shard_map/ppermute | solution.py:437
  11.4 0.1 copy.10.pair_ref
  11.5 0.1 copy.9.wpair_ref
  11.6 0.0 collective-permute-done.edge0_ref
  11.6 1.8 %collective-permute-done.1.edge1_ref = f32[4,128]{1,0:T(4,128)S(1)} collective-permute-done((f32[4,128]{1,0:T(4,128)S(1)}, f32[4,128]{1,0:T(4,128)S(1)}, u32[]{:S(2)}, u32[]{:S(2)}) %collective-permute-start.1) | collective-permute-done | bytes 2080 | tf_op jit(solution)/shard_map/ppermute | solution.py:437
  13.4 6.5 %own_pass.1 = (bf16[24,128,96]{2,1,0:T(8,128)(2,1)S(1)}, f32[960,128]{1,0:T(8,128)S(1)}) custom-call(f32[192,128]{1,0:T(8,128)S(1)} %bitcast.13, f32[24,128]{1,0:T(8,128)S(1)} %copy-done.1, f32[4,128]{1,0:T(4,128)S(1)} %collective-permute-done.edge0_ref, f32[4,128]{1,0:T(4,128)S(1)} %collective-permute-done.1.edge1_ref, s32[24,4]{1,0:T(8,128)S(1)} %copy.9.wpair_ref, ...), custom_call_target="tpu_custom_call" | custom-call | flops 1572864000 | tf_op jit(solution)/shard_map/own_pass/pallas_call | solution.py:351
  19.9 0.0 all-to-all-done
  20.0 20.7 %fluid_pass.1 = (f32[24,128]{1,0:T(8,128)}, f32[3,3072]{1,0:T(4,128)}, f32[8,128]{1,0:T(8,128)S(1)}) custom-call(f32[192,128]{1,0:T(8,128)S(1)} %bitcast.14, f32[384,128]{1,0:T(8,128)S(1)} %bitcast.11, s32[24,14]{1,0:T(8,128)S(1)} %copy.10.pair_ref, s32[1]{0:T(128)} %bitcast.5.place_ref, bf16[24,128,96]{2,1,0:T(8,128)(2,1)S(1)} %get-tuple-element.16.tgt, ...), custom_call_target="tpu_custom_call" | custom-call | flops 5505024000 | tf_op jit(solution)/shard_map/fluid_pass/pallas_call | solution.py:369
  40.7 0.3 collective-permute-start.2
  40.9 0.9 %collective-permute-done.2 = f32[8,128]{1,0:T(8,128)S(1)} collective-permute-done((f32[8,128]{1,0:T(8,128)S(1)}, f32[8,128]{1,0:T(8,128)S(1)}, u32[]{:S(2)}, u32[]{:S(2)}) %collective-permute-start.2) | collective-permute-done | bytes 4128 | tf_op jit(solution)/shard_map/ppermute | solution.py:429
  41.8 1.6 %collective-permute-start.3 = (f32[8,128]{1,0:T(8,128)S(1)}, f32[8,128]{1,0:T(8,128)S(1)}, u32[]{:S(2)}, u32[]{:S(2)}) collective-permute-start(f32[8,128]{1,0:T(8,128)S(1)} %max.15), channel_id=1, source_target_pairs={{0,2},{1,3},{2,0},{3,1},{4,6},{5,7},{6,4},{7,5},{8,10},{9,11},{10,... | collective-permute-start | bytes 12296 | tf_op jit(solution)/shard_map/ppermute | solution.py:429
  43.4 2.0 %collective-permute-done.3 = f32[8,128]{1,0:T(8,128)S(1)} collective-permute-done((f32[8,128]{1,0:T(8,128)S(1)}, f32[8,128]{1,0:T(8,128)S(1)}, u32[]{:S(2)}, u32[]{:S(2)}) %collective-permute-start.3) | collective-permute-done | bytes 4128 | tf_op jit(solution)/shard_map/ppermute | solution.py:429
  45.4 2.1 %collective-permute-start.4 = (f32[8,128]{1,0:T(8,128)S(1)}, f32[8,128]{1,0:T(8,128)S(1)}, u32[]{:S(2)}, u32[]{:S(2)}) collective-permute-start(f32[8,128]{1,0:T(8,128)S(1)} %max.16), channel_id=1, source_target_pairs={{0,4},{4,0},{8,12},{12,8},{16,20},{20,16},{24,28},{28,24},{1,5},{5... | collective-permute-start | bytes 12296 | tf_op jit(solution)/shard_map/ppermute | solution.py:429
  47.5 1.6 %collective-permute-done.4 = f32[8,128]{1,0:T(8,128)S(1)} collective-permute-done((f32[8,128]{1,0:T(8,128)S(1)}, f32[8,128]{1,0:T(8,128)S(1)}, u32[]{:S(2)}, u32[]{:S(2)}) %collective-permute-start.4) | collective-permute-done | bytes 4128 | tf_op jit(solution)/shard_map/ppermute | solution.py:429
  49.1 2.0 %collective-permute-start.5 = (f32[8,128]{1,0:T(8,128)S(1)}, f32[8,128]{1,0:T(8,128)S(1)}, u32[]{:S(2)}, u32[]{:S(2)}) collective-permute-start(f32[8,128]{1,0:T(8,128)S(1)} %max.17), channel_id=1, source_target_pairs={{0,8},{4,12},{8,0},{12,4},{16,24},{20,28},{24,16},{28,20},{1,9},{5... | collective-permute-start | bytes 12296 | tf_op jit(solution)/shard_map/ppermute | solution.py:429
  51.1 1.6 %collective-permute-done.5 = f32[8,128]{1,0:T(8,128)S(1)} collective-permute-done((f32[8,128]{1,0:T(8,128)S(1)}, f32[8,128]{1,0:T(8,128)S(1)}, u32[]{:S(2)}, u32[]{:S(2)}) %collective-permute-start.5) | collective-permute-done | bytes 4128 | tf_op jit(solution)/shard_map/ppermute | solution.py:429
  52.7 2.9 %collective-permute-start.6 = (f32[8,128]{1,0:T(8,128)S(1)}, f32[8,128]{1,0:T(8,128)S(1)}, u32[]{:S(2)}, u32[]{:S(2)}) collective-permute-start(f32[8,128]{1,0:T(8,128)S(1)} %max.18), channel_id=1, source_target_pairs={{0,16},{4,20},{8,24},{12,28},{16,0},{20,4},{24,8},{28,12},{1,17},{... | collective-permute-start | bytes 12296 | tf_op jit(solution)/shard_map/ppermute | solution.py:429
  55.7 1.6 %collective-permute-done.6 = f32[8,128]{1,0:T(8,128)S(1)} collective-permute-done((f32[8,128]{1,0:T(8,128)S(1)}, f32[8,128]{1,0:T(8,128)S(1)}, u32[]{:S(2)}, u32[]{:S(2)}) %collective-permute-start.6) | collective-permute-done | bytes 4128 | tf_op jit(solution)/shard_map/ppermute | solution.py:429
  57.3 0.5 slice.3
  (15 shorter events, 0.0 us)
Async XLA Ops:
  2.3 7.4 %copy-start.5 = (f32[4,128]{1,0:T(4,128)S(1)}, f32[4,128]{1,0:T(4,128)}, u32[]{:S(2)}) copy-start(f32[4,128]{1,0:T(4,128)} %get-tuple-element.14) | copy-start | bytes 6148
  2.3 9.1 %copy-start.2 = (s32[24,14]{0,1:T(8,128)S(1)}, s32[24,14]{0,1:T(8,128)}, u32[]{:S(2)}) copy-start(s32[24,14]{0,1:T(8,128)} %param.8) | copy-start | bytes 4036
  2.3 11.1 %copy-start = (f32[8,3072]{1,0:T(8,128)S(1)}, f32[8,3072]{1,0:T(8,128)}, u32[]{:S(2)}) copy-start(f32[8,3072]{1,0:T(8,128)} %param.6) | copy-start | bytes 294916
  2.3 17.6 %all-to-all-start = ((f32[8,48,128]{2,1,0:T(8,128)}), f32[8,48,128]{2,1,0:T(8,128)S(1)}, u32[]{:S(2)}, u32[]{:S(2)}) async-start(f32[8,48,128]{2,1,0:T(8,128)} %bitcast.15), calls=%async_computation | async-start | bytes 393216 | tf_op jit(solution)/shard_map/all_to_all | solution.py:449
  9.7 0.7 %copy-start.4 = (f32[4,128]{1,0:T(4,128)S(1)}, f32[4,128]{1,0:T(4,128)}, u32[]{:S(2)}) copy-start(f32[4,128]{1,0:T(4,128)} %get-tuple-element.15) | copy-start | bytes 6148
  9.7 1.9 %collective-permute-start = (f32[4,128]{1,0:T(4,128)S(1)}, f32[4,128]{1,0:T(4,128)S(1)}, u32[]{:S(2)}, u32[]{:S(2)}) collective-permute-start(f32[4,128]{1,0:T(4,128)S(1)} %copy-done.5), channel_id=1, source_target_pairs={{0,1},{2,3},{1,0},{3,2},{4,5},{6,7},{5,4},{7,6},{8,9},{10,11},{9,8... | collective-permute-start | bytes 6152 | tf_op jit(solution)/shard_map/ppermute | solution.py:437
  10.4 1.1 %copy-start.3 = (s32[24,4]{0,1:T(4,128)S(1)}, s32[24,4]{0,1:T(4,128)}, u32[]{:S(2)}) copy-start(s32[24,4]{0,1:T(4,128)} %param.11) | copy-start | bytes 1156
  10.4 3.0 %collective-permute-start.1 = (f32[4,128]{1,0:T(4,128)S(1)}, f32[4,128]{1,0:T(4,128)S(1)}, u32[]{:S(2)}, u32[]{:S(2)}) collective-permute-start(f32[4,128]{1,0:T(4,128)S(1)} %copy-done.4), channel_id=1, source_target_pairs={{1,2},{3,0},{2,1},{0,3},{5,6},{7,4},{6,5},{4,7},{9,10},{11,8},{10,... | collective-permute-start | bytes 6152 | tf_op jit(solution)/shard_map/ppermute | solution.py:437
  11.5 1.9 %copy-start.1 = (f32[24,128]{1,0:T(8,128)S(1)}, f32[24,128]{1,0:T(8,128)}, u32[]{:S(2)}) copy-start(f32[24,128]{1,0:T(8,128)} %get-tuple-element.13.wall_ref) | copy-start | bytes 36868
  40.7 1.2 %collective-permute-start.2 = (f32[8,128]{1,0:T(8,128)S(1)}, f32[8,128]{1,0:T(8,128)S(1)}, u32[]{:S(2)}, u32[]{:S(2)}) collective-permute-start(f32[8,128]{1,0:T(8,128)S(1)} %get-tuple-element.20), channel_id=1, source_target_pairs={{0,1},{1,0},{2,3},{3,2},{4,5},{5,4},{6,7},{7,6},{8,9},{9,8},{10,11... | collective-permute-start | bytes 12296 | tf_op jit(solution)/shard_map/ppermute | solution.py:429
  41.8 3.6 %collective-permute-start.3 = (f32[8,128]{1,0:T(8,128)S(1)}, f32[8,128]{1,0:T(8,128)S(1)}, u32[]{:S(2)}, u32[]{:S(2)}) collective-permute-start(f32[8,128]{1,0:T(8,128)S(1)} %max.15), channel_id=1, source_target_pairs={{0,2},{1,3},{2,0},{3,1},{4,6},{5,7},{6,4},{7,5},{8,10},{9,11},{10,... | collective-permute-start | bytes 12296 | tf_op jit(solution)/shard_map/ppermute | solution.py:429
  45.4 3.7 %collective-permute-start.4 = (f32[8,128]{1,0:T(8,128)S(1)}, f32[8,128]{1,0:T(8,128)S(1)}, u32[]{:S(2)}, u32[]{:S(2)}) collective-permute-start(f32[8,128]{1,0:T(8,128)S(1)} %max.16), channel_id=1, source_target_pairs={{0,4},{4,0},{8,12},{12,8},{16,20},{20,16},{24,28},{28,24},{1,5},{5... | collective-permute-start | bytes 12296 | tf_op jit(solution)/shard_map/ppermute | solution.py:429
  49.1 3.6 %collective-permute-start.5 = (f32[8,128]{1,0:T(8,128)S(1)}, f32[8,128]{1,0:T(8,128)S(1)}, u32[]{:S(2)}, u32[]{:S(2)}) collective-permute-start(f32[8,128]{1,0:T(8,128)S(1)} %max.17), channel_id=1, source_target_pairs={{0,8},{4,12},{8,0},{12,4},{16,24},{20,28},{24,16},{28,20},{1,9},{5... | collective-permute-start | bytes 12296 | tf_op jit(solution)/shard_map/ppermute | solution.py:429
  52.7 4.5 %collective-permute-start.6 = (f32[8,128]{1,0:T(8,128)S(1)}, f32[8,128]{1,0:T(8,128)S(1)}, u32[]{:S(2)}, u32[]{:S(2)}) collective-permute-start(f32[8,128]{1,0:T(8,128)S(1)} %max.18), channel_id=1, source_target_pairs={{0,16},{4,20},{8,24},{12,28},{16,0},{20,4},{24,8},{28,12},{1,17},{... | collective-permute-start | bytes 12296 | tf_op jit(solution)/shard_map/ppermute | solution.py:429

commit v12 on v11

--- a/solution.py
+++ b/solution.py
@@ -14,7 +14,7 @@
 DEPTH = 12 * ROWS
 MOMENTS = 4 * ROWS
 SUMS = MOMENTS + ROWS
-UNROLL = 12
+UNROLL = 24
 VALUES = 3
 GROUP = 2
 WALL_TARGETS = 24
@@ -425,8 +425,20 @@
     )(own, ghost_list, place, wall_state, wall_count, along)
 
 
-def swapped(shard, axis, bit):
-    return lax.ppermute(shard, axis, [(i, i ^ 1 << bit) for i in range(lax.axis_size(axis))])
+def swapped(shard, axis, mask):
+    count = math.prod(lax.axis_size(name) for name in axis)
+    return lax.ppermute(shard, axis, [(i, i ^ mask) for i in range(count)])
+
+
+def largest(peak, outer, inner):
+    count, width = lax.axis_size(outer), lax.axis_size(inner)
+    other = 1 if width > 1 else 0
+    masks = [other] if other else []
+    masks += [1 << bit | other for bit in range(1, (width - 1).bit_length())]
+    masks += [width << bit | other for bit in range((count - 1).bit_length())]
+    for mask in masks:
+        peak = jnp.maximum(peak, swapped(peak, (outer, inner), mask))
+    return peak
 
 
 def facing(edges, axis):
@@ -457,11 +469,7 @@
     rate, acceleration, local_peak = fluid_pass(
         own, landed.reshape(-1, LANES), pair_list, place, own_results
     )
-    peak = local_peak
-    for axis in ("wall", "orb"):
-        for bit in range((lax.axis_size(axis) - 1).bit_length()):
-            peak = jnp.maximum(peak, swapped(peak, axis, bit))
-    peak = peak[0, 0]
+    peak = largest(local_peak, "orb", "wall")[0, 0]
     time_step = courant * jnp.sqrt(smoothing / (peak + 1e-06))
     return (rate.reshape(-1), acceleration, time_step)
 

time: 59.9 us -> 57.4 us (0.958)
  starting transfers between devices: 17.4 us -> 16.1 us
  waiting for transfers between devices: 9.44 us -> 8.55 us
    ppermute x5, starting transfers between devices: 8.92 us -> 7.58 us  [swapped(): return lax.ppermute(shard, axis, [(i, i ^ mask) for i in range(count)])]
    ppermute x5, waiting for transfers between devices: 7.65 us -> 6.76 us  [swapped(): return lax.ppermute(shard, axis, [(i, i ^ mask) for i in range(count)])]
where the time goes in v12:
time: 57.4 us; the launch traced here: 57.1 us
  Pallas kernels  28.6 us (50%)
  starting transfers between devices  16.1 us (28%)
  waiting for transfers between devices  8.55 us (15%)
  between operations  2.55 us (4%)
  local copies, waits for them, and re-layouts  1.28 us (2%)
    pallas_call x1, Pallas kernels, fluid_pass(): pl.pallas_call(fluid_kernel, out_shape=(jax.ShapeDtypeStruct((blocks, LAN...  20.7 us
    ppermute x5, starting transfers between devices, swapped(): return lax.ppermute(shard, axis, [(i, i ^ mask) for i in range(count)])  7.58 us
    all_to_all x1, starting transfers between devices, per_device(): lax.all_to_all(sent.reshape(8, -1, LANES), 'orb', 0, 0, axis_index_groups...  7.4 us
    ppermute x5, waiting for transfers between devices, swapped(): return lax.ppermute(shard, axis, [(i, i ^ mask) for i in range(count)])  6.76 us
    pallas_call x1, Pallas kernels, own_pass(): pl.pallas_call(own_kernel, out_shape=[jax.ShapeDtypeStruct(*out) for out...  6.28 us
    ppermute x2, waiting for transfers between devices, facing(): landed.append(lax.ppermute(sent, axis, pairs + [(j, i) for i, j in pairs]))  1.78 us
    pallas_call x1, Pallas kernels, outgoing_pass(): pl.pallas_call(functools.partial(outgoing_kernel, lax.axis_size('wall')),...  1.65 us
  transfers between devices with their start and end apart: 8, of which 6 were waited for; matrix products, arithmetic and copies ran while one was open for 0% of the time, Pallas kernels for 11%

profile of v12, /device:TPU:0, one launch (start us, length us, event | category | flops | bytes accessed | tf_op | source)
XLA Modules:
  0.0 57.1 jit_solution(14837845963310488034)
XLA Ops:
  0.6 1.7 %outgoing_pass.1 = (f32[384,128]{1,0:T(8,128)}, f32[24,128]{1,0:T(8,128)}, f32[4,128]{1,0:T(4,128)}, f32[4,128]{1,0:T(4,128)}) custom-call(f32[192,128]{1,0:T(8,128)} %bitcast.12, s32[7,6]{1,0:T(8,128)} %list_ref.1, s32[1]{0:T(128)} %bitcast.5.place_ref, f32[4,768]{1,0:T(4,128)} %wall_ref.1, s32[6]{0:T(128)} %count_ref.1, s32[1]{0:T(128)} %bitcast.6.along_ref), custom_call_target="tpu_custom_call" | custom-call | tf_op jit(solution)/shard_map/outgoing_pass/pallas_call | solution.py:419
  2.3 0.0 copy-start
  2.3 7.4 %all-to-all-start = ((f32[8,48,128]{2,1,0:T(8,128)}), f32[8,48,128]{2,1,0:T(8,128)S(1)}, u32[]{:S(2)}, u32[]{:S(2)}) async-start(f32[8,48,128]{2,1,0:T(8,128)} %bitcast.15), calls=%async_computation | async-start | bytes 393216 | tf_op jit(solution)/shard_map/all_to_all | solution.py:461
  9.7 0.1 collective-permute-start
  9.8 0.6 %copy-done.4 = f32[4,128]{1,0:T(4,128)S(1)} copy-done((f32[4,128]{1,0:T(4,128)S(1)}, f32[4,128]{1,0:T(4,128)}, u32[]{:S(2)}) %copy-start.4) | copy-done | bytes 2072
  10.4 1.0 %collective-permute-start.1 = (f32[4,128]{1,0:T(4,128)S(1)}, f32[4,128]{1,0:T(4,128)S(1)}, u32[]{:S(2)}, u32[]{:S(2)}) collective-permute-start(f32[4,128]{1,0:T(4,128)S(1)} %copy-done.4), channel_id=1, source_target_pairs={{1,2},{3,0},{2,1},{0,3},{5,6},{7,4},{6,5},{4,7},{9,10},{11,8},{10,... | collective-permute-start | bytes 6152 | tf_op jit(solution)/shard_map/ppermute | solution.py:449
  11.4 0.1 copy.10.pair_ref
  11.5 0.1 copy.9.wpair_ref
  11.6 0.0 collective-permute-done.edge0_ref
  11.6 1.8 %collective-permute-done.1.edge1_ref = f32[4,128]{1,0:T(4,128)S(1)} collective-permute-done((f32[4,128]{1,0:T(4,128)S(1)}, f32[4,128]{1,0:T(4,128)S(1)}, u32[]{:S(2)}, u32[]{:S(2)}) %collective-permute-start.1) | collective-permute-done | bytes 2080 | tf_op jit(solution)/shard_map/ppermute | solution.py:449
  13.4 6.3 %own_pass.1 = (bf16[24,128,96]{2,1,0:T(8,128)(2,1)S(1)}, f32[960,128]{1,0:T(8,128)S(1)}) custom-call(f32[192,128]{1,0:T(8,128)S(1)} %bitcast.13, f32[24,128]{1,0:T(8,128)S(1)} %copy-done.1, f32[4,128]{1,0:T(4,128)S(1)} %collective-permute-done.edge0_ref, f32[4,128]{1,0:T(4,128)S(1)} %collective-permute-done.1.edge1_ref, s32[24,4]{1,0:T(8,128)S(1)} %copy.9.wpair_ref, ...), custom_call_target="tpu_custom_call" | custom-call | flops 1572864000 | tf_op jit(solution)/shard_map/own_pass/pallas_call | solution.py:351
  19.7 0.0 all-to-all-done
  19.7 20.7 %fluid_pass.1 = (f32[24,128]{1,0:T(8,128)}, f32[3,3072]{1,0:T(4,128)}, f32[8,128]{1,0:T(8,128)S(1)}) custom-call(f32[192,128]{1,0:T(8,128)S(1)} %bitcast.14, f32[384,128]{1,0:T(8,128)S(1)} %bitcast.11, s32[24,14]{1,0:T(8,128)S(1)} %copy.10.pair_ref, s32[1]{0:T(128)} %bitcast.5.place_ref, bf16[24,128,96]{2,1,0:T(8,128)(2,1)S(1)} %get-tuple-element.16.tgt, ...), custom_call_target="tpu_custom_call" | custom-call | flops 5505024000 | tf_op jit(solution)/shard_map/fluid_pass/pallas_call | solution.py:369
  40.4 0.2 collective-permute-start.2
  40.6 1.0 %collective-permute-done.2 = f32[8,128]{1,0:T(8,128)S(1)} collective-permute-done((f32[8,128]{1,0:T(8,128)S(1)}, f32[8,128]{1,0:T(8,128)S(1)}, u32[]{:S(2)}, u32[]{:S(2)}) %collective-permute-start.2) | collective-permute-done | bytes 4128 | tf_op jit(solution)/shard_map/ppermute | solution.py:430
  41.5 1.3 %collective-permute-start.3 = (f32[8,128]{1,0:T(8,128)S(1)}, f32[8,128]{1,0:T(8,128)S(1)}, u32[]{:S(2)}, u32[]{:S(2)}) collective-permute-start(f32[8,128]{1,0:T(8,128)S(1)} %max.15), channel_id=1, source_target_pairs={{0,3},{1,2},{2,1},{3,0},{4,7},{5,6},{6,5},{7,4},{8,11},{9,10},{10,... | collective-permute-start | bytes 12296 | tf_op jit(solution)/shard_map/ppermute | solution.py:430
  42.8 1.7 %collective-permute-done.3 = f32[8,128]{1,0:T(8,128)S(1)} collective-permute-done((f32[8,128]{1,0:T(8,128)S(1)}, f32[8,128]{1,0:T(8,128)S(1)}, u32[]{:S(2)}, u32[]{:S(2)}) %collective-permute-start.3) | collective-permute-done | bytes 4128 | tf_op jit(solution)/shard_map/ppermute | solution.py:430
  44.6 1.8 %collective-permute-start.4 = (f32[8,128]{1,0:T(8,128)S(1)}, f32[8,128]{1,0:T(8,128)S(1)}, u32[]{:S(2)}, u32[]{:S(2)}) collective-permute-start(f32[8,128]{1,0:T(8,128)S(1)} %max.16), channel_id=1, source_target_pairs={{0,5},{1,4},{2,7},{3,6},{4,1},{5,0},{6,3},{7,2},{8,13},{9,12},{10,... | collective-permute-start | bytes 12296 | tf_op jit(solution)/shard_map/ppermute | solution.py:430
  46.4 1.3 %collective-permute-done.4 = f32[8,128]{1,0:T(8,128)S(1)} collective-permute-done((f32[8,128]{1,0:T(8,128)S(1)}, f32[8,128]{1,0:T(8,128)S(1)}, u32[]{:S(2)}, u32[]{:S(2)}) %collective-permute-start.4) | collective-permute-done | bytes 4128 | tf_op jit(solution)/shard_map/ppermute | solution.py:430
  47.7 1.8 %collective-permute-start.5 = (f32[8,128]{1,0:T(8,128)S(1)}, f32[8,128]{1,0:T(8,128)S(1)}, u32[]{:S(2)}, u32[]{:S(2)}) collective-permute-start(f32[8,128]{1,0:T(8,128)S(1)} %max.17), channel_id=1, source_target_pairs={{0,9},{1,8},{2,11},{3,10},{4,13},{5,12},{6,15},{7,14},{8,1},{9,0},... | collective-permute-start | bytes 12296 | tf_op jit(solution)/shard_map/ppermute | solution.py:430
  49.5 1.3 %collective-permute-done.5 = f32[8,128]{1,0:T(8,128)S(1)} collective-permute-done((f32[8,128]{1,0:T(8,128)S(1)}, f32[8,128]{1,0:T(8,128)S(1)}, u32[]{:S(2)}, u32[]{:S(2)}) %collective-permute-start.5) | collective-permute-done | bytes 4128 | tf_op jit(solution)/shard_map/ppermute | solution.py:430
  50.8 2.5 %collective-permute-start.6 = (f32[8,128]{1,0:T(8,128)S(1)}, f32[8,128]{1,0:T(8,128)S(1)}, u32[]{:S(2)}, u32[]{:S(2)}) collective-permute-start(f32[8,128]{1,0:T(8,128)S(1)} %max.18), channel_id=1, source_target_pairs={{0,17},{1,16},{2,19},{3,18},{4,21},{5,20},{6,23},{7,22},{8,25},{9,... | collective-permute-start | bytes 12296 | tf_op jit(solution)/shard_map/ppermute | solution.py:430
  53.3 1.4 %collective-permute-done.6 = f32[8,128]{1,0:T(8,128)S(1)} collective-permute-done((f32[8,128]{1,0:T(8,128)S(1)}, f32[8,128]{1,0:T(8,128)S(1)}, u32[]{:S(2)}, u32[]{:S(2)}) %collective-permute-start.6) | collective-permute-done | bytes 4128 | tf_op jit(solution)/shard_map/ppermute | solution.py:430
  54.7 0.5 slice.3
  (15 shorter events, 0.0 us)
Async XLA Ops:
  2.3 7.4 %copy-start.5 = (f32[4,128]{1,0:T(4,128)S(1)}, f32[4,128]{1,0:T(4,128)}, u32[]{:S(2)}) copy-start(f32[4,128]{1,0:T(4,128)} %get-tuple-element.14) | copy-start | bytes 6148
  2.3 9.1 %copy-start.2 = (s32[24,14]{0,1:T(8,128)S(1)}, s32[24,14]{0,1:T(8,128)}, u32[]{:S(2)}) copy-start(s32[24,14]{0,1:T(8,128)} %param.8) | copy-start | bytes 4036
  2.3 11.1 %copy-start = (f32[8,3072]{1,0:T(8,128)S(1)}, f32[8,3072]{1,0:T(8,128)}, u32[]{:S(2)}) copy-start(f32[8,3072]{1,0:T(8,128)} %param.6) | copy-start | bytes 294916
  2.3 17.4 %all-to-all-start = ((f32[8,48,128]{2,1,0:T(8,128)}), f32[8,48,128]{2,1,0:T(8,128)S(1)}, u32[]{:S(2)}, u32[]{:S(2)}) async-start(f32[8,48,128]{2,1,0:T(8,128)} %bitcast.15), calls=%async_computation | async-start | bytes 393216 | tf_op jit(solution)/shard_map/all_to_all | solution.py:461
  9.7 0.7 %copy-start.4 = (f32[4,128]{1,0:T(4,128)S(1)}, f32[4,128]{1,0:T(4,128)}, u32[]{:S(2)}) copy-start(f32[4,128]{1,0:T(4,128)} %get-tuple-element.15) | copy-start | bytes 6148
  9.7 1.9 %collective-permute-start = (f32[4,128]{1,0:T(4,128)S(1)}, f32[4,128]{1,0:T(4,128)S(1)}, u32[]{:S(2)}, u32[]{:S(2)}) collective-permute-start(f32[4,128]{1,0:T(4,128)S(1)} %copy-done.5), channel_id=1, source_target_pairs={{0,1},{2,3},{1,0},{3,2},{4,5},{6,7},{5,4},{7,6},{8,9},{10,11},{9,8... | collective-permute-start | bytes 6152 | tf_op jit(solution)/shard_map/ppermute | solution.py:449
  10.4 1.1 %copy-start.3 = (s32[24,4]{0,1:T(4,128)S(1)}, s32[24,4]{0,1:T(4,128)}, u32[]{:S(2)}) copy-start(s32[24,4]{0,1:T(4,128)} %param.11) | copy-start | bytes 1156
  10.4 3.0 %collective-permute-start.1 = (f32[4,128]{1,0:T(4,128)S(1)}, f32[4,128]{1,0:T(4,128)S(1)}, u32[]{:S(2)}, u32[]{:S(2)}) collective-permute-start(f32[4,128]{1,0:T(4,128)S(1)} %copy-done.4), channel_id=1, source_target_pairs={{1,2},{3,0},{2,1},{0,3},{5,6},{7,4},{6,5},{4,7},{9,10},{11,8},{10,... | collective-permute-start | bytes 6152 | tf_op jit(solution)/shard_map/ppermute | solution.py:449
  11.5 1.9 %copy-start.1 = (f32[24,128]{1,0:T(8,128)S(1)}, f32[24,128]{1,0:T(8,128)}, u32[]{:S(2)}) copy-start(f32[24,128]{1,0:T(8,128)} %get-tuple-element.13.wall_ref) | copy-start | bytes 36868
  40.4 1.2 %collective-permute-start.2 = (f32[8,128]{1,0:T(8,128)S(1)}, f32[8,128]{1,0:T(8,128)S(1)}, u32[]{:S(2)}, u32[]{:S(2)}) collective-permute-start(f32[8,128]{1,0:T(8,128)S(1)} %get-tuple-element.20), channel_id=1, source_target_pairs={{0,1},{1,0},{2,3},{3,2},{4,5},{5,4},{6,7},{7,6},{8,9},{9,8},{10,11... | collective-permute-start | bytes 12296 | tf_op jit(solution)/shard_map/ppermute | solution.py:430
  41.5 3.0 %collective-permute-start.3 = (f32[8,128]{1,0:T(8,128)S(1)}, f32[8,128]{1,0:T(8,128)S(1)}, u32[]{:S(2)}, u32[]{:S(2)}) collective-permute-start(f32[8,128]{1,0:T(8,128)S(1)} %max.15), channel_id=1, source_target_pairs={{0,3},{1,2},{2,1},{3,0},{4,7},{5,6},{6,5},{7,4},{8,11},{9,10},{10,... | collective-permute-start | bytes 12296 | tf_op jit(solution)/shard_map/ppermute | solution.py:430
  44.6 3.1 %collective-permute-start.4 = (f32[8,128]{1,0:T(8,128)S(1)}, f32[8,128]{1,0:T(8,128)S(1)}, u32[]{:S(2)}, u32[]{:S(2)}) collective-permute-start(f32[8,128]{1,0:T(8,128)S(1)} %max.16), channel_id=1, source_target_pairs={{0,5},{1,4},{2,7},{3,6},{4,1},{5,0},{6,3},{7,2},{8,13},{9,12},{10,... | collective-permute-start | bytes 12296 | tf_op jit(solution)/shard_map/ppermute | solution.py:430
  47.7 3.1 %collective-permute-start.5 = (f32[8,128]{1,0:T(8,128)S(1)}, f32[8,128]{1,0:T(8,128)S(1)}, u32[]{:S(2)}, u32[]{:S(2)}) collective-permute-start(f32[8,128]{1,0:T(8,128)S(1)} %max.17), channel_id=1, source_target_pairs={{0,9},{1,8},{2,11},{3,10},{4,13},{5,12},{6,15},{7,14},{8,1},{9,0},... | collective-permute-start | bytes 12296 | tf_op jit(solution)/shard_map/ppermute | solution.py:430
  50.8 3.9 %collective-permute-start.6 = (f32[8,128]{1,0:T(8,128)S(1)}, f32[8,128]{1,0:T(8,128)S(1)}, u32[]{:S(2)}, u32[]{:S(2)}) collective-permute-start(f32[8,128]{1,0:T(8,128)S(1)} %max.18), channel_id=1, source_target_pairs={{0,17},{1,16},{2,19},{3,18},{4,21},{5,20},{6,23},{7,22},{8,25},{9,... | collective-permute-start | bytes 12296 | tf_op jit(solution)/shard_map/ppermute | solution.py:430

commit v13 on v12

--- a/solution.py
+++ b/solution.py
@@ -211,17 +211,16 @@
     return pl.ds(pl.multiple_of(b * SUMS, ROWS), SUMS)
 
 
-def own_kernel(
-    own_ref, wall_ref, edge0_ref, edge1_ref, wpair_ref, along_ref,
-    tgt, sums, wsrc, table,
-):
-    blocks = tgt.shape[0]
-
+def target_kernel(own_ref, tgt):
     def build(b, carry):
         put_target(state_of(own_ref[rows_at(b), :]), b, tgt)
         return carry
 
-    lax.fori_loop(0, blocks, build, 0, unroll=UNROLL)
+    lax.fori_loop(0, tgt.shape[0], build, 0, unroll=UNROLL)
+
+
+def wall_kernel(tgt, wall_ref, edge0_ref, edge1_ref, wpair_ref, along_ref, sums, wsrc, table):
+    blocks = tgt.shape[0]
     row = row_index()
     count = 0
     for ref in (wall_ref, edge0_ref, edge1_ref):
@@ -328,6 +327,7 @@
 
 SMEM = pl.BlockSpec(memory_space=pltpu.SMEM)
 VMEM = pl.BlockSpec(memory_space=pltpu.VMEM)
+ANY = pl.BlockSpec(memory_space=pl.ANY)
 PARAMS = pltpu.CompilerParams(vmem_limit_bytes=18 * 1024 * 1024)
 
 
@@ -341,26 +341,35 @@
     return (count, DEPTH + 2 * ROWS, VALUES * LANES), jnp.bfloat16
 
 
-def own_pass(own, walls, edges, wall_pairs, along):
+def target_pass(own):
     blocks = own.shape[0] // ROWS
+    return pl.pallas_call(
+        target_kernel,
+        out_shape=jax.ShapeDtypeStruct((blocks, LANES, DEPTH), jnp.bfloat16),
+        in_specs=[VMEM],
+        out_specs=VMEM,
+        compiler_params=PARAMS,
+        cost_estimate=tile_cost(blocks),
+        name="target_pass",
+    )(own)
+
+
+def wall_pass(tgt, walls, edges, wall_pairs, along):
+    blocks = tgt.shape[0]
     wall_blocks = (walls.shape[0] + 2 * edges[0].shape[0]) // 4
-    outs = [
-        ((blocks, LANES, DEPTH), jnp.bfloat16),
-        ((blocks * SUMS, LANES), jnp.float32),
-    ]
     return pl.pallas_call(
-        own_kernel,
-        out_shape=[jax.ShapeDtypeStruct(*out) for out in outs],
+        wall_kernel,
+        out_shape=jax.ShapeDtypeStruct((blocks * SUMS, LANES), jnp.float32),
         in_specs=[VMEM, VMEM, VMEM, VMEM, SMEM, SMEM],
-        out_specs=[VMEM] * len(outs),
+        out_specs=VMEM,
         scratch_shapes=[
             pltpu.VMEM(*source_shape(wall_blocks)),
             pltpu.SMEM((wall_blocks,), jnp.int32),
         ],
         compiler_params=PARAMS,
         cost_estimate=tile_cost(wall_pairs.size),
-        name="own_pass",
-    )(own, walls, *edges, wall_pairs, along)
+        name="wall_pass",
+    )(tgt, walls, *edges, wall_pairs, along)
 
 
 def fluid_pass(own, ghosts, pair_list, place, own_results):
@@ -390,14 +399,17 @@
 
 def outgoing_kernel(
     row_length, own_ref, list_ref, place_ref, wall_ref, count_ref, along_ref,
-    sent_ref, live_ref, edge0_ref, edge1_ref,
+    sent_ref, live_ref, edge0_ref, edge1_ref, copied,
 ):
+    copies = []
     for slot in range(8):
         mask = jnp.bitwise_xor(place_ref[0], slot)
         for g in range(list_ref.shape[1]):
             block = list_ref[jnp.maximum(mask - 1, 0), g]
-            first = (slot * list_ref.shape[1] + g) * ROWS
-            sent_ref[first : first + ROWS, :] = own_ref[rows_at(block), :]
+            n = slot * list_ref.shape[1] + g
+            target = sent_ref.at[n * ROWS : (n + 1) * ROWS, :]
+            copies.append(pltpu.make_async_copy(own_ref.at[rows_at(block), :], target, copied.at[n]))
+            copies[-1].start()
     lane = lax.broadcasted_iota(jnp.int32, (4, LANES), 1)
     row = lax.broadcasted_iota(jnp.int32, (4, LANES), 0)
     for c in range(wall_ref.shape[1] // LANES):
@@ -411,6 +423,8 @@
     end = row_length - row_length % 2 - 1
     inside = jnp.where((along == 0) | (along == end), 0.0, 1.0)
     edge1_ref[...] = jnp.where(along % 2 == 0, first, last) * inside
+    for copy in copies:
+        copy.wait()
 
 
 def outgoing_pass(own, ghost_list, place, wall_state, wall_count, along):
@@ -419,8 +433,9 @@
     return pl.pallas_call(
         functools.partial(outgoing_kernel, lax.axis_size("wall")),
         out_shape=[jax.ShapeDtypeStruct((row, LANES), jnp.float32) for row in rows],
-        in_specs=[VMEM, SMEM, SMEM, VMEM, SMEM, SMEM],
-        out_specs=[VMEM] * len(rows),
+        in_specs=[ANY, SMEM, SMEM, VMEM, SMEM, SMEM],
+        out_specs=[ANY] + [VMEM] * (len(rows) - 1),
+        scratch_shapes=[pltpu.SemaphoreType.DMA((8 * ghost_list.shape[1],))],
         name="outgoing_pass",
     )(own, ghost_list, place, wall_state, wall_count, along)
 
@@ -465,11 +480,12 @@
         0,
         axis_index_groups=groups if len(groups) > 1 else None,
     )
-    own_results = own_pass(own, walls, edges, wall_pairs, along)
+    tgt = target_pass(own)
+    own_results = (tgt, wall_pass(tgt, walls, edges, wall_pairs, along))
     rate, acceleration, local_peak = fluid_pass(
         own, landed.reshape(-1, LANES), pair_list, place, own_results
     )
-    peak = largest(local_peak, "orb", "wall")[0, 0]
+    peak = jnp.max(largest(local_peak, "orb", "wall"))
     time_step = courant * jnp.sqrt(smoothing / (peak + 1e-06))
     return (rate.reshape(-1), acceleration, time_step)
 

time: 57.4 us -> 64.7 us (1.13)
  Pallas kernels: 28.6 us -> 35.9 us
  waiting for transfers between devices: 8.55 us -> 7.34 us
    pallas_call x1, Pallas kernels: 1.65 us -> 8.97 us  [outgoing_pass(): pl.pallas_call(functools.partial(outgoing_kernel, lax.axis_size('wall')),...]
    ppermute x2, waiting for transfers between devices: 1.78 us -> 0.6 us  [facing(): landed.append(lax.ppermute(sent, axis, pairs + [(j, i) for i, j in pairs]))]
    pallas_call x1 -> x2, Pallas kernels: 6.28 us -> 6.38 us  [the longest x1 5.82 us: wall_pass(): pl.pallas_call(wall_kernel, out_shape=jax.ShapeDtypeStruct((blocks * SUMS...]
  transfers between devices with their start and end apart: 8 -> 8, of which waited for: 6 -> 6; matrix products, arithmetic and copies ran while one was open for 0% -> 0% of each run, Pallas kernels for 11% -> 10%
where the time goes in v13:
time: 64.7 us; the launch traced here: 64.3 us
  Pallas kernels  35.9 us (55%)
  starting transfers between devices  16.5 us (26%)
  waiting for transfers between devices  7.34 us (11%)
  between operations  2.59 us (4%)
  local copies, waits for them, and re-layouts  1.37 us (2%)
    pallas_call x1, Pallas kernels, fluid_pass(): pl.pallas_call(fluid_kernel, out_shape=(jax.ShapeDtypeStruct((blocks, LAN...  20.6 us
    pallas_call x1, Pallas kernels, outgoing_pass(): pl.pallas_call(functools.partial(outgoing_kernel, lax.axis_size('wall')),...  8.97 us
    ppermute x5, starting transfers between devices, swapped(): return lax.ppermute(shard, axis, [(i, i ^ mask) for i in range(count)])  7.98 us
    all_to_all x1, starting transfers between devices, per_device(): lax.all_to_all(sent.reshape(8, -1, LANES), 'orb', 0, 0, axis_index_groups...  7.4 us
    ppermute x5, waiting for transfers between devices, swapped(): return lax.ppermute(shard, axis, [(i, i ^ mask) for i in range(count)])  6.73 us
    pallas_call x1, Pallas kernels, wall_pass(): pl.pallas_call(wall_kernel, out_shape=jax.ShapeDtypeStruct((blocks * SUMS...  5.82 us
    unnamed x14, local copies, waits for them, and re-layouts  1.37 us
  transfers between devices with their start and end apart: 8, of which 6 were waited for; matrix products, arithmetic and copies ran while one was open for 0% of the time, Pallas kernels for 10%

profile of v13, /device:TPU:0, one launch (start us, length us, event | category | flops | bytes accessed | tf_op | source)
XLA Modules:
  0.0 64.3 jit_solution(6092615119642686764)
XLA Ops:
  0.6 9.0 %outgoing_pass.1 = (f32[384,128]{1,0:T(8,128)}, f32[24,128]{1,0:T(8,128)}, f32[4,128]{1,0:T(4,128)}, f32[4,128]{1,0:T(4,128)}) custom-call(f32[192,128]{1,0:T(8,128)} %bitcast.11, s32[7,6]{1,0:T(8,128)} %list_ref.1, s32[1]{0:T(128)} %bitcast.5.place_ref, f32[4,768]{1,0:T(4,128)} %wall_ref.1, s32[6]{0:T(128)} %count_ref.1, s32[1]{0:T(128)} %bitcast.6.along_ref), custom_call_target="tpu_custom_call" | custom-call | tf_op jit(solution)/shard_map/outgoing_pass/pallas_call | solution.py:433
  9.6 7.4 %all-to-all-start = ((f32[8,48,128]{2,1,0:T(8,128)}), f32[8,48,128]{2,1,0:T(8,128)S(1)}, u32[]{:S(2)}, u32[]{:S(2)}) async-start(f32[8,48,128]{2,1,0:T(8,128)} %bitcast.14), calls=%async_computation | async-start | bytes 393216 | tf_op jit(solution)/shard_map/all_to_all | solution.py:476
  17.1 0.1 collective-permute-start
  17.1 0.6 copy-done.4
  17.7 1.1 %collective-permute-start.1 = (f32[4,128]{1,0:T(4,128)S(1)}, f32[4,128]{1,0:T(4,128)S(1)}, u32[]{:S(2)}, u32[]{:S(2)}) collective-permute-start(f32[4,128]{1,0:T(4,128)S(1)} %copy-done.4), channel_id=1, source_target_pairs={{1,2},{3,0},{2,1},{0,3},{5,6},{7,4},{6,5},{4,7},{9,10},{11,8},{10,... | collective-permute-start | bytes 6152 | tf_op jit(solution)/shard_map/ppermute | solution.py:464
  18.8 0.6 target_pass.1.tgt
  19.4 0.1 copy.10.pair_ref
  19.4 0.6 copy-done.3
  20.0 0.1 copy.9.wpair_ref
  20.1 0.6 collective-permute-done.1.edge1_ref
  20.7 0.0 copy-done.1
  20.7 5.8 %wall_pass.1.own_sums = f32[960,128]{1,0:T(8,128)S(1)} custom-call(bf16[24,128,96]{2,1,0:T(8,128)(2,1)S(1)} %target_pass.1.tgt, f32[24,128]{1,0:T(8,128)S(1)} %copy-done.1, f32[4,128]{1,0:T(4,128)S(1)} %collective-permute-done.edge0_ref, f32[4,128]{1,0:T(4,128)S(1)} %collective-permute-done.1.edge1_ref, s32[24,4]{1,0:T(8,128)S(1)} %copy.9.wpair_ref, ...), custom_call_target="tpu_custom_call" | custom-call | flops 1572864000 | tf_op jit(solution)/shard_map/wall_pass/pallas_call | solution.py:360
  26.6 20.6 %fluid_pass.1 = (f32[24,128]{1,0:T(8,128)}, f32[3,3072]{1,0:T(4,128)}, f32[8,128]{1,0:T(8,128)S(1)}) custom-call(f32[192,128]{1,0:T(8,128)S(1)} %bitcast.13, f32[384,128]{1,0:T(8,128)S(1)} %bitcast.10, s32[24,14]{1,0:T(8,128)S(1)} %copy.10.pair_ref, s32[1]{0:T(128)} %bitcast.5.place_ref, bf16[24,128,96]{2,1,0:T(8,128)(2,1)S(1)} %target_pass.1.tgt, ...), custom_call_target="tpu_custom_call" | custom-call | flops 5505024000 | tf_op jit(solution)/shard_map/fluid_pass/pallas_call | solution.py:378
  47.1 0.6 collective-permute-start.2
  47.7 0.8 %collective-permute-done.2 = f32[8,128]{1,0:T(8,128)S(1)} collective-permute-done((f32[8,128]{1,0:T(8,128)S(1)}, f32[8,128]{1,0:T(8,128)S(1)}, u32[]{:S(2)}, u32[]{:S(2)}) %collective-permute-start.2) | collective-permute-done | bytes 4128 | tf_op jit(solution)/shard_map/ppermute | solution.py:445
  48.6 1.1 %collective-permute-start.3 = (f32[8,128]{1,0:T(8,128)S(1)}, f32[8,128]{1,0:T(8,128)S(1)}, u32[]{:S(2)}, u32[]{:S(2)}) collective-permute-start(f32[8,128]{1,0:T(8,128)S(1)} %max.15), channel_id=1, source_target_pairs={{0,3},{1,2},{2,1},{3,0},{4,7},{5,6},{6,5},{7,4},{8,11},{9,10},{10,... | collective-permute-start | bytes 12296 | tf_op jit(solution)/shard_map/ppermute | solution.py:445
  49.7 1.9 %collective-permute-done.3 = f32[8,128]{1,0:T(8,128)S(1)} collective-permute-done((f32[8,128]{1,0:T(8,128)S(1)}, f32[8,128]{1,0:T(8,128)S(1)}, u32[]{:S(2)}, u32[]{:S(2)}) %collective-permute-start.3) | collective-permute-done | bytes 4128 | tf_op jit(solution)/shard_map/ppermute | solution.py:445
  51.6 1.9 %collective-permute-start.4 = (f32[8,128]{1,0:T(8,128)S(1)}, f32[8,128]{1,0:T(8,128)S(1)}, u32[]{:S(2)}, u32[]{:S(2)}) collective-permute-start(f32[8,128]{1,0:T(8,128)S(1)} %max.16), channel_id=1, source_target_pairs={{0,5},{1,4},{2,7},{3,6},{4,1},{5,0},{6,3},{7,2},{8,13},{9,12},{10,... | collective-permute-start | bytes 12296 | tf_op jit(solution)/shard_map/ppermute | solution.py:445
  53.5 1.3 %collective-permute-done.4 = f32[8,128]{1,0:T(8,128)S(1)} collective-permute-done((f32[8,128]{1,0:T(8,128)S(1)}, f32[8,128]{1,0:T(8,128)S(1)}, u32[]{:S(2)}, u32[]{:S(2)}) %collective-permute-start.4) | collective-permute-done | bytes 4128 | tf_op jit(solution)/shard_map/ppermute | solution.py:445
  54.8 1.8 %collective-permute-start.5 = (f32[8,128]{1,0:T(8,128)S(1)}, f32[8,128]{1,0:T(8,128)S(1)}, u32[]{:S(2)}, u32[]{:S(2)}) collective-permute-start(f32[8,128]{1,0:T(8,128)S(1)} %max.17), channel_id=1, source_target_pairs={{0,9},{1,8},{2,11},{3,10},{4,13},{5,12},{6,15},{7,14},{8,1},{9,0},... | collective-permute-start | bytes 12296 | tf_op jit(solution)/shard_map/ppermute | solution.py:445
  56.6 1.3 %collective-permute-done.5 = f32[8,128]{1,0:T(8,128)S(1)} collective-permute-done((f32[8,128]{1,0:T(8,128)S(1)}, f32[8,128]{1,0:T(8,128)S(1)}, u32[]{:S(2)}, u32[]{:S(2)}) %collective-permute-start.5) | collective-permute-done | bytes 4128 | tf_op jit(solution)/shard_map/ppermute | solution.py:445
  57.9 2.6 %collective-permute-start.6 = (f32[8,128]{1,0:T(8,128)S(1)}, f32[8,128]{1,0:T(8,128)S(1)}, u32[]{:S(2)}, u32[]{:S(2)}) collective-permute-start(f32[8,128]{1,0:T(8,128)S(1)} %max.18), channel_id=1, source_target_pairs={{0,17},{1,16},{2,19},{3,18},{4,21},{5,20},{6,23},{7,22},{8,25},{9,... | collective-permute-start | bytes 12296 | tf_op jit(solution)/shard_map/ppermute | solution.py:445
  60.5 1.3 %collective-permute-done.6 = f32[8,128]{1,0:T(8,128)S(1)} collective-permute-done((f32[8,128]{1,0:T(8,128)S(1)}, f32[8,128]{1,0:T(8,128)S(1)}, u32[]{:S(2)}, u32[]{:S(2)}) %collective-permute-start.6) | collective-permute-done | bytes 4128 | tf_op jit(solution)/shard_map/ppermute | solution.py:445
  61.9 0.6 maximum_reduce_fusion
  (15 shorter events, 0.0 us)
Async XLA Ops:
  9.6 7.4 %copy-start.5 = (f32[4,128]{1,0:T(4,128)S(1)}, f32[4,128]{1,0:T(4,128)}, u32[]{:S(2)}) copy-start(f32[4,128]{1,0:T(4,128)} %get-tuple-element.12) | copy-start | bytes 6148
  9.6 9.1 %copy-start = (f32[8,3072]{1,0:T(8,128)S(1)}, f32[8,3072]{1,0:T(8,128)}, u32[]{:S(2)}) copy-start(f32[8,3072]{1,0:T(8,128)} %param.6) | copy-start | bytes 294916
  9.6 16.9 %all-to-all-start = ((f32[8,48,128]{2,1,0:T(8,128)}), f32[8,48,128]{2,1,0:T(8,128)S(1)}, u32[]{:S(2)}, u32[]{:S(2)}) async-start(f32[8,48,128]{2,1,0:T(8,128)} %bitcast.14), calls=%async_computation | async-start | bytes 393216 | tf_op jit(solution)/shard_map/all_to_all | solution.py:476
  17.0 0.7 %copy-start.4 = (f32[4,128]{1,0:T(4,128)S(1)}, f32[4,128]{1,0:T(4,128)}, u32[]{:S(2)}) copy-start(f32[4,128]{1,0:T(4,128)} %get-tuple-element.13) | copy-start | bytes 6148
  17.1 3.1 %collective-permute-start = (f32[4,128]{1,0:T(4,128)S(1)}, f32[4,128]{1,0:T(4,128)S(1)}, u32[]{:S(2)}, u32[]{:S(2)}) collective-permute-start(f32[4,128]{1,0:T(4,128)S(1)} %copy-done.5), channel_id=1, source_target_pairs={{0,1},{2,3},{1,0},{3,2},{4,5},{6,7},{5,4},{7,6},{8,9},{10,11},{9,8... | collective-permute-start | bytes 6152 | tf_op jit(solution)/shard_map/ppermute | solution.py:464
  17.7 1.6 %copy-start.2 = (s32[24,14]{0,1:T(8,128)S(1)}, s32[24,14]{0,1:T(8,128)}, u32[]{:S(2)}) copy-start(s32[24,14]{0,1:T(8,128)} %param.8) | copy-start | bytes 4036
  17.7 3.0 %collective-permute-start.1 = (f32[4,128]{1,0:T(4,128)S(1)}, f32[4,128]{1,0:T(4,128)S(1)}, u32[]{:S(2)}, u32[]{:S(2)}) collective-permute-start(f32[4,128]{1,0:T(4,128)S(1)} %copy-done.4), channel_id=1, source_target_pairs={{1,2},{3,0},{2,1},{0,3},{5,6},{7,4},{6,5},{4,7},{9,10},{11,8},{10,... | collective-permute-start | bytes 6152 | tf_op jit(solution)/shard_map/ppermute | solution.py:464
  19.3 0.7 %copy-start.3 = (s32[24,4]{0,1:T(4,128)S(1)}, s32[24,4]{0,1:T(4,128)}, u32[]{:S(2)}) copy-start(s32[24,4]{0,1:T(4,128)} %param.11) | copy-start | bytes 1156
  20.0 0.7 %copy-start.1 = (f32[24,128]{1,0:T(8,128)S(1)}, f32[24,128]{1,0:T(8,128)}, u32[]{:S(2)}) copy-start(f32[24,128]{1,0:T(8,128)} %get-tuple-element.11.wall_ref) | copy-start | bytes 36868
  47.1 1.4 %collective-permute-start.2 = (f32[8,128]{1,0:T(8,128)S(1)}, f32[8,128]{1,0:T(8,128)S(1)}, u32[]{:S(2)}, u32[]{:S(2)}) collective-permute-start(f32[8,128]{1,0:T(8,128)S(1)} %get-tuple-element.16), channel_id=1, source_target_pairs={{0,1},{1,0},{2,3},{3,2},{4,5},{5,4},{6,7},{7,6},{8,9},{9,8},{10,11... | collective-permute-start | bytes 12296 | tf_op jit(solution)/shard_map/ppermute | solution.py:445
  48.6 3.0 %collective-permute-start.3 = (f32[8,128]{1,0:T(8,128)S(1)}, f32[8,128]{1,0:T(8,128)S(1)}, u32[]{:S(2)}, u32[]{:S(2)}) collective-permute-start(f32[8,128]{1,0:T(8,128)S(1)} %max.15), channel_id=1, source_target_pairs={{0,3},{1,2},{2,1},{3,0},{4,7},{5,6},{6,5},{7,4},{8,11},{9,10},{10,... | collective-permute-start | bytes 12296 | tf_op jit(solution)/shard_map/ppermute | solution.py:445
  51.6 3.3 %collective-permute-start.4 = (f32[8,128]{1,0:T(8,128)S(1)}, f32[8,128]{1,0:T(8,128)S(1)}, u32[]{:S(2)}, u32[]{:S(2)}) collective-permute-start(f32[8,128]{1,0:T(8,128)S(1)} %max.16), channel_id=1, source_target_pairs={{0,5},{1,4},{2,7},{3,6},{4,1},{5,0},{6,3},{7,2},{8,13},{9,12},{10,... | collective-permute-start | bytes 12296 | tf_op jit(solution)/shard_map/ppermute | solution.py:445
  54.8 3.1 %collective-permute-start.5 = (f32[8,128]{1,0:T(8,128)S(1)}, f32[8,128]{1,0:T(8,128)S(1)}, u32[]{:S(2)}, u32[]{:S(2)}) collective-permute-start(f32[8,128]{1,0:T(8,128)S(1)} %max.17), channel_id=1, source_target_pairs={{0,9},{1,8},{2,11},{3,10},{4,13},{5,12},{6,15},{7,14},{8,1},{9,0},... | collective-permute-start | bytes 12296 | tf_op jit(solution)/shard_map/ppermute | solution.py:445
  57.9 3.9 %collective-permute-start.6 = (f32[8,128]{1,0:T(8,128)S(1)}, f32[8,128]{1,0:T(8,128)S(1)}, u32[]{:S(2)}, u32[]{:S(2)}) collective-permute-start(f32[8,128]{1,0:T(8,128)S(1)} %max.18), channel_id=1, source_target_pairs={{0,17},{1,16},{2,19},{3,18},{4,21},{5,20},{6,23},{7,22},{8,25},{9,... | collective-permute-start | bytes 12296 | tf_op jit(solution)/shard_map/ppermute | solution.py:445

commit v14 on v12

--- a/solution.py
+++ b/solution.py
@@ -96,18 +96,16 @@
     turned = jnp.where(row < 3, pltpu.roll(y, 5, axis=0), pltpu.roll(y, 3, axis=0))
     along = m * jnp.where(row < 6, turned, chosen(0.0, (7, -1.0))), chosen(0.0, (6, -m * e))
     if wall:
-        press_part = chosen(0.0, (5, 2.0 * cohesion / adhesion), (6, -0.75))
-        return near, along, (None, press_part)
+        return near, along
     return near, along, (m * r * near[0], m * chosen(minus, (3, n), (4, 1.0), (6, r * n)))
 
 
 def put_source(block, s, src, press=None, mass_factor=1.0):
     state = state_of(block)
     for n, (first, second) in enumerate(source_groups(state, press is None)):
-        firsts = split(first) if first is not None else [jnp.zeros((ROWS, LANES))] * 3
         pieces = [
             jnp.concatenate(pair, axis=0).astype(jnp.bfloat16)
-            for pair in zip(firsts, split(second))
+            for pair in zip(split(first), split(second))
         ]
         lanes = slice(n * LANES, (n + 1) * LANES)
         for k, (_, piece) in enumerate(SPLITS):
@@ -121,13 +119,15 @@
         press[s] = state[5]
 
 
-def put_target(state, b, tgt):
+def put_target(state, b, choice, tgt, wide):
     pieces = [jnp.concatenate(pair, axis=0) for pair in zip(*map(split, target_groups(state)))]
     rows = jnp.concatenate([pieces[piece] for piece, _ in SPLITS], axis=0).astype(jnp.bfloat16)
     row = lax.broadcasted_iota(jnp.int32, (LANES, LANES), 0)
     lane = lax.broadcasted_iota(jnp.int32, (LANES, LANES), 1)
     unit = jnp.where(row == lane, 1.0, 0.0).astype(jnp.bfloat16)
-    tgt[b] = across(unit, rows).astype(jnp.bfloat16)
+    features = across(unit, rows).astype(jnp.bfloat16)
+    tgt[b] = features
+    wide[b] = jnp.dot(features, choice, preferred_element_type=jnp.float32)
 
 
 def press_choice():
@@ -144,20 +144,18 @@
 
 
 def weights_of(product, press_i, press_j):
-    near, approach, last = [product[:, n * LANES : (n + 1) * LANES] for n in range(VALUES)]
-    guarded = jnp.maximum(near, 1e-30)
+    values = [product[:, first : first + LANES] for first in range(0, product.shape[1], LANES)]
+    guarded = jnp.maximum(values[0], 1e-30)
     falloff = jnp.maximum(1.0 - guarded * lax.rsqrt(guarded), 0.0)
     cubed = falloff * falloff * falloff
-    if press_j is None:
-        blend = falloff + last
-    else:
-        blend = falloff + press_i
+    blend = falloff + press_i
+    if press_j is not None:
         blend += jnp.concatenate([press_j[...]] * (LANES // ROWS), axis=0)
-        blend += jnp.maximum(approach, 0.0) * pl.reciprocal(last, approx=True)
+        blend += jnp.maximum(values[1], 0.0) * pl.reciprocal(values[2], approx=True)
     weight = cubed * blend
     high = weight.astype(jnp.bfloat16)
     low = (weight - high.astype(jnp.float32)).astype(jnp.bfloat16)
-    return [high, low], cubed * approach
+    return [high, low], cubed * values[1]
 
 
 def across(left, right):
@@ -166,7 +164,7 @@
     )
 
 
-def run_targets(targets, finish):
+def run_targets(targets, values, finish):
     steps = [
         (n, tiles[k : k + GROUP])
         for n, (_, _, tiles) in enumerate(targets)
@@ -177,7 +175,8 @@
 
     def product_of(step):
         n, group = step
-        columns = jnp.concatenate([source[:DEPTH, :] for source, _ in group], axis=1)
+        parts = [source[:DEPTH, : values * LANES] for source, _ in group]
+        columns = jnp.concatenate(parts, axis=1)
         return jnp.dot(targets[n][0], columns, preferred_element_type=jnp.float32)
 
     def add_up(n, moments, weights, last):
@@ -195,7 +194,7 @@
             ahead = product_of(steps[k + 1])
         moments, weights = [], []
         for m, (source, press_j) in enumerate(group):
-            columns = slice(m * VALUES * LANES, (m + 1) * VALUES * LANES)
+            columns = slice(m * values * LANES, (m + 1) * values * LANES)
             pair, part = weights_of(product[:, columns], targets[n][1], press_j)
             rates[n] += part
             weights += pair
@@ -213,12 +212,14 @@
 
 def own_kernel(
     own_ref, wall_ref, edge0_ref, edge1_ref, wpair_ref, along_ref,
-    tgt, sums, wsrc, table,
+    tgt, sums, wide, wsrc, table,
 ):
     blocks = tgt.shape[0]
 
+    choice = press_choice()
+
     def build(b, carry):
-        put_target(state_of(own_ref[rows_at(b), :]), b, tgt)
+        put_target(state_of(own_ref[rows_at(b), :]), b, choice, tgt, wide)
         return carry
 
     lax.fori_loop(0, blocks, build, 0, unroll=UNROLL)
@@ -241,18 +242,20 @@
         table[edge + inner + c] = inner + odd * edge + c
 
     together = math.gcd(blocks, WALL_TARGETS)
+    factor = 2.0 * cohesion / adhesion
 
     def targets_from(i, carry):
         first = i * together
         targets = []
         for n in range(together):
             slots = [table[wpair_ref[first + n, k]] for k in range(wpair_ref.shape[1])]
-            targets.append((tgt[first + n], None, [(wsrc.at[s], None) for s in slots]))
+            press_i = factor * wide[first + n] + 0.75 * (factor - 1.0)
+            targets.append((tgt[first + n], press_i, [(wsrc.at[s], None) for s in slots]))
 
         def finish(n, total):
             sums[sums_at(first + n), :] = total
 
-        run_targets(targets, finish)
+        run_targets(targets, VALUES - 1, finish)
         return carry
 
     lax.fori_loop(0, blocks // together, targets_from, 0)
@@ -301,7 +304,7 @@
             rows = sums_at(first + n)
             sums[rows, :] = own_sums[rows, :] + total
 
-        run_targets(targets, finish)
+        run_targets(targets, VALUES, finish)
         return carry
 
     lax.fori_loop(0, blocks // together, targets_from, 0)
@@ -354,6 +357,7 @@
         in_specs=[VMEM, VMEM, VMEM, VMEM, SMEM, SMEM],
         out_specs=[VMEM] * len(outs),
         scratch_shapes=[
+            pltpu.VMEM((blocks, LANES, LANES), jnp.float32),
             pltpu.VMEM(*source_shape(wall_blocks)),
             pltpu.SMEM((wall_blocks,), jnp.int32),
         ],

time: 57.4 us -> 59.6 us (1.038)
  Pallas kernels: 28.6 us -> 30.8 us
    pallas_call x1, Pallas kernels: 6.28 us -> 8.46 us  [own_pass(): pl.pallas_call(own_kernel, out_shape=[jax.ShapeDtypeStruct(*out) for out...]
  transfers between devices with their start and end apart: 8 -> 8, of which waited for: 6 -> 6; matrix products, arithmetic and copies ran while one was open for 0% -> 0% of each run, Pallas kernels for 11% -> 14%
where the time goes in v14:
time: 59.6 us; the launch traced here: 59.3 us
  Pallas kernels  30.8 us (52%)
  starting transfers between devices  16.1 us (27%)
  waiting for transfers between devices  8.51 us (14%)
  between operations  2.55 us (4%)
  local copies, waits for them, and re-layouts  1.28 us (2%)
    pallas_call x1, Pallas kernels, fluid_pass(): pl.pallas_call(fluid_kernel, out_shape=(jax.ShapeDtypeStruct((blocks, LAN...  20.7 us
    pallas_call x1, Pallas kernels, own_pass(): pl.pallas_call(own_kernel, out_shape=[jax.ShapeDtypeStruct(*out) for out...  8.46 us
    ppermute x5, starting transfers between devices, swapped(): return lax.ppermute(shard, axis, [(i, i ^ mask) for i in range(count)])  7.59 us
    all_to_all x1, starting transfers between devices, per_device(): lax.all_to_all(sent.reshape(8, -1, LANES), 'orb', 0, 0, axis_index_groups...  7.4 us
    ppermute x5, waiting for transfers between devices, swapped(): return lax.ppermute(shard, axis, [(i, i ^ mask) for i in range(count)])  6.72 us
    ppermute x2, waiting for transfers between devices, facing(): landed.append(lax.ppermute(sent, axis, pairs + [(j, i) for i, j in pairs]))  1.78 us
    pallas_call x1, Pallas kernels, outgoing_pass(): pl.pallas_call(functools.partial(outgoing_kernel, lax.axis_size('wall')),...  1.65 us
  transfers between devices with their start and end apart: 8, of which 6 were waited for; matrix products, arithmetic and copies ran while one was open for 0% of the time, Pallas kernels for 14%

profile of v14, /device:TPU:0, one launch (start us, length us, event | category | flops | bytes accessed | tf_op | source)
XLA Modules:
  0.0 59.3 jit_solution(18352776624128350890)
XLA Ops:
  0.6 1.7 %outgoing_pass.1 = (f32[384,128]{1,0:T(8,128)}, f32[24,128]{1,0:T(8,128)}, f32[4,128]{1,0:T(4,128)}, f32[4,128]{1,0:T(4,128)}) custom-call(f32[192,128]{1,0:T(8,128)} %bitcast.12, s32[7,6]{1,0:T(8,128)} %list_ref.1, s32[1]{0:T(128)} %bitcast.5.place_ref, f32[4,768]{1,0:T(4,128)} %wall_ref.1, s32[6]{0:T(128)} %count_ref.1, s32[1]{0:T(128)} %bitcast.6.along_ref), custom_call_target="tpu_custom_call" | custom-call | tf_op jit(solution)/shard_map/outgoing_pass/pallas_call | solution.py:423
  2.3 0.0 copy-start
  2.3 7.4 %all-to-all-start = ((f32[8,48,128]{2,1,0:T(8,128)}), f32[8,48,128]{2,1,0:T(8,128)S(1)}, u32[]{:S(2)}, u32[]{:S(2)}) async-start(f32[8,48,128]{2,1,0:T(8,128)} %bitcast.15), calls=%async_computation | async-start | bytes 393216 | tf_op jit(solution)/shard_map/all_to_all | solution.py:465
  9.7 0.1 collective-permute-start
  9.8 0.6 copy-done.4
  10.4 1.0 %collective-permute-start.1 = (f32[4,128]{1,0:T(4,128)S(1)}, f32[4,128]{1,0:T(4,128)S(1)}, u32[]{:S(2)}, u32[]{:S(2)}) collective-permute-start(f32[4,128]{1,0:T(4,128)S(1)} %copy-done.4), channel_id=1, source_target_pairs={{1,2},{3,0},{2,1},{0,3},{5,6},{7,4},{6,5},{4,7},{9,10},{11,8},{10,... | collective-permute-start | bytes 6152 | tf_op jit(solution)/shard_map/ppermute | solution.py:453
  11.4 0.1 copy.10.pair_ref
  11.5 0.1 copy.9.wpair_ref
  11.6 0.0 collective-permute-done.edge0_ref
  11.6 1.8 %collective-permute-done.1.edge1_ref = f32[4,128]{1,0:T(4,128)S(1)} collective-permute-done((f32[4,128]{1,0:T(4,128)S(1)}, f32[4,128]{1,0:T(4,128)S(1)}, u32[]{:S(2)}, u32[]{:S(2)}) %collective-permute-start.1) | collective-permute-done | bytes 2080 | tf_op jit(solution)/shard_map/ppermute | solution.py:453
  13.4 8.5 %own_pass.1 = (bf16[24,128,96]{2,1,0:T(8,128)(2,1)S(1)}, f32[960,128]{1,0:T(8,128)S(1)}) custom-call(f32[192,128]{1,0:T(8,128)S(1)} %bitcast.13, f32[24,128]{1,0:T(8,128)S(1)} %copy-done.1, f32[4,128]{1,0:T(4,128)S(1)} %collective-permute-done.edge0_ref, f32[4,128]{1,0:T(4,128)S(1)} %collective-permute-done.1.edge1_ref, s32[24,4]{1,0:T(8,128)S(1)} %copy.9.wpair_ref, ...), custom_call_target="tpu_custom_call" | custom-call | flops 1572864000 | tf_op jit(solution)/shard_map/own_pass/pallas_call | solution.py:354
  21.9 0.0 all-to-all-done
  21.9 20.7 %fluid_pass.1 = (f32[24,128]{1,0:T(8,128)}, f32[3,3072]{1,0:T(4,128)}, f32[8,128]{1,0:T(8,128)S(1)}) custom-call(f32[192,128]{1,0:T(8,128)S(1)} %bitcast.14, f32[384,128]{1,0:T(8,128)S(1)} %bitcast.11, s32[24,14]{1,0:T(8,128)S(1)} %copy.10.pair_ref, s32[1]{0:T(128)} %bitcast.5.place_ref, bf16[24,128,96]{2,1,0:T(8,128)(2,1)S(1)} %get-tuple-element.16.tgt, ...), custom_call_target="tpu_custom_call" | custom-call | flops 5505024000 | tf_op jit(solution)/shard_map/fluid_pass/pallas_call | solution.py:373
  42.6 0.2 collective-permute-start.2
  42.7 1.0 %collective-permute-done.2 = f32[8,128]{1,0:T(8,128)S(1)} collective-permute-done((f32[8,128]{1,0:T(8,128)S(1)}, f32[8,128]{1,0:T(8,128)S(1)}, u32[]{:S(2)}, u32[]{:S(2)}) %collective-permute-start.2) | collective-permute-done | bytes 4128 | tf_op jit(solution)/shard_map/ppermute | solution.py:434
  43.8 1.3 %collective-permute-start.3 = (f32[8,128]{1,0:T(8,128)S(1)}, f32[8,128]{1,0:T(8,128)S(1)}, u32[]{:S(2)}, u32[]{:S(2)}) collective-permute-start(f32[8,128]{1,0:T(8,128)S(1)} %max.15), channel_id=1, source_target_pairs={{0,3},{1,2},{2,1},{3,0},{4,7},{5,6},{6,5},{7,4},{8,11},{9,10},{10,... | collective-permute-start | bytes 12296 | tf_op jit(solution)/shard_map/ppermute | solution.py:434
  45.1 1.7 %collective-permute-done.3 = f32[8,128]{1,0:T(8,128)S(1)} collective-permute-done((f32[8,128]{1,0:T(8,128)S(1)}, f32[8,128]{1,0:T(8,128)S(1)}, u32[]{:S(2)}, u32[]{:S(2)}) %collective-permute-start.3) | collective-permute-done | bytes 4128 | tf_op jit(solution)/shard_map/ppermute | solution.py:434
  46.8 1.8 %collective-permute-start.4 = (f32[8,128]{1,0:T(8,128)S(1)}, f32[8,128]{1,0:T(8,128)S(1)}, u32[]{:S(2)}, u32[]{:S(2)}) collective-permute-start(f32[8,128]{1,0:T(8,128)S(1)} %max.16), channel_id=1, source_target_pairs={{0,5},{1,4},{2,7},{3,6},{4,1},{5,0},{6,3},{7,2},{8,13},{9,12},{10,... | collective-permute-start | bytes 12296 | tf_op jit(solution)/shard_map/ppermute | solution.py:434
  48.6 1.3 %collective-permute-done.4 = f32[8,128]{1,0:T(8,128)S(1)} collective-permute-done((f32[8,128]{1,0:T(8,128)S(1)}, f32[8,128]{1,0:T(8,128)S(1)}, u32[]{:S(2)}, u32[]{:S(2)}) %collective-permute-start.4) | collective-permute-done | bytes 4128 | tf_op jit(solution)/shard_map/ppermute | solution.py:434
  49.9 1.8 %collective-permute-start.5 = (f32[8,128]{1,0:T(8,128)S(1)}, f32[8,128]{1,0:T(8,128)S(1)}, u32[]{:S(2)}, u32[]{:S(2)}) collective-permute-start(f32[8,128]{1,0:T(8,128)S(1)} %max.17), channel_id=1, source_target_pairs={{0,9},{1,8},{2,11},{3,10},{4,13},{5,12},{6,15},{7,14},{8,1},{9,0},... | collective-permute-start | bytes 12296 | tf_op jit(solution)/shard_map/ppermute | solution.py:434
  51.6 1.3 %collective-permute-done.5 = f32[8,128]{1,0:T(8,128)S(1)} collective-permute-done((f32[8,128]{1,0:T(8,128)S(1)}, f32[8,128]{1,0:T(8,128)S(1)}, u32[]{:S(2)}, u32[]{:S(2)}) %collective-permute-start.5) | collective-permute-done | bytes 4128 | tf_op jit(solution)/shard_map/ppermute | solution.py:434
  53.0 2.6 %collective-permute-start.6 = (f32[8,128]{1,0:T(8,128)S(1)}, f32[8,128]{1,0:T(8,128)S(1)}, u32[]{:S(2)}, u32[]{:S(2)}) collective-permute-start(f32[8,128]{1,0:T(8,128)S(1)} %max.18), channel_id=1, source_target_pairs={{0,17},{1,16},{2,19},{3,18},{4,21},{5,20},{6,23},{7,22},{8,25},{9,... | collective-permute-start | bytes 12296 | tf_op jit(solution)/shard_map/ppermute | solution.py:434
  55.6 1.4 %collective-permute-done.6 = f32[8,128]{1,0:T(8,128)S(1)} collective-permute-done((f32[8,128]{1,0:T(8,128)S(1)}, f32[8,128]{1,0:T(8,128)S(1)}, u32[]{:S(2)}, u32[]{:S(2)}) %collective-permute-start.6) | collective-permute-done | bytes 4128 | tf_op jit(solution)/shard_map/ppermute | solution.py:434
  56.9 0.5 slice.3
  (15 shorter events, 0.0 us)
Async XLA Ops:
  2.3 7.4 %copy-start.5 = (f32[4,128]{1,0:T(4,128)S(1)}, f32[4,128]{1,0:T(4,128)}, u32[]{:S(2)}) copy-start(f32[4,128]{1,0:T(4,128)} %get-tuple-element.14) | copy-start | bytes 6148
  2.3 9.1 %copy-start.2 = (s32[24,14]{0,1:T(8,128)S(1)}, s32[24,14]{0,1:T(8,128)}, u32[]{:S(2)}) copy-start(s32[24,14]{0,1:T(8,128)} %param.8) | copy-start | bytes 4036
  2.3 11.1 %copy-start = (f32[8,3072]{1,0:T(8,128)S(1)}, f32[8,3072]{1,0:T(8,128)}, u32[]{:S(2)}) copy-start(f32[8,3072]{1,0:T(8,128)} %param.6) | copy-start | bytes 294916
  2.3 19.5 %all-to-all-start = ((f32[8,48,128]{2,1,0:T(8,128)}), f32[8,48,128]{2,1,0:T(8,128)S(1)}, u32[]{:S(2)}, u32[]{:S(2)}) async-start(f32[8,48,128]{2,1,0:T(8,128)} %bitcast.15), calls=%async_computation | async-start | bytes 393216 | tf_op jit(solution)/shard_map/all_to_all | solution.py:465
  9.7 0.7 %copy-start.4 = (f32[4,128]{1,0:T(4,128)S(1)}, f32[4,128]{1,0:T(4,128)}, u32[]{:S(2)}) copy-start(f32[4,128]{1,0:T(4,128)} %get-tuple-element.15) | copy-start | bytes 6148
  9.7 1.9 %collective-permute-start = (f32[4,128]{1,0:T(4,128)S(1)}, f32[4,128]{1,0:T(4,128)S(1)}, u32[]{:S(2)}, u32[]{:S(2)}) collective-permute-start(f32[4,128]{1,0:T(4,128)S(1)} %copy-done.5), channel_id=1, source_target_pairs={{0,1},{2,3},{1,0},{3,2},{4,5},{6,7},{5,4},{7,6},{8,9},{10,11},{9,8... | collective-permute-start | bytes 6152 | tf_op jit(solution)/shard_map/ppermute | solution.py:453
  10.4 1.1 %copy-start.3 = (s32[24,4]{0,1:T(4,128)S(1)}, s32[24,4]{0,1:T(4,128)}, u32[]{:S(2)}) copy-start(s32[24,4]{0,1:T(4,128)} %param.11) | copy-start | bytes 1156
  10.4 3.0 %collective-permute-start.1 = (f32[4,128]{1,0:T(4,128)S(1)}, f32[4,128]{1,0:T(4,128)S(1)}, u32[]{:S(2)}, u32[]{:S(2)}) collective-permute-start(f32[4,128]{1,0:T(4,128)S(1)} %copy-done.4), channel_id=1, source_target_pairs={{1,2},{3,0},{2,1},{0,3},{5,6},{7,4},{6,5},{4,7},{9,10},{11,8},{10,... | collective-permute-start | bytes 6152 | tf_op jit(solution)/shard_map/ppermute | solution.py:453
  11.5 1.9 %copy-start.1 = (f32[24,128]{1,0:T(8,128)S(1)}, f32[24,128]{1,0:T(8,128)}, u32[]{:S(2)}) copy-start(f32[24,128]{1,0:T(8,128)} %get-tuple-element.13.wall_ref) | copy-start | bytes 36868
  42.6 1.2 %collective-permute-start.2 = (f32[8,128]{1,0:T(8,128)S(1)}, f32[8,128]{1,0:T(8,128)S(1)}, u32[]{:S(2)}, u32[]{:S(2)}) collective-permute-start(f32[8,128]{1,0:T(8,128)S(1)} %get-tuple-element.20), channel_id=1, source_target_pairs={{0,1},{1,0},{2,3},{3,2},{4,5},{5,4},{6,7},{7,6},{8,9},{9,8},{10,11... | collective-permute-start | bytes 12296 | tf_op jit(solution)/shard_map/ppermute | solution.py:434
  43.8 3.0 %collective-permute-start.3 = (f32[8,128]{1,0:T(8,128)S(1)}, f32[8,128]{1,0:T(8,128)S(1)}, u32[]{:S(2)}, u32[]{:S(2)}) collective-permute-start(f32[8,128]{1,0:T(8,128)S(1)} %max.15), channel_id=1, source_target_pairs={{0,3},{1,2},{2,1},{3,0},{4,7},{5,6},{6,5},{7,4},{8,11},{9,10},{10,... | collective-permute-start | bytes 12296 | tf_op jit(solution)/shard_map/ppermute | solution.py:434
  46.8 3.1 %collective-permute-start.4 = (f32[8,128]{1,0:T(8,128)S(1)}, f32[8,128]{1,0:T(8,128)S(1)}, u32[]{:S(2)}, u32[]{:S(2)}) collective-permute-start(f32[8,128]{1,0:T(8,128)S(1)} %max.16), channel_id=1, source_target_pairs={{0,5},{1,4},{2,7},{3,6},{4,1},{5,0},{6,3},{7,2},{8,13},{9,12},{10,... | collective-permute-start | bytes 12296 | tf_op jit(solution)/shard_map/ppermute | solution.py:434
  49.9 3.1 %collective-permute-start.5 = (f32[8,128]{1,0:T(8,128)S(1)}, f32[8,128]{1,0:T(8,128)S(1)}, u32[]{:S(2)}, u32[]{:S(2)}) collective-permute-start(f32[8,128]{1,0:T(8,128)S(1)} %max.17), channel_id=1, source_target_pairs={{0,9},{1,8},{2,11},{3,10},{4,13},{5,12},{6,15},{7,14},{8,1},{9,0},... | collective-permute-start | bytes 12296 | tf_op jit(solution)/shard_map/ppermute | solution.py:434
  53.0 3.9 %collective-permute-start.6 = (f32[8,128]{1,0:T(8,128)S(1)}, f32[8,128]{1,0:T(8,128)S(1)}, u32[]{:S(2)}, u32[]{:S(2)}) collective-permute-start(f32[8,128]{1,0:T(8,128)S(1)} %max.18), channel_id=1, source_target_pairs={{0,17},{1,16},{2,19},{3,18},{4,21},{5,20},{6,23},{7,22},{8,25},{9,... | collective-permute-start | bytes 12296 | tf_op jit(solution)/shard_map/ppermute | solution.py:434

commit v15 on v12

--- a/solution.py
+++ b/solution.py
@@ -15,7 +15,6 @@
 MOMENTS = 4 * ROWS
 SUMS = MOMENTS + ROWS
 UNROLL = 24
-VALUES = 3
 GROUP = 2
 WALL_TARGETS = 24
 FLUID_TARGETS = 12
@@ -98,12 +97,13 @@
     if wall:
         press_part = chosen(0.0, (5, 2.0 * cohesion / adhesion), (6, -0.75))
         return near, along, (None, press_part)
-    return near, along, (m * r * near[0], m * chosen(minus, (3, n), (4, 1.0), (6, r * n)))
-
-
-def put_source(block, s, src, press=None, mass_factor=1.0):
+    spread = m * r * near[0], m * chosen(minus, (3, n), (4, 1.0), (6, r * n))
+    return near, along, spread, (None, chosen(0.0, (5, 1.0), (6, press - 0.75)))
+
+
+def put_source(block, s, src, wall=False, mass_factor=1.0):
     state = state_of(block)
-    for n, (first, second) in enumerate(source_groups(state, press is None)):
+    for n, (first, second) in enumerate(source_groups(state, wall)):
         firsts = split(first) if first is not None else [jnp.zeros((ROWS, LANES))] * 3
         pieces = [
             jnp.concatenate(pair, axis=0).astype(jnp.bfloat16)
@@ -117,8 +117,6 @@
     for n in range(2):
         half = jnp.concatenate(moments[2 * n : 2 * n + 2], axis=0)
         src[s, DEPTH:, n * LANES : (n + 1) * LANES] = half.astype(jnp.bfloat16)
-    if press is not None:
-        press[s] = state[5]
 
 
 def put_target(state, b, tgt):
@@ -130,30 +128,20 @@
     tgt[b] = across(unit, rows).astype(jnp.bfloat16)
 
 
-def press_choice():
-    row = lax.broadcasted_iota(jnp.int32, (DEPTH, LANES), 0)
-    value = jnp.where(row == ROWS + 6, -0.75, 0.0)
-    for k, (_, piece) in enumerate(SPLITS):
-        if piece == 0:
-            value = jnp.where(row == 2 * ROWS * k + ROWS + 5, 1.0, value)
-    return value.astype(jnp.bfloat16)
-
-
 def rows_at(index):
     return pl.ds(pl.multiple_of(index * ROWS, ROWS), ROWS)
 
 
-def weights_of(product, press_i, press_j):
-    near, approach, last = [product[:, n * LANES : (n + 1) * LANES] for n in range(VALUES)]
+def weights_of(product):
+    near, approach, *spread, press = [
+        product[:, first : first + LANES] for first in range(0, product.shape[1], LANES)
+    ]
     guarded = jnp.maximum(near, 1e-30)
     falloff = jnp.maximum(1.0 - guarded * lax.rsqrt(guarded), 0.0)
     cubed = falloff * falloff * falloff
-    if press_j is None:
-        blend = falloff + last
-    else:
-        blend = falloff + press_i
-        blend += jnp.concatenate([press_j[...]] * (LANES // ROWS), axis=0)
-        blend += jnp.maximum(approach, 0.0) * pl.reciprocal(last, approx=True)
+    blend = falloff + press
+    if spread:
+        blend += jnp.maximum(approach, 0.0) * pl.reciprocal(spread[0], approx=True)
     weight = cubed * blend
     high = weight.astype(jnp.bfloat16)
     low = (weight - high.astype(jnp.float32)).astype(jnp.bfloat16)
@@ -169,7 +157,7 @@
 def run_targets(targets, finish):
     steps = [
         (n, tiles[k : k + GROUP])
-        for n, (_, _, tiles) in enumerate(targets)
+        for n, (_, tiles) in enumerate(targets)
         for k in range(0, len(tiles), GROUP)
     ]
     totals = [jnp.zeros((MOMENTS, LANES), jnp.float32)] * len(targets)
@@ -177,7 +165,7 @@
 
     def product_of(step):
         n, group = step
-        columns = jnp.concatenate([source[:DEPTH, :] for source, _ in group], axis=1)
+        columns = jnp.concatenate([source[:DEPTH, :] for source in group], axis=1)
         return jnp.dot(targets[n][0], columns, preferred_element_type=jnp.float32)
 
     def add_up(n, moments, weights, last):
@@ -194,9 +182,9 @@
         if k + 1 < len(steps):
             ahead = product_of(steps[k + 1])
         moments, weights = [], []
-        for m, (source, press_j) in enumerate(group):
-            columns = slice(m * VALUES * LANES, (m + 1) * VALUES * LANES)
-            pair, part = weights_of(product[:, columns], targets[n][1], press_j)
+        width = product.shape[1] // len(group)
+        for m, source in enumerate(group):
+            pair, part = weights_of(product[:, m * width : (m + 1) * width])
             rates[n] += part
             weights += pair
             halves = [source[DEPTH:, :LANES], source[DEPTH:, LANES : 2 * LANES]]
@@ -230,7 +218,7 @@
             both = jnp.concatenate([held, held], axis=0)
             density = jnp.where(row == 6, 1.0, 0.0)
             block = jnp.where((row < 3) | (row == 7), both, density)
-            put_source(block, count, wsrc, None, adhesion / cohesion)
+            put_source(block, count, wsrc, True, adhesion / cohesion)
             count += 1
     inner, edge = wall_ref.shape[0] // 4, edge0_ref.shape[0] // 4
     odd = along_ref[0] % 2
@@ -247,7 +235,7 @@
         targets = []
         for n in range(together):
             slots = [table[wpair_ref[first + n, k]] for k in range(wpair_ref.shape[1])]
-            targets.append((tgt[first + n], None, [(wsrc.at[s], None) for s in slots]))
+            targets.append((tgt[first + n], [wsrc.at[s] for s in slots]))
 
         def finish(n, total):
             sums[sums_at(first + n), :] = total
@@ -260,7 +248,7 @@
 
 def fluid_kernel(
     own_ref, ghost_ref, pair_ref, place_ref, tgt, own_sums,
-    rate_ref, accel_ref, peak_ref, src, press, sums, stage, table,
+    rate_ref, accel_ref, peak_ref, src, sums, stage, table,
 ):
     blocks = tgt.shape[0]
     ghosts = ghost_ref.shape[0] // ROWS
@@ -274,18 +262,17 @@
             )
 
     def build_own(b, carry):
-        put_source(own_ref[rows_at(b), :], b, src, press)
+        put_source(own_ref[rows_at(b), :], b, src)
         return carry
 
     def build(g, carry):
-        put_source(ghost_ref[rows_at(g), :], blocks + g, src, press)
+        put_source(ghost_ref[rows_at(g), :], blocks + g, src)
         return carry
 
     lax.fori_loop(0, blocks, build_own, 0, unroll=UNROLL)
 
     lax.fori_loop(0, ghosts, build, 0, unroll=UNROLL)
 
-    choice = press_choice()
     together = math.gcd(blocks, FLUID_TARGETS)
 
     def targets_from(i, carry):
@@ -293,9 +280,7 @@
         targets = []
         for n in range(together):
             slots = [table[pair_ref[first + n, k]] for k in range(pair_ref.shape[1])]
-            target = tgt[first + n]
-            press_i = jnp.dot(target, choice, preferred_element_type=jnp.float32)
-            targets.append((target, press_i, [(src.at[s], press.at[s]) for s in slots]))
+            targets.append((tgt[first + n], [src.at[s] for s in slots]))
 
         def finish(n, total):
             rows = sums_at(first + n)
@@ -337,8 +322,8 @@
     )
 
 
-def source_shape(count):
-    return (count, DEPTH + 2 * ROWS, VALUES * LANES), jnp.bfloat16
+def source_shape(count, values):
+    return (count, DEPTH + 2 * ROWS, values * LANES), jnp.bfloat16
 
 
 def own_pass(own, walls, edges, wall_pairs, along):
@@ -354,7 +339,7 @@
         in_specs=[VMEM, VMEM, VMEM, VMEM, SMEM, SMEM],
         out_specs=[VMEM] * len(outs),
         scratch_shapes=[
-            pltpu.VMEM(*source_shape(wall_blocks)),
+            pltpu.VMEM(*source_shape(wall_blocks, 3)),
             pltpu.SMEM((wall_blocks,), jnp.int32),
         ],
         compiler_params=PARAMS,
@@ -376,8 +361,7 @@
         in_specs=[VMEM, VMEM, SMEM, SMEM] + [VMEM] * len(own_results),
         out_specs=(VMEM, VMEM, VMEM),
         scratch_shapes=[
-            pltpu.VMEM(*source_shape(total)),
-            pltpu.VMEM((total, ROWS, LANES), jnp.float32),
+            pltpu.VMEM(*source_shape(total, 4)),
             pltpu.VMEM((blocks * SUMS, LANES), jnp.float32),
             pltpu.VMEM((blocks * ROWS, LANES), jnp.float32),
             pltpu.SMEM((total,), jnp.int32),

time: 57.4 us -> 57.6 us (level)
  no operation moved by 1% of the time
where the time goes in v15:
time: 57.6 us; the launch traced here: 57.3 us
  Pallas kernels  28.8 us (50%)
  starting transfers between devices  16.2 us (28%)
  waiting for transfers between devices  8.43 us (15%)
  between operations  2.55 us (4%)
  local copies, waits for them, and re-layouts  1.28 us (2%)
    pallas_call x1, Pallas kernels, fluid_pass(): pl.pallas_call(fluid_kernel, out_shape=(jax.ShapeDtypeStruct((blocks, LAN...  20.8 us
    ppermute x5, starting transfers between devices, swapped(): return lax.ppermute(shard, axis, [(i, i ^ mask) for i in range(count)])  7.69 us
    all_to_all x1, starting transfers between devices, per_device(): lax.all_to_all(sent.reshape(8, -1, LANES), 'orb', 0, 0, axis_index_groups...  7.4 us
    ppermute x5, waiting for transfers between devices, swapped(): return lax.ppermute(shard, axis, [(i, i ^ mask) for i in range(count)])  6.64 us
    pallas_call x1, Pallas kernels, own_pass(): pl.pallas_call(own_kernel, out_shape=[jax.ShapeDtypeStruct(*out) for out...  6.28 us
    ppermute x2, waiting for transfers between devices, facing(): landed.append(lax.ppermute(sent, axis, pairs + [(j, i) for i, j in pairs]))  1.78 us
    pallas_call x1, Pallas kernels, outgoing_pass(): pl.pallas_call(functools.partial(outgoing_kernel, lax.axis_size('wall')),...  1.65 us
  transfers between devices with their start and end apart: 8, of which 6 were waited for; matrix products, arithmetic and copies ran while one was open for 0% of the time, Pallas kernels for 11%

profile of v15, /device:TPU:0, one launch (start us, length us, event | category | flops | bytes accessed | tf_op | source)
XLA Modules:
  0.0 57.3 jit_solution(13834038802509953846)
XLA Ops:
  0.6 1.7 %outgoing_pass.1 = (f32[384,128]{1,0:T(8,128)}, f32[24,128]{1,0:T(8,128)}, f32[4,128]{1,0:T(4,128)}, f32[4,128]{1,0:T(4,128)}) custom-call(f32[192,128]{1,0:T(8,128)} %bitcast.12, s32[7,6]{1,0:T(8,128)} %list_ref.1, s32[1]{0:T(128)} %bitcast.5.place_ref, f32[4,768]{1,0:T(4,128)} %wall_ref.1, s32[6]{0:T(128)} %count_ref.1, s32[1]{0:T(128)} %bitcast.6.along_ref), custom_call_target="tpu_custom_call" | custom-call | tf_op jit(solution)/shard_map/outgoing_pass/pallas_call | solution.py:403
  2.3 0.0 copy-start
  2.3 7.4 %all-to-all-start = ((f32[8,48,128]{2,1,0:T(8,128)}), f32[8,48,128]{2,1,0:T(8,128)S(1)}, u32[]{:S(2)}, u32[]{:S(2)}) async-start(f32[8,48,128]{2,1,0:T(8,128)} %bitcast.15), calls=%async_computation | async-start | bytes 393216 | tf_op jit(solution)/shard_map/all_to_all | solution.py:445
  9.7 0.1 collective-permute-start
  9.8 0.6 %copy-done.4 = f32[4,128]{1,0:T(4,128)S(1)} copy-done((f32[4,128]{1,0:T(4,128)S(1)}, f32[4,128]{1,0:T(4,128)}, u32[]{:S(2)}) %copy-start.4) | copy-done | bytes 2072
  10.4 1.0 %collective-permute-start.1 = (f32[4,128]{1,0:T(4,128)S(1)}, f32[4,128]{1,0:T(4,128)S(1)}, u32[]{:S(2)}, u32[]{:S(2)}) collective-permute-start(f32[4,128]{1,0:T(4,128)S(1)} %copy-done.4), channel_id=1, source_target_pairs={{1,2},{3,0},{2,1},{0,3},{5,6},{7,4},{6,5},{4,7},{9,10},{11,8},{10,... | collective-permute-start | bytes 6152 | tf_op jit(solution)/shard_map/ppermute | solution.py:433
  11.4 0.1 copy.10.pair_ref
  11.5 0.1 copy.9.wpair_ref
  11.6 0.0 collective-permute-done.edge0_ref
  11.6 1.8 %collective-permute-done.1.edge1_ref = f32[4,128]{1,0:T(4,128)S(1)} collective-permute-done((f32[4,128]{1,0:T(4,128)S(1)}, f32[4,128]{1,0:T(4,128)S(1)}, u32[]{:S(2)}, u32[]{:S(2)}) %collective-permute-start.1) | collective-permute-done | bytes 2080 | tf_op jit(solution)/shard_map/ppermute | solution.py:433
  13.4 6.3 %own_pass.1 = (bf16[24,128,96]{2,1,0:T(8,128)(2,1)S(1)}, f32[960,128]{1,0:T(8,128)S(1)}) custom-call(f32[192,128]{1,0:T(8,128)S(1)} %bitcast.13, f32[24,128]{1,0:T(8,128)S(1)} %copy-done.1, f32[4,128]{1,0:T(4,128)S(1)} %collective-permute-done.edge0_ref, f32[4,128]{1,0:T(4,128)S(1)} %collective-permute-done.1.edge1_ref, s32[24,4]{1,0:T(8,128)S(1)} %copy.9.wpair_ref, ...), custom_call_target="tpu_custom_call" | custom-call | flops 1572864000 | tf_op jit(solution)/shard_map/own_pass/pallas_call | solution.py:336
  19.7 0.0 all-to-all-done
  19.7 20.8 %fluid_pass.1 = (f32[24,128]{1,0:T(8,128)}, f32[3,3072]{1,0:T(4,128)}, f32[8,128]{1,0:T(8,128)S(1)}) custom-call(f32[192,128]{1,0:T(8,128)S(1)} %bitcast.14, f32[384,128]{1,0:T(8,128)S(1)} %bitcast.11, s32[24,14]{1,0:T(8,128)S(1)} %copy.10.pair_ref, s32[1]{0:T(128)} %bitcast.5.place_ref, bf16[24,128,96]{2,1,0:T(8,128)(2,1)S(1)} %get-tuple-element.16.tgt, ...), custom_call_target="tpu_custom_call" | custom-call | flops 5505024000 | tf_op jit(solution)/shard_map/fluid_pass/pallas_call | solution.py:354
  40.5 0.2 collective-permute-start.2
  40.8 0.9 %collective-permute-done.2 = f32[8,128]{1,0:T(8,128)S(1)} collective-permute-done((f32[8,128]{1,0:T(8,128)S(1)}, f32[8,128]{1,0:T(8,128)S(1)}, u32[]{:S(2)}, u32[]{:S(2)}) %collective-permute-start.2) | collective-permute-done | bytes 4128 | tf_op jit(solution)/shard_map/ppermute | solution.py:414
  41.7 1.3 %collective-permute-start.3 = (f32[8,128]{1,0:T(8,128)S(1)}, f32[8,128]{1,0:T(8,128)S(1)}, u32[]{:S(2)}, u32[]{:S(2)}) collective-permute-start(f32[8,128]{1,0:T(8,128)S(1)} %max.15), channel_id=1, source_target_pairs={{0,3},{1,2},{2,1},{3,0},{4,7},{5,6},{6,5},{7,4},{8,11},{9,10},{10,... | collective-permute-start | bytes 12296 | tf_op jit(solution)/shard_map/ppermute | solution.py:414
  43.0 1.7 %collective-permute-done.3 = f32[8,128]{1,0:T(8,128)S(1)} collective-permute-done((f32[8,128]{1,0:T(8,128)S(1)}, f32[8,128]{1,0:T(8,128)S(1)}, u32[]{:S(2)}, u32[]{:S(2)}) %collective-permute-start.3) | collective-permute-done | bytes 4128 | tf_op jit(solution)/shard_map/ppermute | solution.py:414
  44.7 1.8 %collective-permute-start.4 = (f32[8,128]{1,0:T(8,128)S(1)}, f32[8,128]{1,0:T(8,128)S(1)}, u32[]{:S(2)}, u32[]{:S(2)}) collective-permute-start(f32[8,128]{1,0:T(8,128)S(1)} %max.16), channel_id=1, source_target_pairs={{0,5},{1,4},{2,7},{3,6},{4,1},{5,0},{6,3},{7,2},{8,13},{9,12},{10,... | collective-permute-start | bytes 12296 | tf_op jit(solution)/shard_map/ppermute | solution.py:414
  46.6 1.3 %collective-permute-done.4 = f32[8,128]{1,0:T(8,128)S(1)} collective-permute-done((f32[8,128]{1,0:T(8,128)S(1)}, f32[8,128]{1,0:T(8,128)S(1)}, u32[]{:S(2)}, u32[]{:S(2)}) %collective-permute-start.4) | collective-permute-done | bytes 4128 | tf_op jit(solution)/shard_map/ppermute | solution.py:414
  47.9 1.7 %collective-permute-start.5 = (f32[8,128]{1,0:T(8,128)S(1)}, f32[8,128]{1,0:T(8,128)S(1)}, u32[]{:S(2)}, u32[]{:S(2)}) collective-permute-start(f32[8,128]{1,0:T(8,128)S(1)} %max.17), channel_id=1, source_target_pairs={{0,9},{1,8},{2,11},{3,10},{4,13},{5,12},{6,15},{7,14},{8,1},{9,0},... | collective-permute-start | bytes 12296 | tf_op jit(solution)/shard_map/ppermute | solution.py:414
  49.6 1.3 %collective-permute-done.5 = f32[8,128]{1,0:T(8,128)S(1)} collective-permute-done((f32[8,128]{1,0:T(8,128)S(1)}, f32[8,128]{1,0:T(8,128)S(1)}, u32[]{:S(2)}, u32[]{:S(2)}) %collective-permute-start.5) | collective-permute-done | bytes 4128 | tf_op jit(solution)/shard_map/ppermute | solution.py:414
  50.9 2.6 %collective-permute-start.6 = (f32[8,128]{1,0:T(8,128)S(1)}, f32[8,128]{1,0:T(8,128)S(1)}, u32[]{:S(2)}, u32[]{:S(2)}) collective-permute-start(f32[8,128]{1,0:T(8,128)S(1)} %max.18), channel_id=1, source_target_pairs={{0,17},{1,16},{2,19},{3,18},{4,21},{5,20},{6,23},{7,22},{8,25},{9,... | collective-permute-start | bytes 12296 | tf_op jit(solution)/shard_map/ppermute | solution.py:414
  53.5 1.3 %collective-permute-done.6 = f32[8,128]{1,0:T(8,128)S(1)} collective-permute-done((f32[8,128]{1,0:T(8,128)S(1)}, f32[8,128]{1,0:T(8,128)S(1)}, u32[]{:S(2)}, u32[]{:S(2)}) %collective-permute-start.6) | collective-permute-done | bytes 4128 | tf_op jit(solution)/shard_map/ppermute | solution.py:414
  54.9 0.5 slice.3
  (15 shorter events, 0.0 us)
Async XLA Ops:
  2.3 7.4 %copy-start.5 = (f32[4,128]{1,0:T(4,128)S(1)}, f32[4,128]{1,0:T(4,128)}, u32[]{:S(2)}) copy-start(f32[4,128]{1,0:T(4,128)} %get-tuple-element.14) | copy-start | bytes 6148
  2.3 9.1 %copy-start.2 = (s32[24,14]{0,1:T(8,128)S(1)}, s32[24,14]{0,1:T(8,128)}, u32[]{:S(2)}) copy-start(s32[24,14]{0,1:T(8,128)} %param.8) | copy-start | bytes 4036
  2.3 11.1 %copy-start = (f32[8,3072]{1,0:T(8,128)S(1)}, f32[8,3072]{1,0:T(8,128)}, u32[]{:S(2)}) copy-start(f32[8,3072]{1,0:T(8,128)} %param.6) | copy-start | bytes 294916
  2.3 17.4 %all-to-all-start = ((f32[8,48,128]{2,1,0:T(8,128)}), f32[8,48,128]{2,1,0:T(8,128)S(1)}, u32[]{:S(2)}, u32[]{:S(2)}) async-start(f32[8,48,128]{2,1,0:T(8,128)} %bitcast.15), calls=%async_computation | async-start | bytes 393216 | tf_op jit(solution)/shard_map/all_to_all | solution.py:445
  9.7 0.7 %copy-start.4 = (f32[4,128]{1,0:T(4,128)S(1)}, f32[4,128]{1,0:T(4,128)}, u32[]{:S(2)}) copy-start(f32[4,128]{1,0:T(4,128)} %get-tuple-element.15) | copy-start | bytes 6148
  9.7 1.9 %collective-permute-start = (f32[4,128]{1,0:T(4,128)S(1)}, f32[4,128]{1,0:T(4,128)S(1)}, u32[]{:S(2)}, u32[]{:S(2)}) collective-permute-start(f32[4,128]{1,0:T(4,128)S(1)} %copy-done.5), channel_id=1, source_target_pairs={{0,1},{2,3},{1,0},{3,2},{4,5},{6,7},{5,4},{7,6},{8,9},{10,11},{9,8... | collective-permute-start | bytes 6152 | tf_op jit(solution)/shard_map/ppermute | solution.py:433
  10.4 1.1 %copy-start.3 = (s32[24,4]{0,1:T(4,128)S(1)}, s32[24,4]{0,1:T(4,128)}, u32[]{:S(2)}) copy-start(s32[24,4]{0,1:T(4,128)} %param.11) | copy-start | bytes 1156
  10.4 3.0 %collective-permute-start.1 = (f32[4,128]{1,0:T(4,128)S(1)}, f32[4,128]{1,0:T(4,128)S(1)}, u32[]{:S(2)}, u32[]{:S(2)}) collective-permute-start(f32[4,128]{1,0:T(4,128)S(1)} %copy-done.4), channel_id=1, source_target_pairs={{1,2},{3,0},{2,1},{0,3},{5,6},{7,4},{6,5},{4,7},{9,10},{11,8},{10,... | collective-permute-start | bytes 6152 | tf_op jit(solution)/shard_map/ppermute | solution.py:433
  11.5 1.9 %copy-start.1 = (f32[24,128]{1,0:T(8,128)S(1)}, f32[24,128]{1,0:T(8,128)}, u32[]{:S(2)}) copy-start(f32[24,128]{1,0:T(8,128)} %get-tuple-element.13.wall_ref) | copy-start | bytes 36868
  40.5 1.2 %collective-permute-start.2 = (f32[8,128]{1,0:T(8,128)S(1)}, f32[8,128]{1,0:T(8,128)S(1)}, u32[]{:S(2)}, u32[]{:S(2)}) collective-permute-start(f32[8,128]{1,0:T(8,128)S(1)} %get-tuple-element.20), channel_id=1, source_target_pairs={{0,1},{1,0},{2,3},{3,2},{4,5},{5,4},{6,7},{7,6},{8,9},{9,8},{10,11... | collective-permute-start | bytes 12296 | tf_op jit(solution)/shard_map/ppermute | solution.py:414
  41.7 3.0 %collective-permute-start.3 = (f32[8,128]{1,0:T(8,128)S(1)}, f32[8,128]{1,0:T(8,128)S(1)}, u32[]{:S(2)}, u32[]{:S(2)}) collective-permute-start(f32[8,128]{1,0:T(8,128)S(1)} %max.15), channel_id=1, source_target_pairs={{0,3},{1,2},{2,1},{3,0},{4,7},{5,6},{6,5},{7,4},{8,11},{9,10},{10,... | collective-permute-start | bytes 12296 | tf_op jit(solution)/shard_map/ppermute | solution.py:414
  44.7 3.2 %collective-permute-start.4 = (f32[8,128]{1,0:T(8,128)S(1)}, f32[8,128]{1,0:T(8,128)S(1)}, u32[]{:S(2)}, u32[]{:S(2)}) collective-permute-start(f32[8,128]{1,0:T(8,128)S(1)} %max.16), channel_id=1, source_target_pairs={{0,5},{1,4},{2,7},{3,6},{4,1},{5,0},{6,3},{7,2},{8,13},{9,12},{10,... | collective-permute-start | bytes 12296 | tf_op jit(solution)/shard_map/ppermute | solution.py:414
  47.9 3.0 %collective-permute-start.5 = (f32[8,128]{1,0:T(8,128)S(1)}, f32[8,128]{1,0:T(8,128)S(1)}, u32[]{:S(2)}, u32[]{:S(2)}) collective-permute-start(f32[8,128]{1,0:T(8,128)S(1)} %max.17), channel_id=1, source_target_pairs={{0,9},{1,8},{2,11},{3,10},{4,13},{5,12},{6,15},{7,14},{8,1},{9,0},... | collective-permute-start | bytes 12296 | tf_op jit(solution)/shard_map/ppermute | solution.py:414
  50.9 3.9 %collective-permute-start.6 = (f32[8,128]{1,0:T(8,128)S(1)}, f32[8,128]{1,0:T(8,128)S(1)}, u32[]{:S(2)}, u32[]{:S(2)}) collective-permute-start(f32[8,128]{1,0:T(8,128)S(1)} %max.18), channel_id=1, source_target_pairs={{0,17},{1,16},{2,19},{3,18},{4,21},{5,20},{6,23},{7,22},{8,25},{9,... | collective-permute-start | bytes 12296 | tf_op jit(solution)/shard_map/ppermute | solution.py:414

commit v16 on v12

--- a/solution.py
+++ b/solution.py
@@ -16,7 +16,7 @@
 SUMS = MOMENTS + ROWS
 UNROLL = 24
 VALUES = 3
-GROUP = 2
+GROUP = 7
 WALL_TARGETS = 24
 FLUID_TARGETS = 12
 

time: 57.4 us -> 61.3 us (1.068)
  Pallas kernels: 28.6 us -> 32.5 us
    pallas_call x1, Pallas kernels: 20.7 us -> 24.4 us  [fluid_pass(): pl.pallas_call(fluid_kernel, out_shape=(jax.ShapeDtypeStruct((blocks, LAN...]
where the time goes in v16:
time: 61.3 us; the launch traced here: 61 us
  Pallas kernels  32.5 us (53%)
  starting transfers between devices  16.2 us (26%)
  waiting for transfers between devices  8.44 us (14%)
  between operations  2.55 us (4%)
  local copies, waits for them, and re-layouts  1.28 us (2%)
    pallas_call x1, Pallas kernels, fluid_pass(): pl.pallas_call(fluid_kernel, out_shape=(jax.ShapeDtypeStruct((blocks, LAN...  24.4 us
    ppermute x5, starting transfers between devices, swapped(): return lax.ppermute(shard, axis, [(i, i ^ mask) for i in range(count)])  7.68 us
    all_to_all x1, starting transfers between devices, per_device(): lax.all_to_all(sent.reshape(8, -1, LANES), 'orb', 0, 0, axis_index_groups...  7.4 us
    ppermute x5, waiting for transfers between devices, swapped(): return lax.ppermute(shard, axis, [(i, i ^ mask) for i in range(count)])  6.66 us
    pallas_call x1, Pallas kernels, own_pass(): pl.pallas_call(own_kernel, out_shape=[jax.ShapeDtypeStruct(*out) for out...  6.45 us
    ppermute x2, waiting for transfers between devices, facing(): landed.append(lax.ppermute(sent, axis, pairs + [(j, i) for i, j in pairs]))  1.78 us
    pallas_call x1, Pallas kernels, outgoing_pass(): pl.pallas_call(functools.partial(outgoing_kernel, lax.axis_size('wall')),...  1.65 us
  transfers between devices with their start and end apart: 8, of which 6 were waited for; matrix products, arithmetic and copies ran while one was open for 0% of the time, Pallas kernels for 11%

profile of v16, /device:TPU:0, one launch (start us, length us, event | category | flops | bytes accessed | tf_op | source)
XLA Modules:
  0.0 61.0 jit_solution(14045543242450822190)
XLA Ops:
  0.6 1.7 %outgoing_pass.1 = (f32[384,128]{1,0:T(8,128)}, f32[24,128]{1,0:T(8,128)}, f32[4,128]{1,0:T(4,128)}, f32[4,128]{1,0:T(4,128)}) custom-call(f32[192,128]{1,0:T(8,128)} %bitcast.12, s32[7,6]{1,0:T(8,128)} %list_ref.1, s32[1]{0:T(128)} %bitcast.5.place_ref, f32[4,768]{1,0:T(4,128)} %wall_ref.1, s32[6]{0:T(128)} %count_ref.1, s32[1]{0:T(128)} %bitcast.6.along_ref), custom_call_target="tpu_custom_call" | custom-call | tf_op jit(solution)/shard_map/outgoing_pass/pallas_call | solution.py:419
  2.3 0.0 copy-start
  2.3 7.4 %all-to-all-start = ((f32[8,48,128]{2,1,0:T(8,128)}), f32[8,48,128]{2,1,0:T(8,128)S(1)}, u32[]{:S(2)}, u32[]{:S(2)}) async-start(f32[8,48,128]{2,1,0:T(8,128)} %bitcast.15), calls=%async_computation | async-start | bytes 393216 | tf_op jit(solution)/shard_map/all_to_all | solution.py:461
  9.7 0.1 collective-permute-start
  9.8 0.6 copy-done.4
  10.4 1.0 %collective-permute-start.1 = (f32[4,128]{1,0:T(4,128)S(1)}, f32[4,128]{1,0:T(4,128)S(1)}, u32[]{:S(2)}, u32[]{:S(2)}) collective-permute-start(f32[4,128]{1,0:T(4,128)S(1)} %copy-done.4), channel_id=1, source_target_pairs={{1,2},{3,0},{2,1},{0,3},{5,6},{7,4},{6,5},{4,7},{9,10},{11,8},{10,... | collective-permute-start | bytes 6152 | tf_op jit(solution)/shard_map/ppermute | solution.py:449
  11.4 0.1 copy.10.pair_ref
  11.5 0.1 copy.9.wpair_ref
  11.6 0.0 collective-permute-done.edge0_ref
  11.6 1.8 %collective-permute-done.1.edge1_ref = f32[4,128]{1,0:T(4,128)S(1)} collective-permute-done((f32[4,128]{1,0:T(4,128)S(1)}, f32[4,128]{1,0:T(4,128)S(1)}, u32[]{:S(2)}, u32[]{:S(2)}) %collective-permute-start.1) | collective-permute-done | bytes 2080 | tf_op jit(solution)/shard_map/ppermute | solution.py:449
  13.4 6.4 %own_pass.1 = (bf16[24,128,96]{2,1,0:T(8,128)(2,1)S(1)}, f32[960,128]{1,0:T(8,128)S(1)}) custom-call(f32[192,128]{1,0:T(8,128)S(1)} %bitcast.13, f32[24,128]{1,0:T(8,128)S(1)} %copy-done.1, f32[4,128]{1,0:T(4,128)S(1)} %collective-permute-done.edge0_ref, f32[4,128]{1,0:T(4,128)S(1)} %collective-permute-done.1.edge1_ref, s32[24,4]{1,0:T(8,128)S(1)} %copy.9.wpair_ref, ...), custom_call_target="tpu_custom_call" | custom-call | flops 1572864000 | tf_op jit(solution)/shard_map/own_pass/pallas_call | solution.py:351
  19.8 0.0 all-to-all-done
  19.9 24.4 %fluid_pass.1 = (f32[24,128]{1,0:T(8,128)}, f32[3,3072]{1,0:T(4,128)}, f32[8,128]{1,0:T(8,128)S(1)}) custom-call(f32[192,128]{1,0:T(8,128)S(1)} %bitcast.14, f32[384,128]{1,0:T(8,128)S(1)} %bitcast.11, s32[24,14]{1,0:T(8,128)S(1)} %copy.10.pair_ref, s32[1]{0:T(128)} %bitcast.5.place_ref, bf16[24,128,96]{2,1,0:T(8,128)(2,1)S(1)} %get-tuple-element.16.tgt, ...), custom_call_target="tpu_custom_call" | custom-call | flops 5505024000 | tf_op jit(solution)/shard_map/fluid_pass/pallas_call | solution.py:369
  44.3 0.2 collective-permute-start.2
  44.5 1.0 %collective-permute-done.2 = f32[8,128]{1,0:T(8,128)S(1)} collective-permute-done((f32[8,128]{1,0:T(8,128)S(1)}, f32[8,128]{1,0:T(8,128)S(1)}, u32[]{:S(2)}, u32[]{:S(2)}) %collective-permute-start.2) | collective-permute-done | bytes 4128 | tf_op jit(solution)/shard_map/ppermute | solution.py:430
  45.5 1.4 %collective-permute-start.3 = (f32[8,128]{1,0:T(8,128)S(1)}, f32[8,128]{1,0:T(8,128)S(1)}, u32[]{:S(2)}, u32[]{:S(2)}) collective-permute-start(f32[8,128]{1,0:T(8,128)S(1)} %max.15), channel_id=1, source_target_pairs={{0,3},{1,2},{2,1},{3,0},{4,7},{5,6},{6,5},{7,4},{8,11},{9,10},{10,... | collective-permute-start | bytes 12296 | tf_op jit(solution)/shard_map/ppermute | solution.py:430
  46.8 1.7 %collective-permute-done.3 = f32[8,128]{1,0:T(8,128)S(1)} collective-permute-done((f32[8,128]{1,0:T(8,128)S(1)}, f32[8,128]{1,0:T(8,128)S(1)}, u32[]{:S(2)}, u32[]{:S(2)}) %collective-permute-start.3) | collective-permute-done | bytes 4128 | tf_op jit(solution)/shard_map/ppermute | solution.py:430
  48.5 1.8 %collective-permute-start.4 = (f32[8,128]{1,0:T(8,128)S(1)}, f32[8,128]{1,0:T(8,128)S(1)}, u32[]{:S(2)}, u32[]{:S(2)}) collective-permute-start(f32[8,128]{1,0:T(8,128)S(1)} %max.16), channel_id=1, source_target_pairs={{0,5},{1,4},{2,7},{3,6},{4,1},{5,0},{6,3},{7,2},{8,13},{9,12},{10,... | collective-permute-start | bytes 12296 | tf_op jit(solution)/shard_map/ppermute | solution.py:430
  50.3 1.3 %collective-permute-done.4 = f32[8,128]{1,0:T(8,128)S(1)} collective-permute-done((f32[8,128]{1,0:T(8,128)S(1)}, f32[8,128]{1,0:T(8,128)S(1)}, u32[]{:S(2)}, u32[]{:S(2)}) %collective-permute-start.4) | collective-permute-done | bytes 4128 | tf_op jit(solution)/shard_map/ppermute | solution.py:430
  51.6 1.7 %collective-permute-start.5 = (f32[8,128]{1,0:T(8,128)S(1)}, f32[8,128]{1,0:T(8,128)S(1)}, u32[]{:S(2)}, u32[]{:S(2)}) collective-permute-start(f32[8,128]{1,0:T(8,128)S(1)} %max.17), channel_id=1, source_target_pairs={{0,9},{1,8},{2,11},{3,10},{4,13},{5,12},{6,15},{7,14},{8,1},{9,0},... | collective-permute-start | bytes 12296 | tf_op jit(solution)/shard_map/ppermute | solution.py:430
  53.4 1.3 %collective-permute-done.5 = f32[8,128]{1,0:T(8,128)S(1)} collective-permute-done((f32[8,128]{1,0:T(8,128)S(1)}, f32[8,128]{1,0:T(8,128)S(1)}, u32[]{:S(2)}, u32[]{:S(2)}) %collective-permute-start.5) | collective-permute-done | bytes 4128 | tf_op jit(solution)/shard_map/ppermute | solution.py:430
  54.7 2.6 %collective-permute-start.6 = (f32[8,128]{1,0:T(8,128)S(1)}, f32[8,128]{1,0:T(8,128)S(1)}, u32[]{:S(2)}, u32[]{:S(2)}) collective-permute-start(f32[8,128]{1,0:T(8,128)S(1)} %max.18), channel_id=1, source_target_pairs={{0,17},{1,16},{2,19},{3,18},{4,21},{5,20},{6,23},{7,22},{8,25},{9,... | collective-permute-start | bytes 12296 | tf_op jit(solution)/shard_map/ppermute | solution.py:430
  57.3 1.4 %collective-permute-done.6 = f32[8,128]{1,0:T(8,128)S(1)} collective-permute-done((f32[8,128]{1,0:T(8,128)S(1)}, f32[8,128]{1,0:T(8,128)S(1)}, u32[]{:S(2)}, u32[]{:S(2)}) %collective-permute-start.6) | collective-permute-done | bytes 4128 | tf_op jit(solution)/shard_map/ppermute | solution.py:430
  58.7 0.5 slice.3
  (15 shorter events, 0.0 us)
Async XLA Ops:
  2.3 7.4 %copy-start.5 = (f32[4,128]{1,0:T(4,128)S(1)}, f32[4,128]{1,0:T(4,128)}, u32[]{:S(2)}) copy-start(f32[4,128]{1,0:T(4,128)} %get-tuple-element.14) | copy-start | bytes 6148
  2.3 9.1 %copy-start.2 = (s32[24,14]{0,1:T(8,128)S(1)}, s32[24,14]{0,1:T(8,128)}, u32[]{:S(2)}) copy-start(s32[24,14]{0,1:T(8,128)} %param.8) | copy-start | bytes 4036
  2.3 11.1 %copy-start = (f32[8,3072]{1,0:T(8,128)S(1)}, f32[8,3072]{1,0:T(8,128)}, u32[]{:S(2)}) copy-start(f32[8,3072]{1,0:T(8,128)} %param.6) | copy-start | bytes 294916
  2.3 17.5 %all-to-all-start = ((f32[8,48,128]{2,1,0:T(8,128)}), f32[8,48,128]{2,1,0:T(8,128)S(1)}, u32[]{:S(2)}, u32[]{:S(2)}) async-start(f32[8,48,128]{2,1,0:T(8,128)} %bitcast.15), calls=%async_computation | async-start | bytes 393216 | tf_op jit(solution)/shard_map/all_to_all | solution.py:461
  9.7 0.7 %copy-start.4 = (f32[4,128]{1,0:T(4,128)S(1)}, f32[4,128]{1,0:T(4,128)}, u32[]{:S(2)}) copy-start(f32[4,128]{1,0:T(4,128)} %get-tuple-element.15) | copy-start | bytes 6148
  9.7 1.9 %collective-permute-start = (f32[4,128]{1,0:T(4,128)S(1)}, f32[4,128]{1,0:T(4,128)S(1)}, u32[]{:S(2)}, u32[]{:S(2)}) collective-permute-start(f32[4,128]{1,0:T(4,128)S(1)} %copy-done.5), channel_id=1, source_target_pairs={{0,1},{2,3},{1,0},{3,2},{4,5},{6,7},{5,4},{7,6},{8,9},{10,11},{9,8... | collective-permute-start | bytes 6152 | tf_op jit(solution)/shard_map/ppermute | solution.py:449
  10.4 1.1 %copy-start.3 = (s32[24,4]{0,1:T(4,128)S(1)}, s32[24,4]{0,1:T(4,128)}, u32[]{:S(2)}) copy-start(s32[24,4]{0,1:T(4,128)} %param.11) | copy-start | bytes 1156
  10.4 3.0 %collective-permute-start.1 = (f32[4,128]{1,0:T(4,128)S(1)}, f32[4,128]{1,0:T(4,128)S(1)}, u32[]{:S(2)}, u32[]{:S(2)}) collective-permute-start(f32[4,128]{1,0:T(4,128)S(1)} %copy-done.4), channel_id=1, source_target_pairs={{1,2},{3,0},{2,1},{0,3},{5,6},{7,4},{6,5},{4,7},{9,10},{11,8},{10,... | collective-permute-start | bytes 6152 | tf_op jit(solution)/shard_map/ppermute | solution.py:449
  11.5 1.9 %copy-start.1 = (f32[24,128]{1,0:T(8,128)S(1)}, f32[24,128]{1,0:T(8,128)}, u32[]{:S(2)}) copy-start(f32[24,128]{1,0:T(8,128)} %get-tuple-element.13.wall_ref) | copy-start | bytes 36868
  44.3 1.2 %collective-permute-start.2 = (f32[8,128]{1,0:T(8,128)S(1)}, f32[8,128]{1,0:T(8,128)S(1)}, u32[]{:S(2)}, u32[]{:S(2)}) collective-permute-start(f32[8,128]{1,0:T(8,128)S(1)} %get-tuple-element.20), channel_id=1, source_target_pairs={{0,1},{1,0},{2,3},{3,2},{4,5},{5,4},{6,7},{7,6},{8,9},{9,8},{10,11... | collective-permute-start | bytes 12296 | tf_op jit(solution)/shard_map/ppermute | solution.py:430
  45.5 3.0 %collective-permute-start.3 = (f32[8,128]{1,0:T(8,128)S(1)}, f32[8,128]{1,0:T(8,128)S(1)}, u32[]{:S(2)}, u32[]{:S(2)}) collective-permute-start(f32[8,128]{1,0:T(8,128)S(1)} %max.15), channel_id=1, source_target_pairs={{0,3},{1,2},{2,1},{3,0},{4,7},{5,6},{6,5},{7,4},{8,11},{9,10},{10,... | collective-permute-start | bytes 12296 | tf_op jit(solution)/shard_map/ppermute | solution.py:430
  48.5 3.1 %collective-permute-start.4 = (f32[8,128]{1,0:T(8,128)S(1)}, f32[8,128]{1,0:T(8,128)S(1)}, u32[]{:S(2)}, u32[]{:S(2)}) collective-permute-start(f32[8,128]{1,0:T(8,128)S(1)} %max.16), channel_id=1, source_target_pairs={{0,5},{1,4},{2,7},{3,6},{4,1},{5,0},{6,3},{7,2},{8,13},{9,12},{10,... | collective-permute-start | bytes 12296 | tf_op jit(solution)/shard_map/ppermute | solution.py:430
  51.6 3.1 %collective-permute-start.5 = (f32[8,128]{1,0:T(8,128)S(1)}, f32[8,128]{1,0:T(8,128)S(1)}, u32[]{:S(2)}, u32[]{:S(2)}) collective-permute-start(f32[8,128]{1,0:T(8,128)S(1)} %max.17), channel_id=1, source_target_pairs={{0,9},{1,8},{2,11},{3,10},{4,13},{5,12},{6,15},{7,14},{8,1},{9,0},... | collective-permute-start | bytes 12296 | tf_op jit(solution)/shard_map/ppermute | solution.py:430
  54.7 3.9 %collective-permute-start.6 = (f32[8,128]{1,0:T(8,128)S(1)}, f32[8,128]{1,0:T(8,128)S(1)}, u32[]{:S(2)}, u32[]{:S(2)}) collective-permute-start(f32[8,128]{1,0:T(8,128)S(1)} %max.18), channel_id=1, source_target_pairs={{0,17},{1,16},{2,19},{3,18},{4,21},{5,20},{6,23},{7,22},{8,25},{9,... | collective-permute-start | bytes 12296 | tf_op jit(solution)/shard_map/ppermute | solution.py:430

commit v17 on v16

--- a/solution.py
+++ b/solution.py
@@ -16,7 +16,7 @@
 SUMS = MOMENTS + ROWS
 UNROLL = 24
 VALUES = 3
-GROUP = 7
+GROUP = 1
 WALL_TARGETS = 24
 FLUID_TARGETS = 12
 

time: 61.3 us -> 62.8 us (1.024)
  Pallas kernels: 32.5 us -> 34 us
    pallas_call x1, Pallas kernels: 6.45 us -> 8.03 us  [own_pass(): pl.pallas_call(own_kernel, out_shape=[jax.ShapeDtypeStruct(*out) for out...]
  transfers between devices with their start and end apart: 8 -> 8, of which waited for: 6 -> 6; matrix products, arithmetic and copies ran while one was open for 0% -> 0% of each run, Pallas kernels for 11% -> 13%
where the time goes in v17:
time: 62.8 us; the launch traced here: 62.5 us
  Pallas kernels  34 us (54%)
  starting transfers between devices  16.2 us (26%)
  waiting for transfers between devices  8.47 us (13%)
  between operations  2.56 us (4%)
  local copies, waits for them, and re-layouts  1.28 us (2%)
    pallas_call x1, Pallas kernels, fluid_pass(): pl.pallas_call(fluid_kernel, out_shape=(jax.ShapeDtypeStruct((blocks, LAN...  24.4 us
    pallas_call x1, Pallas kernels, own_pass(): pl.pallas_call(own_kernel, out_shape=[jax.ShapeDtypeStruct(*out) for out...  8.03 us
    ppermute x5, starting transfers between devices, swapped(): return lax.ppermute(shard, axis, [(i, i ^ mask) for i in range(count)])  7.65 us
    all_to_all x1, starting transfers between devices, per_device(): lax.all_to_all(sent.reshape(8, -1, LANES), 'orb', 0, 0, axis_index_groups...  7.4 us
    ppermute x5, waiting for transfers between devices, swapped(): return lax.ppermute(shard, axis, [(i, i ^ mask) for i in range(count)])  6.66 us
    ppermute x2, waiting for transfers between devices, facing(): landed.append(lax.ppermute(sent, axis, pairs + [(j, i) for i, j in pairs]))  1.78 us
    pallas_call x1, Pallas kernels, outgoing_pass(): pl.pallas_call(functools.partial(outgoing_kernel, lax.axis_size('wall')),...  1.65 us
  transfers between devices with their start and end apart: 8, of which 6 were waited for; matrix products, arithmetic and copies ran while one was open for 0% of the time, Pallas kernels for 13%

profile of v17, /device:TPU:0, one launch (start us, length us, event | category | flops | bytes accessed | tf_op | source)
XLA Modules:
  0.0 62.5 jit_solution(6496681929343258559)
XLA Ops:
  0.6 1.7 %outgoing_pass.1 = (f32[384,128]{1,0:T(8,128)}, f32[24,128]{1,0:T(8,128)}, f32[4,128]{1,0:T(4,128)}, f32[4,128]{1,0:T(4,128)}) custom-call(f32[192,128]{1,0:T(8,128)} %bitcast.12, s32[7,6]{1,0:T(8,128)} %list_ref.1, s32[1]{0:T(128)} %bitcast.5.place_ref, f32[4,768]{1,0:T(4,128)} %wall_ref.1, s32[6]{0:T(128)} %count_ref.1, s32[1]{0:T(128)} %bitcast.6.along_ref), custom_call_target="tpu_custom_call" | custom-call | tf_op jit(solution)/shard_map/outgoing_pass/pallas_call | solution.py:419
  2.3 0.0 copy-start
  2.3 7.4 %all-to-all-start = ((f32[8,48,128]{2,1,0:T(8,128)}), f32[8,48,128]{2,1,0:T(8,128)S(1)}, u32[]{:S(2)}, u32[]{:S(2)}) async-start(f32[8,48,128]{2,1,0:T(8,128)} %bitcast.15), calls=%async_computation | async-start | bytes 393216 | tf_op jit(solution)/shard_map/all_to_all | solution.py:461
  9.7 0.1 collective-permute-start
  9.8 0.6 copy-done.4
  10.4 1.0 %collective-permute-start.1 = (f32[4,128]{1,0:T(4,128)S(1)}, f32[4,128]{1,0:T(4,128)S(1)}, u32[]{:S(2)}, u32[]{:S(2)}) collective-permute-start(f32[4,128]{1,0:T(4,128)S(1)} %copy-done.4), channel_id=1, source_target_pairs={{1,2},{3,0},{2,1},{0,3},{5,6},{7,4},{6,5},{4,7},{9,10},{11,8},{10,... | collective-permute-start | bytes 6152 | tf_op jit(solution)/shard_map/ppermute | solution.py:449
  11.4 0.1 copy.10.pair_ref
  11.5 0.1 copy.9.wpair_ref
  11.6 0.0 collective-permute-done.edge0_ref
  11.6 1.8 %collective-permute-done.1.edge1_ref = f32[4,128]{1,0:T(4,128)S(1)} collective-permute-done((f32[4,128]{1,0:T(4,128)S(1)}, f32[4,128]{1,0:T(4,128)S(1)}, u32[]{:S(2)}, u32[]{:S(2)}) %collective-permute-start.1) | collective-permute-done | bytes 2080 | tf_op jit(solution)/shard_map/ppermute | solution.py:449
  13.4 8.0 %own_pass.1 = (bf16[24,128,96]{2,1,0:T(8,128)(2,1)S(1)}, f32[960,128]{1,0:T(8,128)S(1)}) custom-call(f32[192,128]{1,0:T(8,128)S(1)} %bitcast.13, f32[24,128]{1,0:T(8,128)S(1)} %copy-done.1, f32[4,128]{1,0:T(4,128)S(1)} %collective-permute-done.edge0_ref, f32[4,128]{1,0:T(4,128)S(1)} %collective-permute-done.1.edge1_ref, s32[24,4]{1,0:T(8,128)S(1)} %copy.9.wpair_ref, ...), custom_call_target="tpu_custom_call" | custom-call | flops 1572864000 | tf_op jit(solution)/shard_map/own_pass/pallas_call | solution.py:351
  21.4 0.0 all-to-all-done
  21.5 24.4 %fluid_pass.1 = (f32[24,128]{1,0:T(8,128)}, f32[3,3072]{1,0:T(4,128)}, f32[8,128]{1,0:T(8,128)S(1)}) custom-call(f32[192,128]{1,0:T(8,128)S(1)} %bitcast.14, f32[384,128]{1,0:T(8,128)S(1)} %bitcast.11, s32[24,14]{1,0:T(8,128)S(1)} %copy.10.pair_ref, s32[1]{0:T(128)} %bitcast.5.place_ref, bf16[24,128,96]{2,1,0:T(8,128)(2,1)S(1)} %get-tuple-element.16.tgt, ...), custom_call_target="tpu_custom_call" | custom-call | flops 5505024000 | tf_op jit(solution)/shard_map/fluid_pass/pallas_call | solution.py:369
  45.8 0.2 collective-permute-start.2
  46.0 0.9 %collective-permute-done.2 = f32[8,128]{1,0:T(8,128)S(1)} collective-permute-done((f32[8,128]{1,0:T(8,128)S(1)}, f32[8,128]{1,0:T(8,128)S(1)}, u32[]{:S(2)}, u32[]{:S(2)}) %collective-permute-start.2) | collective-permute-done | bytes 4128 | tf_op jit(solution)/shard_map/ppermute | solution.py:430
  47.0 1.3 %collective-permute-start.3 = (f32[8,128]{1,0:T(8,128)S(1)}, f32[8,128]{1,0:T(8,128)S(1)}, u32[]{:S(2)}, u32[]{:S(2)}) collective-permute-start(f32[8,128]{1,0:T(8,128)S(1)} %max.15), channel_id=1, source_target_pairs={{0,3},{1,2},{2,1},{3,0},{4,7},{5,6},{6,5},{7,4},{8,11},{9,10},{10,... | collective-permute-start | bytes 12296 | tf_op jit(solution)/shard_map/ppermute | solution.py:430
  48.3 1.7 %collective-permute-done.3 = f32[8,128]{1,0:T(8,128)S(1)} collective-permute-done((f32[8,128]{1,0:T(8,128)S(1)}, f32[8,128]{1,0:T(8,128)S(1)}, u32[]{:S(2)}, u32[]{:S(2)}) %collective-permute-start.3) | collective-permute-done | bytes 4128 | tf_op jit(solution)/shard_map/ppermute | solution.py:430
  50.0 1.8 %collective-permute-start.4 = (f32[8,128]{1,0:T(8,128)S(1)}, f32[8,128]{1,0:T(8,128)S(1)}, u32[]{:S(2)}, u32[]{:S(2)}) collective-permute-start(f32[8,128]{1,0:T(8,128)S(1)} %max.16), channel_id=1, source_target_pairs={{0,5},{1,4},{2,7},{3,6},{4,1},{5,0},{6,3},{7,2},{8,13},{9,12},{10,... | collective-permute-start | bytes 12296 | tf_op jit(solution)/shard_map/ppermute | solution.py:430
  51.8 1.3 %collective-permute-done.4 = f32[8,128]{1,0:T(8,128)S(1)} collective-permute-done((f32[8,128]{1,0:T(8,128)S(1)}, f32[8,128]{1,0:T(8,128)S(1)}, u32[]{:S(2)}, u32[]{:S(2)}) %collective-permute-start.4) | collective-permute-done | bytes 4128 | tf_op jit(solution)/shard_map/ppermute | solution.py:430
  53.2 1.7 %collective-permute-start.5 = (f32[8,128]{1,0:T(8,128)S(1)}, f32[8,128]{1,0:T(8,128)S(1)}, u32[]{:S(2)}, u32[]{:S(2)}) collective-permute-start(f32[8,128]{1,0:T(8,128)S(1)} %max.17), channel_id=1, source_target_pairs={{0,9},{1,8},{2,11},{3,10},{4,13},{5,12},{6,15},{7,14},{8,1},{9,0},... | collective-permute-start | bytes 12296 | tf_op jit(solution)/shard_map/ppermute | solution.py:430
  54.9 1.3 %collective-permute-done.5 = f32[8,128]{1,0:T(8,128)S(1)} collective-permute-done((f32[8,128]{1,0:T(8,128)S(1)}, f32[8,128]{1,0:T(8,128)S(1)}, u32[]{:S(2)}, u32[]{:S(2)}) %collective-permute-start.5) | collective-permute-done | bytes 4128 | tf_op jit(solution)/shard_map/ppermute | solution.py:430
  56.2 2.6 %collective-permute-start.6 = (f32[8,128]{1,0:T(8,128)S(1)}, f32[8,128]{1,0:T(8,128)S(1)}, u32[]{:S(2)}, u32[]{:S(2)}) collective-permute-start(f32[8,128]{1,0:T(8,128)S(1)} %max.18), channel_id=1, source_target_pairs={{0,17},{1,16},{2,19},{3,18},{4,21},{5,20},{6,23},{7,22},{8,25},{9,... | collective-permute-start | bytes 12296 | tf_op jit(solution)/shard_map/ppermute | solution.py:430
  58.8 1.3 %collective-permute-done.6 = f32[8,128]{1,0:T(8,128)S(1)} collective-permute-done((f32[8,128]{1,0:T(8,128)S(1)}, f32[8,128]{1,0:T(8,128)S(1)}, u32[]{:S(2)}, u32[]{:S(2)}) %collective-permute-start.6) | collective-permute-done | bytes 4128 | tf_op jit(solution)/shard_map/ppermute | solution.py:430
  60.1 0.5 slice.3
  (15 shorter events, 0.0 us)
Async XLA Ops:
  2.3 7.4 %copy-start.5 = (f32[4,128]{1,0:T(4,128)S(1)}, f32[4,128]{1,0:T(4,128)}, u32[]{:S(2)}) copy-start(f32[4,128]{1,0:T(4,128)} %get-tuple-element.14) | copy-start | bytes 6148
  2.3 9.1 %copy-start.2 = (s32[24,14]{0,1:T(8,128)S(1)}, s32[24,14]{0,1:T(8,128)}, u32[]{:S(2)}) copy-start(s32[24,14]{0,1:T(8,128)} %param.8) | copy-start | bytes 4036
  2.3 11.1 %copy-start = (f32[8,3072]{1,0:T(8,128)S(1)}, f32[8,3072]{1,0:T(8,128)}, u32[]{:S(2)}) copy-start(f32[8,3072]{1,0:T(8,128)} %param.6) | copy-start | bytes 294916
  2.3 19.1 %all-to-all-start = ((f32[8,48,128]{2,1,0:T(8,128)}), f32[8,48,128]{2,1,0:T(8,128)S(1)}, u32[]{:S(2)}, u32[]{:S(2)}) async-start(f32[8,48,128]{2,1,0:T(8,128)} %bitcast.15), calls=%async_computation | async-start | bytes 393216 | tf_op jit(solution)/shard_map/all_to_all | solution.py:461
  9.7 0.7 %copy-start.4 = (f32[4,128]{1,0:T(4,128)S(1)}, f32[4,128]{1,0:T(4,128)}, u32[]{:S(2)}) copy-start(f32[4,128]{1,0:T(4,128)} %get-tuple-element.15) | copy-start | bytes 6148
  9.7 1.9 %collective-permute-start = (f32[4,128]{1,0:T(4,128)S(1)}, f32[4,128]{1,0:T(4,128)S(1)}, u32[]{:S(2)}, u32[]{:S(2)}) collective-permute-start(f32[4,128]{1,0:T(4,128)S(1)} %copy-done.5), channel_id=1, source_target_pairs={{0,1},{2,3},{1,0},{3,2},{4,5},{6,7},{5,4},{7,6},{8,9},{10,11},{9,8... | collective-permute-start | bytes 6152 | tf_op jit(solution)/shard_map/ppermute | solution.py:449
  10.4 1.1 %copy-start.3 = (s32[24,4]{0,1:T(4,128)S(1)}, s32[24,4]{0,1:T(4,128)}, u32[]{:S(2)}) copy-start(s32[24,4]{0,1:T(4,128)} %param.11) | copy-start | bytes 1156
  10.4 3.0 %collective-permute-start.1 = (f32[4,128]{1,0:T(4,128)S(1)}, f32[4,128]{1,0:T(4,128)S(1)}, u32[]{:S(2)}, u32[]{:S(2)}) collective-permute-start(f32[4,128]{1,0:T(4,128)S(1)} %copy-done.4), channel_id=1, source_target_pairs={{1,2},{3,0},{2,1},{0,3},{5,6},{7,4},{6,5},{4,7},{9,10},{11,8},{10,... | collective-permute-start | bytes 6152 | tf_op jit(solution)/shard_map/ppermute | solution.py:449
  11.5 1.9 %copy-start.1 = (f32[24,128]{1,0:T(8,128)S(1)}, f32[24,128]{1,0:T(8,128)}, u32[]{:S(2)}) copy-start(f32[24,128]{1,0:T(8,128)} %get-tuple-element.13.wall_ref) | copy-start | bytes 36868
  45.8 1.2 %collective-permute-start.2 = (f32[8,128]{1,0:T(8,128)S(1)}, f32[8,128]{1,0:T(8,128)S(1)}, u32[]{:S(2)}, u32[]{:S(2)}) collective-permute-start(f32[8,128]{1,0:T(8,128)S(1)} %get-tuple-element.20), channel_id=1, source_target_pairs={{0,1},{1,0},{2,3},{3,2},{4,5},{5,4},{6,7},{7,6},{8,9},{9,8},{10,11... | collective-permute-start | bytes 12296 | tf_op jit(solution)/shard_map/ppermute | solution.py:430
  47.0 3.0 %collective-permute-start.3 = (f32[8,128]{1,0:T(8,128)S(1)}, f32[8,128]{1,0:T(8,128)S(1)}, u32[]{:S(2)}, u32[]{:S(2)}) collective-permute-start(f32[8,128]{1,0:T(8,128)S(1)} %max.15), channel_id=1, source_target_pairs={{0,3},{1,2},{2,1},{3,0},{4,7},{5,6},{6,5},{7,4},{8,11},{9,10},{10,... | collective-permute-start | bytes 12296 | tf_op jit(solution)/shard_map/ppermute | solution.py:430
  50.0 3.1 %collective-permute-start.4 = (f32[8,128]{1,0:T(8,128)S(1)}, f32[8,128]{1,0:T(8,128)S(1)}, u32[]{:S(2)}, u32[]{:S(2)}) collective-permute-start(f32[8,128]{1,0:T(8,128)S(1)} %max.16), channel_id=1, source_target_pairs={{0,5},{1,4},{2,7},{3,6},{4,1},{5,0},{6,3},{7,2},{8,13},{9,12},{10,... | collective-permute-start | bytes 12296 | tf_op jit(solution)/shard_map/ppermute | solution.py:430
  53.2 3.0 %collective-permute-start.5 = (f32[8,128]{1,0:T(8,128)S(1)}, f32[8,128]{1,0:T(8,128)S(1)}, u32[]{:S(2)}, u32[]{:S(2)}) collective-permute-start(f32[8,128]{1,0:T(8,128)S(1)} %max.17), channel_id=1, source_target_pairs={{0,9},{1,8},{2,11},{3,10},{4,13},{5,12},{6,15},{7,14},{8,1},{9,0},... | collective-permute-start | bytes 12296 | tf_op jit(solution)/shard_map/ppermute | solution.py:430
  56.2 3.9 %collective-permute-start.6 = (f32[8,128]{1,0:T(8,128)S(1)}, f32[8,128]{1,0:T(8,128)S(1)}, u32[]{:S(2)}, u32[]{:S(2)}) collective-permute-start(f32[8,128]{1,0:T(8,128)S(1)} %max.18), channel_id=1, source_target_pairs={{0,17},{1,16},{2,19},{3,18},{4,21},{5,20},{6,23},{7,22},{8,25},{9,... | collective-permute-start | bytes 12296 | tf_op jit(solution)/shard_map/ppermute | solution.py:430
